TPU v7x, 256 devices: a whole 4x4x8 slice. The times are simulated.
256 devices in a mesh: facet: 8 (over y, z_hi), tile: 32 (over x, z_lo, core).
Axes of the slice: x: 4, y: 4, z: 8 (z_hi: 2, z_lo: 4; z = z_hi * 4 + z_lo), core: 2. Of those that a mesh axis runs over, the one named last changes fastest.
Arguments:
- sectioned_rows: bfloat16 [8, 512, 2048], P('facet', 'tile'), may hold values from -6 to 6
- reader: int32 [32, 8], P('tile'), may hold values from 0 to 7, each once within a row
- baseline_coords: float32 [8, 2, 512], P(None, None, 'tile'), may hold values from -8 to 8
- subgrid_index: int32 [8, 512], P(None, 'tile'), may hold values from 0 to 127
- stations: int32 [8, 2, 512], P(None, None, 'tile'), may hold values from 0 to 511
- plane_index: int32 [8, 512], P(None, 'tile'), may hold values from 0 to 31
- model_grid: bfloat16 [8, 128, 2048], P('facet', 'tile'), may hold values from -0.1875 to 0.1875
- beam_screens: bfloat16 [8, 512, 2048], P('facet'), may hold values from -3.5 to 3.5
- plane_phase: float32 [32, 1024], replicated, may hold values from -3.140625 to 3.140625
- channel_freq: float32 [1024], replicated, may hold values from 0.25 to 1.75
Outputs:
- residual: float32 [8, 512, 2048], P('facet', 'tile')
- dirty_grid: float32 [8, 128, 2048], P('facet', 'tile')
Inputs may be any that keep to these rules, and one draw needn't show every extreme that they name: `reader`: for each run of baselines, each facet group read exactly one block.
All inputs are finite; a program needn't handle non-finite values.
Results may differ from a plain program's by a relative error of at most 0.0033.
Values may be sent and summed in bfloat16 or wider, within the bound.
No kernel may reach another device: no remote copies, remote signals or barrier semaphores. Data moves between devices by JAX's collectives and lax.ppermute only.
A program may use at most 128 MiB of HBM per device.

v0:
```python
import math

import jax
import jax.numpy as jnp
from jax import lax
from jax.sharding import PartitionSpec as P

TWO_PI = 2.0 * math.pi


def phasor_tables(coords, channel_freq, edge_cells):
    offsets = (jnp.arange(edge_cells, dtype=jnp.float32) - edge_cells // 2) / edge_cells
    angles = TWO_PI * coords[:, None, None] * offsets[None, :, None] * channel_freq[None, None, :]
    return (jnp.cos(angles).astype(jnp.bfloat16), jnp.sin(angles).astype(jnp.bfloat16))


def north_matrix(north_cos, north_sin):
    upper_half = jnp.concatenate([north_cos, north_sin], axis=2)
    lower_half = jnp.concatenate([-north_sin, north_cos], axis=2)
    return jnp.concatenate([upper_half, lower_half], axis=1)


def screen_parts(screens, station_pair, plane_rows, plane_phase):
    pixels = plane_phase.shape[1]
    station_one = screens[station_pair[0]].astype(jnp.float32)
    station_two = screens[station_pair[1]].astype(jnp.float32)
    one_re, one_im = (station_one[:, :pixels], station_one[:, pixels:])
    two_re, two_im = (station_two[:, :pixels], station_two[:, pixels:])
    pair_re = one_re * two_re + one_im * two_im
    pair_im = one_im * two_re - one_re * two_im
    angles = plane_phase[plane_rows]
    wave_re, wave_im = (jnp.cos(angles), jnp.sin(angles))
    return (pair_re * wave_re - pair_im * wave_im, pair_re * wave_im + pair_im * wave_re)


def degrid_rows(model_rows, screen_re, screen_im, east_cos, east_sin, north_mat):
    row_count = model_rows.shape[0]
    pixels = model_rows.shape[1] // 2
    edge_cells = east_cos.shape[1]
    channels = east_cos.shape[2]
    model_f = model_rows.astype(jnp.float32)
    model_re, model_im = (model_f[:, :pixels], model_f[:, pixels:])
    image_re = screen_re * model_re - screen_im * model_im
    image_im = screen_re * model_im + screen_im * model_re
    operand = jnp.concatenate(
        [
            image_re.reshape(row_count, edge_cells, edge_cells),
            image_im.reshape(row_count, edge_cells, edge_cells),
        ],
        axis=2,
    ).astype(jnp.bfloat16)
    inner_sum = jnp.einsum("rxy,ryc->rxc", operand, north_mat, preferred_element_type=jnp.float32)
    inner_re, inner_im = (inner_sum[:, :, :channels], inner_sum[:, :, channels:])
    cos_f, sin_f = (east_cos.astype(jnp.float32), east_sin.astype(jnp.float32))
    vis_re = jnp.sum(cos_f * inner_re - sin_f * inner_im, axis=1)
    vis_im = jnp.sum(cos_f * inner_im + sin_f * inner_re, axis=1)
    return jnp.concatenate([vis_re, vis_im], axis=1)


def grid_rows(resid_rows, screen_re, screen_im, east_cos, east_sin, north_mat, grid_scale):
    row_count = resid_rows.shape[0]
    edge_cells = east_cos.shape[1]
    channels = east_cos.shape[2]
    resid_re, resid_im = (resid_rows[:, None, :channels], resid_rows[:, None, channels:])
    cos_f, sin_f = (east_cos.astype(jnp.float32), east_sin.astype(jnp.float32))
    weighted_re = cos_f * resid_re + sin_f * resid_im
    weighted_im = cos_f * resid_im - sin_f * resid_re
    operand = jnp.concatenate([weighted_re, weighted_im], axis=2).astype(jnp.bfloat16)
    gridded = jnp.einsum("rxc,ryc->rxy", operand, north_mat, preferred_element_type=jnp.float32)
    grid_re = gridded[:, :, :edge_cells].reshape(row_count, edge_cells * edge_cells)
    grid_im = gridded[:, :, edge_cells:].reshape(row_count, edge_cells * edge_cells)
    out_re = (screen_re * grid_re + screen_im * grid_im) * grid_scale
    out_im = (screen_re * grid_im - screen_im * grid_re) * grid_scale
    return jnp.concatenate([out_re, out_im], axis=1).astype(jnp.bfloat16)


def local(
    sectioned_rows,
    reader,
    baseline_coords,
    subgrid_index,
    stations,
    plane_index,
    model_grid,
    beam_screens,
    plane_phase,
    channel_freq,
):
    n_facet = lax.axis_size("facet")
    n_tile = lax.axis_size("tile")
    facet_id = lax.axis_index("facet")
    channels = channel_freq.shape[0]
    pixels = plane_phase.shape[1]
    edge_cells = math.isqrt(pixels)
    row_block = sectioned_rows.shape[1]
    owned = model_grid.shape[1]
    subgrid_count = owned * n_tile
    grid_scale = 1.0 / math.sqrt(channels * n_facet * (row_block * n_tile) / subgrid_count)
    arrived = lax.all_gather(sectioned_rows, "facet", axis=0, tiled=True)
    visible = jnp.take(arrived, reader[0], axis=0)
    model_all = lax.all_gather(model_grid, "tile", axis=1, tiled=True)[0]
    screens_own = beam_screens[0]
    block_ids = jnp.arange(n_facet, dtype=jnp.int32)

    def geometry(block_id):
        east_cos, east_sin = phasor_tables(baseline_coords[block_id, 0], channel_freq, edge_cells)
        north_cos, north_sin = phasor_tables(baseline_coords[block_id, 1], channel_freq, edge_cells)
        screen_re, screen_im = screen_parts(
            screens_own, stations[block_id], plane_index[block_id], plane_phase
        )
        return (east_cos, east_sin, north_matrix(north_cos, north_sin), screen_re, screen_im)

    tables = lax.map(geometry, block_ids)

    def predict(inputs):
        rows_sub, east_cos, east_sin, north_mat, screen_re, screen_im = inputs
        return degrid_rows(model_all[rows_sub], screen_re, screen_im, east_cos, east_sin, north_mat)

    predicted = lax.map(predict, (subgrid_index,) + tuple(tables))
    total = lax.psum(predicted, "facet")
    resid_all = visible.astype(jnp.float32) - total
    mine = lax.dynamic_index_in_dim(resid_all, facet_id, 0, keepdims=True)

    def regrid(inputs):
        resid_block, east_cos, east_sin, north_mat, screen_re, screen_im = inputs
        return grid_rows(
            resid_block, screen_re, screen_im, east_cos, east_sin, north_mat, grid_scale
        )

    regridded = lax.map(regrid, (resid_all,) + tuple(tables)).reshape(
        n_facet * row_block, 2 * pixels
    )
    targets = subgrid_index.reshape(-1)
    onehot = (jnp.arange(subgrid_count, dtype=jnp.int32)[:, None] == targets[None, :]).astype(
        jnp.bfloat16
    )
    partial_sums = jnp.dot(onehot, regridded, preferred_element_type=jnp.float32)
    dirty = lax.psum_scatter(partial_sums, "tile", scatter_dimension=0, tiled=True)
    return (mine, dirty[None])


def solution(mesh):
    return jax.shard_map(
        local,
        mesh=mesh,
        in_specs=(
            P("facet", "tile", None),
            P("tile", None),
            P(None, None, "tile"),
            P(None, "tile"),
            P(None, None, "tile"),
            P(None, "tile"),
            P("facet", "tile", None),
            P("facet", None, None),
            P(),
            P(),
        ),
        out_specs=(P("facet", "tile", None), P("facet", "tile", None)),
        check_vma=False,
    )
```

profile of v0, /device:TPU:1, one launch (start us, length us, event | category | flops | bytes accessed | tf_op | source)
XLA Modules:
  0.0 893.0 jit_solution(12168331247861420813)
XLA Ops:
  7.3 288.3 %while.40 = (s32[]{:T(128)}, bf16[8,16,32,1024]{3,2,1,0:T(8,128)(2,1)}, bf16[8,16,32,1024]{3,2,1,0:T(8,128)(2,1)}, bf16[8,16,64,2048]{3,2,1,0:T(8,128)(2,1)}, f3...) while((s32[]{:T(128)}, ...), condition=%wide.region_1.2_spmd, body=%wide.region_0.1_spmd.sunk | while | flops 22810868 | bytes 23451556 | solution.py:113
  10.9 8.7 fusion.76
  19.6 7.9 fusion.77
  29.8 8.8 fusion.75
  46.9 8.7 fusion.76
  55.7 7.9 fusion.77
  65.9 8.7 fusion.75
  83.0 8.7 fusion.76
  91.7 7.9 fusion.77
  101.9 8.8 fusion.75
  119.0 8.7 fusion.76
  127.8 7.9 fusion.77
  137.9 8.8 fusion.75
  155.1 8.7 fusion.76
  163.8 7.9 fusion.77
  173.9 8.7 fusion.75
  191.1 8.7 fusion.76
  199.8 7.9 fusion.77
  210.0 8.7 fusion.75
  227.1 8.7 fusion.76
  235.8 7.9 fusion.77
  246.0 8.8 fusion.75
  263.2 8.7 fusion.76
  271.9 7.9 fusion.77
  282.0 8.8 fusion.75
  295.6 50.7 %all_gather.7 = bf16[1,128,2048]{2,0,1:T(2,128)(2,1)S(1)} all-gather(bf16[1,4,2048]{2,0,1:T(2,128)(2,1)S(1)} %copy.13), channel_id=1, replica_groups=mesh['facet'=8,'tile'=32] {'tile'}, dimensions={1}, use_global_device_ids=true | all-gather | bytes 540672 | tf_op jit(solution)/shard_map/all_gather | solution.py:101
  346.7 64.9 %while.41 = (s32[]{:T(128)}, f32[8,16,2048]{2,1,0:T(8,128)}, bf16[8,16,32,1024]{3,2,1,0:T(8,128)(2,1)}, f32[8,16,1024]{2,1,0:T(8,128)}, s32[8,16]{1,0:T(8,128)S(...) while((s32[]{:T(128)}, f32[8,16,2048]{2,1,0:T(8,128)}, ...), condition=%wide.region_5.6_spmd, body=%wide.region_2.5_spmd.sunk | while | flops 139756592 | bytes 15930737 | solution.py:119
  348.6 3.0 fusion.85
  351.6 2.6 fusion.86
  356.7 3.0 fusion.85
  364.8 3.0 fusion.85
  372.9 3.0 fusion.85
  381.0 3.0 fusion.85
  389.2 3.0 fusion.85
  397.3 3.0 fusion.85
  405.4 3.0 fusion.85
  411.8 55.6 %all_gather.6 = bf16[8,16,2048]{2,1,0:T(8,128)(2,1)S(1)} all-gather(bf16[1,16,2048]{2,1,0:T(8,128)(2,1)S(1)} %copy-done.3), channel_id=1, replica_groups=mesh['facet'=8,'tile'=32] {'facet'}, dimensions={0}, use_global_device_ids=true | all-gather | bytes 589824 | tf_op jit(solution)/shard_map/all_gather | solution.py:99
  468.1 81.8 %all-reduce.4.cloned.1.call-done = f32[8,16,2048]{2,1,0:T(8,128)} async-done(((f32[8,16,2048]{2,1,0:T(8,128)}), f32[8,16,2048]{2,1,0:T(8,128)}) %all-reduce.4.cloned.1.call-update) | async-done | bytes 1048592 | tf_op jit(solution)/shard_map/psum | solution.py:120
  551.3 57.2 %while.42 = (s32[]{:T(128)}, bf16[8,16,2048]{2,1,0:T(8,128)(2,1)S(1)}, f32[8,16,1024]{2,1,0:T(8,128)}, bf16[8,16,32,1024]{3,2,1,0:T(8,128)(2,1)}, f32[8,16,2048]...) while((s32[]{:T(128)}, ...), condition=%wide.region_8.9_spmd, body=%wide.region_7.8_spmd.sunk | while | flops 143949824 | bytes 12255853 | solution.py:130
  553.7 3.4 fusion.92
  560.8 3.4 fusion.92
  568.0 3.4 fusion.92
  575.1 3.4 fusion.92
  582.3 3.4 fusion.92
  589.4 3.4 fusion.92
  596.6 3.4 fusion.92
  603.7 3.4 fusion.92
  611.7 272.9 %all-reduce.6.cloned.1.call-done = f32[128,2048]{1,0:T(8,128)} async-done(((f32[128,2048]{1,0:T(8,128)}), f32[128,2048]{1,0:T(8,128)}) %all-reduce.6.cloned.1.call-update) | async-done | bytes 1048592
  (361 shorter events, 141.8 us)
Async XLA Ops:
  7.2 542.7 %all-reduce.4.cloned.1.call-start = ((), (), s32[]{:S(2)}) async-start(), calls=%async_computation | async-start | bytes 2097152 | tf_op jit(solution)/shard_map/psum | solution.py:120
  7.3 288.3 %copy-start.4 = (bf16[1,4,2048]{2,1,0:T(4,128)(2,1)S(1)}, bf16[1,4,2048]{2,1,0:T(4,128)(2,1)}, u32[]{:S(2)}) copy-start(bf16[1,4,2048]{2,1,0:T(4,128)(2,1)} %param.22) | copy-start | bytes 49156
  7.3 339.4 %copy-start.5 = (s32[8,16]{1,0:T(8,128)S(1)}, s32[8,16]{1,0:T(8,128)}, u32[]{:S(2)}) copy-start(s32[8,16]{1,0:T(8,128)} %param.19) | copy-start | bytes 1540
  19.6 10.2 %copy-start.2 = (f32[1024]{0:T(1024)S(1)}, f32[1024]{0:T(1024)}, u32[]{:S(2)}) copy-start(f32[1024]{0:T(1024)} %get-tuple-element.630) | copy-start | bytes 12292 | tf_op jit(solution)/shard_map/while
  27.6 12.3 %copy-start = (f32[32,1024]{1,0:T(8,128)S(1)}, f32[32,1024]{1,0:T(8,128)}, u32[]{:S(2)}) copy-start(f32[32,1024]{1,0:T(8,128)} %get-tuple-element.634) | copy-start | bytes 393220 | tf_op jit(solution)/shard_map/while
  27.6 13.2 %copy-start.1 = (bf16[512,2048]{1,0:T(8,128)(2,1)S(1)}, bf16[512,2048]{1,0:T(8,128)(2,1)}, u32[]{:S(2)}) copy-start(bf16[512,2048]{1,0:T(8,128)(2,1)} %get-tuple-element.632) | copy-start | bytes 6291460 | tf_op jit(solution)/shard_map/while
  55.7 10.2 %copy-start.2 = (f32[1024]{0:T(1024)S(1)}, f32[1024]{0:T(1024)}, u32[]{:S(2)}) copy-start(f32[1024]{0:T(1024)} %get-tuple-element.630) | copy-start | bytes 12292 | tf_op jit(solution)/shard_map/while
  63.6 12.4 %copy-start = (f32[32,1024]{1,0:T(8,128)S(1)}, f32[32,1024]{1,0:T(8,128)}, u32[]{:S(2)}) copy-start(f32[32,1024]{1,0:T(8,128)} %get-tuple-element.634) | copy-start | bytes 393220 | tf_op jit(solution)/shard_map/while
  63.6 13.2 %copy-start.1 = (bf16[512,2048]{1,0:T(8,128)(2,1)S(1)}, bf16[512,2048]{1,0:T(8,128)(2,1)}, u32[]{:S(2)}) copy-start(bf16[512,2048]{1,0:T(8,128)(2,1)} %get-tuple-element.632) | copy-start | bytes 6291460 | tf_op jit(solution)/shard_map/while
  91.7 10.2 %copy-start.2 = (f32[1024]{0:T(1024)S(1)}, f32[1024]{0:T(1024)}, u32[]{:S(2)}) copy-start(f32[1024]{0:T(1024)} %get-tuple-element.630) | copy-start | bytes 12292 | tf_op jit(solution)/shard_map/while
  99.7 12.3 %copy-start = (f32[32,1024]{1,0:T(8,128)S(1)}, f32[32,1024]{1,0:T(8,128)}, u32[]{:S(2)}) copy-start(f32[32,1024]{1,0:T(8,128)} %get-tuple-element.634) | copy-start | bytes 393220 | tf_op jit(solution)/shard_map/while
  99.7 13.2 %copy-start.1 = (bf16[512,2048]{1,0:T(8,128)(2,1)S(1)}, bf16[512,2048]{1,0:T(8,128)(2,1)}, u32[]{:S(2)}) copy-start(bf16[512,2048]{1,0:T(8,128)(2,1)} %get-tuple-element.632) | copy-start | bytes 6291460 | tf_op jit(solution)/shard_map/while
  127.8 10.1 %copy-start.2 = (f32[1024]{0:T(1024)S(1)}, f32[1024]{0:T(1024)}, u32[]{:S(2)}) copy-start(f32[1024]{0:T(1024)} %get-tuple-element.630) | copy-start | bytes 12292 | tf_op jit(solution)/shard_map/while
  135.7 12.3 %copy-start = (f32[32,1024]{1,0:T(8,128)S(1)}, f32[32,1024]{1,0:T(8,128)}, u32[]{:S(2)}) copy-start(f32[32,1024]{1,0:T(8,128)} %get-tuple-element.634) | copy-start | bytes 393220 | tf_op jit(solution)/shard_map/while
  135.7 13.2 %copy-start.1 = (bf16[512,2048]{1,0:T(8,128)(2,1)S(1)}, bf16[512,2048]{1,0:T(8,128)(2,1)}, u32[]{:S(2)}) copy-start(bf16[512,2048]{1,0:T(8,128)(2,1)} %get-tuple-element.632) | copy-start | bytes 6291460 | tf_op jit(solution)/shard_map/while
  163.8 10.2 %copy-start.2 = (f32[1024]{0:T(1024)S(1)}, f32[1024]{0:T(1024)}, u32[]{:S(2)}) copy-start(f32[1024]{0:T(1024)} %get-tuple-element.630) | copy-start | bytes 12292 | tf_op jit(solution)/shard_map/while
  171.7 12.3 %copy-start = (f32[32,1024]{1,0:T(8,128)S(1)}, f32[32,1024]{1,0:T(8,128)}, u32[]{:S(2)}) copy-start(f32[32,1024]{1,0:T(8,128)} %get-tuple-element.634) | copy-start | bytes 393220 | tf_op jit(solution)/shard_map/while
  171.8 13.2 %copy-start.1 = (bf16[512,2048]{1,0:T(8,128)(2,1)S(1)}, bf16[512,2048]{1,0:T(8,128)(2,1)}, u32[]{:S(2)}) copy-start(bf16[512,2048]{1,0:T(8,128)(2,1)} %get-tuple-element.632) | copy-start | bytes 6291460 | tf_op jit(solution)/shard_map/while
  199.8 10.2 %copy-start.2 = (f32[1024]{0:T(1024)S(1)}, f32[1024]{0:T(1024)}, u32[]{:S(2)}) copy-start(f32[1024]{0:T(1024)} %get-tuple-element.630) | copy-start | bytes 12292 | tf_op jit(solution)/shard_map/while
  207.8 12.4 %copy-start = (f32[32,1024]{1,0:T(8,128)S(1)}, f32[32,1024]{1,0:T(8,128)}, u32[]{:S(2)}) copy-start(f32[32,1024]{1,0:T(8,128)} %get-tuple-element.634) | copy-start | bytes 393220 | tf_op jit(solution)/shard_map/while
  207.8 13.2 %copy-start.1 = (bf16[512,2048]{1,0:T(8,128)(2,1)S(1)}, bf16[512,2048]{1,0:T(8,128)(2,1)}, u32[]{:S(2)}) copy-start(bf16[512,2048]{1,0:T(8,128)(2,1)} %get-tuple-element.632) | copy-start | bytes 6291460 | tf_op jit(solution)/shard_map/while
  235.8 10.2 %copy-start.2 = (f32[1024]{0:T(1024)S(1)}, f32[1024]{0:T(1024)}, u32[]{:S(2)}) copy-start(f32[1024]{0:T(1024)} %get-tuple-element.630) | copy-start | bytes 12292 | tf_op jit(solution)/shard_map/while
  243.8 12.4 %copy-start = (f32[32,1024]{1,0:T(8,128)S(1)}, f32[32,1024]{1,0:T(8,128)}, u32[]{:S(2)}) copy-start(f32[32,1024]{1,0:T(8,128)} %get-tuple-element.634) | copy-start | bytes 393220 | tf_op jit(solution)/shard_map/while
  243.8 13.2 %copy-start.1 = (bf16[512,2048]{1,0:T(8,128)(2,1)S(1)}, bf16[512,2048]{1,0:T(8,128)(2,1)}, u32[]{:S(2)}) copy-start(bf16[512,2048]{1,0:T(8,128)(2,1)} %get-tuple-element.632) | copy-start | bytes 6291460 | tf_op jit(solution)/shard_map/while
  271.9 10.1 %copy-start.2 = (f32[1024]{0:T(1024)S(1)}, f32[1024]{0:T(1024)}, u32[]{:S(2)}) copy-start(f32[1024]{0:T(1024)} %get-tuple-element.630) | copy-start | bytes 12292 | tf_op jit(solution)/shard_map/while
  279.8 12.3 %copy-start = (f32[32,1024]{1,0:T(8,128)S(1)}, f32[32,1024]{1,0:T(8,128)}, u32[]{:S(2)}) copy-start(f32[32,1024]{1,0:T(8,128)} %get-tuple-element.634) | copy-start | bytes 393220 | tf_op jit(solution)/shard_map/while
  279.9 13.2 %copy-start.1 = (bf16[512,2048]{1,0:T(8,128)(2,1)S(1)}, bf16[512,2048]{1,0:T(8,128)(2,1)}, u32[]{:S(2)}) copy-start(bf16[512,2048]{1,0:T(8,128)(2,1)} %get-tuple-element.632) | copy-start | bytes 6291460 | tf_op jit(solution)/shard_map/while
  346.7 65.1 %copy-start.6 = (s32[1,8]{1,0:T(1,128)S(1)}, s32[1,8]{1,0:T(1,128)}, u32[]{:S(2)}) copy-start(s32[1,8]{1,0:T(1,128)} %param.17) | copy-start | bytes 100
  346.7 65.1 %copy-start.3 = (bf16[1,16,2048]{2,1,0:T(8,128)(2,1)S(1)}, bf16[1,16,2048]{2,1,0:T(8,128)(2,1)}, u32[]{:S(2)}) copy-start(bf16[1,16,2048]{2,1,0:T(8,128)(2,1)} %param.16) | copy-start | bytes 196612
  411.7 473.0 %all-reduce.6.cloned.1.call-start = ((), (), s32[]{:S(2)}) async-start(), calls=%async_computation.1 | async-start | bytes 2097152
  551.3 58.5 %copy-start.7 = (u32[256]{0:T(256)S(1)}, u32[256]{0:T(256)}, u32[]{:S(2)}) copy-start(u32[256]{0:T(256)} %constant.137) | copy-start | bytes 3076
Sparse Core Ops, SparseCore 0:
  411.8 138.0 all-reduce.3
  609.9 274.7 all-reduce.5
where the time goes:
time: 896 us; the launch traced here: 893 us
  waiting for transfers between devices  355 us (40%)
  other arithmetic  305 us (34%)
  blocking collectives  106 us (12%)
  matrix products  52.3 us (6%)
  local copies, waits for them, and re-layouts  41.6 us (5%)
  loops' own time  18.2 us (2%)
  between operations  14.9 us (2%)
    unnamed x3, waiting for transfers between devices  273 us
    dynamic_update_slice x32, other arithmetic, local(): tables = lax.map(geometry, block_ids)  97.9 us
    psum x1, waiting for transfers between devices, local(): total = lax.psum(predicted, 'facet')  81.8 us
    convert_element_type x8, other arithmetic, phasor_tables(): jnp.sin(angles).astype(jnp.bfloat16)  69.8 us
    neg x8, other arithmetic, north_matrix(): lower_half = jnp.concatenate([-north_sin, north_cos], axis=2)  63.5 us
    all_gather x1, blocking collectives, local(): arrived = lax.all_gather(sectioned_rows, 'facet', axis=0, tiled=True)  55.6 us
    all_gather x1, blocking collectives, local(): model_all = lax.all_gather(model_grid, 'tile', axis=1, tiled=True)[0]  50.7 us
    another operation x28, other arithmetic  32.9 us
  transfers between devices with their start and end apart: 2, of which 2 were waited for; matrix products, arithmetic and copies ran while one was open for 0% of the time, Pallas kernels for 0%

commit v1 on v0

v1 whole, which is shorter than its diff:
```python
import math

import jax
import jax.numpy as jnp
from jax import lax
from jax.experimental import pallas as pl
from jax.experimental.pallas import tpu as pltpu
from jax.sharding import Mesh
from jax.sharding import PartitionSpec as P

TWO_PI = 2.0 * math.pi
F32 = jnp.float32
BF16 = jnp.bfloat16
FACET = ("y", "h")
TILE = ("x", "z", "c")
VMEM = pl.BlockSpec(memory_space=pltpu.VMEM)


def params(mib):
    return pltpu.CompilerParams(vmem_limit_bytes=mib << 20)


def cmul(a, b):
    return (a[0] * b[0] - a[1] * b[1], a[0] * b[1] + a[1] * b[0])


def conj(a):
    return (a[0], -a[1])


def onehot_rows(column, count):
    lanes = lax.broadcasted_iota(jnp.int32, (column.shape[0], count), 1)
    return jnp.where(column == lanes, 1.0, 0.0).astype(BF16)


def screen_kernel(index_ref, phase_ref, beam_ref, screen_ref):
    stations = beam_ref.shape[0]
    planes, pixels = phase_ref.shape
    one = onehot_rows(index_ref[:, 0:1], stations)
    two = onehot_rows(index_ref[:, 1:2], stations)
    plane = onehot_rows(index_ref[:, 2:3], planes).astype(F32)
    width = 256
    for at in range(0, pixels, width):
        re, im = pl.ds(at, width), pl.ds(pixels + at, width)
        one_re = jnp.dot(one, beam_ref[:, re], preferred_element_type=F32)
        one_im = jnp.dot(one, beam_ref[:, im], preferred_element_type=F32)
        two_re = jnp.dot(two, beam_ref[:, re], preferred_element_type=F32)
        two_im = jnp.dot(two, beam_ref[:, im], preferred_element_type=F32)
        pair_re = one_re * two_re + one_im * two_im
        pair_im = one_im * two_re - one_re * two_im
        phase = phase_ref[:, re]
        exact = lax.Precision.HIGHEST
        wave_re = jnp.dot(plane, jnp.cos(phase), precision=exact, preferred_element_type=F32)
        wave_im = jnp.dot(plane, jnp.sin(phase), precision=exact, preferred_element_type=F32)
        screen_ref[:, re] = pair_re * wave_re - pair_im * wave_im
        screen_ref[:, im] = pair_re * wave_im + pair_im * wave_re


def table_kernel(coords_ref, freq_ref, east_ref, north_re_ref, north_im_ref, *powers):
    rows = coords_ref.shape[0] // 2
    angle = (TWO_PI * coords_ref[...]) * (1.0 / 32.0) * freq_ref[...]
    z1 = (jnp.cos(angle), jnp.sin(angle))
    z2 = cmul(z1, z1)
    z4 = cmul(z2, z2)
    z8 = cmul(z4, z4)
    z16 = cmul(z8, z8)
    low16 = conj(z16)
    for at, value in enumerate((z1, z2, z4, z8, z16)):
        powers[0][2 * at] = value[0]
        powers[0][2 * at + 1] = value[1]
    for at, value in enumerate((low16, cmul(low16, z1), cmul(low16, z2), cmul(low16, cmul(z1, z2)))):
        powers[1][2 * at] = value[0]
        powers[1][2 * at + 1] = value[1]
    sub = lax.broadcasted_iota(jnp.int32, (8, angle.shape[1]), 0)

    def row_of(ref, at, row):
        return (ref[2 * at, pl.ds(row, 1), :], ref[2 * at + 1, pl.ds(row, 1), :])

    def picked(factor, bit):
        on = (sub & bit) != 0
        return (jnp.where(on, factor[0], 1.0), jnp.where(on, factor[1], 0.0))

    def bits(factors):
        return cmul(cmul(picked(factors[0], 1), picked(factors[1], 2)), picked(factors[2], 4))

    def body(b, carry):
        base = bits([row_of(powers[0], at, b) for at in (2, 3, 4)])
        parts = [cmul(base, row_of(powers[1], at, b)) for at in range(4)]
        cos = jnp.concatenate([part[0] for part in parts], axis=0)
        sin = jnp.concatenate([part[1] for part in parts], axis=0)
        east_ref[b] = jnp.concatenate([cos, sin], axis=0).astype(BF16)
        row = b + rows
        base = bits([row_of(powers[0], at, row) for at in (0, 1, 2)])
        up8 = row_of(powers[0], 3, row)
        parts = [cmul(base, row_of(powers[1], 0, row)), cmul(base, conj(up8)), base, cmul(base, up8)]
        cos = jnp.concatenate([part[0] for part in parts], axis=0)
        sin = jnp.concatenate([part[1] for part in parts], axis=0)
        north_re_ref[b] = jnp.concatenate([cos, -sin], axis=0).astype(BF16)
        north_im_ref[b] = jnp.concatenate([sin, cos], axis=0).astype(BF16)
        return carry

    lax.fori_loop(0, rows, body, 0)


def image_kernel(index_ref, near_ref, far_ref, screen_ref, image_ref):
    half = near_ref.shape[0]
    pixels = screen_ref.shape[1] // 2
    blocks = image_ref.shape[0]
    slots = onehot_rows(index_ref[:, 3:4], 2 * half)
    near, far = (slots[:, :half], slots[:, half:])
    tiles = pixels // 128
    width = 256

    def rows_of(cells):
        return jnp.dot(near, near_ref[:, cells], preferred_element_type=F32) + jnp.dot(
            far, far_ref[:, cells], preferred_element_type=F32
        )

    for at in range(0, pixels, width):
        re, im = pl.ds(at, width), pl.ds(pixels + at, width)
        model_re, model_im = (rows_of(re), rows_of(im))
        screen_re, screen_im = (screen_ref[:, re], screen_ref[:, im])
        image_re = (screen_re * model_re - screen_im * model_im).astype(BF16)
        image_im = (screen_re * model_im + screen_im * model_re).astype(BF16)
        for off in range(0, width, 128):
            q = (at + off) // 128
            image_ref[:, 16 * q : 16 * q + 16, :] = image_re[:, off : off + 128].reshape(blocks, 16, 128)
            q = q + tiles
            image_ref[:, 16 * q : 16 * q + 16, :] = image_im[:, off : off + 128].reshape(blocks, 16, 128)


def visibility_kernel(
    images_ref, visible_ref, east_ref, north_re_ref, north_im_ref, resid_ref, grid_ref, cells_ref, out_ref
):
    rows, channels = (resid_ref.shape[0], resid_ref.shape[1] // 2)
    facets = images_ref.shape[0]
    total = images_ref[0].astype(F32)
    for at in range(1, facets):
        total = total + images_ref[at].astype(F32)
    cells_ref[...] = total
    resid_ref[...] = visible_ref[...].astype(F32)
    width = 256

    def degrid(b, carry):
        cells = cells_ref[pl.ds(b, 16, stride=16), :]
        pieces = [
            jnp.concatenate(
                [cells[0:8, 32 * p : 32 * p + 32], cells[8:16, 32 * p : 32 * p + 32]], axis=1
            )
            for p in range(4)
        ]
        image = jnp.concatenate(pieces, axis=0)
        high = image.astype(BF16)
        low = (image - high.astype(F32)).astype(BF16)
        operand = jnp.concatenate([high, low], axis=0)
        for at in range(0, channels, width):
            chans = pl.ds(at, width)
            inner_re = jnp.dot(operand, north_re_ref[b, :, chans], preferred_element_type=F32)
            inner_im = jnp.dot(operand, north_im_ref[b, :, chans], preferred_element_type=F32)
            inner_re = inner_re[:32] + inner_re[32:]
            inner_im = inner_im[:32] + inner_im[32:]
            east = east_ref[b, :, chans].astype(F32)
            cos, sin = (east[:32], east[32:])
            vis_re = jnp.sum(cos * inner_re - sin * inner_im, axis=0, keepdims=True)
            vis_im = jnp.sum(cos * inner_im + sin * inner_re, axis=0, keepdims=True)
            row = pl.ds(b, 1)
            late = pl.ds(channels + at, width)
            resid_ref[row, chans] = resid_ref[row, chans] - vis_re
            resid_ref[row, late] = resid_ref[row, late] - vis_im
        return carry

    def grid(b, carry):
        gridded = jnp.zeros((32, 64), F32)
        over = (((1,), (1,)), ((), ()))
        for at in range(0, channels, width):
            chans, late = (pl.ds(at, width), pl.ds(channels + at, width))
            resid_re, resid_im = (resid_ref[pl.ds(b, 1), chans], resid_ref[pl.ds(b, 1), late])
            east = east_ref[b, :, chans].astype(F32)
            cos, sin = (east[:32], east[32:])
            weighted_re = (cos * resid_re + sin * resid_im).astype(BF16)
            weighted_im = (cos * resid_im - sin * resid_re).astype(BF16)
            gridded = gridded + lax.dot_general(
                weighted_re, north_re_ref[b, :, chans], over, preferred_element_type=F32
            )
            gridded = gridded + lax.dot_general(
                weighted_im, north_im_ref[b, :, chans], over, preferred_element_type=F32
            )
        halves = [
            jnp.concatenate([gridded[8 * p : 8 * p + 8, at : at + 32] for p in range(4)], axis=1)
            for at in (0, 32)
        ]
        out_ref[pl.ds(b, 16, stride=16), :] = jnp.concatenate(halves, axis=0)
        return carry

    lax.fori_loop(0, rows, degrid, 0, unroll=4)
    lax.fori_loop(0, rows, grid, 0, unroll=4)
    packed = out_ref[...].astype(BF16)
    for at in range(facets):
        grid_ref[at] = packed


def regrid_kernel(scale, target_ref, grid_ref, screen_ref, near_ref, far_ref):
    half = near_ref.shape[0]
    pixels = screen_ref.shape[1] // 2
    tiles = pixels // 128
    count = screen_ref.shape[0]
    subs = lax.broadcasted_iota(jnp.int32, (2 * half, count), 0)
    onehot = jnp.where(target_ref[...] == subs, 1.0, 0.0).astype(BF16)
    near, far = (onehot[:half], onehot[half:])
    for q in range(tiles):
        re, im = pl.ds(128 * q, 128), pl.ds(pixels + 128 * q, 128)
        grid_re = grid_ref[:, 16 * q : 16 * q + 16, :].reshape(count, 128).astype(F32)
        grid_im = grid_ref[:, 16 * (q + tiles) : 16 * (q + tiles) + 16, :].reshape(count, 128).astype(F32)
        screen_re, screen_im = (screen_ref[:, re], screen_ref[:, im])
        out_re = (screen_re * grid_re + screen_im * grid_im) * scale
        out_im = (screen_re * grid_im - screen_im * grid_re) * scale
        for cells, value in ((re, out_re), (im, out_im)):
            high = value.astype(BF16)
            low = (value - high.astype(F32)).astype(BF16)
            near_ref[:, cells] = jnp.dot(near, high, preferred_element_type=F32) + jnp.dot(
                near, low, preferred_element_type=F32
            )
            far_ref[:, cells] = jnp.dot(far, high, preferred_element_type=F32) + jnp.dot(
                far, low, preferred_element_type=F32
            )


def shift(value, axis, by):
    size = lax.axis_size(axis)
    return lax.ppermute(value, axis, [(i, (i + by) % size) for i in range(size)])


def local(
    sectioned_rows,
    reader,
    baseline_coords,
    subgrid_index,
    stations,
    plane_index,
    model_grid,
    beam_screens,
    plane_phase,
    channel_freq,
):
    n_y, n_h, n_x, n_z, n_c = (lax.axis_size(axis) for axis in FACET + TILE)
    at_y, at_h, at_x, at_z, at_c = (lax.axis_index(axis) for axis in FACET + TILE)
    n_facet = n_y * n_h
    facet_id = at_y * n_h + at_h
    channels = channel_freq.shape[0]
    planes, pixels = plane_phase.shape
    row_block = sectioned_rows.shape[1]
    count = n_facet * row_block
    owned = model_grid.shape[1]
    subgrid_count = owned * n_x * n_z * n_c
    grid_scale = 1.0 / math.sqrt(channels * n_facet * (row_block * n_x * n_z * n_c) / subgrid_count)

    with jax.named_scope("model_gather"):
        own = model_grid[0]
        column = jnp.concatenate([own] + [shift(own, "z", by) for by in range(1, n_z)], axis=0)
        near = jnp.concatenate([column] + [shift(column, "x", by) for by in range(1, n_x)], axis=0)
        far = shift(near, "c", 1)

    with jax.named_scope("visible_route"):
        rows = sectioned_rows[0]
        other = shift(rows, "h", 1)
        read_by = reader[0]
        block_of = jnp.sum(
            jnp.where(
                read_by[None, :] == jnp.arange(n_facet, dtype=jnp.int32)[:, None],
                jnp.arange(n_facet, dtype=jnp.int32)[None, :],
                0,
            ),
            axis=1,
        )
        mine_to = block_of[facet_id]
        source = read_by[facet_id]
        visible = jnp.where(source // n_h == at_y, jnp.where(source % n_h == at_h, rows, other), 0)
        for by in range(1, n_y):
            to = ((at_y + by) % n_y) * n_h + at_h
            came = shift(jnp.where(mine_to == to, rows, other), "y", by)
            visible = jnp.where((source // n_h + by) % n_y == at_y, came, visible)

    sub = subgrid_index.reshape(count)
    sub_row, sub_c = (sub % owned, (sub // owned) % n_c)
    sub_z, sub_x = ((sub // (owned * n_c)) % n_z, sub // (owned * n_c * n_z))
    core = (sub_c - at_c) % n_c
    slot = ((core * n_x + (at_x - sub_x) % n_x) * n_z + (at_z - sub_z) % n_z) * owned + sub_row
    target = ((core * n_x + sub_x) * n_z + sub_z) * owned + sub_row
    index = jnp.stack(
        [stations[:, 0].reshape(count), stations[:, 1].reshape(count), plane_index.reshape(count), slot], axis=1
    )

    screen = pl.pallas_call(
        screen_kernel,
        out_shape=jax.ShapeDtypeStruct((count, 2 * pixels), F32),
        in_specs=[VMEM] * 3,
        out_specs=VMEM,
        compiler_params=params(32),
        cost_estimate=pl.CostEstimate(flops=10**9, bytes_accessed=4 << 20, transcendentals=1 << 16),
        name="screens",
    )(index, plane_phase, beam_screens[0])

    coords = lax.dynamic_index_in_dim(baseline_coords, facet_id, 0, keepdims=False).reshape(2 * row_block, 1)
    east, north_re, north_im = pl.pallas_call(
        table_kernel,
        out_shape=[jax.ShapeDtypeStruct((row_block, 64, channels), BF16)] * 3,
        in_specs=[VMEM] * 2,
        out_specs=[VMEM] * 3,
        scratch_shapes=[
            pltpu.VMEM((10, 2 * row_block, channels), F32),
            pltpu.VMEM((8, 2 * row_block, channels), F32),
        ],
        compiler_params=params(32),
        cost_estimate=pl.CostEstimate(flops=10**8, bytes_accessed=6 << 20, transcendentals=1 << 16),
        name="tables",
    )(coords, channel_freq.reshape(1, channels))

    images = pl.pallas_call(
        image_kernel,
        out_shape=jax.ShapeDtypeStruct((n_facet, 2 * pixels // 128 * row_block, 128), BF16),
        in_specs=[VMEM] * 4,
        out_specs=VMEM,
        compiler_params=params(32),
        cost_estimate=pl.CostEstimate(flops=10**8, bytes_accessed=2 << 20, transcendentals=0),
        name="images",
    )(index, near, far, screen)

    arrived = lax.all_to_all(images, FACET, split_axis=0, concat_axis=0, tiled=True)

    cell_rows = 2 * pixels // 128 * row_block
    residual, gridded = pl.pallas_call(
        visibility_kernel,
        out_shape=[
            jax.ShapeDtypeStruct((row_block, 2 * channels), F32),
            jax.ShapeDtypeStruct((n_facet, cell_rows, 128), BF16),
        ],
        in_specs=[VMEM] * 5,
        out_specs=[VMEM] * 2,
        scratch_shapes=[pltpu.VMEM((cell_rows, 128), F32), pltpu.VMEM((cell_rows, 128), F32)],
        compiler_params=params(48),
        cost_estimate=pl.CostEstimate(flops=10**9, bytes_accessed=8 << 20, transcendentals=0),
        name="visibilities",
    )(arrived, visible, east, north_re, north_im)

    gathered = lax.all_to_all(gridded, FACET, split_axis=0, concat_axis=0, tiled=True)

    half = subgrid_count // n_c
    near_sum, far_sum = pl.pallas_call(
        lambda *refs: regrid_kernel(grid_scale, *refs),
        out_shape=[jax.ShapeDtypeStruct((half, 2 * pixels), F32)] * 2,
        in_specs=[VMEM] * 3,
        out_specs=[VMEM] * 2,
        compiler_params=params(32),
        cost_estimate=pl.CostEstimate(flops=10**8, bytes_accessed=3 << 20, transcendentals=0),
        name="regrid",
    )(target.reshape(1, count), gathered, screen)

    with jax.named_scope("dirty_scatter"):
        chip_sum = (near_sum + shift(far_sum, "c", 1)).astype(BF16).reshape(n_x * n_z, owned, 2 * pixels)
        chips = lax.all_to_all(chip_sum, ("x", "z"), split_axis=0, concat_axis=0, tiled=True)
        dirty = jnp.sum(chips.astype(F32), axis=0)
    return (residual[None], dirty[None])


def solution(mesh):
    split = Mesh(mesh.devices.reshape(4, 2, 4, 4, 2), FACET + TILE)
    return jax.shard_map(
        local,
        mesh=split,
        in_specs=(
            P(FACET, TILE, None),
            P(TILE, None),
            P(None, None, TILE),
            P(None, TILE),
            P(None, None, TILE),
            P(None, TILE),
            P(FACET, TILE, None),
            P(FACET, None, None),
            P(),
            P(),
        ),
        out_specs=(P(FACET, TILE, None), P(FACET, TILE, None)),
        check_vma=False,
    )
```

time: 896 us -> 110 us (0.12)
  waiting for transfers between devices: 355 us -> 18.7 us
  other arithmetic: 305 us -> 2.5 us
  blocking collectives: 106 us -> 17.7 us
  matrix products: 52.3 us -> 0 us
  starting transfers between devices: 0.08 us -> 39.6 us
  local copies, waits for them, and re-layouts: 41.6 us -> 12.4 us
  loops' own time: 18.2 us -> 0 us
  Pallas kernels: 0 us -> 13.5 us
  between operations: 14.9 us -> 5.46 us
    unnamed x3 -> x0, waiting for transfers between devices: 273 us -> none
    all_gather x2 -> x0, blocking collectives: 106 us -> none  [the longest x1 55.6 us: local(): arrived = lax.all_gather(sectioned_rows, 'facet', axis=0, tiled=True)]
    dynamic_update_slice x48 -> x0, other arithmetic: 103 us -> none  [the longest x32 97.9 us: local(): tables = lax.map(geometry, block_ids)]
    psum x1 -> x0, waiting for transfers between devices: 81.8 us -> none  [local(): total = lax.psum(predicted, 'facet')]
    convert_element_type x32 -> x1, other arithmetic: 70.1 us -> 0.07 us  [local(): (near_sum + shift(far_sum, 'c', 1)).astype(BF16)]
    neg x8 -> x0, other arithmetic: 63.5 us -> none  [north_matrix(): lower_half = jnp.concatenate([-north_sin, north_cos], axis=2)]
    dot_general x17 -> x0, matrix products: 52.3 us -> none  [the longest x8 27.3 us: grid_rows(): jnp.einsum('rxc,ryc->rxy', operand, north_mat, preferred_element_type=jnp...]
    another operation x28 -> x1, other arithmetic: 32.9 us -> 0.01 us  [local(): jnp.stack([stations[:, 0].reshape(count), stations[:, 1].reshape(count),...]
  transfers between devices with their start and end apart: 2 -> 14, of which waited for: 2 -> 5; matrix products, arithmetic and copies ran while one was open for 0% -> 6% of each run, Pallas kernels for 0% -> 6%
where the time goes in v1:
time: 110 us
  starting transfers between devices  39.6 us (36%)
  waiting for transfers between devices  18.7 us (17%)
  blocking collectives  17.7 us (16%)
  Pallas kernels  13.5 us (12%)
  local copies, waits for them, and re-layouts  12.4 us (11%)
  between operations  5.46 us (5%)
  other arithmetic  2.5 us (2%)
    ppermute x12, starting transfers between devices, shift(): lax.ppermute(value, axis, [(i, (i + by) % size) for i in range(size)])  26.5 us
    all_to_all x1, blocking collectives, local(): lax.all_to_all(chip_sum, ('x', 'z'), split_axis=0, concat_axis=0, tiled=T...  17.7 us
    all_to_all x1, waiting for transfers between devices, local(): lax.all_to_all(gridded, FACET, split_axis=0, concat_axis=0, tiled=True)  12.1 us
    unnamed x22, local copies, waits for them, and re-layouts  7.55 us
    all_to_all x1, starting transfers between devices, local(): lax.all_to_all(images, FACET, split_axis=0, concat_axis=0, tiled=True)  7.52 us
    pallas_call x1, Pallas kernels, local(): pl.pallas_call(visibility_kernel, out_shape=[jax.ShapeDtypeStruct((row_bl...  6.24 us
    all_to_all x1, starting transfers between devices, local(): lax.all_to_all(gridded, FACET, split_axis=0, concat_axis=0, tiled=True)  5.61 us
    ppermute x12, waiting for transfers between devices, shift(): lax.ppermute(value, axis, [(i, (i + by) % size) for i in range(size)])  4.94 us
  transfers between devices with their start and end apart: 14, of which 5 were waited for; matrix products, arithmetic and copies ran while one was open for 6% of the time, Pallas kernels for 6%

profile of v1, /device:TPU:1, one launch (start us, length us, event | category | flops | bytes accessed | tf_op | source)
XLA Modules:
  0.0 109.8 jit_solution(3574086839729776048)
XLA Ops:
  0.6 0.0 copy-start
  0.6 5.3 %collective-permute-start.2 = (bf16[4,2048]{1,0:T(4,128)(2,1)}, bf16[4,2048]{1,0:T(4,128)(2,1)S(1)}, u32[]{:S(2)}, u32[]{:S(2)}) collective-permute-start(bf16[4,2048]{1,0:T(4,128)(2,1)} %bitcast.16), channel_id=1, source_target_pairs={{0,6},{2,0},{4,2},{6,4},{1,7},{3,1},{5,3},{7,5},{8,14},{10,8},{12,... | collective-permute-start | bytes 49160 | tf_op jit(solution)/shard_map/model_gather/ppermute | solution.py:230
  5.9 0.4 collective-permute-start
  6.3 4.8 %collective-permute-start.7 = (bf16[16,2048]{1,0:T(8,128)(2,1)}, bf16[16,2048]{1,0:T(8,128)(2,1)S(1)}, u32[]{:S(2)}, u32[]{:S(2)}) collective-permute-start(bf16[16,2048]{1,0:T(8,128)(2,1)} %bitcast.15), channel_id=1, source_target_pairs={{0,32},{32,0},{1,33},{33,1},{2,34},{34,2},{3,35},{35,3},{4,36},{36... | collective-permute-start | bytes 196616 | tf_op jit(solution)/shard_map/visible_route/ppermute | solution.py:230
  11.1 0.8 reshape.644
  12.0 0.8 pad_maximum_fusion
  12.7 2.6 %collective-permute-start.5 = (bf16[16,2048]{1,0:T(8,128)(2,1)S(1)}, bf16[16,2048]{1,0:T(8,128)(2,1)S(1)}, u32[]{:S(2)}, u32[]{:S(2)}) collective-permute-start(bf16[16,2048]{1,0:T(8,128)(2,1)S(1)} %pad_maximum_fusion), channel_id=1, source_target_pairs={{0,24},{8,0},{16,8},{24,16},{1,25},{9,1},{17,9},{25,17},{2,26},{10... | collective-permute-start | bytes 196616 | tf_op jit(solution)/shard_map/model_gather/ppermute | solution.py:230
  15.3 0.5 collective-permute-start.4
  15.8 0.6 collective-permute-start.3
  16.4 0.8 slice_reduce_fusion.1
  17.2 2.7 %collective-permute-done.4 = bf16[16,2048]{1,0:T(8,128)(2,1)S(1)} collective-permute-done((bf16[16,2048]{1,0:T(8,128)(2,1)S(1)}, bf16[16,2048]{1,0:T(8,128)(2,1)S(1)}, u32[]{:S(2)}, u32[]{:S(2)}) %collective-permute-start.4) | collective-permute-done | bytes 65568 | tf_op jit(solution)/shard_map/model_gather/ppermute | solution.py:230
  19.9 0.7 collective-permute-done.3
  20.6 0.8 concatenate.8.near_ref
  21.4 3.3 %collective-permute-start.6 = (bf16[64,2048]{1,0:T(8,128)(2,1)S(1)}, bf16[64,2048]{1,0:T(8,128)(2,1)S(1)}, u32[]{:S(2)}, u32[]{:S(2)}) collective-permute-start(bf16[64,2048]{1,0:T(8,128)(2,1)S(1)} %concatenate.8.near_ref), channel_id=1, source_target_pairs={{0,1},{1,0},{2,3},{3,2},{4,5},{5,4},{6,7},{7,6},{8,9},{9,8},{10,11... | collective-permute-start | bytes 786440 | tf_op jit(solution)/shard_map/model_gather/ppermute | solution.py:230
  24.7 0.8 select_reduce_fusion
  25.5 0.8 stack_reshape.3
  26.3 0.6 dynamic_slice.11
  28.8 0.1 stack_reshape_squeeze.6
  28.9 0.1 stack_reshape_squeeze.7
  29.0 0.1 copy.32.index_ref
  29.1 1.6 %copy-done.5 = bf16[1,512,2048]{2,1,0:T(8,128)(2,1)S(1)} copy-done((bf16[1,512,2048]{2,1,0:T(8,128)(2,1)S(1)}, bf16[1,512,2048]{2,1,0:T(8,128)(2,1)}, u32[]{:S(2)}) %copy-start.5) | copy-done | bytes 2097176
  30.7 0.9 copy-done.6
  31.6 1.9 %screens.1.screen_ref.refs_2_ = f32[128,2048]{1,0:T(8,128)S(1)} custom-call(s32[128,4]{1,0:T(8,128)S(1)} %copy.32.index_ref, f32[32,1024]{1,0:T(8,128)S(1)} %copy-done.6, bf16[512,2048]{1,0:T(8,128)(2,1)S(1)} %bitcast.13), custom_call_target="tpu_custom_call" | custom-call | flops 1000000000 | bytes 4194304 | tf_op jit(solution)/shard_map/screens/pallas_call | solution.py:293
  33.6 1.3 %images.1 = bf16[8,256,128]{2,1,0:T(8,128)(2,1)} custom-call(s32[128,4]{1,0:T(8,128)S(1)} %copy.32.index_ref, bf16[64,2048]{1,0:T(8,128)(2,1)S(1)} %concatenate.8.near_ref, bf16[64,2048]{1,0:T(8,128)(2,1)S(1)} %collective-permute-done.6.far_ref, f32[128,2048]{1,0:T(8,128)S(1)} %screens.1.screen_ref.refs_2_), custom_call_target="tpu_custom_call" | custom-call | flops 100000000 | bytes 2097152 | tf_op jit(solution)/shard_map/images/pallas_call | solution.py:318
  34.9 7.5 %all-to-all-start = ((bf16[8,256,128]{2,1,0:T(8,128)(2,1)}), bf16[8,256,128]{2,1,0:T(8,128)(2,1)}, u32[]{:S(2)}, u32[]{:S(2)}) async-start(bf16[8,256,128]{2,1,0:T(8,128)(2,1)} %images.1), calls=%async_computation | async-start | bytes 1048576 | tf_op jit(solution)/shard_map/all_to_all | solution.py:328
  42.5 1.5 %collective-permute-start.10 = (bf16[16,2048]{1,0:T(8,128)(2,1)S(1)}, bf16[16,2048]{1,0:T(8,128)(2,1)}, u32[]{:S(2)}, u32[]{:S(2)}) collective-permute-start(bf16[16,2048]{1,0:T(8,128)(2,1)S(1)} %get-tuple-element.18), channel_id=1, source_target_pairs={{0,64},{64,128},{128,192},{192,0},{1,65},{65,129},{129,193},{193,1... | collective-permute-start | bytes 196616 | tf_op jit(solution)/shard_map/visible_route/ppermute | solution.py:230
  44.0 2.4 %collective-permute-start.9 = (bf16[16,2048]{1,0:T(8,128)(2,1)S(1)}, bf16[16,2048]{1,0:T(8,128)(2,1)}, u32[]{:S(2)}, u32[]{:S(2)}) collective-permute-start(bf16[16,2048]{1,0:T(8,128)(2,1)S(1)} %get-tuple-element.19), channel_id=1, source_target_pairs={{0,128},{64,192},{128,0},{192,64},{1,129},{65,193},{129,1},{193,65... | collective-permute-start | bytes 196616 | tf_op jit(solution)/shard_map/visible_route/ppermute | solution.py:230
  46.4 1.2 %collective-permute-start.8 = (bf16[16,2048]{1,0:T(8,128)(2,1)S(1)}, bf16[16,2048]{1,0:T(8,128)(2,1)}, u32[]{:S(2)}, u32[]{:S(2)}) collective-permute-start(bf16[16,2048]{1,0:T(8,128)(2,1)S(1)} %get-tuple-element.20), channel_id=1, source_target_pairs={{0,192},{64,0},{128,64},{192,128},{1,193},{65,1},{129,65},{193,129... | collective-permute-start | bytes 196616 | tf_op jit(solution)/shard_map/visible_route/ppermute | solution.py:230
  47.6 0.6 constant_dynamic-slice_fusion.1
  50.9 0.1 reshape.649.coords_ref
  51.0 3.2 %tables.1 = (bf16[16,64,1024]{2,1,0:T(8,128)(2,1)S(1)}, bf16[16,64,1024]{2,1,0:T(8,128)(2,1)S(1)}, bf16[16,64,1024]{2,1,0:T(8,128)(2,1)S(1)}) custom-call(f32[32,1]{1,0:T(8,128)S(1)} %reshape.649.coords_ref, f32[1,1024]{1,0:T(1,128)S(1)} %bitcast.14), custom_call_target="tpu_custom_call" | custom-call | flops 100000000 | bytes 6291456 | tf_op jit(solution)/shard_map/tables/pallas_call | solution.py:304
  54.2 1.3 %copy-done.1 = bf16[16,64,1024]{2,1,0:T(8,128)(2,1)} copy-done((bf16[16,64,1024]{2,1,0:T(8,128)(2,1)}, bf16[16,64,1024]{2,1,0:T(8,128)(2,1)S(1)}, u32[]{:S(2)}) %copy-start.1) | copy-done | bytes 2097176
  55.5 1.3 %copy-done.3 = bf16[16,64,1024]{2,1,0:T(8,128)(2,1)} copy-done((bf16[16,64,1024]{2,1,0:T(8,128)(2,1)}, bf16[16,64,1024]{2,1,0:T(8,128)(2,1)S(1)}, u32[]{:S(2)}) %copy-start.3) | copy-done | bytes 2097176
  56.9 0.1 select_select_fusion.visible_ref
  56.9 1.6 %all-to-all-done.images_ref = bf16[8,256,128]{2,1,0:T(8,128)(2,1)} async-done(((bf16[8,256,128]{2,1,0:T(8,128)(2,1)}), bf16[8,256,128]{2,1,0:T(8,128)(2,1)}, u32[]{:S(2)}, u32[]{:S(2)}) %all-to-all-start) | async-done | bytes 524320 | tf_op jit(solution)/shard_map/all_to_all | solution.py:328
  58.5 1.6 %copy-done.2 = bf16[16,64,1024]{2,1,0:T(8,128)(2,1)S(1)} copy-done((bf16[16,64,1024]{2,1,0:T(8,128)(2,1)S(1)}, bf16[16,64,1024]{2,1,0:T(8,128)(2,1)}, u32[]{:S(2)}) %copy-start.2) | copy-done | bytes 2097176
  60.1 6.2 %visibilities.1 = (f32[16,2048]{1,0:T(8,128)}, bf16[8,256,128]{2,1,0:T(8,128)(2,1)S(1)}) custom-call(bf16[8,256,128]{2,1,0:T(8,128)(2,1)} %all-to-all-done.images_ref, bf16[16,2048]{1,0:T(8,128)(2,1)S(1)} %select_select_fusion.visible_ref, bf16[16,64,1024]{2,1,0:T(8,128)(2,1)S(1)} %get-tuple-element.9.east_ref, bf16[16,64,1024]{2,1,0:T(8,128)(2,1)S(1)} %copy-done.2, ...), custom_call_target="tpu_custom_call" | custom-call | flops 1000000000 | bytes 8388608 | tf_op jit(solution)/shard_map/visibilities/pallas_call | solution.py:331
  66.4 0.8 copy-done.4
  67.2 5.6 %all-to-all-start.1 = ((bf16[8,256,128]{2,1,0:T(8,128)(2,1)}), bf16[8,256,128]{2,1,0:T(8,128)(2,1)S(1)}, u32[]{:S(2)}, u32[]{:S(2)}) async-start(bf16[8,256,128]{2,1,0:T(8,128)(2,1)} %copy-done.4), calls=%async_computation.1 | async-start | bytes 1048576 | tf_op jit(solution)/shard_map/all_to_all | solution.py:345
  72.8 0.1 reshape.647
  72.9 12.1 %all-to-all-done.1.refs_1_ = bf16[8,256,128]{2,1,0:T(8,128)(2,1)S(1)} async-done(((bf16[8,256,128]{2,1,0:T(8,128)(2,1)}), bf16[8,256,128]{2,1,0:T(8,128)(2,1)S(1)}, u32[]{:S(2)}, u32[]{:S(2)}) %all-to-all-start.1) | async-done | bytes 524320 | tf_op jit(solution)/shard_map/all_to_all | solution.py:345
  85.0 0.7 regrid.1
  85.7 3.9 %collective-permute-start.11 = (f32[64,2048]{1,0:T(8,128)S(1)}, f32[64,2048]{1,0:T(8,128)S(1)}, u32[]{:S(2)}, u32[]{:S(2)}) collective-permute-start(f32[64,2048]{1,0:T(8,128)S(1)} %get-tuple-element.15), channel_id=1, source_target_pairs={{0,1},{1,0},{2,3},{3,2},{4,5},{5,4},{6,7},{7,6},{8,9},{9,8},{10,11... | collective-permute-start | bytes 1572872 | tf_op jit(solution)/shard_map/dirty_scatter/ppermute | solution.py:230
  89.6 1.5 %collective-permute-done.11 = f32[64,2048]{1,0:T(8,128)S(1)} collective-permute-done((f32[64,2048]{1,0:T(8,128)S(1)}, f32[64,2048]{1,0:T(8,128)S(1)}, u32[]{:S(2)}, u32[]{:S(2)}) %collective-permute-start.11) | collective-permute-done | bytes 524320 | tf_op jit(solution)/shard_map/dirty_scatter/ppermute | solution.py:230
  91.1 0.1 add_convert_fusion
  91.2 0.1 reshape.648
  91.3 17.7 %all_to_all.15 = bf16[16,4,2048]{2,1,0:T(4,128)(2,1)S(1)} all-to-all(bf16[16,4,2048]{2,1,0:T(4,128)(2,1)S(1)} %reshape.648), channel_id=1, replica_groups=mesh['y'=4,'h'=2,'x'=4,'z'=4,'c'=2] {'x','z'}, dimensions={0} | all-to-all | bytes 524288 | tf_op jit(solution)/shard_map/dirty_scatter/all_to_all | solution.py:360
  109.0 0.7 convert_reduce_fusion
  (30 shorter events, 0.2 us)
Async XLA Ops:
  0.6 47.0 %copy-start = (f32[8,2,16]{2,1,0:T(2,128)S(1)}, f32[8,2,16]{2,1,0:T(2,128)}, u32[]{:S(2)}) copy-start(f32[8,2,16]{2,1,0:T(2,128)} %param.12) | copy-start | bytes 3076
  0.6 11.3 %collective-permute-start.2 = (bf16[4,2048]{1,0:T(4,128)(2,1)}, bf16[4,2048]{1,0:T(4,128)(2,1)S(1)}, u32[]{:S(2)}, u32[]{:S(2)}) collective-permute-start(bf16[4,2048]{1,0:T(4,128)(2,1)} %bitcast.16), channel_id=1, source_target_pairs={{0,6},{2,0},{4,2},{6,4},{1,7},{3,1},{5,3},{7,5},{8,14},{10,8},{12,... | collective-permute-start | bytes 49160 | tf_op jit(solution)/shard_map/model_gather/ppermute | solution.py:230
  5.9 6.0 %collective-permute-start.1 = (bf16[4,2048]{1,0:T(4,128)(2,1)}, bf16[4,2048]{1,0:T(4,128)(2,1)S(1)}, u32[]{:S(2)}, u32[]{:S(2)}) collective-permute-start(bf16[4,2048]{1,0:T(4,128)(2,1)} %bitcast.17), channel_id=1, source_target_pairs={{0,4},{2,6},{4,0},{6,2},{1,5},{3,7},{5,1},{7,3},{8,12},{10,14},{12... | collective-permute-start | bytes 49160 | tf_op jit(solution)/shard_map/model_gather/ppermute | solution.py:230
  5.9 6.0 %collective-permute-start = (bf16[4,2048]{1,0:T(4,128)(2,1)}, bf16[4,2048]{1,0:T(4,128)(2,1)S(1)}, u32[]{:S(2)}, u32[]{:S(2)}) collective-permute-start(bf16[4,2048]{1,0:T(4,128)(2,1)} %bitcast.18), channel_id=1, source_target_pairs={{0,2},{2,4},{4,6},{6,0},{1,3},{3,5},{5,7},{7,1},{8,10},{10,12},{12... | collective-permute-start | bytes 49160 | tf_op jit(solution)/shard_map/model_gather/ppermute | solution.py:230
  6.3 36.2 %collective-permute-start.7 = (bf16[16,2048]{1,0:T(8,128)(2,1)}, bf16[16,2048]{1,0:T(8,128)(2,1)S(1)}, u32[]{:S(2)}, u32[]{:S(2)}) collective-permute-start(bf16[16,2048]{1,0:T(8,128)(2,1)} %bitcast.15), channel_id=1, source_target_pairs={{0,32},{32,0},{1,33},{33,1},{2,34},{34,2},{3,35},{35,3},{4,36},{36... | collective-permute-start | bytes 196616 | tf_op jit(solution)/shard_map/visible_route/ppermute | solution.py:230
  12.7 4.5 %collective-permute-start.5 = (bf16[16,2048]{1,0:T(8,128)(2,1)S(1)}, bf16[16,2048]{1,0:T(8,128)(2,1)S(1)}, u32[]{:S(2)}, u32[]{:S(2)}) collective-permute-start(bf16[16,2048]{1,0:T(8,128)(2,1)S(1)} %pad_maximum_fusion), channel_id=1, source_target_pairs={{0,24},{8,0},{16,8},{24,16},{1,25},{9,1},{17,9},{25,17},{2,26},{10... | collective-permute-start | bytes 196616 | tf_op jit(solution)/shard_map/model_gather/ppermute | solution.py:230
  15.3 4.7 %collective-permute-start.4 = (bf16[16,2048]{1,0:T(8,128)(2,1)S(1)}, bf16[16,2048]{1,0:T(8,128)(2,1)S(1)}, u32[]{:S(2)}, u32[]{:S(2)}) collective-permute-start(bf16[16,2048]{1,0:T(8,128)(2,1)S(1)} %pad_maximum_fusion), channel_id=1, source_target_pairs={{0,16},{8,24},{16,0},{24,8},{1,17},{9,25},{17,1},{25,9},{2,18},{10... | collective-permute-start | bytes 196616 | tf_op jit(solution)/shard_map/model_gather/ppermute | solution.py:230
  15.8 4.8 %collective-permute-start.3 = (bf16[16,2048]{1,0:T(8,128)(2,1)S(1)}, bf16[16,2048]{1,0:T(8,128)(2,1)S(1)}, u32[]{:S(2)}, u32[]{:S(2)}) collective-permute-start(bf16[16,2048]{1,0:T(8,128)(2,1)S(1)} %pad_maximum_fusion), channel_id=1, source_target_pairs={{0,8},{8,16},{16,24},{24,0},{1,9},{9,17},{17,25},{25,1},{2,10},{10... | collective-permute-start | bytes 196616 | tf_op jit(solution)/shard_map/model_gather/ppermute | solution.py:230
  21.4 12.2 %collective-permute-start.6 = (bf16[64,2048]{1,0:T(8,128)(2,1)S(1)}, bf16[64,2048]{1,0:T(8,128)(2,1)S(1)}, u32[]{:S(2)}, u32[]{:S(2)}) collective-permute-start(bf16[64,2048]{1,0:T(8,128)(2,1)S(1)} %concatenate.8.near_ref), channel_id=1, source_target_pairs={{0,1},{1,0},{2,3},{3,2},{4,5},{5,4},{6,7},{7,6},{8,9},{9,8},{10,11... | collective-permute-start | bytes 786440 | tf_op jit(solution)/shard_map/model_gather/ppermute | solution.py:230
  29.1 1.6 %copy-start.5 = (bf16[1,512,2048]{2,1,0:T(8,128)(2,1)S(1)}, bf16[1,512,2048]{2,1,0:T(8,128)(2,1)}, u32[]{:S(2)}) copy-start(bf16[1,512,2048]{2,1,0:T(8,128)(2,1)} %param.17) | copy-start | bytes 6291460
  30.7 0.9 copy-start.6
  33.6 8.9 %copy-start.8 = (bf16[1,16,2048]{2,1,0:T(8,128)(2,1)S(1)}, bf16[1,16,2048]{2,1,0:T(8,128)(2,1)}, u32[]{:S(2)}) copy-start(bf16[1,16,2048]{2,1,0:T(8,128)(2,1)} %param.10) | copy-start | bytes 196612
  33.6 14.1 %copy-start.10 = (s32[1,8]{1,0:T(1,128)S(1)}, s32[1,8]{1,0:T(1,128)}, u32[]{:S(2)}) copy-start(s32[1,8]{1,0:T(1,128)} %param.11) | copy-start | bytes 100
  33.6 17.4 %copy-start.7 = (f32[1024]{0:T(1024)S(1)}, f32[1024]{0:T(1024)}, u32[]{:S(2)}) copy-start(f32[1024]{0:T(1024)} %param.19) | copy-start | bytes 12292
  34.9 23.6 %all-to-all-start = ((bf16[8,256,128]{2,1,0:T(8,128)(2,1)}), bf16[8,256,128]{2,1,0:T(8,128)(2,1)}, u32[]{:S(2)}, u32[]{:S(2)}) async-start(bf16[8,256,128]{2,1,0:T(8,128)(2,1)} %images.1), calls=%async_computation | async-start | bytes 1048576 | tf_op jit(solution)/shard_map/all_to_all | solution.py:328
  42.5 14.3 %collective-permute-start.10 = (bf16[16,2048]{1,0:T(8,128)(2,1)S(1)}, bf16[16,2048]{1,0:T(8,128)(2,1)}, u32[]{:S(2)}, u32[]{:S(2)}) collective-permute-start(bf16[16,2048]{1,0:T(8,128)(2,1)S(1)} %get-tuple-element.18), channel_id=1, source_target_pairs={{0,64},{64,128},{128,192},{192,0},{1,65},{65,129},{129,193},{193,1... | collective-permute-start | bytes 196616 | tf_op jit(solution)/shard_map/visible_route/ppermute | solution.py:230
  44.0 12.8 %collective-permute-start.9 = (bf16[16,2048]{1,0:T(8,128)(2,1)S(1)}, bf16[16,2048]{1,0:T(8,128)(2,1)}, u32[]{:S(2)}, u32[]{:S(2)}) collective-permute-start(bf16[16,2048]{1,0:T(8,128)(2,1)S(1)} %get-tuple-element.19), channel_id=1, source_target_pairs={{0,128},{64,192},{128,0},{192,64},{1,129},{65,193},{129,1},{193,65... | collective-permute-start | bytes 196616 | tf_op jit(solution)/shard_map/visible_route/ppermute | solution.py:230
  46.4 10.4 %collective-permute-start.8 = (bf16[16,2048]{1,0:T(8,128)(2,1)S(1)}, bf16[16,2048]{1,0:T(8,128)(2,1)}, u32[]{:S(2)}, u32[]{:S(2)}) collective-permute-start(bf16[16,2048]{1,0:T(8,128)(2,1)S(1)} %get-tuple-element.20), channel_id=1, source_target_pairs={{0,192},{64,0},{128,64},{192,128},{1,193},{65,1},{129,65},{193,129... | collective-permute-start | bytes 196616 | tf_op jit(solution)/shard_map/visible_route/ppermute | solution.py:230
  54.2 1.3 %copy-start.1 = (bf16[16,64,1024]{2,1,0:T(8,128)(2,1)}, bf16[16,64,1024]{2,1,0:T(8,128)(2,1)S(1)}, u32[]{:S(2)}) copy-start(bf16[16,64,1024]{2,1,0:T(8,128)(2,1)S(1)} %get-tuple-element.10.north_re_ref) | copy-start | bytes 6291460
  55.5 1.3 %copy-start.3 = (bf16[16,64,1024]{2,1,0:T(8,128)(2,1)}, bf16[16,64,1024]{2,1,0:T(8,128)(2,1)S(1)}, u32[]{:S(2)}) copy-start(bf16[16,64,1024]{2,1,0:T(8,128)(2,1)S(1)} %get-tuple-element.11.north_im_ref) | copy-start | bytes 6291460
  58.5 1.6 %copy-start.2 = (bf16[16,64,1024]{2,1,0:T(8,128)(2,1)S(1)}, bf16[16,64,1024]{2,1,0:T(8,128)(2,1)}, u32[]{:S(2)}) copy-start(bf16[16,64,1024]{2,1,0:T(8,128)(2,1)} %copy-done.1) | copy-start | bytes 6291460
  60.1 12.6 %copy-start.9 = (s32[8,16]{1,0:T(8,128)S(1)}, s32[8,16]{1,0:T(8,128)}, u32[]{:S(2)}) copy-start(s32[8,16]{1,0:T(8,128)} %param.13) | copy-start | bytes 1540
  66.4 0.8 copy-start.4
  67.2 17.9 %all-to-all-start.1 = ((bf16[8,256,128]{2,1,0:T(8,128)(2,1)}), bf16[8,256,128]{2,1,0:T(8,128)(2,1)S(1)}, u32[]{:S(2)}, u32[]{:S(2)}) async-start(bf16[8,256,128]{2,1,0:T(8,128)(2,1)} %copy-done.4), calls=%async_computation.1 | async-start | bytes 1048576 | tf_op jit(solution)/shard_map/all_to_all | solution.py:345
  85.7 5.4 %collective-permute-start.11 = (f32[64,2048]{1,0:T(8,128)S(1)}, f32[64,2048]{1,0:T(8,128)S(1)}, u32[]{:S(2)}, u32[]{:S(2)}) collective-permute-start(f32[64,2048]{1,0:T(8,128)S(1)} %get-tuple-element.15), channel_id=1, source_target_pairs={{0,1},{1,0},{2,3},{3,2},{4,5},{5,4},{6,7},{7,6},{8,9},{9,8},{10,11... | collective-permute-start | bytes 1572872 | tf_op jit(solution)/shard_map/dirty_scatter/ppermute | solution.py:230

commit v2 on v1

--- a/solution.py
+++ b/solution.py
@@ -1,3 +1,4 @@
+import functools
 import math
 
 import jax
@@ -14,6 +15,7 @@
 FACET = ("y", "h")
 TILE = ("x", "z", "c")
 VMEM = pl.BlockSpec(memory_space=pltpu.VMEM)
+SMEM = pl.BlockSpec(memory_space=pltpu.SMEM)
 
 
 def params(mib):
@@ -28,17 +30,34 @@
     return (a[0], -a[1])
 
 
-def onehot_rows(column, count):
-    lanes = lax.broadcasted_iota(jnp.int32, (column.shape[0], count), 1)
-    return jnp.where(column == lanes, 1.0, 0.0).astype(BF16)
-
-
-def screen_kernel(index_ref, phase_ref, beam_ref, screen_ref):
+def row_of_blocks(values):
+    return jnp.concatenate([values[at : at + 1, :] for at in range(values.shape[0])], axis=1)
+
+
+def down(row):
+    return jnp.broadcast_to(row, (128, 128)).T
+
+
+def onehot(column, first, count):
+    lanes = lax.broadcasted_iota(jnp.int32, (128, 128), 1)
+    width = min(count, 128)
+    parts = [
+        jnp.where(column == lanes + (first + at), 1.0, 0.0).astype(BF16)[:, :width] for at in range(0, count, 128)
+    ]
+    return parts[0] if len(parts) == 1 else jnp.concatenate(parts, axis=1)
+
+
+def slot_of(subgrid, core, cores, owned):
+    held = lax.rem(lax.div(subgrid, owned) + (cores - core), cores)
+    return (held * (128 // cores)) + lax.div(subgrid, owned * cores) * owned + lax.rem(subgrid, owned)
+
+
+def screen_kernel(stations_ref, plane_ref, phase_ref, beam_ref, screen_ref):
     stations = beam_ref.shape[0]
     planes, pixels = phase_ref.shape
-    one = onehot_rows(index_ref[:, 0:1], stations)
-    two = onehot_rows(index_ref[:, 1:2], stations)
-    plane = onehot_rows(index_ref[:, 2:3], planes).astype(F32)
+    one = onehot(down(row_of_blocks(stations_ref[:, 0, :])), 0, stations)
+    two = onehot(down(row_of_blocks(stations_ref[:, 1, :])), 0, stations)
+    plane = onehot(down(row_of_blocks(plane_ref[...])), 0, planes).astype(F32)
     width = 256
     for at in range(0, pixels, width):
         re, im = pl.ds(at, width), pl.ds(pixels + at, width)
@@ -56,9 +75,12 @@
         screen_ref[:, im] = pair_re * wave_im + pair_im * wave_re
 
 
-def table_kernel(coords_ref, freq_ref, east_ref, north_re_ref, north_im_ref, *powers):
-    rows = coords_ref.shape[0] // 2
-    angle = (TWO_PI * coords_ref[...]) * (1.0 / 32.0) * freq_ref[...]
+def table_kernel(place_ref, coords_ref, freq_ref, east_ref, north_re_ref, north_im_ref, *powers):
+    rows = coords_ref.shape[2]
+    coords = coords_ref[place_ref[0]]
+    row = jnp.concatenate([coords[0:1], coords[1:2], jnp.zeros((1, 128 - 2 * rows), F32)], axis=1)
+    column = (TWO_PI * down(row)[: 2 * rows]) * (1.0 / 32.0)
+    angle = jnp.concatenate([column] * (freq_ref.shape[1] // 128), axis=1) * freq_ref[...]
     z1 = (jnp.cos(angle), jnp.sin(angle))
     z2 = cmul(z1, z1)
     z4 = cmul(z2, z2)
@@ -102,12 +124,12 @@
     lax.fori_loop(0, rows, body, 0)
 
 
-def image_kernel(index_ref, near_ref, far_ref, screen_ref, image_ref):
+def image_kernel(cores, owned, place_ref, subgrid_ref, near_ref, far_ref, screen_ref, image_ref):
     half = near_ref.shape[0]
     pixels = screen_ref.shape[1] // 2
     blocks = image_ref.shape[0]
-    slots = onehot_rows(index_ref[:, 3:4], 2 * half)
-    near, far = (slots[:, :half], slots[:, half:])
+    slots = down(slot_of(row_of_blocks(subgrid_ref[...]), place_ref[3], cores, owned))
+    near, far = (onehot(slots, 0, half), onehot(slots, half, half))
     tiles = pixels // 128
     width = 256
 
@@ -129,8 +151,40 @@
             image_ref[:, 16 * q : 16 * q + 16, :] = image_im[:, off : off + 128].reshape(blocks, 16, 128)
 
 
+def route_kernel(n_y, n_h, place_ref, reader_ref, rows_ref, other_ref, *out_refs):
+    block = jnp.int32(0)
+    for at in range(n_y * n_h):
+        block = jnp.where(reader_ref[0, at] == place_ref[0], at, block)
+    for by, out_ref in enumerate(out_refs, 1):
+        to = lax.rem(place_ref[1] + by, n_y) * n_h + place_ref[2]
+
+        @pl.when(block == to)
+        def _():
+            out_ref[...] = rows_ref[...]
+
+        @pl.when(block != to)
+        def _():
+            out_ref[...] = other_ref[...]
+
+
 def visibility_kernel(
-    images_ref, visible_ref, east_ref, north_re_ref, north_im_ref, resid_ref, grid_ref, cells_ref, out_ref
+    n_y,
+    n_h,
+    place_ref,
+    reader_ref,
+    images_ref,
+    rows_ref,
+    other_ref,
+    came_1_ref,
+    came_2_ref,
+    came_3_ref,
+    east_ref,
+    north_re_ref,
+    north_im_ref,
+    resid_ref,
+    grid_ref,
+    cells_ref,
+    out_ref,
 ):
     rows, channels = (resid_ref.shape[0], resid_ref.shape[1] // 2)
     facets = images_ref.shape[0]
@@ -138,7 +192,16 @@
     for at in range(1, facets):
         total = total + images_ref[at].astype(F32)
     cells_ref[...] = total
-    resid_ref[...] = visible_ref[...].astype(F32)
+    source = reader_ref[0, place_ref[0]]
+    steps = lax.rem(place_ref[1] + n_y - lax.div(source, n_h), n_y)
+    here = jnp.where(lax.rem(source, n_h) == place_ref[2], 0, 1)
+    pick = jnp.where(steps == 0, here, steps + 1)
+    for at, ref in enumerate((rows_ref, other_ref, came_1_ref, came_2_ref, came_3_ref)):
+
+        @pl.when(pick == at)
+        def _():
+            resid_ref[...] = ref[...].astype(F32)
+
     width = 256
 
     def degrid(b, carry):
@@ -194,19 +257,23 @@
 
     lax.fori_loop(0, rows, degrid, 0, unroll=4)
     lax.fori_loop(0, rows, grid, 0, unroll=4)
-    packed = out_ref[...].astype(BF16)
-    for at in range(facets):
-        grid_ref[at] = packed
-
-
-def regrid_kernel(scale, target_ref, grid_ref, screen_ref, near_ref, far_ref):
+    grid_ref[...] = out_ref[...].astype(BF16)
+
+
+def regrid_kernel(scale, n_y, n_h, cores, owned, place_ref, subgrid_ref, screen_ref, *refs):
+    grids, (near_ref, far_ref, grid_ref) = (refs[:-3], refs[-3:])
+    for at, ref in enumerate(grids):
+        by, flip = divmod(at, n_h)
+        block = lax.rem(place_ref[1] + (n_y - by), n_y) * n_h + lax.rem(place_ref[2] + flip, n_h)
+        grid_ref[block] = ref[...]
     half = near_ref.shape[0]
     pixels = screen_ref.shape[1] // 2
     tiles = pixels // 128
     count = screen_ref.shape[0]
     subs = lax.broadcasted_iota(jnp.int32, (2 * half, count), 0)
-    onehot = jnp.where(target_ref[...] == subs, 1.0, 0.0).astype(BF16)
-    near, far = (onehot[:half], onehot[half:])
+    target = slot_of(row_of_blocks(subgrid_ref[...]), place_ref[3], cores, owned)
+    sums = jnp.where(target == subs, 1.0, 0.0).astype(BF16)
+    near, far = (sums[:half], sums[half:])
     for q in range(tiles):
         re, im = pl.ds(128 * q, 128), pl.ds(pixels + 128 * q, 128)
         grid_re = grid_ref[:, 16 * q : 16 * q + 16, :].reshape(count, 128).astype(F32)
@@ -245,115 +312,107 @@
     n_y, n_h, n_x, n_z, n_c = (lax.axis_size(axis) for axis in FACET + TILE)
     at_y, at_h, at_x, at_z, at_c = (lax.axis_index(axis) for axis in FACET + TILE)
     n_facet = n_y * n_h
-    facet_id = at_y * n_h + at_h
     channels = channel_freq.shape[0]
-    planes, pixels = plane_phase.shape
+    pixels = plane_phase.shape[1]
     row_block = sectioned_rows.shape[1]
     count = n_facet * row_block
     owned = model_grid.shape[1]
     subgrid_count = owned * n_x * n_z * n_c
+    cell_rows = 2 * pixels // 128 * row_block
     grid_scale = 1.0 / math.sqrt(channels * n_facet * (row_block * n_x * n_z * n_c) / subgrid_count)
+    ids = jnp.arange(4, dtype=jnp.int32)
+    place = jnp.where(
+        ids == 0, at_y * n_h + at_h, jnp.where(ids == 1, at_y, jnp.where(ids == 2, at_h, at_c))
+    ).astype(jnp.int32)
 
     with jax.named_scope("model_gather"):
-        own = model_grid[0]
-        column = jnp.concatenate([own] + [shift(own, "z", by) for by in range(1, n_z)], axis=0)
-        near = jnp.concatenate([column] + [shift(column, "x", by) for by in range(1, n_x)], axis=0)
+        copies = jnp.broadcast_to(model_grid, (n_x * n_z, owned, 2 * pixels))
+        near = lax.all_to_all(copies, ("x", "z"), split_axis=0, concat_axis=0, tiled=True)
+        near = near.reshape(n_x * n_z * owned, 2 * pixels)
         far = shift(near, "c", 1)
-
-    with jax.named_scope("visible_route"):
-        rows = sectioned_rows[0]
-        other = shift(rows, "h", 1)
-        read_by = reader[0]
-        block_of = jnp.sum(
-            jnp.where(
-                read_by[None, :] == jnp.arange(n_facet, dtype=jnp.int32)[:, None],
-                jnp.arange(n_facet, dtype=jnp.int32)[None, :],
-                0,
-            ),
-            axis=1,
-        )
-        mine_to = block_of[facet_id]
-        source = read_by[facet_id]
-        visible = jnp.where(source // n_h == at_y, jnp.where(source % n_h == at_h, rows, other), 0)
-        for by in range(1, n_y):
-            to = ((at_y + by) % n_y) * n_h + at_h
-            came = shift(jnp.where(mine_to == to, rows, other), "y", by)
-            visible = jnp.where((source // n_h + by) % n_y == at_y, came, visible)
-
-    sub = subgrid_index.reshape(count)
-    sub_row, sub_c = (sub % owned, (sub // owned) % n_c)
-    sub_z, sub_x = ((sub // (owned * n_c)) % n_z, sub // (owned * n_c * n_z))
-    core = (sub_c - at_c) % n_c
-    slot = ((core * n_x + (at_x - sub_x) % n_x) * n_z + (at_z - sub_z) % n_z) * owned + sub_row
-    target = ((core * n_x + sub_x) * n_z + sub_z) * owned + sub_row
-    index = jnp.stack(
-        [stations[:, 0].reshape(count), stations[:, 1].reshape(count), plane_index.reshape(count), slot], axis=1
-    )
 
     screen = pl.pallas_call(
         screen_kernel,
         out_shape=jax.ShapeDtypeStruct((count, 2 * pixels), F32),
-        in_specs=[VMEM] * 3,
+        in_specs=[VMEM] * 4,
         out_specs=VMEM,
-        compiler_params=params(32),
+        compiler_params=params(16),
         cost_estimate=pl.CostEstimate(flops=10**9, bytes_accessed=4 << 20, transcendentals=1 << 16),
         name="screens",
-    )(index, plane_phase, beam_screens[0])
-
-    coords = lax.dynamic_index_in_dim(baseline_coords, facet_id, 0, keepdims=False).reshape(2 * row_block, 1)
+    )(stations, plane_index, plane_phase, beam_screens[0])
+
     east, north_re, north_im = pl.pallas_call(
         table_kernel,
         out_shape=[jax.ShapeDtypeStruct((row_block, 64, channels), BF16)] * 3,
-        in_specs=[VMEM] * 2,
+        in_specs=[SMEM, VMEM, VMEM],
         out_specs=[VMEM] * 3,
         scratch_shapes=[
             pltpu.VMEM((10, 2 * row_block, channels), F32),
             pltpu.VMEM((8, 2 * row_block, channels), F32),
         ],
-        compiler_params=params(32),
+        compiler_params=params(16),
         cost_estimate=pl.CostEstimate(flops=10**8, bytes_accessed=6 << 20, transcendentals=1 << 16),
         name="tables",
-    )(coords, channel_freq.reshape(1, channels))
-
+    )(place, baseline_coords, channel_freq.reshape(1, channels))
+
+    with jax.named_scope("visible_route"):
+        rows, east = lax.optimization_barrier((sectioned_rows[0], east))
+        other = shift(rows, "h", 1)
+        sent = pl.pallas_call(
+            functools.partial(route_kernel, n_y, n_h),
+            out_shape=[jax.ShapeDtypeStruct(rows.shape, BF16)] * (n_y - 1),
+            in_specs=[SMEM, SMEM, VMEM, VMEM],
+            out_specs=[VMEM] * (n_y - 1),
+            compiler_params=params(4),
+            cost_estimate=pl.CostEstimate(flops=10**6, bytes_accessed=1 << 18, transcendentals=0),
+            name="route",
+        )(place, reader, rows, other)
+
+    near, far, screen, east = lax.optimization_barrier((near, far, screen, east))
     images = pl.pallas_call(
-        image_kernel,
-        out_shape=jax.ShapeDtypeStruct((n_facet, 2 * pixels // 128 * row_block, 128), BF16),
-        in_specs=[VMEM] * 4,
+        functools.partial(image_kernel, n_c, owned),
+        out_shape=jax.ShapeDtypeStruct((n_facet, cell_rows, 128), BF16),
+        in_specs=[SMEM] + [VMEM] * 4,
         out_specs=VMEM,
-        compiler_params=params(32),
+        compiler_params=params(8),
         cost_estimate=pl.CostEstimate(flops=10**8, bytes_accessed=2 << 20, transcendentals=0),
         name="images",
-    )(index, near, far, screen)
+    )(place, subgrid_index, near, far, screen)
 
     arrived = lax.all_to_all(images, FACET, split_axis=0, concat_axis=0, tiled=True)
-
-    cell_rows = 2 * pixels // 128 * row_block
+    came = [shift(value, "y", by) for by, value in enumerate(sent, 1)]
+
     residual, gridded = pl.pallas_call(
-        visibility_kernel,
+        functools.partial(visibility_kernel, n_y, n_h),
         out_shape=[
             jax.ShapeDtypeStruct((row_block, 2 * channels), F32),
-            jax.ShapeDtypeStruct((n_facet, cell_rows, 128), BF16),
+            jax.ShapeDtypeStruct((cell_rows, 128), BF16),
         ],
-        in_specs=[VMEM] * 5,
+        in_specs=[SMEM] * 2 + [VMEM] * 9,
         out_specs=[VMEM] * 2,
         scratch_shapes=[pltpu.VMEM((cell_rows, 128), F32), pltpu.VMEM((cell_rows, 128), F32)],
-        compiler_params=params(48),
+        compiler_params=params(16),
         cost_estimate=pl.CostEstimate(flops=10**9, bytes_accessed=8 << 20, transcendentals=0),
         name="visibilities",
-    )(arrived, visible, east, north_re, north_im)
-
-    gathered = lax.all_to_all(gridded, FACET, split_axis=0, concat_axis=0, tiled=True)
+    )(place, reader, arrived, rows, other, *came, east, north_re, north_im)
+
+    with jax.named_scope("grid_gather"):
+        beside = shift(gridded, "h", 1)
+        grids = [gridded, beside]
+        for by in range(1, n_y):
+            grids += [shift(gridded, "y", by), shift(beside, "y", by)]
 
     half = subgrid_count // n_c
     near_sum, far_sum = pl.pallas_call(
-        lambda *refs: regrid_kernel(grid_scale, *refs),
+        functools.partial(regrid_kernel, grid_scale, n_y, n_h, n_c, owned),
         out_shape=[jax.ShapeDtypeStruct((half, 2 * pixels), F32)] * 2,
-        in_specs=[VMEM] * 3,
+        in_specs=[SMEM] + [VMEM] * (2 + n_facet),
         out_specs=[VMEM] * 2,
-        compiler_params=params(32),
+        scratch_shapes=[pltpu.VMEM((n_facet, cell_rows, 128), BF16)],
+        compiler_params=params(8),
         cost_estimate=pl.CostEstimate(flops=10**8, bytes_accessed=3 << 20, transcendentals=0),
         name="regrid",
-    )(target.reshape(1, count), gathered, screen)
+    )(place, subgrid_index, screen, *grids)
 
     with jax.named_scope("dirty_scatter"):
         chip_sum = (near_sum + shift(far_sum, "c", 1)).astype(BF16).reshape(n_x * n_z, owned, 2 * pixels)

time: 110 us -> 119 us (1.082)
  blocking collectives: 17.7 us -> 33 us
  between operations: 5.46 us -> 0.75 us
  starting transfers between devices: 39.6 us -> 35.2 us
  waiting for transfers between devices: 18.7 us -> 21.2 us
  Pallas kernels: 13.5 us -> 15.6 us
  other arithmetic: 2.5 us -> 0.79 us
    all_to_all x0 -> x1, blocking collectives: none -> 18.5 us  [local(): lax.all_to_all(copies, ('x', 'z'), split_axis=0, concat_axis=0, tiled=True)]
    ppermute x12 -> x13, waiting for transfers between devices: 4.94 us -> 21.1 us  [shift(): lax.ppermute(value, axis, [(i, (i + by) % size) for i in range(size)])]
    all_to_all x1 -> x0, waiting for transfers between devices: 12.1 us -> none  [local(): lax.all_to_all(gridded, FACET, split_axis=0, concat_axis=0, tiled=True)]
    all_to_all x1 -> x0, starting transfers between devices: 5.61 us -> none  [local(): lax.all_to_all(gridded, FACET, split_axis=0, concat_axis=0, tiled=True)]
    unnamed x22 -> x26, local copies, waits for them, and re-layouts: 7.55 us -> 11.1 us
    all_to_all x1, blocking collectives: 17.7 us -> 14.5 us  [local(): lax.all_to_all(chip_sum, ('x', 'z'), split_axis=0, concat_axis=0, tiled=T...]
    all_to_all x1, waiting for transfers between devices: 1.62 us -> 0.01 us  [local(): lax.all_to_all(images, FACET, split_axis=0, concat_axis=0, tiled=True)]
    pallas_call x3 -> x4, Pallas kernels: 8.29 us -> 9.77 us  [the longest x1 5.53 us: local(): pl.pallas_call(functools.partial(visibility_kernel, n_y, n_h), out_shape=...]
  transfers between devices with their start and end apart: 14 -> 14, of which waited for: 5 -> 8; matrix products, arithmetic and copies ran while one was open for 6% -> 0% of each run, Pallas kernels for 6% -> 5%
where the time goes in v2:
time: 119 us
  starting transfers between devices  35.2 us (30%)
  blocking collectives  33 us (28%)
  waiting for transfers between devices  21.2 us (18%)
  Pallas kernels  15.6 us (13%)
  local copies, waits for them, and re-layouts  12.1 us (10%)
    ppermute x13, starting transfers between devices, shift(): lax.ppermute(value, axis, [(i, (i + by) % size) for i in range(size)])  27.1 us
    ppermute x13, waiting for transfers between devices, shift(): lax.ppermute(value, axis, [(i, (i + by) % size) for i in range(size)])  21.1 us
    all_to_all x1, blocking collectives, local(): lax.all_to_all(copies, ('x', 'z'), split_axis=0, concat_axis=0, tiled=True)  18.5 us
    all_to_all x1, blocking collectives, local(): lax.all_to_all(chip_sum, ('x', 'z'), split_axis=0, concat_axis=0, tiled=T...  14.5 us
    unnamed x26, local copies, waits for them, and re-layouts  11.1 us
    all_to_all x1, starting transfers between devices, local(): lax.all_to_all(images, FACET, split_axis=0, concat_axis=0, tiled=True)  8.12 us
    pallas_call x1, Pallas kernels, local(): pl.pallas_call(functools.partial(visibility_kernel, n_y, n_h), out_shape=...  5.53 us
    pallas_call x1, Pallas kernels, local(): pl.pallas_call(table_kernel, out_shape=[jax.ShapeDtypeStruct((row_block,...  3.83 us
  transfers between devices with their start and end apart: 14, of which 8 were waited for; matrix products, arithmetic and copies ran while one was open for 0% of the time, Pallas kernels for 5%

profile of v2, /device:TPU:1, one launch (start us, length us, event | category | flops | bytes accessed | tf_op | source)
XLA Modules:
  0.0 118.6 jit_solution(8770616492839933317)
XLA Ops:
  0.6 0.8 broadcast_in_dim.33
  1.5 18.5 %all_to_all.15 = bf16[16,4,2048]{2,1,0:T(4,128)(2,1)S(1)} all-to-all(bf16[16,4,2048]{2,1,0:T(4,128)(2,1)S(1)} %broadcast_in_dim.33), channel_id=1, replica_groups=mesh['y'=4,'h'=2,'x'=4,'z'=4,'c'=2] {'x','z'}, dimensions={0} | all-to-all | bytes 524288 | tf_op jit(solution)/shard_map/model_gather/all_to_all | solution.py:330
  20.0 0.1 reshape.13.near_ref
  20.0 0.0 copy-start.5
  20.0 2.2 %collective-permute-start = (bf16[64,2048]{1,0:T(8,128)(2,1)S(1)}, bf16[64,2048]{1,0:T(8,128)(2,1)}, u32[]{:S(2)}, u32[]{:S(2)}) collective-permute-start(bf16[64,2048]{1,0:T(8,128)(2,1)S(1)} %reshape.13.near_ref), channel_id=1, source_target_pairs={{0,1},{1,0},{2,3},{3,2},{4,5},{5,4},{6,7},{7,6},{8,9},{9,8},{10,11... | collective-permute-start | bytes 786440 | tf_op jit(solution)/shard_map/model_gather/ppermute | solution.py:297
  22.3 0.7 copy-done.9
  23.0 0.7 copy-done.11
  23.7 3.8 %tables.1 = (bf16[16,64,1024]{2,1,0:T(8,128)(2,1)S(1)}, bf16[16,64,1024]{2,1,0:T(8,128)(2,1)S(1)}, bf16[16,64,1024]{2,1,0:T(8,128)(2,1)S(1)}) custom-call(s32[4]{0:T(128)S(1)} %compare_select_fusion.2.place_ref, f32[8,2,16]{2,1,0:T(2,128)S(1)} %copy-done.9, f32[1,1024]{1,0:T(1,128)S(1)} %bitcast.10), custom_call_target="tpu_custom_call" | custom-call | flops 100000000 | bytes 6291456 | tf_op jit(solution)/shard_map/tables/pallas_call | solution.py:344
  27.5 1.3 %copy-done = bf16[16,64,1024]{2,1,0:T(8,128)(2,1)} copy-done((bf16[16,64,1024]{2,1,0:T(8,128)(2,1)}, bf16[16,64,1024]{2,1,0:T(8,128)(2,1)S(1)}, u32[]{:S(2)}) %copy-start) | copy-done | bytes 2097176
  28.8 1.3 %copy-done.2 = bf16[16,64,1024]{2,1,0:T(8,128)(2,1)} copy-done((bf16[16,64,1024]{2,1,0:T(8,128)(2,1)}, bf16[16,64,1024]{2,1,0:T(8,128)(2,1)S(1)}, u32[]{:S(2)}) %copy-start.2) | copy-done | bytes 2097176
  30.1 1.6 %copy-done.7 = bf16[1,512,2048]{2,1,0:T(8,128)(2,1)S(1)} copy-done((bf16[1,512,2048]{2,1,0:T(8,128)(2,1)S(1)}, bf16[1,512,2048]{2,1,0:T(8,128)(2,1)}, u32[]{:S(2)}) %copy-start.7) | copy-done | bytes 2097176
  31.7 0.9 copy-done.8
  32.6 0.7 copy-done.10
  33.3 0.7 copy-done.12
  34.0 2.0 %screens.1.screen_ref = f32[128,2048]{1,0:T(8,128)S(1)} custom-call(s32[8,2,16]{2,1,0:T(2,128)S(1)} %copy-done.10, s32[8,16]{1,0:T(8,128)S(1)} %copy-done.12, f32[32,1024]{1,0:T(8,128)S(1)} %copy-done.8, bf16[512,2048]{1,0:T(8,128)(2,1)S(1)} %bitcast.9), custom_call_target="tpu_custom_call" | custom-call | flops 1000000000 | bytes 4194304 | tf_op jit(solution)/shard_map/screens/pallas_call | solution.py:334
  36.0 0.0 copy-start.4
  36.0 0.0 copy-start.6
  36.1 0.0 collective-permute-done.far_ref
  36.1 2.3 %images.1 = bf16[8,256,128]{2,1,0:T(8,128)(2,1)} custom-call(s32[4]{0:T(128)S(1)} %compare_select_fusion.2.place_ref, s32[8,16]{1,0:T(8,128)S(1)} %copy-done.5, bf16[64,2048]{1,0:T(8,128)(2,1)S(1)} %reshape.13.near_ref, bf16[64,2048]{1,0:T(8,128)(2,1)} %collective-permute-done.far_ref, f32[128,2048]{1,0:T(8,128)S(1)} %screens.1.screen_ref), custom_call_target="tpu_custom_call" | custom-call | flops 100000000 | bytes 2097152 | tf_op jit(solution)/shard_map/images/pallas_call | solution.py:372
  38.4 8.1 %all-to-all-start.1 = ((bf16[8,256,128]{2,1,0:T(8,128)(2,1)}), bf16[8,256,128]{2,1,0:T(8,128)(2,1)}, u32[]{:S(2)}, u32[]{:S(2)}) async-start(bf16[8,256,128]{2,1,0:T(8,128)(2,1)} %images.1), calls=%async_computation.1 | async-start | bytes 1048576 | tf_op jit(solution)/shard_map/all_to_all | solution.py:382
  46.5 5.4 %collective-permute-start.1 = (bf16[16,2048]{1,0:T(8,128)(2,1)S(1)}, bf16[16,2048]{1,0:T(8,128)(2,1)S(1)}, u32[]{:S(2)}, u32[]{:S(2)}) collective-permute-start(bf16[16,2048]{1,0:T(8,128)(2,1)S(1)} %bitcast.6), channel_id=1, source_target_pairs={{0,32},{32,0},{1,33},{33,1},{2,34},{34,2},{3,35},{35,3},{4,36},{36... | collective-permute-start | bytes 196616 | tf_op jit(solution)/shard_map/visible_route/ppermute | solution.py:297
  51.9 9.6 %collective-permute-done.1.other_ref = bf16[16,2048]{1,0:T(8,128)(2,1)S(1)} collective-permute-done((bf16[16,2048]{1,0:T(8,128)(2,1)S(1)}, bf16[16,2048]{1,0:T(8,128)(2,1)S(1)}, u32[]{:S(2)}, u32[]{:S(2)}) %collective-permute-start.1) | collective-permute-done | bytes 65568 | tf_op jit(solution)/shard_map/visible_route/ppermute | solution.py:297
  61.5 0.6 route.1
  62.1 3.7 %collective-permute-start.2 = (bf16[16,2048]{1,0:T(8,128)(2,1)S(1)}, bf16[16,2048]{1,0:T(8,128)(2,1)S(1)}, u32[]{:S(2)}, u32[]{:S(2)}) collective-permute-start(bf16[16,2048]{1,0:T(8,128)(2,1)S(1)} %get-tuple-element.24), channel_id=1, source_target_pairs={{0,64},{64,128},{128,192},{192,0},{1,65},{65,129},{129,193},{193,1... | collective-permute-start | bytes 196616 | tf_op jit(solution)/shard_map/ppermute | solution.py:297
  65.7 2.5 %collective-permute-start.3 = (bf16[16,2048]{1,0:T(8,128)(2,1)S(1)}, bf16[16,2048]{1,0:T(8,128)(2,1)S(1)}, u32[]{:S(2)}, u32[]{:S(2)}) collective-permute-start(bf16[16,2048]{1,0:T(8,128)(2,1)S(1)} %get-tuple-element.25), channel_id=1, source_target_pairs={{0,128},{64,192},{128,0},{192,64},{1,129},{65,193},{129,1},{193,65... | collective-permute-start | bytes 196616 | tf_op jit(solution)/shard_map/ppermute | solution.py:297
  68.2 1.1 collective-permute-start.4
  69.3 1.3 %collective-permute-done.3.came_2_ref = bf16[16,2048]{1,0:T(8,128)(2,1)S(1)} collective-permute-done((bf16[16,2048]{1,0:T(8,128)(2,1)S(1)}, bf16[16,2048]{1,0:T(8,128)(2,1)S(1)}, u32[]{:S(2)}, u32[]{:S(2)}) %collective-permute-start.3) | collective-permute-done | bytes 65568 | tf_op jit(solution)/shard_map/ppermute | solution.py:297
  70.6 1.1 collective-permute-done.4.came_3_ref
  71.7 1.6 %copy-done.1 = bf16[16,64,1024]{2,1,0:T(8,128)(2,1)S(1)} copy-done((bf16[16,64,1024]{2,1,0:T(8,128)(2,1)S(1)}, bf16[16,64,1024]{2,1,0:T(8,128)(2,1)}, u32[]{:S(2)}) %copy-start.1) | copy-done | bytes 2097176
  73.3 1.6 %copy-done.3 = bf16[16,64,1024]{2,1,0:T(8,128)(2,1)S(1)} copy-done((bf16[16,64,1024]{2,1,0:T(8,128)(2,1)S(1)}, bf16[16,64,1024]{2,1,0:T(8,128)(2,1)}, u32[]{:S(2)}) %copy-start.3) | copy-done | bytes 2097176
  74.8 5.5 %visibilities.1 = (f32[16,2048]{1,0:T(8,128)}, bf16[256,128]{1,0:T(8,128)(2,1)S(1)}) custom-call(s32[4]{0:T(128)S(1)} %compare_select_fusion.2.place_ref, s32[1,8]{1,0:T(1,128)S(1)} %copy-done.6, bf16[8,256,128]{2,1,0:T(8,128)(2,1)} %all-to-all-done.1.images_ref, bf16[16,2048]{1,0:T(8,128)(2,1)S(1)} %bitcast.8, ...), custom_call_target="tpu_custom_call" | custom-call | flops 1000000000 | bytes 8388608 | tf_op jit(solution)/shard_map/visibilities/pallas_call | solution.py:385
  80.4 0.8 collective-permute-start.5
  81.2 2.4 %collective-permute-start.10 = (bf16[256,128]{1,0:T(8,128)(2,1)S(1)}, bf16[256,128]{1,0:T(8,128)(2,1)S(1)}, u32[]{:S(2)}, u32[]{:S(2)}) collective-permute-start(bf16[256,128]{1,0:T(8,128)(2,1)S(1)} %get-tuple-element.31.refs_0_), channel_id=1, source_target_pairs={{0,192},{64,0},{128,64},{192,128},{1,193},{65,1},{129,65},{193,129... | collective-permute-start | bytes 196616 | tf_op jit(solution)/shard_map/grid_gather/ppermute | solution.py:297
  83.6 0.6 collective-permute-start.6
  84.1 3.3 %collective-permute-done.5.refs_1_ = bf16[256,128]{1,0:T(8,128)(2,1)S(1)} collective-permute-done((bf16[256,128]{1,0:T(8,128)(2,1)S(1)}, bf16[256,128]{1,0:T(8,128)(2,1)S(1)}, u32[]{:S(2)}, u32[]{:S(2)}) %collective-permute-start.5) | collective-permute-done | bytes 65568 | tf_op jit(solution)/shard_map/grid_gather/ppermute | solution.py:297
  87.4 2.0 %collective-permute-start.11 = (bf16[256,128]{1,0:T(8,128)(2,1)S(1)}, bf16[256,128]{1,0:T(8,128)(2,1)S(1)}, u32[]{:S(2)}, u32[]{:S(2)}) collective-permute-start(bf16[256,128]{1,0:T(8,128)(2,1)S(1)} %collective-permute-done.5.refs_1_), channel_id=1, source_target_pairs={{0,192},{64,0},{128,64},{192,128},{1,193},{65,1},{129,65},{193,129... | collective-permute-start | bytes 196616 | tf_op jit(solution)/shard_map/grid_gather/ppermute | solution.py:297
  89.4 0.0 collective-permute-start.9
  89.4 0.6 collective-permute-start.7
  90.0 1.3 %collective-permute-done.11.refs_7_ = bf16[256,128]{1,0:T(8,128)(2,1)S(1)} collective-permute-done((bf16[256,128]{1,0:T(8,128)(2,1)S(1)}, bf16[256,128]{1,0:T(8,128)(2,1)S(1)}, u32[]{:S(2)}, u32[]{:S(2)}) %collective-permute-start.11) | collective-permute-done | bytes 65568 | tf_op jit(solution)/shard_map/grid_gather/ppermute | solution.py:297
  91.3 2.8 %collective-permute-done.9.refs_5_ = bf16[256,128]{1,0:T(8,128)(2,1)S(1)} collective-permute-done((bf16[256,128]{1,0:T(8,128)(2,1)S(1)}, bf16[256,128]{1,0:T(8,128)(2,1)S(1)}, u32[]{:S(2)}, u32[]{:S(2)}) %collective-permute-start.9) | collective-permute-done | bytes 65568 | tf_op jit(solution)/shard_map/grid_gather/ppermute | solution.py:297
  94.1 0.3 collective-permute-done.7.refs_3_
  94.4 1.3 %regrid.1 = (f32[64,2048]{1,0:T(8,128)S(1)}, f32[64,2048]{1,0:T(8,128)S(1)}) custom-call(s32[4]{0:T(128)S(1)} %compare_select_fusion.2.place_ref, s32[8,16]{1,0:T(8,128)S(1)} %copy-done.5, f32[128,2048]{1,0:T(8,128)S(1)} %screens.1.screen_ref, bf16[256,128]{1,0:T(8,128)(2,1)S(1)} %get-tuple-element.31.refs_0_, ...), custom_call_target="tpu_custom_call" | custom-call | flops 100000000 | bytes 3145728 | tf_op jit(solution)/shard_map/regrid/pallas_call | solution.py:406
  95.7 5.9 %collective-permute-start.12 = (f32[64,2048]{1,0:T(8,128)S(1)}, f32[64,2048]{1,0:T(8,128)S(1)}, u32[]{:S(2)}, u32[]{:S(2)}) collective-permute-start(f32[64,2048]{1,0:T(8,128)S(1)} %get-tuple-element.33), channel_id=1, source_target_pairs={{0,1},{1,0},{2,3},{3,2},{4,5},{5,4},{6,7},{7,6},{8,9},{9,8},{10,11... | collective-permute-start | bytes 1572872 | tf_op jit(solution)/shard_map/dirty_scatter/ppermute | solution.py:297
  101.7 1.5 %collective-permute-done.12 = f32[64,2048]{1,0:T(8,128)S(1)} collective-permute-done((f32[64,2048]{1,0:T(8,128)S(1)}, f32[64,2048]{1,0:T(8,128)S(1)}, u32[]{:S(2)}, u32[]{:S(2)}) %collective-permute-start.12) | collective-permute-done | bytes 524320 | tf_op jit(solution)/shard_map/dirty_scatter/ppermute | solution.py:297
  103.2 0.1 add_convert_fusion
  103.3 0.1 reshape.15
  103.4 14.5 %all_to_all.16 = bf16[16,4,2048]{2,1,0:T(4,128)(2,1)S(1)} all-to-all(bf16[16,4,2048]{2,1,0:T(4,128)(2,1)S(1)} %reshape.15), channel_id=1, replica_groups=mesh['y'=4,'h'=2,'x'=4,'z'=4,'c'=2] {'x','z'}, dimensions={0} | all-to-all | bytes 524288 | tf_op jit(solution)/shard_map/dirty_scatter/all_to_all | solution.py:419
  117.9 0.7 convert_reduce_fusion
  (20 shorter events, 0.0 us)
Async XLA Ops:
  20.0 16.0 %copy-start.5 = (s32[8,16]{1,0:T(8,128)S(1)}, s32[8,16]{1,0:T(8,128)}, u32[]{:S(2)}) copy-start(s32[8,16]{1,0:T(8,128)} %subgrid_ref.3) | copy-start | bytes 1540
  20.0 16.0 %collective-permute-start = (bf16[64,2048]{1,0:T(8,128)(2,1)S(1)}, bf16[64,2048]{1,0:T(8,128)(2,1)}, u32[]{:S(2)}, u32[]{:S(2)}) collective-permute-start(bf16[64,2048]{1,0:T(8,128)(2,1)S(1)} %reshape.13.near_ref), channel_id=1, source_target_pairs={{0,1},{1,0},{2,3},{3,2},{4,5},{5,4},{6,7},{7,6},{8,9},{9,8},{10,11... | collective-permute-start | bytes 786440 | tf_op jit(solution)/shard_map/model_gather/ppermute | solution.py:297
  22.3 0.7 copy-start.9
  23.0 0.7 copy-start.11
  27.5 1.3 %copy-start = (bf16[16,64,1024]{2,1,0:T(8,128)(2,1)}, bf16[16,64,1024]{2,1,0:T(8,128)(2,1)S(1)}, u32[]{:S(2)}) copy-start(bf16[16,64,1024]{2,1,0:T(8,128)(2,1)S(1)} %get-tuple-element.28.north_re_ref) | copy-start | bytes 6291460
  28.8 1.3 %copy-start.2 = (bf16[16,64,1024]{2,1,0:T(8,128)(2,1)}, bf16[16,64,1024]{2,1,0:T(8,128)(2,1)S(1)}, u32[]{:S(2)}) copy-start(bf16[16,64,1024]{2,1,0:T(8,128)(2,1)S(1)} %get-tuple-element.29.north_im_ref) | copy-start | bytes 6291460
  30.1 1.6 %copy-start.7 = (bf16[1,512,2048]{2,1,0:T(8,128)(2,1)S(1)}, bf16[1,512,2048]{2,1,0:T(8,128)(2,1)}, u32[]{:S(2)}) copy-start(bf16[1,512,2048]{2,1,0:T(8,128)(2,1)} %param.17) | copy-start | bytes 6291460
  31.7 0.9 copy-start.8
  32.6 0.7 copy-start.10
  33.3 0.7 copy-start.12
  36.0 10.5 %copy-start.4 = (bf16[1,16,2048]{2,1,0:T(8,128)(2,1)S(1)}, bf16[1,16,2048]{2,1,0:T(8,128)(2,1)}, u32[]{:S(2)}) copy-start(bf16[1,16,2048]{2,1,0:T(8,128)(2,1)} %param.10) | copy-start | bytes 196612
  36.0 25.4 %copy-start.6 = (s32[1,8]{1,0:T(1,128)S(1)}, s32[1,8]{1,0:T(1,128)}, u32[]{:S(2)}) copy-start(s32[1,8]{1,0:T(1,128)} %reader_ref.3) | copy-start | bytes 100
  38.4 33.2 %all-to-all-start.1 = ((bf16[8,256,128]{2,1,0:T(8,128)(2,1)}), bf16[8,256,128]{2,1,0:T(8,128)(2,1)}, u32[]{:S(2)}, u32[]{:S(2)}) async-start(bf16[8,256,128]{2,1,0:T(8,128)(2,1)} %images.1), calls=%async_computation.1 | async-start | bytes 1048576 | tf_op jit(solution)/shard_map/all_to_all | solution.py:382
  46.5 14.9 %collective-permute-start.1 = (bf16[16,2048]{1,0:T(8,128)(2,1)S(1)}, bf16[16,2048]{1,0:T(8,128)(2,1)S(1)}, u32[]{:S(2)}, u32[]{:S(2)}) collective-permute-start(bf16[16,2048]{1,0:T(8,128)(2,1)S(1)} %bitcast.6), channel_id=1, source_target_pairs={{0,32},{32,0},{1,33},{33,1},{2,34},{34,2},{3,35},{35,3},{4,36},{36... | collective-permute-start | bytes 196616 | tf_op jit(solution)/shard_map/visible_route/ppermute | solution.py:297
  62.1 7.2 %collective-permute-start.2 = (bf16[16,2048]{1,0:T(8,128)(2,1)S(1)}, bf16[16,2048]{1,0:T(8,128)(2,1)S(1)}, u32[]{:S(2)}, u32[]{:S(2)}) collective-permute-start(bf16[16,2048]{1,0:T(8,128)(2,1)S(1)} %get-tuple-element.24), channel_id=1, source_target_pairs={{0,64},{64,128},{128,192},{192,0},{1,65},{65,129},{129,193},{193,1... | collective-permute-start | bytes 196616 | tf_op jit(solution)/shard_map/ppermute | solution.py:297
  65.7 4.9 %collective-permute-start.3 = (bf16[16,2048]{1,0:T(8,128)(2,1)S(1)}, bf16[16,2048]{1,0:T(8,128)(2,1)S(1)}, u32[]{:S(2)}, u32[]{:S(2)}) collective-permute-start(bf16[16,2048]{1,0:T(8,128)(2,1)S(1)} %get-tuple-element.25), channel_id=1, source_target_pairs={{0,128},{64,192},{128,0},{192,64},{1,129},{65,193},{129,1},{193,65... | collective-permute-start | bytes 196616 | tf_op jit(solution)/shard_map/ppermute | solution.py:297
  68.2 3.4 %collective-permute-start.4 = (bf16[16,2048]{1,0:T(8,128)(2,1)S(1)}, bf16[16,2048]{1,0:T(8,128)(2,1)S(1)}, u32[]{:S(2)}, u32[]{:S(2)}) collective-permute-start(bf16[16,2048]{1,0:T(8,128)(2,1)S(1)} %get-tuple-element.26), channel_id=1, source_target_pairs={{0,192},{64,0},{128,64},{192,128},{1,193},{65,1},{129,65},{193,129... | collective-permute-start | bytes 196616 | tf_op jit(solution)/shard_map/ppermute | solution.py:297
  71.7 1.6 %copy-start.1 = (bf16[16,64,1024]{2,1,0:T(8,128)(2,1)S(1)}, bf16[16,64,1024]{2,1,0:T(8,128)(2,1)}, u32[]{:S(2)}) copy-start(bf16[16,64,1024]{2,1,0:T(8,128)(2,1)} %copy-done) | copy-start | bytes 6291460
  73.2 1.6 %copy-start.3 = (bf16[16,64,1024]{2,1,0:T(8,128)(2,1)S(1)}, bf16[16,64,1024]{2,1,0:T(8,128)(2,1)}, u32[]{:S(2)}) copy-start(bf16[16,64,1024]{2,1,0:T(8,128)(2,1)} %copy-done.2) | copy-start | bytes 6291460
  80.4 7.0 %collective-permute-start.5 = (bf16[256,128]{1,0:T(8,128)(2,1)S(1)}, bf16[256,128]{1,0:T(8,128)(2,1)S(1)}, u32[]{:S(2)}, u32[]{:S(2)}) collective-permute-start(bf16[256,128]{1,0:T(8,128)(2,1)S(1)} %get-tuple-element.31.refs_0_), channel_id=1, source_target_pairs={{0,32},{32,0},{1,33},{33,1},{2,34},{34,2},{3,35},{35,3},{4,36},{36... | collective-permute-start | bytes 196616 | tf_op jit(solution)/shard_map/grid_gather/ppermute | solution.py:297
  81.2 8.2 %collective-permute-start.10 = (bf16[256,128]{1,0:T(8,128)(2,1)S(1)}, bf16[256,128]{1,0:T(8,128)(2,1)S(1)}, u32[]{:S(2)}, u32[]{:S(2)}) collective-permute-start(bf16[256,128]{1,0:T(8,128)(2,1)S(1)} %get-tuple-element.31.refs_0_), channel_id=1, source_target_pairs={{0,192},{64,0},{128,64},{192,128},{1,193},{65,1},{129,65},{193,129... | collective-permute-start | bytes 196616 | tf_op jit(solution)/shard_map/grid_gather/ppermute | solution.py:297
  83.6 6.4 %collective-permute-start.8 = (bf16[256,128]{1,0:T(8,128)(2,1)S(1)}, bf16[256,128]{1,0:T(8,128)(2,1)S(1)}, u32[]{:S(2)}, u32[]{:S(2)}) collective-permute-start(bf16[256,128]{1,0:T(8,128)(2,1)S(1)} %get-tuple-element.31.refs_0_), channel_id=1, source_target_pairs={{0,128},{64,192},{128,0},{192,64},{1,129},{65,193},{129,1},{193,65... | collective-permute-start | bytes 196616 | tf_op jit(solution)/shard_map/grid_gather/ppermute | solution.py:297
  83.6 6.4 %collective-permute-start.6 = (bf16[256,128]{1,0:T(8,128)(2,1)S(1)}, bf16[256,128]{1,0:T(8,128)(2,1)S(1)}, u32[]{:S(2)}, u32[]{:S(2)}) collective-permute-start(bf16[256,128]{1,0:T(8,128)(2,1)S(1)} %get-tuple-element.31.refs_0_), channel_id=1, source_target_pairs={{0,64},{64,128},{128,192},{192,0},{1,65},{65,129},{129,193},{193,1... | collective-permute-start | bytes 196616 | tf_op jit(solution)/shard_map/grid_gather/ppermute | solution.py:297
  87.4 3.9 %collective-permute-start.11 = (bf16[256,128]{1,0:T(8,128)(2,1)S(1)}, bf16[256,128]{1,0:T(8,128)(2,1)S(1)}, u32[]{:S(2)}, u32[]{:S(2)}) collective-permute-start(bf16[256,128]{1,0:T(8,128)(2,1)S(1)} %collective-permute-done.5.refs_1_), channel_id=1, source_target_pairs={{0,192},{64,0},{128,64},{192,128},{1,193},{65,1},{129,65},{193,129... | collective-permute-start | bytes 196616 | tf_op jit(solution)/shard_map/grid_gather/ppermute | solution.py:297
  89.4 4.7 %collective-permute-start.9 = (bf16[256,128]{1,0:T(8,128)(2,1)S(1)}, bf16[256,128]{1,0:T(8,128)(2,1)S(1)}, u32[]{:S(2)}, u32[]{:S(2)}) collective-permute-start(bf16[256,128]{1,0:T(8,128)(2,1)S(1)} %collective-permute-done.5.refs_1_), channel_id=1, source_target_pairs={{0,128},{64,192},{128,0},{192,64},{1,129},{65,193},{129,1},{193,65... | collective-permute-start | bytes 196616 | tf_op jit(solution)/shard_map/grid_gather/ppermute | solution.py:297
  89.4 5.0 %collective-permute-start.7 = (bf16[256,128]{1,0:T(8,128)(2,1)S(1)}, bf16[256,128]{1,0:T(8,128)(2,1)S(1)}, u32[]{:S(2)}, u32[]{:S(2)}) collective-permute-start(bf16[256,128]{1,0:T(8,128)(2,1)S(1)} %collective-permute-done.5.refs_1_), channel_id=1, source_target_pairs={{0,64},{64,128},{128,192},{192,0},{1,65},{65,129},{129,193},{193,1... | collective-permute-start | bytes 196616 | tf_op jit(solution)/shard_map/grid_gather/ppermute | solution.py:297
  95.7 7.5 %collective-permute-start.12 = (f32[64,2048]{1,0:T(8,128)S(1)}, f32[64,2048]{1,0:T(8,128)S(1)}, u32[]{:S(2)}, u32[]{:S(2)}) collective-permute-start(f32[64,2048]{1,0:T(8,128)S(1)} %get-tuple-element.33), channel_id=1, source_target_pairs={{0,1},{1,0},{2,3},{3,2},{4,5},{5,4},{6,7},{7,6},{8,9},{9,8},{10,11... | collective-permute-start | bytes 1572872 | tf_op jit(solution)/shard_map/dirty_scatter/ppermute | solution.py:297

commit v3 on v2

--- a/solution.py
+++ b/solution.py
@@ -16,6 +16,7 @@
 TILE = ("x", "z", "c")
 VMEM = pl.BlockSpec(memory_space=pltpu.VMEM)
 SMEM = pl.BlockSpec(memory_space=pltpu.SMEM)
+ANY = pl.BlockSpec(memory_space=pl.ANY)
 
 
 def params(mib):
@@ -52,7 +53,66 @@
     return (held * (128 // cores)) + lax.div(subgrid, owned * cores) * owned + lax.rem(subgrid, owned)
 
 
-def screen_kernel(stations_ref, plane_ref, phase_ref, beam_ref, screen_ref):
+def prepare_kernel(place_ref, *refs):
+    sources, (east_to, north_to, screen_ref) = (refs[:6], refs[6:9])
+    east_ref, north_ref, powers, groups, sems, out_sems = refs[15:]
+    copies = [pltpu.make_async_copy(src, dst, sems.at[at]) for at, (src, dst) in enumerate(zip(sources, refs[9:15]))]
+    for copy in copies:
+        copy.start()
+    coords_ref, freq_ref, stations_ref, plane_ref, phase_ref, beam_ref = refs[9:15]
+    copies[0].wait()
+    copies[1].wait()
+    rows = coords_ref.shape[2]
+    coords = coords_ref[place_ref[0]]
+    row = jnp.concatenate([coords[0:1], coords[1:2], jnp.zeros((1, 128 - 2 * rows), F32)], axis=1)
+    column = (TWO_PI * down(row)[: 2 * rows]) * (1.0 / 32.0)
+    angle = jnp.concatenate([column] * (freq_ref.shape[1] // 128), axis=1) * freq_ref[...]
+    z1 = (jnp.cos(angle), jnp.sin(angle))
+    z2 = cmul(z1, z1)
+    z4 = cmul(z2, z2)
+    z8 = cmul(z4, z4)
+    z16 = cmul(z8, z8)
+    low16 = conj(z16)
+    for at, value in enumerate((z1, z2, z4, z8, z16)):
+        powers[2 * at] = value[0]
+        powers[2 * at + 1] = value[1]
+    for at, value in enumerate((low16, cmul(low16, z1), cmul(low16, z2), cmul(low16, cmul(z1, z2)))):
+        groups[2 * at] = value[0]
+        groups[2 * at + 1] = value[1]
+    sub = lax.broadcasted_iota(jnp.int32, (8, angle.shape[1]), 0)
+
+    def row_of(ref, at, row):
+        return (ref[2 * at, pl.ds(row, 1), :], ref[2 * at + 1, pl.ds(row, 1), :])
+
+    def picked(factor, bit):
+        on = (sub & bit) != 0
+        return (jnp.where(on, factor[0], 1.0), jnp.where(on, factor[1], 0.0))
+
+    def bits(factors):
+        return cmul(cmul(picked(factors[0], 1), picked(factors[1], 2)), picked(factors[2], 4))
+
+    def stacked(parts):
+        return jnp.concatenate([part[0] for part in parts] + [part[1] for part in parts], axis=0).astype(BF16)
+
+    def body(b, carry):
+        base = bits([row_of(powers, at, b) for at in (2, 3, 4)])
+        east_ref[b] = stacked([cmul(base, row_of(groups, at, b)) for at in range(4)])
+        row = b + rows
+        base = bits([row_of(powers, at, row) for at in (0, 1, 2)])
+        up8 = row_of(powers, 3, row)
+        north_ref[b] = stacked([cmul(base, row_of(groups, 0, row)), cmul(base, conj(up8)), base, cmul(base, up8)])
+        return carry
+
+    lax.fori_loop(0, rows, body, 0)
+    stores = [
+        pltpu.make_async_copy(src, dst, out_sems.at[at])
+        for at, (src, dst) in enumerate(((east_ref, east_to), (north_ref, north_to)))
+    ]
+    for store in stores:
+        store.start()
+
+    for copy in copies[2:]:
+        copy.wait()
     stations = beam_ref.shape[0]
     planes, pixels = phase_ref.shape
     one = onehot(down(row_of_blocks(stations_ref[:, 0, :])), 0, stations)
@@ -73,59 +133,12 @@
         wave_im = jnp.dot(plane, jnp.sin(phase), precision=exact, preferred_element_type=F32)
         screen_ref[:, re] = pair_re * wave_re - pair_im * wave_im
         screen_ref[:, im] = pair_re * wave_im + pair_im * wave_re
-
-
-def table_kernel(place_ref, coords_ref, freq_ref, east_ref, north_re_ref, north_im_ref, *powers):
-    rows = coords_ref.shape[2]
-    coords = coords_ref[place_ref[0]]
-    row = jnp.concatenate([coords[0:1], coords[1:2], jnp.zeros((1, 128 - 2 * rows), F32)], axis=1)
-    column = (TWO_PI * down(row)[: 2 * rows]) * (1.0 / 32.0)
-    angle = jnp.concatenate([column] * (freq_ref.shape[1] // 128), axis=1) * freq_ref[...]
-    z1 = (jnp.cos(angle), jnp.sin(angle))
-    z2 = cmul(z1, z1)
-    z4 = cmul(z2, z2)
-    z8 = cmul(z4, z4)
-    z16 = cmul(z8, z8)
-    low16 = conj(z16)
-    for at, value in enumerate((z1, z2, z4, z8, z16)):
-        powers[0][2 * at] = value[0]
-        powers[0][2 * at + 1] = value[1]
-    for at, value in enumerate((low16, cmul(low16, z1), cmul(low16, z2), cmul(low16, cmul(z1, z2)))):
-        powers[1][2 * at] = value[0]
-        powers[1][2 * at + 1] = value[1]
-    sub = lax.broadcasted_iota(jnp.int32, (8, angle.shape[1]), 0)
-
-    def row_of(ref, at, row):
-        return (ref[2 * at, pl.ds(row, 1), :], ref[2 * at + 1, pl.ds(row, 1), :])
-
-    def picked(factor, bit):
-        on = (sub & bit) != 0
-        return (jnp.where(on, factor[0], 1.0), jnp.where(on, factor[1], 0.0))
-
-    def bits(factors):
-        return cmul(cmul(picked(factors[0], 1), picked(factors[1], 2)), picked(factors[2], 4))
-
-    def body(b, carry):
-        base = bits([row_of(powers[0], at, b) for at in (2, 3, 4)])
-        parts = [cmul(base, row_of(powers[1], at, b)) for at in range(4)]
-        cos = jnp.concatenate([part[0] for part in parts], axis=0)
-        sin = jnp.concatenate([part[1] for part in parts], axis=0)
-        east_ref[b] = jnp.concatenate([cos, sin], axis=0).astype(BF16)
-        row = b + rows
-        base = bits([row_of(powers[0], at, row) for at in (0, 1, 2)])
-        up8 = row_of(powers[0], 3, row)
-        parts = [cmul(base, row_of(powers[1], 0, row)), cmul(base, conj(up8)), base, cmul(base, up8)]
-        cos = jnp.concatenate([part[0] for part in parts], axis=0)
-        sin = jnp.concatenate([part[1] for part in parts], axis=0)
-        north_re_ref[b] = jnp.concatenate([cos, -sin], axis=0).astype(BF16)
-        north_im_ref[b] = jnp.concatenate([sin, cos], axis=0).astype(BF16)
-        return carry
-
-    lax.fori_loop(0, rows, body, 0)
+    for store in stores:
+        store.wait()
 
 
 def image_kernel(cores, owned, place_ref, subgrid_ref, near_ref, far_ref, screen_ref, image_ref):
-    half = near_ref.shape[0]
+    half = near_ref.shape[0] * near_ref.shape[1]
     pixels = screen_ref.shape[1] // 2
     blocks = image_ref.shape[0]
     slots = down(slot_of(row_of_blocks(subgrid_ref[...]), place_ref[3], cores, owned))
@@ -134,9 +147,8 @@
     width = 256
 
     def rows_of(cells):
-        return jnp.dot(near, near_ref[:, cells], preferred_element_type=F32) + jnp.dot(
-            far, far_ref[:, cells], preferred_element_type=F32
-        )
+        held = (near_ref[:, :, cells].reshape(half, width), far_ref[:, :, cells].reshape(half, width))
+        return jnp.dot(near, held[0], preferred_element_type=F32) + jnp.dot(far, held[1], preferred_element_type=F32)
 
     for at in range(0, pixels, width):
         re, im = pl.ds(at, width), pl.ds(pixels + at, width)
@@ -178,16 +190,30 @@
     came_1_ref,
     came_2_ref,
     came_3_ref,
-    east_ref,
-    north_re_ref,
-    north_im_ref,
+    east_from,
+    north_from,
     resid_ref,
     grid_ref,
     cells_ref,
     out_ref,
+    east_ref,
+    north_ref,
+    sems,
 ):
     rows, channels = (resid_ref.shape[0], resid_ref.shape[1] // 2)
     facets = images_ref.shape[0]
+
+    run = rows // 4
+    copies = [
+        [
+            pltpu.make_async_copy(src.at[pl.ds(at * run, run)], dst.at[pl.ds(at * run, run)], sems.at[kind, at])
+            for kind, (src, dst) in enumerate(((east_from, east_ref), (north_from, north_ref)))
+        ]
+        for at in range(4)
+    ]
+    for pair in copies:
+        for copy in pair:
+            copy.start()
     total = images_ref[0].astype(F32)
     for at in range(1, facets):
         total = total + images_ref[at].astype(F32)
@@ -204,24 +230,27 @@
 
     width = 256
 
-    def degrid(b, carry):
+    def degrid(b):
         cells = cells_ref[pl.ds(b, 16, stride=16), :]
-        pieces = [
-            jnp.concatenate(
-                [cells[0:8, 32 * p : 32 * p + 32], cells[8:16, 32 * p : 32 * p + 32]], axis=1
+
+        def spread(first, second):
+            return jnp.concatenate(
+                [
+                    jnp.concatenate([first[:, 32 * p : 32 * p + 32], second[:, 32 * p : 32 * p + 32]], axis=1)
+                    for p in range(4)
+                ],
+                axis=0,
             )
-            for p in range(4)
-        ]
-        image = jnp.concatenate(pieces, axis=0)
+
+        image = jnp.concatenate([spread(cells[0:8], -cells[8:16]), spread(cells[8:16], cells[0:8])], axis=0)
         high = image.astype(BF16)
         low = (image - high.astype(F32)).astype(BF16)
         operand = jnp.concatenate([high, low], axis=0)
         for at in range(0, channels, width):
             chans = pl.ds(at, width)
-            inner_re = jnp.dot(operand, north_re_ref[b, :, chans], preferred_element_type=F32)
-            inner_im = jnp.dot(operand, north_im_ref[b, :, chans], preferred_element_type=F32)
-            inner_re = inner_re[:32] + inner_re[32:]
-            inner_im = inner_im[:32] + inner_im[32:]
+            inner = jnp.dot(operand, north_ref[b, :, chans], preferred_element_type=F32)
+            inner = inner[:64] + inner[64:]
+            inner_re, inner_im = (inner[:32], inner[32:])
             east = east_ref[b, :, chans].astype(F32)
             cos, sin = (east[:32], east[32:])
             vis_re = jnp.sum(cos * inner_re - sin * inner_im, axis=0, keepdims=True)
@@ -230,55 +259,63 @@
             late = pl.ds(channels + at, width)
             resid_ref[row, chans] = resid_ref[row, chans] - vis_re
             resid_ref[row, late] = resid_ref[row, late] - vis_im
-        return carry
-
-    def grid(b, carry):
-        gridded = jnp.zeros((32, 64), F32)
-        over = (((1,), (1,)), ((), ()))
+
+    def grid(b):
+        products = jnp.zeros((64, 64), F32)
         for at in range(0, channels, width):
             chans, late = (pl.ds(at, width), pl.ds(channels + at, width))
             resid_re, resid_im = (resid_ref[pl.ds(b, 1), chans], resid_ref[pl.ds(b, 1), late])
             east = east_ref[b, :, chans].astype(F32)
             cos, sin = (east[:32], east[32:])
-            weighted_re = (cos * resid_re + sin * resid_im).astype(BF16)
-            weighted_im = (cos * resid_im - sin * resid_re).astype(BF16)
-            gridded = gridded + lax.dot_general(
-                weighted_re, north_re_ref[b, :, chans], over, preferred_element_type=F32
+            weighted = jnp.concatenate([cos * resid_re + sin * resid_im, cos * resid_im - sin * resid_re], axis=0)
+            products = products + lax.dot_general(
+                weighted.astype(BF16),
+                north_ref[b, :, chans],
+                (((1,), (1,)), ((), ())),
+                preferred_element_type=F32,
             )
-            gridded = gridded + lax.dot_general(
-                weighted_im, north_im_ref[b, :, chans], over, preferred_element_type=F32
-            )
-        halves = [
-            jnp.concatenate([gridded[8 * p : 8 * p + 8, at : at + 32] for p in range(4)], axis=1)
-            for at in (0, 32)
-        ]
-        out_ref[pl.ds(b, 16, stride=16), :] = jnp.concatenate(halves, axis=0)
-        return carry
-
-    lax.fori_loop(0, rows, degrid, 0, unroll=4)
-    lax.fori_loop(0, rows, grid, 0, unroll=4)
+        halves = (products[:32, :32] + products[32:, 32:], products[32:, :32] - products[:32, 32:])
+        out_ref[pl.ds(b, 16, stride=16), :] = jnp.concatenate(
+            [jnp.concatenate([half[8 * p : 8 * p + 8] for p in range(4)], axis=1) for half in halves], axis=0
+        )
+
+    for at, pair in enumerate(copies):
+        for copy in pair:
+            copy.wait()
+        for b in range(at * run, at * run + run):
+            degrid(b)
+    for b in range(rows):
+        grid(b)
     grid_ref[...] = out_ref[...].astype(BF16)
 
 
 def regrid_kernel(scale, n_y, n_h, cores, owned, place_ref, subgrid_ref, screen_ref, *refs):
-    grids, (near_ref, far_ref, grid_ref) = (refs[:-3], refs[-3:])
-    for at, ref in enumerate(grids):
+    grids, (near_ref, far_ref) = (refs[:-2], refs[-2:])
+    blocks = []
+    for at in range(len(grids)):
         by, flip = divmod(at, n_h)
-        block = lax.rem(place_ref[1] + (n_y - by), n_y) * n_h + lax.rem(place_ref[2] + flip, n_h)
-        grid_ref[block] = ref[...]
+        blocks.append(lax.rem(place_ref[1] + (n_y - by), n_y) * n_h + lax.rem(place_ref[2] + flip, n_h))
     half = near_ref.shape[0]
     pixels = screen_ref.shape[1] // 2
     tiles = pixels // 128
     count = screen_ref.shape[0]
+
+    def screen_of(cells):
+        rows = [screen_ref[pl.ds(pl.multiple_of(block * 16, 16), 16), cells] for block in blocks]
+        return jnp.concatenate(rows, axis=0)
+
+    def grid_of(q):
+        return jnp.concatenate([ref[16 * q : 16 * q + 16, :] for ref in grids], axis=0).astype(F32)
+
     subs = lax.broadcasted_iota(jnp.int32, (2 * half, count), 0)
-    target = slot_of(row_of_blocks(subgrid_ref[...]), place_ref[3], cores, owned)
+    target = jnp.concatenate([subgrid_ref[pl.ds(block, 1), :] for block in blocks], axis=1)
+    target = slot_of(target, place_ref[3], cores, owned)
     sums = jnp.where(target == subs, 1.0, 0.0).astype(BF16)
     near, far = (sums[:half], sums[half:])
     for q in range(tiles):
         re, im = pl.ds(128 * q, 128), pl.ds(pixels + 128 * q, 128)
-        grid_re = grid_ref[:, 16 * q : 16 * q + 16, :].reshape(count, 128).astype(F32)
-        grid_im = grid_ref[:, 16 * (q + tiles) : 16 * (q + tiles) + 16, :].reshape(count, 128).astype(F32)
-        screen_re, screen_im = (screen_ref[:, re], screen_ref[:, im])
+        grid_re, grid_im = (grid_of(q), grid_of(q + tiles))
+        screen_re, screen_im = (screen_of(re), screen_of(im))
         out_re = (screen_re * grid_re + screen_im * grid_im) * scale
         out_im = (screen_re * grid_im - screen_im * grid_re) * scale
         for cells, value in ((re, out_re), (im, out_im)):
@@ -328,36 +365,33 @@
     with jax.named_scope("model_gather"):
         copies = jnp.broadcast_to(model_grid, (n_x * n_z, owned, 2 * pixels))
         near = lax.all_to_all(copies, ("x", "z"), split_axis=0, concat_axis=0, tiled=True)
-        near = near.reshape(n_x * n_z * owned, 2 * pixels)
-        far = shift(near, "c", 1)
-
-    screen = pl.pallas_call(
-        screen_kernel,
-        out_shape=jax.ShapeDtypeStruct((count, 2 * pixels), F32),
-        in_specs=[VMEM] * 4,
-        out_specs=VMEM,
-        compiler_params=params(16),
-        cost_estimate=pl.CostEstimate(flops=10**9, bytes_accessed=4 << 20, transcendentals=1 << 16),
-        name="screens",
-    )(stations, plane_index, plane_phase, beam_screens[0])
-
-    east, north_re, north_im = pl.pallas_call(
-        table_kernel,
-        out_shape=[jax.ShapeDtypeStruct((row_block, 64, channels), BF16)] * 3,
-        in_specs=[SMEM, VMEM, VMEM],
-        out_specs=[VMEM] * 3,
-        scratch_shapes=[
+
+    operands = (baseline_coords, channel_freq.reshape(1, channels), stations, plane_index, plane_phase, beam_screens[0])
+    east, north, screen = pl.pallas_call(
+        prepare_kernel,
+        out_shape=[jax.ShapeDtypeStruct((row_block, 64, channels), BF16)] * 2
+        + [jax.ShapeDtypeStruct((count, 2 * pixels), F32)],
+        in_specs=[SMEM] + [ANY] * len(operands),
+        out_specs=[ANY, ANY, VMEM],
+        scratch_shapes=[pltpu.VMEM(value.shape, value.dtype) for value in operands]
+        + [
+            pltpu.VMEM((row_block, 64, channels), BF16),
+            pltpu.VMEM((row_block, 64, channels), BF16),
             pltpu.VMEM((10, 2 * row_block, channels), F32),
             pltpu.VMEM((8, 2 * row_block, channels), F32),
+            pltpu.SemaphoreType.DMA((len(operands),)),
+            pltpu.SemaphoreType.DMA((2,)),
         ],
-        compiler_params=params(16),
-        cost_estimate=pl.CostEstimate(flops=10**8, bytes_accessed=6 << 20, transcendentals=1 << 16),
-        name="tables",
-    )(place, baseline_coords, channel_freq.reshape(1, channels))
+        compiler_params=params(61),
+        cost_estimate=pl.CostEstimate(flops=10**9, bytes_accessed=8 << 20, transcendentals=1 << 17),
+        name="prepare",
+    )(place, *operands)
 
     with jax.named_scope("visible_route"):
-        rows, east = lax.optimization_barrier((sectioned_rows[0], east))
+        rows = sectioned_rows[0]
         other = shift(rows, "h", 1)
+        near, other, east, north, screen = lax.optimization_barrier((near, other, east, north, screen))
+        far = shift(near, "c", 1)
         sent = pl.pallas_call(
             functools.partial(route_kernel, n_y, n_h),
             out_shape=[jax.ShapeDtypeStruct(rows.shape, BF16)] * (n_y - 1),
@@ -368,7 +402,6 @@
             name="route",
         )(place, reader, rows, other)
 
-    near, far, screen, east = lax.optimization_barrier((near, far, screen, east))
     images = pl.pallas_call(
         functools.partial(image_kernel, n_c, owned),
         out_shape=jax.ShapeDtypeStruct((n_facet, cell_rows, 128), BF16),
@@ -388,13 +421,19 @@
             jax.ShapeDtypeStruct((row_block, 2 * channels), F32),
             jax.ShapeDtypeStruct((cell_rows, 128), BF16),
         ],
-        in_specs=[SMEM] * 2 + [VMEM] * 9,
+        in_specs=[SMEM] * 2 + [VMEM] * 6 + [ANY] * 2,
         out_specs=[VMEM] * 2,
-        scratch_shapes=[pltpu.VMEM((cell_rows, 128), F32), pltpu.VMEM((cell_rows, 128), F32)],
-        compiler_params=params(16),
+        scratch_shapes=[
+            pltpu.VMEM((cell_rows, 128), F32),
+            pltpu.VMEM((cell_rows, 128), F32),
+            pltpu.VMEM(east.shape, BF16),
+            pltpu.VMEM(north.shape, BF16),
+            pltpu.SemaphoreType.DMA((2, 4)),
+        ],
+        compiler_params=params(61),
         cost_estimate=pl.CostEstimate(flops=10**9, bytes_accessed=8 << 20, transcendentals=0),
         name="visibilities",
-    )(place, reader, arrived, rows, other, *came, east, north_re, north_im)
+    )(place, reader, arrived, rows, other, *came, east, north)
 
     with jax.named_scope("grid_gather"):
         beside = shift(gridded, "h", 1)
@@ -408,7 +447,6 @@
         out_shape=[jax.ShapeDtypeStruct((half, 2 * pixels), F32)] * 2,
         in_specs=[SMEM] + [VMEM] * (2 + n_facet),
         out_specs=[VMEM] * 2,
-        scratch_shapes=[pltpu.VMEM((n_facet, cell_rows, 128), BF16)],
         compiler_params=params(8),
         cost_estimate=pl.CostEstimate(flops=10**8, bytes_accessed=3 << 20, transcendentals=0),
         name="regrid",

time: 119 us -> 99.6 us (0.84)
  blocking collectives: 33 us -> 14 us
  local copies, waits for them, and re-layouts: 12.1 us -> 4.55 us
  starting transfers between devices: 35.2 us -> 41.9 us
  waiting for transfers between devices: 21.2 us -> 18.9 us
  Pallas kernels: 15.6 us -> 17.7 us
    all_to_all x1 -> x0, blocking collectives: 18.5 us -> none  [local(): lax.all_to_all(copies, ('x', 'z'), split_axis=0, concat_axis=0, tiled=True)]
    ppermute x13, waiting for transfers between devices: 21.1 us -> 12 us  [shift(): lax.ppermute(value, axis, [(i, (i + by) % size) for i in range(size)])]
    all_to_all x0 -> x1, starting transfers between devices: none -> 9.15 us  [local(): lax.all_to_all(copies, ('x', 'z'), split_axis=0, concat_axis=0, tiled=True)]
    unnamed x26, local copies, waits for them, and re-layouts: 11.1 us -> 2.91 us
    all_to_all x1, waiting for transfers between devices: 0.01 us -> 6.88 us  [local(): lax.all_to_all(images, FACET, split_axis=0, concat_axis=0, tiled=True)]
    ppermute x13, starting transfers between devices: 27.1 us -> 24.6 us  [shift(): lax.ppermute(value, axis, [(i, (i + by) % size) for i in range(size)])]
    pallas_call x2 -> x1, Pallas kernels: 5.83 us -> 7.76 us  [local(): pl.pallas_call(prepare_kernel, out_shape=[jax.ShapeDtypeStruct((row_block...]
  transfers between devices with their start and end apart: 14 -> 15, of which waited for: 8 -> 9; matrix products, arithmetic and copies ran while one was open for 0% -> 1% of each run, Pallas kernels for 5% -> 8%
where the time goes in v3:
time: 99.6 us; the launch traced here: 99 us
  starting transfers between devices  41.9 us (42%)
  waiting for transfers between devices  18.9 us (19%)
  Pallas kernels  17.7 us (18%)
  blocking collectives  14 us (14%)
  local copies, waits for them, and re-layouts  4.55 us (5%)
  other arithmetic  1.3 us (1%)
    ppermute x13, starting transfers between devices, shift(): lax.ppermute(value, axis, [(i, (i + by) % size) for i in range(size)])  24.6 us
    all_to_all x1, blocking collectives, local(): lax.all_to_all(chip_sum, ('x', 'z'), split_axis=0, concat_axis=0, tiled=T...  14 us
    ppermute x13, waiting for transfers between devices, shift(): lax.ppermute(value, axis, [(i, (i + by) % size) for i in range(size)])  12 us
    all_to_all x1, starting transfers between devices, local(): lax.all_to_all(copies, ('x', 'z'), split_axis=0, concat_axis=0, tiled=True)  9.15 us
    all_to_all x1, starting transfers between devices, local(): lax.all_to_all(images, FACET, split_axis=0, concat_axis=0, tiled=True)  8.12 us
    pallas_call x1, Pallas kernels, local(): pl.pallas_call(prepare_kernel, out_shape=[jax.ShapeDtypeStruct((row_block...  7.76 us
    all_to_all x1, waiting for transfers between devices, local(): lax.all_to_all(images, FACET, split_axis=0, concat_axis=0, tiled=True)  6.88 us
    pallas_call x1, Pallas kernels, local(): pl.pallas_call(functools.partial(visibility_kernel, n_y, n_h), out_shape=...  6.08 us
  transfers between devices with their start and end apart: 15, of which 9 were waited for; matrix products, arithmetic and copies ran while one was open for 1% of the time, Pallas kernels for 8%

profile of v3, /device:TPU:1, one launch (start us, length us, event | category | flops | bytes accessed | tf_op | source)
XLA Modules:
  0.0 99.0 jit_solution(12872598783019350606)
XLA Ops:
  0.6 1.5 %broadcast_in_dim.33 = bf16[16,4,2048]{2,1,0:T(4,128)(2,1)} broadcast(bf16[4,2048]{1,0:T(4,128)(2,1)} %bitcast.10), dimensions={1,2} | broadcast | bytes 278528 | tf_op jit(solution)/shard_map/model_gather/broadcast_in_dim | solution.py:366
  2.2 9.1 %all-to-all-start = ((bf16[16,4,2048]{2,1,0:T(4,128)(2,1)}), bf16[16,4,2048]{2,1,0:T(4,128)(2,1)S(1)}, u32[]{:S(2)}, u32[]{:S(2)}) async-start(bf16[16,4,2048]{2,1,0:T(4,128)(2,1)} %broadcast_in_dim.33), calls=%async_computation | async-start | bytes 524288 | tf_op jit(solution)/shard_map/model_gather/all_to_all | solution.py:367
  11.3 4.3 %collective-permute-start = (bf16[16,2048]{1,0:T(8,128)(2,1)}, bf16[16,2048]{1,0:T(8,128)(2,1)S(1)}, u32[]{:S(2)}, u32[]{:S(2)}) collective-permute-start(bf16[16,2048]{1,0:T(8,128)(2,1)} %bitcast.6), channel_id=1, source_target_pairs={{0,32},{32,0},{1,33},{33,1},{2,34},{34,2},{3,35},{35,3},{4,36},{36... | collective-permute-start | bytes 196616 | tf_op jit(solution)/shard_map/visible_route/ppermute | solution.py:334
  15.6 0.5 compare_select_fusion.2.place_ref
  16.1 7.8 %prepare.1 = (bf16[16,64,1024]{2,1,0:T(8,128)(2,1)}, bf16[16,64,1024]{2,1,0:T(8,128)(2,1)}, f32[128,2048]{1,0:T(8,128)}) custom-call(s32[4]{0:T(128)} %compare_select_fusion.2.place_ref, f32[8,2,16]{2,1,0:T(2,128)} %refs_0_.1, f32[1,1024]{1,0:T(1,128)} %bitcast.13, s32[8,2,16]{2,1,0:T(2,128)} %refs_2_.1, s32[8,16]{1,0:T(8,128)} %refs_3_.1, ...), custom_call_target="tpu_custom_call" | custom-call | flops 1000000000 | bytes 8388608 | tf_op jit(solution)/shard_map/prepare/pallas_call | solution.py:370
  23.9 0.0 copy-start.8
  23.9 0.0 collective-permute-done.other_ref
  23.9 0.0 all-to-all-done.near_ref
  23.9 2.0 %collective-permute-start.1 = (bf16[16,4,2048]{2,1,0:T(4,128)(2,1)S(1)}, bf16[16,4,2048]{2,1,0:T(4,128)(2,1)S(1)}, u32[]{:S(2)}, u32[]{:S(2)}) collective-permute-start(bf16[16,4,2048]{2,1,0:T(4,128)(2,1)S(1)} %all-to-all-done.near_ref), channel_id=1, source_target_pairs={{0,1},{1,0},{2,3},{3,2},{4,5},{5,4},{6,7},{7,6},{8,9},{9,8},{10,11... | collective-permute-start | bytes 786440 | tf_op jit(solution)/shard_map/visible_route/ppermute | solution.py:334
  26.0 1.2 %collective-permute-done.1.far_ref = bf16[16,4,2048]{2,1,0:T(4,128)(2,1)S(1)} collective-permute-done((bf16[16,4,2048]{2,1,0:T(4,128)(2,1)S(1)}, bf16[16,4,2048]{2,1,0:T(4,128)(2,1)S(1)}, u32[]{:S(2)}, u32[]{:S(2)}) %collective-permute-start.1) | collective-permute-done | bytes 262176 | tf_op jit(solution)/shard_map/visible_route/ppermute | solution.py:334
  27.1 1.2 %copy-done = f32[128,2048]{1,0:T(8,128)S(1)} copy-done((f32[128,2048]{1,0:T(8,128)S(1)}, f32[128,2048]{1,0:T(8,128)}, u32[]{:S(2)}) %copy-start) | copy-done | bytes 1048600
  28.4 1.9 %images.1 = bf16[8,256,128]{2,1,0:T(8,128)(2,1)} custom-call(s32[4]{0:T(128)S(1)} %copy-done.6, s32[8,16]{1,0:T(8,128)S(1)} %copy-done.5, bf16[16,4,2048]{2,1,0:T(4,128)(2,1)S(1)} %all-to-all-done.near_ref, bf16[16,4,2048]{2,1,0:T(4,128)(2,1)S(1)} %collective-permute-done.1.far_ref, f32[128,2048]{1,0:T(8,128)S(1)} %copy-done), custom_call_target="tpu_custom_call" | custom-call | flops 100000000 | bytes 2097152 | tf_op jit(solution)/shard_map/images/pallas_call | solution.py:405
  30.3 8.1 %all-to-all-start.1 = ((bf16[8,256,128]{2,1,0:T(8,128)(2,1)}), bf16[8,256,128]{2,1,0:T(8,128)(2,1)S(1)}, u32[]{:S(2)}, u32[]{:S(2)}) async-start(bf16[8,256,128]{2,1,0:T(8,128)(2,1)} %images.1), calls=%async_computation.1 | async-start | bytes 1048576 | tf_op jit(solution)/shard_map/all_to_all | solution.py:415
  38.4 0.0 copy-done.2
  38.4 0.0 copy-done.8
  38.4 0.6 route.1
  39.0 1.5 %collective-permute-start.2 = (bf16[16,2048]{1,0:T(8,128)(2,1)S(1)}, bf16[16,2048]{1,0:T(8,128)(2,1)S(1)}, u32[]{:S(2)}, u32[]{:S(2)}) collective-permute-start(bf16[16,2048]{1,0:T(8,128)(2,1)S(1)} %get-tuple-element.23), channel_id=1, source_target_pairs={{0,64},{64,128},{128,192},{192,0},{1,65},{65,129},{129,193},{193,1... | collective-permute-start | bytes 196616 | tf_op jit(solution)/shard_map/ppermute | solution.py:334
  40.6 2.4 %collective-permute-start.3 = (bf16[16,2048]{1,0:T(8,128)(2,1)S(1)}, bf16[16,2048]{1,0:T(8,128)(2,1)S(1)}, u32[]{:S(2)}, u32[]{:S(2)}) collective-permute-start(bf16[16,2048]{1,0:T(8,128)(2,1)S(1)} %get-tuple-element.24), channel_id=1, source_target_pairs={{0,128},{64,192},{128,0},{192,64},{1,129},{65,193},{129,1},{193,65... | collective-permute-start | bytes 196616 | tf_op jit(solution)/shard_map/ppermute | solution.py:334
  43.0 1.2 %collective-permute-start.4 = (bf16[16,2048]{1,0:T(8,128)(2,1)S(1)}, bf16[16,2048]{1,0:T(8,128)(2,1)S(1)}, u32[]{:S(2)}, u32[]{:S(2)}) collective-permute-start(bf16[16,2048]{1,0:T(8,128)(2,1)S(1)} %get-tuple-element.25), channel_id=1, source_target_pairs={{0,192},{64,0},{128,64},{192,128},{1,193},{65,1},{129,65},{193,129... | collective-permute-start | bytes 196616 | tf_op jit(solution)/shard_map/ppermute | solution.py:334
  44.1 0.8 collective-permute-done.2.came_1_ref
  44.9 2.4 %collective-permute-done.3.came_2_ref = bf16[16,2048]{1,0:T(8,128)(2,1)S(1)} collective-permute-done((bf16[16,2048]{1,0:T(8,128)(2,1)S(1)}, bf16[16,2048]{1,0:T(8,128)(2,1)S(1)}, u32[]{:S(2)}, u32[]{:S(2)}) %collective-permute-start.3) | collective-permute-done | bytes 65568 | tf_op jit(solution)/shard_map/ppermute | solution.py:334
  47.3 0.0 collective-permute-done.4.came_3_ref
  47.3 6.9 %all-to-all-done.1.images_ref = bf16[8,256,128]{2,1,0:T(8,128)(2,1)S(1)} async-done(((bf16[8,256,128]{2,1,0:T(8,128)(2,1)}), bf16[8,256,128]{2,1,0:T(8,128)(2,1)S(1)}, u32[]{:S(2)}, u32[]{:S(2)}) %all-to-all-start.1) | async-done | bytes 524320 | tf_op jit(solution)/shard_map/all_to_all | solution.py:415
  54.2 0.0 copy-done.10
  54.2 0.8 copy-done.9
  55.0 6.1 %visibilities.1 = (f32[16,2048]{1,0:T(8,128)}, bf16[256,128]{1,0:T(8,128)(2,1)}) custom-call(s32[4]{0:T(128)} %compare_select_fusion.2.place_ref, s32[1,8]{1,0:T(1,128)} %reader_ref.3, bf16[8,256,128]{2,1,0:T(8,128)(2,1)} %copy-done.9, bf16[16,2048]{1,0:T(8,128)(2,1)} %bitcast.7, bf16[16,2048]{1,0:T(8,128)(2,1)} %copy-done.3, bf16[16,2048]{1,0:T(8,128)(2,1)} %copy-done.10, ...), custom_call_target="tpu_custom_call" | custom-call | flops 1000000000 | bytes 8388608 | tf_op jit(solution)/shard_map/visibilities/pallas_call | solution.py:418
  61.1 1.7 %collective-permute-start.5 = (bf16[256,128]{1,0:T(8,128)(2,1)}, bf16[256,128]{1,0:T(8,128)(2,1)S(1)}, u32[]{:S(2)}, u32[]{:S(2)}) collective-permute-start(bf16[256,128]{1,0:T(8,128)(2,1)} %get-tuple-element.29.refs_0_), channel_id=1, source_target_pairs={{0,32},{32,0},{1,33},{33,1},{2,34},{34,2},{3,35},{35,3},{4,36},{36... | collective-permute-start | bytes 196616 | tf_op jit(solution)/shard_map/grid_gather/ppermute | solution.py:334
  62.8 1.8 %collective-permute-start.10 = (bf16[256,128]{1,0:T(8,128)(2,1)}, bf16[256,128]{1,0:T(8,128)(2,1)S(1)}, u32[]{:S(2)}, u32[]{:S(2)}) collective-permute-start(bf16[256,128]{1,0:T(8,128)(2,1)} %get-tuple-element.29.refs_0_), channel_id=1, source_target_pairs={{0,192},{64,0},{128,64},{192,128},{1,193},{65,1},{129,65},{193,129... | collective-permute-start | bytes 196616 | tf_op jit(solution)/shard_map/grid_gather/ppermute | solution.py:334
  64.6 0.0 collective-permute-start.6
  64.6 1.2 %collective-permute-start.8 = (bf16[256,128]{1,0:T(8,128)(2,1)}, bf16[256,128]{1,0:T(8,128)(2,1)S(1)}, u32[]{:S(2)}, u32[]{:S(2)}) collective-permute-start(bf16[256,128]{1,0:T(8,128)(2,1)} %get-tuple-element.29.refs_0_), channel_id=1, source_target_pairs={{0,128},{64,192},{128,0},{192,64},{1,129},{65,193},{129,1},{193,65... | collective-permute-start | bytes 196616 | tf_op jit(solution)/shard_map/grid_gather/ppermute | solution.py:334
  65.9 2.6 %collective-permute-done.5.refs_1_ = bf16[256,128]{1,0:T(8,128)(2,1)S(1)} collective-permute-done((bf16[256,128]{1,0:T(8,128)(2,1)}, bf16[256,128]{1,0:T(8,128)(2,1)S(1)}, u32[]{:S(2)}, u32[]{:S(2)}) %collective-permute-start.5) | collective-permute-done | bytes 65568 | tf_op jit(solution)/shard_map/grid_gather/ppermute | solution.py:334
  68.4 1.1 %collective-permute-start.11 = (bf16[256,128]{1,0:T(8,128)(2,1)S(1)}, bf16[256,128]{1,0:T(8,128)(2,1)S(1)}, u32[]{:S(2)}, u32[]{:S(2)}) collective-permute-start(bf16[256,128]{1,0:T(8,128)(2,1)S(1)} %collective-permute-done.5.refs_1_), channel_id=1, source_target_pairs={{0,192},{64,0},{128,64},{192,128},{1,193},{65,1},{129,65},{193,129... | collective-permute-start | bytes 196616 | tf_op jit(solution)/shard_map/grid_gather/ppermute | solution.py:334
  69.6 0.4 collective-permute-start.7
  69.9 0.0 collective-permute-done.10.refs_6_
  69.9 1.1 %collective-permute-start.9 = (bf16[256,128]{1,0:T(8,128)(2,1)S(1)}, bf16[256,128]{1,0:T(8,128)(2,1)S(1)}, u32[]{:S(2)}, u32[]{:S(2)}) collective-permute-start(bf16[256,128]{1,0:T(8,128)(2,1)S(1)} %collective-permute-done.5.refs_1_), channel_id=1, source_target_pairs={{0,128},{64,192},{128,0},{192,64},{1,129},{65,193},{129,1},{193,65... | collective-permute-start | bytes 196616 | tf_op jit(solution)/shard_map/grid_gather/ppermute | solution.py:334
  71.0 0.0 collective-permute-done.6.refs_2_
  71.0 0.0 collective-permute-done.8.refs_4_
  71.0 1.0 %collective-permute-done.11.refs_7_ = bf16[256,128]{1,0:T(8,128)(2,1)S(1)} collective-permute-done((bf16[256,128]{1,0:T(8,128)(2,1)S(1)}, bf16[256,128]{1,0:T(8,128)(2,1)S(1)}, u32[]{:S(2)}, u32[]{:S(2)}) %collective-permute-start.11) | collective-permute-done | bytes 65568 | tf_op jit(solution)/shard_map/grid_gather/ppermute | solution.py:334
  72.0 1.8 %collective-permute-done.7.refs_3_ = bf16[256,128]{1,0:T(8,128)(2,1)S(1)} collective-permute-done((bf16[256,128]{1,0:T(8,128)(2,1)S(1)}, bf16[256,128]{1,0:T(8,128)(2,1)S(1)}, u32[]{:S(2)}, u32[]{:S(2)}) %collective-permute-start.7) | collective-permute-done | bytes 65568 | tf_op jit(solution)/shard_map/grid_gather/ppermute | solution.py:334
  73.9 0.7 collective-permute-done.9.refs_5_
  74.6 0.8 copy-done.4
  75.4 1.3 %regrid.1 = (f32[64,2048]{1,0:T(8,128)S(1)}, f32[64,2048]{1,0:T(8,128)S(1)}) custom-call(s32[4]{0:T(128)S(1)} %copy-done.7, s32[8,16]{1,0:T(8,128)S(1)} %copy-done.5, f32[128,2048]{1,0:T(8,128)S(1)} %copy-done.1, bf16[256,128]{1,0:T(8,128)(2,1)S(1)} %copy-done.4, bf16[256,128]{1,0:T(8,128)(2,1)S(1)} %collective-permute-done.5.refs_1_, ...), custom_call_target="tpu_custom_call" | custom-call | flops 100000000 | bytes 3145728 | tf_op jit(solution)/shard_map/regrid/pallas_call | solution.py:445
  76.7 5.9 %collective-permute-start.12 = (f32[64,2048]{1,0:T(8,128)S(1)}, f32[64,2048]{1,0:T(8,128)S(1)}, u32[]{:S(2)}, u32[]{:S(2)}) collective-permute-start(f32[64,2048]{1,0:T(8,128)S(1)} %get-tuple-element.31), channel_id=1, source_target_pairs={{0,1},{1,0},{2,3},{3,2},{4,5},{5,4},{6,7},{7,6},{8,9},{9,8},{10,11... | collective-permute-start | bytes 1572872 | tf_op jit(solution)/shard_map/dirty_scatter/ppermute | solution.py:334
  82.6 1.5 %collective-permute-done.12 = f32[64,2048]{1,0:T(8,128)S(1)} collective-permute-done((f32[64,2048]{1,0:T(8,128)S(1)}, f32[64,2048]{1,0:T(8,128)S(1)}, u32[]{:S(2)}, u32[]{:S(2)}) %collective-permute-start.12) | collective-permute-done | bytes 524320 | tf_op jit(solution)/shard_map/dirty_scatter/ppermute | solution.py:334
  84.2 0.1 add_convert_fusion
  84.2 0.1 reshape.11
  84.3 14.0 %all_to_all.15 = bf16[16,4,2048]{2,1,0:T(4,128)(2,1)S(1)} all-to-all(bf16[16,4,2048]{2,1,0:T(4,128)(2,1)S(1)} %reshape.11), channel_id=1, replica_groups=mesh['y'=4,'h'=2,'x'=4,'z'=4,'c'=2] {'x','z'}, dimensions={0} | all-to-all | bytes 524288 | tf_op jit(solution)/shard_map/dirty_scatter/all_to_all | solution.py:457
  98.3 0.7 convert_reduce_fusion
  (19 shorter events, 0.0 us)
Async XLA Ops:
  2.2 25.0 %copy-start.5 = (s32[8,16]{1,0:T(8,128)S(1)}, s32[8,16]{1,0:T(8,128)}, u32[]{:S(2)}) copy-start(s32[8,16]{1,0:T(8,128)} %subgrid_ref.3) | copy-start | bytes 1540
  2.2 21.8 %all-to-all-start = ((bf16[16,4,2048]{2,1,0:T(4,128)(2,1)}), bf16[16,4,2048]{2,1,0:T(4,128)(2,1)S(1)}, u32[]{:S(2)}, u32[]{:S(2)}) async-start(bf16[16,4,2048]{2,1,0:T(4,128)(2,1)} %broadcast_in_dim.33), calls=%async_computation | async-start | bytes 524288 | tf_op jit(solution)/shard_map/model_gather/all_to_all | solution.py:367
  11.3 12.6 %collective-permute-start = (bf16[16,2048]{1,0:T(8,128)(2,1)}, bf16[16,2048]{1,0:T(8,128)(2,1)S(1)}, u32[]{:S(2)}, u32[]{:S(2)}) collective-permute-start(bf16[16,2048]{1,0:T(8,128)(2,1)} %bitcast.6), channel_id=1, source_target_pairs={{0,32},{32,0},{1,33},{33,1},{2,34},{34,2},{3,35},{35,3},{4,36},{36... | collective-permute-start | bytes 196616 | tf_op jit(solution)/shard_map/visible_route/ppermute | solution.py:334
  16.1 11.0 %copy-start.6 = (s32[4]{0:T(128)S(1)}, s32[4]{0:T(128)}, u32[]{:S(2)}) copy-start(s32[4]{0:T(128)} %compare_select_fusion.2.place_ref) | copy-start | bytes 52
  16.1 22.3 %copy-start.2 = (bf16[1,16,2048]{2,1,0:T(8,128)(2,1)S(1)}, bf16[1,16,2048]{2,1,0:T(8,128)(2,1)}, u32[]{:S(2)}) copy-start(bf16[1,16,2048]{2,1,0:T(8,128)(2,1)} %param.10) | copy-start | bytes 196612
  23.9 14.5 %copy-start.8 = (s32[1,8]{1,0:T(1,128)S(1)}, s32[1,8]{1,0:T(1,128)}, u32[]{:S(2)}) copy-start(s32[1,8]{1,0:T(1,128)} %reader_ref.3) | copy-start | bytes 100
  23.9 30.3 %copy-start.3 = (bf16[16,2048]{1,0:T(8,128)(2,1)}, bf16[16,2048]{1,0:T(8,128)(2,1)S(1)}, u32[]{:S(2)}) copy-start(bf16[16,2048]{1,0:T(8,128)(2,1)S(1)} %collective-permute-done.other_ref) | copy-start | bytes 196612
  23.9 3.2 %collective-permute-start.1 = (bf16[16,4,2048]{2,1,0:T(4,128)(2,1)S(1)}, bf16[16,4,2048]{2,1,0:T(4,128)(2,1)S(1)}, u32[]{:S(2)}, u32[]{:S(2)}) collective-permute-start(bf16[16,4,2048]{2,1,0:T(4,128)(2,1)S(1)} %all-to-all-done.near_ref), channel_id=1, source_target_pairs={{0,1},{1,0},{2,3},{3,2},{4,5},{5,4},{6,7},{7,6},{8,9},{9,8},{10,11... | collective-permute-start | bytes 786440 | tf_op jit(solution)/shard_map/visible_route/ppermute | solution.py:334
  27.1 1.2 %copy-start = (f32[128,2048]{1,0:T(8,128)S(1)}, f32[128,2048]{1,0:T(8,128)}, u32[]{:S(2)}) copy-start(f32[128,2048]{1,0:T(8,128)} %get-tuple-element.21.screen_ref) | copy-start | bytes 3145732
  30.3 23.9 %all-to-all-start.1 = ((bf16[8,256,128]{2,1,0:T(8,128)(2,1)}), bf16[8,256,128]{2,1,0:T(8,128)(2,1)S(1)}, u32[]{:S(2)}, u32[]{:S(2)}) async-start(bf16[8,256,128]{2,1,0:T(8,128)(2,1)} %images.1), calls=%async_computation.1 | async-start | bytes 1048576 | tf_op jit(solution)/shard_map/all_to_all | solution.py:415
  39.0 5.9 %collective-permute-start.2 = (bf16[16,2048]{1,0:T(8,128)(2,1)S(1)}, bf16[16,2048]{1,0:T(8,128)(2,1)S(1)}, u32[]{:S(2)}, u32[]{:S(2)}) collective-permute-start(bf16[16,2048]{1,0:T(8,128)(2,1)S(1)} %get-tuple-element.23), channel_id=1, source_target_pairs={{0,64},{64,128},{128,192},{192,0},{1,65},{65,129},{129,193},{193,1... | collective-permute-start | bytes 196616 | tf_op jit(solution)/shard_map/ppermute | solution.py:334
  40.6 6.8 %collective-permute-start.3 = (bf16[16,2048]{1,0:T(8,128)(2,1)S(1)}, bf16[16,2048]{1,0:T(8,128)(2,1)S(1)}, u32[]{:S(2)}, u32[]{:S(2)}) collective-permute-start(bf16[16,2048]{1,0:T(8,128)(2,1)S(1)} %get-tuple-element.24), channel_id=1, source_target_pairs={{0,128},{64,192},{128,0},{192,64},{1,129},{65,193},{129,1},{193,65... | collective-permute-start | bytes 196616 | tf_op jit(solution)/shard_map/ppermute | solution.py:334
  43.0 31.6 %copy-start.1 = (f32[128,2048]{1,0:T(8,128)S(1)}, f32[128,2048]{1,0:T(8,128)}, u32[]{:S(2)}) copy-start(f32[128,2048]{1,0:T(8,128)} %get-tuple-element.21.screen_ref) | copy-start | bytes 3145732
  43.0 31.6 %copy-start.7 = (s32[4]{0:T(128)S(1)}, s32[4]{0:T(128)}, u32[]{:S(2)}) copy-start(s32[4]{0:T(128)} %compare_select_fusion.2.place_ref) | copy-start | bytes 52
  43.0 4.4 %collective-permute-start.4 = (bf16[16,2048]{1,0:T(8,128)(2,1)S(1)}, bf16[16,2048]{1,0:T(8,128)(2,1)S(1)}, u32[]{:S(2)}, u32[]{:S(2)}) collective-permute-start(bf16[16,2048]{1,0:T(8,128)(2,1)S(1)} %get-tuple-element.25), channel_id=1, source_target_pairs={{0,192},{64,0},{128,64},{192,128},{1,193},{65,1},{129,65},{193,129... | collective-permute-start | bytes 196616 | tf_op jit(solution)/shard_map/ppermute | solution.py:334
  44.9 9.3 %copy-start.10 = (bf16[16,2048]{1,0:T(8,128)(2,1)}, bf16[16,2048]{1,0:T(8,128)(2,1)S(1)}, u32[]{:S(2)}) copy-start(bf16[16,2048]{1,0:T(8,128)(2,1)S(1)} %collective-permute-done.2.came_1_ref) | copy-start | bytes 196612
  47.3 6.9 %copy-start.11 = (bf16[16,2048]{1,0:T(8,128)(2,1)}, bf16[16,2048]{1,0:T(8,128)(2,1)S(1)}, u32[]{:S(2)}) copy-start(bf16[16,2048]{1,0:T(8,128)(2,1)S(1)} %collective-permute-done.3.came_2_ref) | copy-start | bytes 196612
  47.3 6.9 %copy-start.12 = (bf16[16,2048]{1,0:T(8,128)(2,1)}, bf16[16,2048]{1,0:T(8,128)(2,1)S(1)}, u32[]{:S(2)}) copy-start(bf16[16,2048]{1,0:T(8,128)(2,1)S(1)} %collective-permute-done.4.came_3_ref) | copy-start | bytes 196612
  54.2 0.8 copy-start.9
  61.1 7.3 %collective-permute-start.5 = (bf16[256,128]{1,0:T(8,128)(2,1)}, bf16[256,128]{1,0:T(8,128)(2,1)S(1)}, u32[]{:S(2)}, u32[]{:S(2)}) collective-permute-start(bf16[256,128]{1,0:T(8,128)(2,1)} %get-tuple-element.29.refs_0_), channel_id=1, source_target_pairs={{0,32},{32,0},{1,33},{33,1},{2,34},{34,2},{3,35},{35,3},{4,36},{36... | collective-permute-start | bytes 196616 | tf_op jit(solution)/shard_map/grid_gather/ppermute | solution.py:334
  62.8 7.1 %collective-permute-start.10 = (bf16[256,128]{1,0:T(8,128)(2,1)}, bf16[256,128]{1,0:T(8,128)(2,1)S(1)}, u32[]{:S(2)}, u32[]{:S(2)}) collective-permute-start(bf16[256,128]{1,0:T(8,128)(2,1)} %get-tuple-element.29.refs_0_), channel_id=1, source_target_pairs={{0,192},{64,0},{128,64},{192,128},{1,193},{65,1},{129,65},{193,129... | collective-permute-start | bytes 196616 | tf_op jit(solution)/shard_map/grid_gather/ppermute | solution.py:334
  64.6 6.4 %collective-permute-start.6 = (bf16[256,128]{1,0:T(8,128)(2,1)}, bf16[256,128]{1,0:T(8,128)(2,1)S(1)}, u32[]{:S(2)}, u32[]{:S(2)}) collective-permute-start(bf16[256,128]{1,0:T(8,128)(2,1)} %get-tuple-element.29.refs_0_), channel_id=1, source_target_pairs={{0,64},{64,128},{128,192},{192,0},{1,65},{65,129},{129,193},{193,1... | collective-permute-start | bytes 196616 | tf_op jit(solution)/shard_map/grid_gather/ppermute | solution.py:334
  64.6 6.4 %collective-permute-start.8 = (bf16[256,128]{1,0:T(8,128)(2,1)}, bf16[256,128]{1,0:T(8,128)(2,1)S(1)}, u32[]{:S(2)}, u32[]{:S(2)}) collective-permute-start(bf16[256,128]{1,0:T(8,128)(2,1)} %get-tuple-element.29.refs_0_), channel_id=1, source_target_pairs={{0,128},{64,192},{128,0},{192,64},{1,129},{65,193},{129,1},{193,65... | collective-permute-start | bytes 196616 | tf_op jit(solution)/shard_map/grid_gather/ppermute | solution.py:334
  68.4 3.6 %collective-permute-start.11 = (bf16[256,128]{1,0:T(8,128)(2,1)S(1)}, bf16[256,128]{1,0:T(8,128)(2,1)S(1)}, u32[]{:S(2)}, u32[]{:S(2)}) collective-permute-start(bf16[256,128]{1,0:T(8,128)(2,1)S(1)} %collective-permute-done.5.refs_1_), channel_id=1, source_target_pairs={{0,192},{64,0},{128,64},{192,128},{1,193},{65,1},{129,65},{193,129... | collective-permute-start | bytes 196616 | tf_op jit(solution)/shard_map/grid_gather/ppermute | solution.py:334
  69.6 4.3 %collective-permute-start.7 = (bf16[256,128]{1,0:T(8,128)(2,1)S(1)}, bf16[256,128]{1,0:T(8,128)(2,1)S(1)}, u32[]{:S(2)}, u32[]{:S(2)}) collective-permute-start(bf16[256,128]{1,0:T(8,128)(2,1)S(1)} %collective-permute-done.5.refs_1_), channel_id=1, source_target_pairs={{0,64},{64,128},{128,192},{192,0},{1,65},{65,129},{129,193},{193,1... | collective-permute-start | bytes 196616 | tf_op jit(solution)/shard_map/grid_gather/ppermute | solution.py:334
  69.9 4.7 %collective-permute-start.9 = (bf16[256,128]{1,0:T(8,128)(2,1)S(1)}, bf16[256,128]{1,0:T(8,128)(2,1)S(1)}, u32[]{:S(2)}, u32[]{:S(2)}) collective-permute-start(bf16[256,128]{1,0:T(8,128)(2,1)S(1)} %collective-permute-done.5.refs_1_), channel_id=1, source_target_pairs={{0,128},{64,192},{128,0},{192,64},{1,129},{65,193},{129,1},{193,65... | collective-permute-start | bytes 196616 | tf_op jit(solution)/shard_map/grid_gather/ppermute | solution.py:334
  74.6 0.8 copy-start.4
  76.7 7.4 %collective-permute-start.12 = (f32[64,2048]{1,0:T(8,128)S(1)}, f32[64,2048]{1,0:T(8,128)S(1)}, u32[]{:S(2)}, u32[]{:S(2)}) collective-permute-start(f32[64,2048]{1,0:T(8,128)S(1)} %get-tuple-element.31), channel_id=1, source_target_pairs={{0,1},{1,0},{2,3},{3,2},{4,5},{5,4},{6,7},{7,6},{8,9},{9,8},{10,11... | collective-permute-start | bytes 1572872 | tf_op jit(solution)/shard_map/dirty_scatter/ppermute | solution.py:334

commit v4 on v3

--- a/solution.py
+++ b/solution.py
@@ -53,15 +53,7 @@
     return (held * (128 // cores)) + lax.div(subgrid, owned * cores) * owned + lax.rem(subgrid, owned)
 
 
-def prepare_kernel(place_ref, *refs):
-    sources, (east_to, north_to, screen_ref) = (refs[:6], refs[6:9])
-    east_ref, north_ref, powers, groups, sems, out_sems = refs[15:]
-    copies = [pltpu.make_async_copy(src, dst, sems.at[at]) for at, (src, dst) in enumerate(zip(sources, refs[9:15]))]
-    for copy in copies:
-        copy.start()
-    coords_ref, freq_ref, stations_ref, plane_ref, phase_ref, beam_ref = refs[9:15]
-    copies[0].wait()
-    copies[1].wait()
+def table_kernel(place_ref, coords_ref, freq_ref, table_ref, powers, groups):
     rows = coords_ref.shape[2]
     coords = coords_ref[place_ref[0]]
     row = jnp.concatenate([coords[0:1], coords[1:2], jnp.zeros((1, 128 - 2 * rows), F32)], axis=1)
@@ -94,24 +86,27 @@
     def stacked(parts):
         return jnp.concatenate([part[0] for part in parts] + [part[1] for part in parts], axis=0).astype(BF16)
 
-    def body(b, carry):
+    def body(b):
         base = bits([row_of(powers, at, b) for at in (2, 3, 4)])
-        east_ref[b] = stacked([cmul(base, row_of(groups, at, b)) for at in range(4)])
+        table_ref[0, b] = stacked([cmul(base, row_of(groups, at, b)) for at in range(4)])
         row = b + rows
         base = bits([row_of(powers, at, row) for at in (0, 1, 2)])
         up8 = row_of(powers, 3, row)
-        north_ref[b] = stacked([cmul(base, row_of(groups, 0, row)), cmul(base, conj(up8)), base, cmul(base, up8)])
-        return carry
-
-    lax.fori_loop(0, rows, body, 0)
-    stores = [
-        pltpu.make_async_copy(src, dst, out_sems.at[at])
-        for at, (src, dst) in enumerate(((east_ref, east_to), (north_ref, north_to)))
-    ]
-    for store in stores:
-        store.start()
-
-    for copy in copies[2:]:
+        table_ref[1, b] = stacked(
+            [cmul(base, row_of(groups, 0, row)), cmul(base, conj(up8)), base, cmul(base, up8)]
+        )
+
+    for b in range(rows):
+        body(b)
+
+
+def screen_kernel(stations_from, plane_from, phase_from, beam_from, screen_ref, *refs):
+    sources, held, sems = ((stations_from, plane_from, phase_from, beam_from), refs[:4], refs[4])
+    copies = [pltpu.make_async_copy(src, dst, sems.at[at]) for at, (src, dst) in enumerate(zip(sources, held))]
+    for copy in copies:
+        copy.start()
+    stations_ref, plane_ref, phase_ref, beam_ref = held
+    for copy in copies:
         copy.wait()
     stations = beam_ref.shape[0]
     planes, pixels = phase_ref.shape
@@ -133,15 +128,26 @@
         wave_im = jnp.dot(plane, jnp.sin(phase), precision=exact, preferred_element_type=F32)
         screen_ref[:, re] = pair_re * wave_re - pair_im * wave_im
         screen_ref[:, im] = pair_re * wave_im + pair_im * wave_re
-    for store in stores:
-        store.wait()
-
-
-def image_kernel(cores, owned, place_ref, subgrid_ref, near_ref, far_ref, screen_ref, image_ref):
+
+
+def blocks_from(place_ref, n_y, n_h, sign):
+    return [
+        lax.rem(place_ref[1] + (n_y + sign * by) % n_y, n_y) * n_h + lax.rem(place_ref[2] + flip, n_h)
+        for by in range(n_y)
+        for flip in range(n_h)
+    ]
+
+
+def rows_of_blocks(ref, blocks, cells):
+    return jnp.concatenate([ref[pl.ds(pl.multiple_of(block * 16, 16), 16), cells] for block in blocks], axis=0)
+
+
+def image_kernel(n_y, n_h, cores, owned, place_ref, subgrid_ref, near_ref, far_ref, screen_ref, *image_refs):
     half = near_ref.shape[0] * near_ref.shape[1]
     pixels = screen_ref.shape[1] // 2
-    blocks = image_ref.shape[0]
-    slots = down(slot_of(row_of_blocks(subgrid_ref[...]), place_ref[3], cores, owned))
+    blocks = blocks_from(place_ref, n_y, n_h, 1)
+    subgrids = jnp.concatenate([subgrid_ref[pl.ds(block, 1), :] for block in blocks], axis=1)
+    slots = down(slot_of(subgrids, place_ref[3], cores, owned))
     near, far = (onehot(slots, 0, half), onehot(slots, half, half))
     tiles = pixels // 128
     width = 256
@@ -153,14 +159,24 @@
     for at in range(0, pixels, width):
         re, im = pl.ds(at, width), pl.ds(pixels + at, width)
         model_re, model_im = (rows_of(re), rows_of(im))
-        screen_re, screen_im = (screen_ref[:, re], screen_ref[:, im])
+        screen_re, screen_im = (rows_of_blocks(screen_ref, blocks, re), rows_of_blocks(screen_ref, blocks, im))
         image_re = (screen_re * model_re - screen_im * model_im).astype(BF16)
         image_im = (screen_re * model_im + screen_im * model_re).astype(BF16)
         for off in range(0, width, 128):
-            q = (at + off) // 128
-            image_ref[:, 16 * q : 16 * q + 16, :] = image_re[:, off : off + 128].reshape(blocks, 16, 128)
-            q = q + tiles
-            image_ref[:, 16 * q : 16 * q + 16, :] = image_im[:, off : off + 128].reshape(blocks, 16, 128)
+            for image, q in ((image_re, (at + off) // 128), (image_im, (at + off) // 128 + tiles)):
+                for j in range(len(blocks)):
+                    image_refs[j // n_h][j % n_h, 16 * q : 16 * q + 16, :] = image[
+                        16 * j : 16 * j + 16, off : off + 128
+                    ]
+
+
+def sum_kernel(*refs):
+    pieces, sums = (refs[:-2], refs[-2:])
+    for flip, sum_ref in enumerate(sums):
+        total = pieces[0][flip].astype(F32)
+        for piece in pieces[1:]:
+            total = total + piece[flip].astype(F32)
+        sum_ref[...] = total
 
 
 def route_kernel(n_y, n_h, place_ref, reader_ref, rows_ref, other_ref, *out_refs):
@@ -184,40 +200,21 @@
     n_h,
     place_ref,
     reader_ref,
-    images_ref,
+    near_ref,
+    far_ref,
     rows_ref,
     other_ref,
     came_1_ref,
     came_2_ref,
     came_3_ref,
-    east_from,
-    north_from,
+    table_ref,
     resid_ref,
     grid_ref,
     cells_ref,
     out_ref,
-    east_ref,
-    north_ref,
-    sems,
 ):
     rows, channels = (resid_ref.shape[0], resid_ref.shape[1] // 2)
-    facets = images_ref.shape[0]
-
-    run = rows // 4
-    copies = [
-        [
-            pltpu.make_async_copy(src.at[pl.ds(at * run, run)], dst.at[pl.ds(at * run, run)], sems.at[kind, at])
-            for kind, (src, dst) in enumerate(((east_from, east_ref), (north_from, north_ref)))
-        ]
-        for at in range(4)
-    ]
-    for pair in copies:
-        for copy in pair:
-            copy.start()
-    total = images_ref[0].astype(F32)
-    for at in range(1, facets):
-        total = total + images_ref[at].astype(F32)
-    cells_ref[...] = total
+    cells_ref[...] = near_ref[...] + far_ref[...]
     source = reader_ref[0, place_ref[0]]
     steps = lax.rem(place_ref[1] + n_y - lax.div(source, n_h), n_y)
     here = jnp.where(lax.rem(source, n_h) == place_ref[2], 0, 1)
@@ -245,13 +242,13 @@
         image = jnp.concatenate([spread(cells[0:8], -cells[8:16]), spread(cells[8:16], cells[0:8])], axis=0)
         high = image.astype(BF16)
         low = (image - high.astype(F32)).astype(BF16)
-        operand = jnp.concatenate([high, low], axis=0)
+        operand = jnp.concatenate([high, low], axis=1)
         for at in range(0, channels, width):
             chans = pl.ds(at, width)
-            inner = jnp.dot(operand, north_ref[b, :, chans], preferred_element_type=F32)
-            inner = inner[:64] + inner[64:]
+            north = table_ref[1, b, :, chans]
+            inner = jnp.dot(operand, jnp.concatenate([north, north], axis=0), preferred_element_type=F32)
             inner_re, inner_im = (inner[:32], inner[32:])
-            east = east_ref[b, :, chans].astype(F32)
+            east = table_ref[0, b, :, chans].astype(F32)
             cos, sin = (east[:32], east[32:])
             vis_re = jnp.sum(cos * inner_re - sin * inner_im, axis=0, keepdims=True)
             vis_im = jnp.sum(cos * inner_im + sin * inner_re, axis=0, keepdims=True)
@@ -265,12 +262,12 @@
         for at in range(0, channels, width):
             chans, late = (pl.ds(at, width), pl.ds(channels + at, width))
             resid_re, resid_im = (resid_ref[pl.ds(b, 1), chans], resid_ref[pl.ds(b, 1), late])
-            east = east_ref[b, :, chans].astype(F32)
+            east = table_ref[0, b, :, chans].astype(F32)
             cos, sin = (east[:32], east[32:])
             weighted = jnp.concatenate([cos * resid_re + sin * resid_im, cos * resid_im - sin * resid_re], axis=0)
             products = products + lax.dot_general(
                 weighted.astype(BF16),
-                north_ref[b, :, chans],
+                table_ref[1, b, :, chans],
                 (((1,), (1,)), ((), ())),
                 preferred_element_type=F32,
             )
@@ -279,11 +276,8 @@
             [jnp.concatenate([half[8 * p : 8 * p + 8] for p in range(4)], axis=1) for half in halves], axis=0
         )
 
-    for at, pair in enumerate(copies):
-        for copy in pair:
-            copy.wait()
-        for b in range(at * run, at * run + run):
-            degrid(b)
+    for b in range(rows):
+        degrid(b)
     for b in range(rows):
         grid(b)
     grid_ref[...] = out_ref[...].astype(BF16)
@@ -291,18 +285,11 @@
 
 def regrid_kernel(scale, n_y, n_h, cores, owned, place_ref, subgrid_ref, screen_ref, *refs):
     grids, (near_ref, far_ref) = (refs[:-2], refs[-2:])
-    blocks = []
-    for at in range(len(grids)):
-        by, flip = divmod(at, n_h)
-        blocks.append(lax.rem(place_ref[1] + (n_y - by), n_y) * n_h + lax.rem(place_ref[2] + flip, n_h))
+    blocks = blocks_from(place_ref, n_y, n_h, -1)
     half = near_ref.shape[0]
     pixels = screen_ref.shape[1] // 2
     tiles = pixels // 128
     count = screen_ref.shape[0]
-
-    def screen_of(cells):
-        rows = [screen_ref[pl.ds(pl.multiple_of(block * 16, 16), 16), cells] for block in blocks]
-        return jnp.concatenate(rows, axis=0)
 
     def grid_of(q):
         return jnp.concatenate([ref[16 * q : 16 * q + 16, :] for ref in grids], axis=0).astype(F32)
@@ -315,7 +302,7 @@
     for q in range(tiles):
         re, im = pl.ds(128 * q, 128), pl.ds(pixels + 128 * q, 128)
         grid_re, grid_im = (grid_of(q), grid_of(q + tiles))
-        screen_re, screen_im = (screen_of(re), screen_of(im))
+        screen_re, screen_im = (rows_of_blocks(screen_ref, blocks, re), rows_of_blocks(screen_ref, blocks, im))
         out_re = (screen_re * grid_re + screen_im * grid_im) * scale
         out_im = (screen_re * grid_im - screen_im * grid_re) * scale
         for cells, value in ((re, out_re), (im, out_im)):
@@ -366,32 +353,34 @@
         copies = jnp.broadcast_to(model_grid, (n_x * n_z, owned, 2 * pixels))
         near = lax.all_to_all(copies, ("x", "z"), split_axis=0, concat_axis=0, tiled=True)
 
-    operands = (baseline_coords, channel_freq.reshape(1, channels), stations, plane_index, plane_phase, beam_screens[0])
-    east, north, screen = pl.pallas_call(
-        prepare_kernel,
-        out_shape=[jax.ShapeDtypeStruct((row_block, 64, channels), BF16)] * 2
-        + [jax.ShapeDtypeStruct((count, 2 * pixels), F32)],
-        in_specs=[SMEM] + [ANY] * len(operands),
-        out_specs=[ANY, ANY, VMEM],
+    operands = (stations, plane_index, plane_phase, beam_screens[0])
+    screen = pl.pallas_call(
+        screen_kernel,
+        out_shape=jax.ShapeDtypeStruct((count, 2 * pixels), F32),
+        in_specs=[ANY] * len(operands),
+        out_specs=VMEM,
         scratch_shapes=[pltpu.VMEM(value.shape, value.dtype) for value in operands]
-        + [
-            pltpu.VMEM((row_block, 64, channels), BF16),
-            pltpu.VMEM((row_block, 64, channels), BF16),
-            pltpu.VMEM((10, 2 * row_block, channels), F32),
-            pltpu.VMEM((8, 2 * row_block, channels), F32),
-            pltpu.SemaphoreType.DMA((len(operands),)),
-            pltpu.SemaphoreType.DMA((2,)),
-        ],
-        compiler_params=params(61),
-        cost_estimate=pl.CostEstimate(flops=10**9, bytes_accessed=8 << 20, transcendentals=1 << 17),
-        name="prepare",
-    )(place, *operands)
+        + [pltpu.SemaphoreType.DMA((len(operands),))],
+        compiler_params=params(58),
+        cost_estimate=pl.CostEstimate(flops=10**9, bytes_accessed=4 << 20, transcendentals=1 << 16),
+        name="screens",
+    )(*operands)
+
+    near, screen = lax.optimization_barrier((near, screen))
+    far = shift(near, "c", 1)
+    images = pl.pallas_call(
+        functools.partial(image_kernel, n_y, n_h, n_c, owned),
+        out_shape=[jax.ShapeDtypeStruct((n_h, cell_rows, 128), BF16)] * n_y,
+        in_specs=[SMEM] + [VMEM] * 4,
+        out_specs=[VMEM] * n_y,
+        compiler_params=params(8),
+        cost_estimate=pl.CostEstimate(flops=10**8, bytes_accessed=2 << 20, transcendentals=0),
+        name="images",
+    )(place, subgrid_index, near, far, screen)
+    rows, *images = lax.optimization_barrier((sectioned_rows[0], *images))
 
     with jax.named_scope("visible_route"):
-        rows = sectioned_rows[0]
         other = shift(rows, "h", 1)
-        near, other, east, north, screen = lax.optimization_barrier((near, other, east, north, screen))
-        far = shift(near, "c", 1)
         sent = pl.pallas_call(
             functools.partial(route_kernel, n_y, n_h),
             out_shape=[jax.ShapeDtypeStruct(rows.shape, BF16)] * (n_y - 1),
@@ -402,17 +391,33 @@
             name="route",
         )(place, reader, rows, other)
 
-    images = pl.pallas_call(
-        functools.partial(image_kernel, n_c, owned),
-        out_shape=jax.ShapeDtypeStruct((n_facet, cell_rows, 128), BF16),
-        in_specs=[SMEM] + [VMEM] * 4,
+    with jax.named_scope("image_sum"):
+        pieces = [images[0]] + [shift(images[by], "y", by) for by in range(1, n_y)]
+        own_sum, other_sum = pl.pallas_call(
+            sum_kernel,
+            out_shape=[jax.ShapeDtypeStruct((cell_rows, 128), F32)] * 2,
+            in_specs=[VMEM] * n_y,
+            out_specs=[VMEM] * 2,
+            compiler_params=params(4),
+            cost_estimate=pl.CostEstimate(flops=10**6, bytes_accessed=1 << 20, transcendentals=0),
+            name="image_sums",
+        )(*pieces)
+        later, own_sum = lax.optimization_barrier((place, own_sum))
+        beside_sum = shift(other_sum, "h", 1)
+
+    tables = pl.pallas_call(
+        table_kernel,
+        out_shape=jax.ShapeDtypeStruct((2, row_block, 64, channels), BF16),
+        in_specs=[SMEM, VMEM, VMEM],
         out_specs=VMEM,
-        compiler_params=params(8),
-        cost_estimate=pl.CostEstimate(flops=10**8, bytes_accessed=2 << 20, transcendentals=0),
-        name="images",
-    )(place, subgrid_index, near, far, screen)
-
-    arrived = lax.all_to_all(images, FACET, split_axis=0, concat_axis=0, tiled=True)
+        scratch_shapes=[
+            pltpu.VMEM((10, 2 * row_block, channels), F32),
+            pltpu.VMEM((8, 2 * row_block, channels), F32),
+        ],
+        compiler_params=params(16),
+        cost_estimate=pl.CostEstimate(flops=10**9, bytes_accessed=8 << 20, transcendentals=1 << 17),
+        name="tables",
+    )(later, baseline_coords, channel_freq.reshape(1, channels))
     came = [shift(value, "y", by) for by, value in enumerate(sent, 1)]
 
     residual, gridded = pl.pallas_call(
@@ -421,19 +426,13 @@
             jax.ShapeDtypeStruct((row_block, 2 * channels), F32),
             jax.ShapeDtypeStruct((cell_rows, 128), BF16),
         ],
-        in_specs=[SMEM] * 2 + [VMEM] * 6 + [ANY] * 2,
+        in_specs=[SMEM] * 2 + [VMEM] * 8,
         out_specs=[VMEM] * 2,
-        scratch_shapes=[
-            pltpu.VMEM((cell_rows, 128), F32),
-            pltpu.VMEM((cell_rows, 128), F32),
-            pltpu.VMEM(east.shape, BF16),
-            pltpu.VMEM(north.shape, BF16),
-            pltpu.SemaphoreType.DMA((2, 4)),
-        ],
-        compiler_params=params(61),
+        scratch_shapes=[pltpu.VMEM((cell_rows, 128), F32), pltpu.VMEM((cell_rows, 128), F32)],
+        compiler_params=params(16),
         cost_estimate=pl.CostEstimate(flops=10**9, bytes_accessed=8 << 20, transcendentals=0),
         name="visibilities",
-    )(place, reader, arrived, rows, other, *came, east, north)
+    )(place, reader, own_sum, beside_sum, rows, other, *came, tables)
 
     with jax.named_scope("grid_gather"):
         beside = shift(gridded, "h", 1)

time: 99.6 us -> 90.3 us (0.907)
  waiting for transfers between devices: 18.9 us -> 16.3 us
  Pallas kernels: 17.7 us -> 15.5 us
  local copies, waits for them, and re-layouts: 4.55 us -> 2.92 us
  blocking collectives: 14 us -> 12.6 us
  starting transfers between devices: 41.9 us -> 40.9 us
    all_to_all x1 -> x0, starting transfers between devices: 8.12 us -> none  [local(): lax.all_to_all(images, FACET, split_axis=0, concat_axis=0, tiled=True)]
    ppermute x13 -> x17, starting transfers between devices: 24.6 us -> 31.9 us  [shift(): lax.ppermute(value, axis, [(i, (i + by) % size) for i in range(size)])]
    all_to_all x1 -> x0, waiting for transfers between devices: 6.88 us -> none  [local(): lax.all_to_all(images, FACET, split_axis=0, concat_axis=0, tiled=True)]
    all_to_all x1, waiting for transfers between devices: 0.01 us -> 4.95 us  [local(): lax.all_to_all(copies, ('x', 'z'), split_axis=0, concat_axis=0, tiled=True)]
    pallas_call x1, Pallas kernels: 6.08 us -> 4.2 us  [local(): pl.pallas_call(functools.partial(visibility_kernel, n_y, n_h), out_shape=...]
    unnamed x26 -> x14, local copies, waits for them, and re-layouts: 2.91 us -> 1.25 us
    all_to_all x1, blocking collectives: 14 us -> 12.6 us  [local(): lax.all_to_all(chip_sum, ('x', 'z'), split_axis=0, concat_axis=0, tiled=T...]
    ppermute x13 -> x17, waiting for transfers between devices: 12 us -> 11.4 us  [shift(): lax.ppermute(value, axis, [(i, (i + by) % size) for i in range(size)])]
  transfers between devices with their start and end apart: 15 -> 18, of which waited for: 9 -> 8; matrix products, arithmetic and copies ran while one was open for 1% -> 0% of each run, Pallas kernels for 8% -> 10%
where the time goes in v4:
time: 90.3 us; the launch traced here: 89.9 us
  starting transfers between devices  40.9 us (45%)
  waiting for transfers between devices  16.3 us (18%)
  Pallas kernels  15.5 us (17%)
  blocking collectives  12.6 us (14%)
  local copies, waits for them, and re-layouts  2.92 us (3%)
    ppermute x17, starting transfers between devices, shift(): lax.ppermute(value, axis, [(i, (i + by) % size) for i in range(size)])  31.9 us
    all_to_all x1, blocking collectives, local(): lax.all_to_all(chip_sum, ('x', 'z'), split_axis=0, concat_axis=0, tiled=T...  12.6 us
    ppermute x17, waiting for transfers between devices, shift(): lax.ppermute(value, axis, [(i, (i + by) % size) for i in range(size)])  11.4 us
    all_to_all x1, starting transfers between devices, local(): lax.all_to_all(copies, ('x', 'z'), split_axis=0, concat_axis=0, tiled=True)  9.01 us
    all_to_all x1, waiting for transfers between devices, local(): lax.all_to_all(copies, ('x', 'z'), split_axis=0, concat_axis=0, tiled=True)  4.95 us
    pallas_call x1, Pallas kernels, local(): pl.pallas_call(screen_kernel, out_shape=jax.ShapeDtypeStruct((count, 2 *...  4.73 us
    pallas_call x1, Pallas kernels, local(): pl.pallas_call(functools.partial(visibility_kernel, n_y, n_h), out_shape=...  4.2 us
    pallas_call x1, Pallas kernels, local(): pl.pallas_call(table_kernel, out_shape=jax.ShapeDtypeStruct((2, row_block...  3.52 us
  transfers between devices with their start and end apart: 18, of which 8 were waited for; matrix products, arithmetic and copies ran while one was open for 0% of the time, Pallas kernels for 10%

profile of v4, /device:TPU:1, one launch (start us, length us, event | category | flops | bytes accessed | tf_op | source)
XLA Modules:
  0.0 89.9 jit_solution(17234662181989580198)
XLA Ops:
  0.7 1.6 %broadcast_in_dim.33 = bf16[16,4,2048]{2,1,0:T(4,128)(2,1)} broadcast(bf16[4,2048]{1,0:T(4,128)(2,1)} %bitcast.11), dimensions={1,2} | broadcast | bytes 278528 | tf_op jit(solution)/shard_map/model_gather/broadcast_in_dim | solution.py:353
  2.2 9.0 %all-to-all-start = ((bf16[16,4,2048]{2,1,0:T(4,128)(2,1)}), bf16[16,4,2048]{2,1,0:T(4,128)(2,1)S(1)}, u32[]{:S(2)}, u32[]{:S(2)}) async-start(bf16[16,4,2048]{2,1,0:T(4,128)(2,1)} %broadcast_in_dim.33), calls=%async_computation | async-start | bytes 524288 | tf_op jit(solution)/shard_map/model_gather/all_to_all | solution.py:354
  11.3 4.7 %screens.1.screen_ref = f32[128,2048]{1,0:T(8,128)} custom-call(s32[8,2,16]{2,1,0:T(2,128)} %stations_from.1, s32[8,16]{1,0:T(8,128)} %plane_from.1, f32[32,1024]{1,0:T(8,128)} %phase_from.1, bf16[512,2048]{1,0:T(8,128)(2,1)} %bitcast.12), custom_call_target="tpu_custom_call" | custom-call | flops 1000000000 | bytes 4194304 | tf_op jit(solution)/shard_map/screens/pallas_call | solution.py:357
  16.0 5.0 %all-to-all-done.near_ref = bf16[16,4,2048]{2,1,0:T(4,128)(2,1)S(1)} async-done(((bf16[16,4,2048]{2,1,0:T(4,128)(2,1)}), bf16[16,4,2048]{2,1,0:T(4,128)(2,1)S(1)}, u32[]{:S(2)}, u32[]{:S(2)}) %all-to-all-start) | async-done | bytes 262176 | tf_op jit(solution)/shard_map/model_gather/all_to_all | solution.py:354
  21.0 2.1 %collective-permute-start = (bf16[16,4,2048]{2,1,0:T(4,128)(2,1)S(1)}, bf16[16,4,2048]{2,1,0:T(4,128)(2,1)S(1)}, u32[]{:S(2)}, u32[]{:S(2)}) collective-permute-start(bf16[16,4,2048]{2,1,0:T(4,128)(2,1)S(1)} %all-to-all-done.near_ref), channel_id=1, source_target_pairs={{0,1},{1,0},{2,3},{3,2},{4,5},{5,4},{6,7},{7,6},{8,9},{9,8},{10,11... | collective-permute-start | bytes 786440 | tf_op jit(solution)/shard_map/ppermute | solution.py:321
  23.1 1.2 %collective-permute-done.far_ref = bf16[16,4,2048]{2,1,0:T(4,128)(2,1)S(1)} collective-permute-done((bf16[16,4,2048]{2,1,0:T(4,128)(2,1)S(1)}, bf16[16,4,2048]{2,1,0:T(4,128)(2,1)S(1)}, u32[]{:S(2)}, u32[]{:S(2)}) %collective-permute-start) | collective-permute-done | bytes 262176 | tf_op jit(solution)/shard_map/ppermute | solution.py:321
  24.3 1.2 %copy-done = f32[128,2048]{1,0:T(8,128)S(1)} copy-done((f32[128,2048]{1,0:T(8,128)S(1)}, f32[128,2048]{1,0:T(8,128)}, u32[]{:S(2)}) %copy-start) | copy-done | bytes 1048600
  25.5 1.1 %images.1 = (bf16[2,256,128]{2,1,0:T(8,128)(2,1)S(1)}, bf16[2,256,128]{2,1,0:T(8,128)(2,1)S(1)}, bf16[2,256,128]{2,1,0:T(8,128)(2,1)S(1)}, bf16[2,256,128]{2,1,0:T(8,128)(2,1)S(1)}) custom-call(s32[4]{0:T(128)S(1)} %compare_select_fusion.2.place_ref, s32[8,16]{1,0:T(8,128)S(1)} %copy-done.3, bf16[16,4,2048]{2,1,0:T(4,128)(2,1)S(1)} %all-to-all-done.near_ref, ...), custom_call_target="tpu_custom_call" | custom-call | flops 100000000 | bytes 2097152 | tf_op jit(solution)/shard_map/images/pallas_call | solution.py:371
  26.6 1.4 %collective-permute-start.1 = (bf16[2,256,128]{2,1,0:T(8,128)(2,1)S(1)}, bf16[2,256,128]{2,1,0:T(8,128)(2,1)S(1)}, u32[]{:S(2)}, u32[]{:S(2)}) collective-permute-start(bf16[2,256,128]{2,1,0:T(8,128)(2,1)S(1)} %get-tuple-element.31), channel_id=1, source_target_pairs={{0,64},{64,128},{128,192},{192,0},{1,65},{65,129},{129,193},{193,1... | collective-permute-start | bytes 393224 | tf_op jit(solution)/shard_map/image_sum/ppermute | solution.py:321
  28.0 2.6 %collective-permute-start.2 = (bf16[2,256,128]{2,1,0:T(8,128)(2,1)S(1)}, bf16[2,256,128]{2,1,0:T(8,128)(2,1)S(1)}, u32[]{:S(2)}, u32[]{:S(2)}) collective-permute-start(bf16[2,256,128]{2,1,0:T(8,128)(2,1)S(1)} %get-tuple-element.32), channel_id=1, source_target_pairs={{0,128},{64,192},{128,0},{192,64},{1,129},{65,193},{129,1},{193,65... | collective-permute-start | bytes 393224 | tf_op jit(solution)/shard_map/image_sum/ppermute | solution.py:321
  30.6 1.1 %collective-permute-start.3 = (bf16[2,256,128]{2,1,0:T(8,128)(2,1)S(1)}, bf16[2,256,128]{2,1,0:T(8,128)(2,1)S(1)}, u32[]{:S(2)}, u32[]{:S(2)}) collective-permute-start(bf16[2,256,128]{2,1,0:T(8,128)(2,1)S(1)} %get-tuple-element.33), channel_id=1, source_target_pairs={{0,192},{64,0},{128,64},{192,128},{1,193},{65,1},{129,65},{193,129... | collective-permute-start | bytes 393224 | tf_op jit(solution)/shard_map/image_sum/ppermute | solution.py:321
  31.7 4.2 %collective-permute-start.5 = (bf16[16,2048]{1,0:T(8,128)(2,1)S(1)}, bf16[16,2048]{1,0:T(8,128)(2,1)S(1)}, u32[]{:S(2)}, u32[]{:S(2)}) collective-permute-start(bf16[16,2048]{1,0:T(8,128)(2,1)S(1)} %bitcast.6), channel_id=1, source_target_pairs={{0,32},{32,0},{1,33},{33,1},{2,34},{34,2},{3,35},{35,3},{4,36},{36... | collective-permute-start | bytes 196616 | tf_op jit(solution)/shard_map/visible_route/ppermute | solution.py:321
  35.9 0.0 collective-permute-done.1.refs_1_
  35.9 0.8 collective-permute-done.2.refs_2_
  36.7 0.0 collective-permute-done.3.refs_3_
  36.7 0.1 image_sums.1
  36.7 4.3 %collective-permute-start.4 = (f32[256,128]{1,0:T(8,128)S(1)}, f32[256,128]{1,0:T(8,128)S(1)}, u32[]{:S(2)}, u32[]{:S(2)}) collective-permute-start(f32[256,128]{1,0:T(8,128)S(1)} %get-tuple-element.36), channel_id=1, source_target_pairs={{0,32},{32,0},{1,33},{33,1},{2,34},{34,2},{3,35},{35,3},{4,36},{36... | collective-permute-start | bytes 393224 | tf_op jit(solution)/shard_map/image_sum/ppermute | solution.py:321
  41.1 0.0 collective-permute-done.5.other_ref
  41.1 0.6 route.1
  41.7 1.0 %collective-permute-start.6 = (bf16[16,2048]{1,0:T(8,128)(2,1)S(1)}, bf16[16,2048]{1,0:T(8,128)(2,1)S(1)}, u32[]{:S(2)}, u32[]{:S(2)}) collective-permute-start(bf16[16,2048]{1,0:T(8,128)(2,1)S(1)} %get-tuple-element.38), channel_id=1, source_target_pairs={{0,64},{64,128},{128,192},{192,0},{1,65},{65,129},{129,193},{193,1... | collective-permute-start | bytes 196616 | tf_op jit(solution)/shard_map/ppermute | solution.py:321
  42.7 2.2 %collective-permute-start.7 = (bf16[16,2048]{1,0:T(8,128)(2,1)S(1)}, bf16[16,2048]{1,0:T(8,128)(2,1)S(1)}, u32[]{:S(2)}, u32[]{:S(2)}) collective-permute-start(bf16[16,2048]{1,0:T(8,128)(2,1)S(1)} %get-tuple-element.39), channel_id=1, source_target_pairs={{0,128},{64,192},{128,0},{192,64},{1,129},{65,193},{129,1},{193,65... | collective-permute-start | bytes 196616 | tf_op jit(solution)/shard_map/ppermute | solution.py:321
  44.9 0.9 %collective-permute-start.8 = (bf16[16,2048]{1,0:T(8,128)(2,1)S(1)}, bf16[16,2048]{1,0:T(8,128)(2,1)S(1)}, u32[]{:S(2)}, u32[]{:S(2)}) collective-permute-start(bf16[16,2048]{1,0:T(8,128)(2,1)S(1)} %get-tuple-element.40), channel_id=1, source_target_pairs={{0,192},{64,0},{128,64},{192,128},{1,193},{65,1},{129,65},{193,129... | collective-permute-start | bytes 196616 | tf_op jit(solution)/shard_map/ppermute | solution.py:321
  45.8 3.5 %tables.1.table_ref = bf16[2,16,64,1024]{3,2,1,0:T(8,128)(2,1)S(1)} custom-call(s32[4]{0:T(128)S(1)} %compare_select_fusion.2.place_ref, f32[8,2,16]{2,1,0:T(2,128)S(1)} %copy-done.4, f32[1,1024]{1,0:T(1,128)S(1)} %bitcast.9), custom_call_target="tpu_custom_call" | custom-call | flops 1000000000 | bytes 8388608 | tf_op jit(solution)/shard_map/tables/pallas_call | solution.py:408
  49.4 0.0 collective-permute-done.6.came_1_ref
  49.4 0.0 collective-permute-done.7.came_2_ref
  49.4 0.0 collective-permute-done.8.came_3_ref
  49.4 0.0 collective-permute-done.4.far_ref
  49.4 4.2 %visibilities.1 = (f32[16,2048]{1,0:T(8,128)}, bf16[256,128]{1,0:T(8,128)(2,1)S(1)}) custom-call(s32[4]{0:T(128)S(1)} %compare_select_fusion.2.place_ref, s32[1,8]{1,0:T(1,128)S(1)} %copy-done.6, f32[256,128]{1,0:T(8,128)S(1)} %get-tuple-element.35.near_ref, f32[256,128]{1,0:T(8,128)S(1)} %collective-permute-done.4.far_ref, bf16[16,2048]{1,0:T(8,128)(2,1)S(1)} %bitcast.8, ...), custom_call_target="tpu_custom_call" | custom-call | flops 1000000000 | bytes 8388608 | tf_op jit(solution)/shard_map/visibilities/pallas_call | solution.py:423
  53.6 1.2 %collective-permute-start.9 = (bf16[256,128]{1,0:T(8,128)(2,1)S(1)}, bf16[256,128]{1,0:T(8,128)(2,1)S(1)}, u32[]{:S(2)}, u32[]{:S(2)}) collective-permute-start(bf16[256,128]{1,0:T(8,128)(2,1)S(1)} %get-tuple-element.43.refs_0_), channel_id=1, source_target_pairs={{0,32},{32,0},{1,33},{33,1},{2,34},{34,2},{3,35},{35,3},{4,36},{36... | collective-permute-start | bytes 196616 | tf_op jit(solution)/shard_map/grid_gather/ppermute | solution.py:321
  54.8 2.0 %collective-permute-start.14 = (bf16[256,128]{1,0:T(8,128)(2,1)S(1)}, bf16[256,128]{1,0:T(8,128)(2,1)S(1)}, u32[]{:S(2)}, u32[]{:S(2)}) collective-permute-start(bf16[256,128]{1,0:T(8,128)(2,1)S(1)} %get-tuple-element.43.refs_0_), channel_id=1, source_target_pairs={{0,192},{64,0},{128,64},{192,128},{1,193},{65,1},{129,65},{193,129... | collective-permute-start | bytes 196616 | tf_op jit(solution)/shard_map/grid_gather/ppermute | solution.py:321
  56.8 0.5 collective-permute-start.12
  57.3 0.1 collective-permute-start.10
  57.4 3.2 %collective-permute-done.9.refs_1_ = bf16[256,128]{1,0:T(8,128)(2,1)S(1)} collective-permute-done((bf16[256,128]{1,0:T(8,128)(2,1)S(1)}, bf16[256,128]{1,0:T(8,128)(2,1)S(1)}, u32[]{:S(2)}, u32[]{:S(2)}) %collective-permute-start.9) | collective-permute-done | bytes 65568 | tf_op jit(solution)/shard_map/grid_gather/ppermute | solution.py:321
  60.6 1.2 %collective-permute-start.15 = (bf16[256,128]{1,0:T(8,128)(2,1)S(1)}, bf16[256,128]{1,0:T(8,128)(2,1)S(1)}, u32[]{:S(2)}, u32[]{:S(2)}) collective-permute-start(bf16[256,128]{1,0:T(8,128)(2,1)S(1)} %collective-permute-done.9.refs_1_), channel_id=1, source_target_pairs={{0,192},{64,0},{128,64},{192,128},{1,193},{65,1},{129,65},{193,129... | collective-permute-start | bytes 196616 | tf_op jit(solution)/shard_map/grid_gather/ppermute | solution.py:321
  61.8 1.2 %collective-permute-start.13 = (bf16[256,128]{1,0:T(8,128)(2,1)S(1)}, bf16[256,128]{1,0:T(8,128)(2,1)S(1)}, u32[]{:S(2)}, u32[]{:S(2)}) collective-permute-start(bf16[256,128]{1,0:T(8,128)(2,1)S(1)} %collective-permute-done.9.refs_1_), channel_id=1, source_target_pairs={{0,128},{64,192},{128,0},{192,64},{1,129},{65,193},{129,1},{193,65... | collective-permute-start | bytes 196616 | tf_op jit(solution)/shard_map/grid_gather/ppermute | solution.py:321
  63.0 0.0 collective-permute-start.11
  63.0 0.0 collective-permute-done.12.refs_4_
  63.0 0.0 collective-permute-done.10.refs_2_
  63.0 1.3 %collective-permute-done.15.refs_7_ = bf16[256,128]{1,0:T(8,128)(2,1)S(1)} collective-permute-done((bf16[256,128]{1,0:T(8,128)(2,1)S(1)}, bf16[256,128]{1,0:T(8,128)(2,1)S(1)}, u32[]{:S(2)}, u32[]{:S(2)}) %collective-permute-start.15) | collective-permute-done | bytes 65568 | tf_op jit(solution)/shard_map/grid_gather/ppermute | solution.py:321
  64.3 2.7 %collective-permute-done.13.refs_5_ = bf16[256,128]{1,0:T(8,128)(2,1)S(1)} collective-permute-done((bf16[256,128]{1,0:T(8,128)(2,1)S(1)}, bf16[256,128]{1,0:T(8,128)(2,1)S(1)}, u32[]{:S(2)}, u32[]{:S(2)}) %collective-permute-start.13) | collective-permute-done | bytes 65568 | tf_op jit(solution)/shard_map/grid_gather/ppermute | solution.py:321
  67.0 0.7 collective-permute-done.11.refs_3_
  67.7 1.3 %regrid.1 = (f32[64,2048]{1,0:T(8,128)S(1)}, f32[64,2048]{1,0:T(8,128)S(1)}) custom-call(s32[4]{0:T(128)S(1)} %compare_select_fusion.2.place_ref, s32[8,16]{1,0:T(8,128)S(1)} %copy-done.3, f32[128,2048]{1,0:T(8,128)S(1)} %copy-done.1, bf16[256,128]{1,0:T(8,128)(2,1)S(1)} %get-tuple-element.43.refs_0_, bf16[256,128]{1,0:T(8,128)(2,1)S(1)} %collective-permute-done.9.refs_1_, ...), custom_call_target="tpu_custom_call" | custom-call | flops 100000000 | bytes 3145728 | tf_op jit(solution)/shard_map/regrid/pallas_call | solution.py:444
  69.0 5.8 %collective-permute-start.16 = (f32[64,2048]{1,0:T(8,128)S(1)}, f32[64,2048]{1,0:T(8,128)S(1)}, u32[]{:S(2)}, u32[]{:S(2)}) collective-permute-start(f32[64,2048]{1,0:T(8,128)S(1)} %get-tuple-element.45), channel_id=1, source_target_pairs={{0,1},{1,0},{2,3},{3,2},{4,5},{5,4},{6,7},{7,6},{8,9},{9,8},{10,11... | collective-permute-start | bytes 1572872 | tf_op jit(solution)/shard_map/dirty_scatter/ppermute | solution.py:321
  74.8 1.5 %collective-permute-done.16 = f32[64,2048]{1,0:T(8,128)S(1)} collective-permute-done((f32[64,2048]{1,0:T(8,128)S(1)}, f32[64,2048]{1,0:T(8,128)S(1)}, u32[]{:S(2)}, u32[]{:S(2)}) %collective-permute-start.16) | collective-permute-done | bytes 524320 | tf_op jit(solution)/shard_map/dirty_scatter/ppermute | solution.py:321
  76.4 0.1 add_convert_fusion
  76.4 0.1 reshape.11
  76.5 12.6 %all_to_all.10 = bf16[16,4,2048]{2,1,0:T(4,128)(2,1)S(1)} all-to-all(bf16[16,4,2048]{2,1,0:T(4,128)(2,1)S(1)} %reshape.11), channel_id=1, replica_groups=mesh['y'=4,'h'=2,'x'=4,'z'=4,'c'=2] {'x','z'}, dimensions={0} | all-to-all | bytes 524288 | tf_op jit(solution)/shard_map/dirty_scatter/all_to_all | solution.py:456
  89.1 0.7 convert_reduce_fusion
  (15 shorter events, 0.0 us)
Async XLA Ops:
  0.6 23.6 %copy-start.3 = (s32[8,16]{1,0:T(8,128)S(1)}, s32[8,16]{1,0:T(8,128)}, u32[]{:S(2)}) copy-start(s32[8,16]{1,0:T(8,128)} %subgrid_ref.3) | copy-start | bytes 1540
  0.6 31.1 %copy-start.2 = (bf16[1,16,2048]{2,1,0:T(8,128)(2,1)S(1)}, bf16[1,16,2048]{2,1,0:T(8,128)(2,1)}, u32[]{:S(2)}) copy-start(bf16[1,16,2048]{2,1,0:T(8,128)(2,1)} %param.10) | copy-start | bytes 196612
  0.7 40.4 %copy-start.6 = (s32[1,8]{1,0:T(1,128)S(1)}, s32[1,8]{1,0:T(1,128)}, u32[]{:S(2)}) copy-start(s32[1,8]{1,0:T(1,128)} %reader_ref.3) | copy-start | bytes 100
  0.7 45.2 %copy-start.5 = (f32[1024]{0:T(1024)S(1)}, f32[1024]{0:T(1024)}, u32[]{:S(2)}) copy-start(f32[1024]{0:T(1024)} %param.19) | copy-start | bytes 12292
  0.7 45.2 %copy-start.4 = (f32[8,2,16]{2,1,0:T(2,128)S(1)}, f32[8,2,16]{2,1,0:T(2,128)}, u32[]{:S(2)}) copy-start(f32[8,2,16]{2,1,0:T(2,128)} %coords_ref.1) | copy-start | bytes 3076
  2.2 18.7 %all-to-all-start = ((bf16[16,4,2048]{2,1,0:T(4,128)(2,1)}), bf16[16,4,2048]{2,1,0:T(4,128)(2,1)S(1)}, u32[]{:S(2)}, u32[]{:S(2)}) async-start(bf16[16,4,2048]{2,1,0:T(4,128)(2,1)} %broadcast_in_dim.33), calls=%async_computation | async-start | bytes 524288 | tf_op jit(solution)/shard_map/model_gather/all_to_all | solution.py:354
  21.0 3.3 %collective-permute-start = (bf16[16,4,2048]{2,1,0:T(4,128)(2,1)S(1)}, bf16[16,4,2048]{2,1,0:T(4,128)(2,1)S(1)}, u32[]{:S(2)}, u32[]{:S(2)}) collective-permute-start(bf16[16,4,2048]{2,1,0:T(4,128)(2,1)S(1)} %all-to-all-done.near_ref), channel_id=1, source_target_pairs={{0,1},{1,0},{2,3},{3,2},{4,5},{5,4},{6,7},{7,6},{8,9},{9,8},{10,11... | collective-permute-start | bytes 786440 | tf_op jit(solution)/shard_map/ppermute | solution.py:321
  24.3 1.2 %copy-start = (f32[128,2048]{1,0:T(8,128)S(1)}, f32[128,2048]{1,0:T(8,128)}, u32[]{:S(2)}) copy-start(f32[128,2048]{1,0:T(8,128)} %screens.1.screen_ref) | copy-start | bytes 3145732
  26.6 9.3 %collective-permute-start.1 = (bf16[2,256,128]{2,1,0:T(8,128)(2,1)S(1)}, bf16[2,256,128]{2,1,0:T(8,128)(2,1)S(1)}, u32[]{:S(2)}, u32[]{:S(2)}) collective-permute-start(bf16[2,256,128]{2,1,0:T(8,128)(2,1)S(1)} %get-tuple-element.31), channel_id=1, source_target_pairs={{0,64},{64,128},{128,192},{192,0},{1,65},{65,129},{129,193},{193,1... | collective-permute-start | bytes 393224 | tf_op jit(solution)/shard_map/image_sum/ppermute | solution.py:321
  28.0 8.7 %collective-permute-start.2 = (bf16[2,256,128]{2,1,0:T(8,128)(2,1)S(1)}, bf16[2,256,128]{2,1,0:T(8,128)(2,1)S(1)}, u32[]{:S(2)}, u32[]{:S(2)}) collective-permute-start(bf16[2,256,128]{2,1,0:T(8,128)(2,1)S(1)} %get-tuple-element.32), channel_id=1, source_target_pairs={{0,128},{64,192},{128,0},{192,64},{1,129},{65,193},{129,1},{193,65... | collective-permute-start | bytes 393224 | tf_op jit(solution)/shard_map/image_sum/ppermute | solution.py:321
  30.6 6.1 %collective-permute-start.3 = (bf16[2,256,128]{2,1,0:T(8,128)(2,1)S(1)}, bf16[2,256,128]{2,1,0:T(8,128)(2,1)S(1)}, u32[]{:S(2)}, u32[]{:S(2)}) collective-permute-start(bf16[2,256,128]{2,1,0:T(8,128)(2,1)S(1)} %get-tuple-element.33), channel_id=1, source_target_pairs={{0,192},{64,0},{128,64},{192,128},{1,193},{65,1},{129,65},{193,129... | collective-permute-start | bytes 393224 | tf_op jit(solution)/shard_map/image_sum/ppermute | solution.py:321
  31.7 9.4 %collective-permute-start.5 = (bf16[16,2048]{1,0:T(8,128)(2,1)S(1)}, bf16[16,2048]{1,0:T(8,128)(2,1)S(1)}, u32[]{:S(2)}, u32[]{:S(2)}) collective-permute-start(bf16[16,2048]{1,0:T(8,128)(2,1)S(1)} %bitcast.6), channel_id=1, source_target_pairs={{0,32},{32,0},{1,33},{33,1},{2,34},{34,2},{3,35},{35,3},{4,36},{36... | collective-permute-start | bytes 196616 | tf_op jit(solution)/shard_map/visible_route/ppermute | solution.py:321
  36.7 12.7 %collective-permute-start.4 = (f32[256,128]{1,0:T(8,128)S(1)}, f32[256,128]{1,0:T(8,128)S(1)}, u32[]{:S(2)}, u32[]{:S(2)}) collective-permute-start(f32[256,128]{1,0:T(8,128)S(1)} %get-tuple-element.36), channel_id=1, source_target_pairs={{0,32},{32,0},{1,33},{33,1},{2,34},{34,2},{3,35},{35,3},{4,36},{36... | collective-permute-start | bytes 393224 | tf_op jit(solution)/shard_map/image_sum/ppermute | solution.py:321
  41.7 7.7 %collective-permute-start.6 = (bf16[16,2048]{1,0:T(8,128)(2,1)S(1)}, bf16[16,2048]{1,0:T(8,128)(2,1)S(1)}, u32[]{:S(2)}, u32[]{:S(2)}) collective-permute-start(bf16[16,2048]{1,0:T(8,128)(2,1)S(1)} %get-tuple-element.38), channel_id=1, source_target_pairs={{0,64},{64,128},{128,192},{192,0},{1,65},{65,129},{129,193},{193,1... | collective-permute-start | bytes 196616 | tf_op jit(solution)/shard_map/ppermute | solution.py:321
  42.7 6.7 %collective-permute-start.7 = (bf16[16,2048]{1,0:T(8,128)(2,1)S(1)}, bf16[16,2048]{1,0:T(8,128)(2,1)S(1)}, u32[]{:S(2)}, u32[]{:S(2)}) collective-permute-start(bf16[16,2048]{1,0:T(8,128)(2,1)S(1)} %get-tuple-element.39), channel_id=1, source_target_pairs={{0,128},{64,192},{128,0},{192,64},{1,129},{65,193},{129,1},{193,65... | collective-permute-start | bytes 196616 | tf_op jit(solution)/shard_map/ppermute | solution.py:321
  44.9 4.5 %collective-permute-start.8 = (bf16[16,2048]{1,0:T(8,128)(2,1)S(1)}, bf16[16,2048]{1,0:T(8,128)(2,1)S(1)}, u32[]{:S(2)}, u32[]{:S(2)}) collective-permute-start(bf16[16,2048]{1,0:T(8,128)(2,1)S(1)} %get-tuple-element.40), channel_id=1, source_target_pairs={{0,192},{64,0},{128,64},{192,128},{1,193},{65,1},{129,65},{193,129... | collective-permute-start | bytes 196616 | tf_op jit(solution)/shard_map/ppermute | solution.py:321
  45.8 21.9 %copy-start.1 = (f32[128,2048]{1,0:T(8,128)S(1)}, f32[128,2048]{1,0:T(8,128)}, u32[]{:S(2)}) copy-start(f32[128,2048]{1,0:T(8,128)} %screens.1.screen_ref) | copy-start | bytes 3145732
  53.6 7.0 %collective-permute-start.9 = (bf16[256,128]{1,0:T(8,128)(2,1)S(1)}, bf16[256,128]{1,0:T(8,128)(2,1)S(1)}, u32[]{:S(2)}, u32[]{:S(2)}) collective-permute-start(bf16[256,128]{1,0:T(8,128)(2,1)S(1)} %get-tuple-element.43.refs_0_), channel_id=1, source_target_pairs={{0,32},{32,0},{1,33},{33,1},{2,34},{34,2},{3,35},{35,3},{4,36},{36... | collective-permute-start | bytes 196616 | tf_op jit(solution)/shard_map/grid_gather/ppermute | solution.py:321
  54.8 8.2 %collective-permute-start.14 = (bf16[256,128]{1,0:T(8,128)(2,1)S(1)}, bf16[256,128]{1,0:T(8,128)(2,1)S(1)}, u32[]{:S(2)}, u32[]{:S(2)}) collective-permute-start(bf16[256,128]{1,0:T(8,128)(2,1)S(1)} %get-tuple-element.43.refs_0_), channel_id=1, source_target_pairs={{0,192},{64,0},{128,64},{192,128},{1,193},{65,1},{129,65},{193,129... | collective-permute-start | bytes 196616 | tf_op jit(solution)/shard_map/grid_gather/ppermute | solution.py:321
  56.8 6.3 %collective-permute-start.12 = (bf16[256,128]{1,0:T(8,128)(2,1)S(1)}, bf16[256,128]{1,0:T(8,128)(2,1)S(1)}, u32[]{:S(2)}, u32[]{:S(2)}) collective-permute-start(bf16[256,128]{1,0:T(8,128)(2,1)S(1)} %get-tuple-element.43.refs_0_), channel_id=1, source_target_pairs={{0,128},{64,192},{128,0},{192,64},{1,129},{65,193},{129,1},{193,65... | collective-permute-start | bytes 196616 | tf_op jit(solution)/shard_map/grid_gather/ppermute | solution.py:321
  57.3 5.8 %collective-permute-start.10 = (bf16[256,128]{1,0:T(8,128)(2,1)S(1)}, bf16[256,128]{1,0:T(8,128)(2,1)S(1)}, u32[]{:S(2)}, u32[]{:S(2)}) collective-permute-start(bf16[256,128]{1,0:T(8,128)(2,1)S(1)} %get-tuple-element.43.refs_0_), channel_id=1, source_target_pairs={{0,64},{64,128},{128,192},{192,0},{1,65},{65,129},{129,193},{193,1... | collective-permute-start | bytes 196616 | tf_op jit(solution)/shard_map/grid_gather/ppermute | solution.py:321
  60.6 3.7 %collective-permute-start.15 = (bf16[256,128]{1,0:T(8,128)(2,1)S(1)}, bf16[256,128]{1,0:T(8,128)(2,1)S(1)}, u32[]{:S(2)}, u32[]{:S(2)}) collective-permute-start(bf16[256,128]{1,0:T(8,128)(2,1)S(1)} %collective-permute-done.9.refs_1_), channel_id=1, source_target_pairs={{0,192},{64,0},{128,64},{192,128},{1,193},{65,1},{129,65},{193,129... | collective-permute-start | bytes 196616 | tf_op jit(solution)/shard_map/grid_gather/ppermute | solution.py:321
  61.8 5.2 %collective-permute-start.13 = (bf16[256,128]{1,0:T(8,128)(2,1)S(1)}, bf16[256,128]{1,0:T(8,128)(2,1)S(1)}, u32[]{:S(2)}, u32[]{:S(2)}) collective-permute-start(bf16[256,128]{1,0:T(8,128)(2,1)S(1)} %collective-permute-done.9.refs_1_), channel_id=1, source_target_pairs={{0,128},{64,192},{128,0},{192,64},{1,129},{65,193},{129,1},{193,65... | collective-permute-start | bytes 196616 | tf_op jit(solution)/shard_map/grid_gather/ppermute | solution.py:321
  63.0 4.7 %collective-permute-start.11 = (bf16[256,128]{1,0:T(8,128)(2,1)S(1)}, bf16[256,128]{1,0:T(8,128)(2,1)S(1)}, u32[]{:S(2)}, u32[]{:S(2)}) collective-permute-start(bf16[256,128]{1,0:T(8,128)(2,1)S(1)} %collective-permute-done.9.refs_1_), channel_id=1, source_target_pairs={{0,64},{64,128},{128,192},{192,0},{1,65},{65,129},{129,193},{193,1... | collective-permute-start | bytes 196616 | tf_op jit(solution)/shard_map/grid_gather/ppermute | solution.py:321
  69.0 7.4 %collective-permute-start.16 = (f32[64,2048]{1,0:T(8,128)S(1)}, f32[64,2048]{1,0:T(8,128)S(1)}, u32[]{:S(2)}, u32[]{:S(2)}) collective-permute-start(f32[64,2048]{1,0:T(8,128)S(1)} %get-tuple-element.45), channel_id=1, source_target_pairs={{0,1},{1,0},{2,3},{3,2},{4,5},{5,4},{6,7},{7,6},{8,9},{9,8},{10,11... | collective-permute-start | bytes 1572872 | tf_op jit(solution)/shard_map/dirty_scatter/ppermute | solution.py:321

commit v5 on v4

--- a/solution.py
+++ b/solution.py
@@ -53,11 +53,11 @@
     return (held * (128 // cores)) + lax.div(subgrid, owned * cores) * owned + lax.rem(subgrid, owned)
 
 
-def table_kernel(place_ref, coords_ref, freq_ref, table_ref, powers, groups):
+def table_kernel(n_h, kind, coords_ref, freq_ref, table_ref, powers, groups):
     rows = coords_ref.shape[2]
-    coords = coords_ref[place_ref[0]]
-    row = jnp.concatenate([coords[0:1], coords[1:2], jnp.zeros((1, 128 - 2 * rows), F32)], axis=1)
-    column = (TWO_PI * down(row)[: 2 * rows]) * (1.0 / 32.0)
+    coords = coords_ref[lax.axis_index("y") * n_h + lax.axis_index("h")]
+    row = jnp.concatenate([coords[kind : kind + 1], jnp.zeros((1, 128 - rows), F32)], axis=1)
+    column = (TWO_PI * down(row)[:rows]) * (1.0 / 32.0)
     angle = jnp.concatenate([column] * (freq_ref.shape[1] // 128), axis=1) * freq_ref[...]
     z1 = (jnp.cos(angle), jnp.sin(angle))
     z2 = cmul(z1, z1)
@@ -87,14 +87,12 @@
         return jnp.concatenate([part[0] for part in parts] + [part[1] for part in parts], axis=0).astype(BF16)
 
     def body(b):
-        base = bits([row_of(powers, at, b) for at in (2, 3, 4)])
-        table_ref[0, b] = stacked([cmul(base, row_of(groups, at, b)) for at in range(4)])
-        row = b + rows
-        base = bits([row_of(powers, at, row) for at in (0, 1, 2)])
-        up8 = row_of(powers, 3, row)
-        table_ref[1, b] = stacked(
-            [cmul(base, row_of(groups, 0, row)), cmul(base, conj(up8)), base, cmul(base, up8)]
-        )
+        base = bits([row_of(powers, at, b) for at in ((2, 3, 4), (0, 1, 2))[kind]])
+        if kind == 0:
+            table_ref[b] = stacked([cmul(base, row_of(groups, at, b)) for at in range(4)])
+        else:
+            up8 = row_of(powers, 3, b)
+            table_ref[b] = stacked([cmul(base, row_of(groups, 0, b)), cmul(base, conj(up8)), base, cmul(base, up8)])
 
     for b in range(rows):
         body(b)
@@ -130,9 +128,10 @@
         screen_ref[:, im] = pair_re * wave_im + pair_im * wave_re
 
 
-def blocks_from(place_ref, n_y, n_h, sign):
+def blocks_from(n_y, n_h, sign):
+    at_y, at_h = (lax.axis_index("y"), lax.axis_index("h"))
     return [
-        lax.rem(place_ref[1] + (n_y + sign * by) % n_y, n_y) * n_h + lax.rem(place_ref[2] + flip, n_h)
+        lax.rem(at_y + (n_y + sign * by) % n_y, n_y) * n_h + lax.rem(at_h + flip, n_h)
         for by in range(n_y)
         for flip in range(n_h)
     ]
@@ -142,12 +141,12 @@
     return jnp.concatenate([ref[pl.ds(pl.multiple_of(block * 16, 16), 16), cells] for block in blocks], axis=0)
 
 
-def image_kernel(n_y, n_h, cores, owned, place_ref, subgrid_ref, near_ref, far_ref, screen_ref, *image_refs):
+def image_kernel(n_y, n_h, cores, owned, subgrid_ref, near_ref, far_ref, screen_ref, *image_refs):
     half = near_ref.shape[0] * near_ref.shape[1]
     pixels = screen_ref.shape[1] // 2
-    blocks = blocks_from(place_ref, n_y, n_h, 1)
+    blocks = blocks_from(n_y, n_h, 1)
     subgrids = jnp.concatenate([subgrid_ref[pl.ds(block, 1), :] for block in blocks], axis=1)
-    slots = down(slot_of(subgrids, place_ref[3], cores, owned))
+    slots = down(slot_of(subgrids, lax.axis_index("c"), cores, owned))
     near, far = (onehot(slots, 0, half), onehot(slots, half, half))
     tiles = pixels // 128
     width = 256
@@ -179,12 +178,18 @@
         sum_ref[...] = total
 
 
-def route_kernel(n_y, n_h, place_ref, reader_ref, rows_ref, other_ref, *out_refs):
+def route_kernel(n_y, n_h, reader_ref, rows_ref, other_ref, pick_ref, *out_refs):
+    at_y, at_h = (lax.axis_index("y"), lax.axis_index("h"))
+    own = at_y * n_h + at_h
+    source = reader_ref[0, own]
+    steps = lax.rem(at_y + n_y - lax.div(source, n_h), n_y)
+    here = jnp.where(lax.rem(source, n_h) == at_h, 0, 1)
+    pick_ref[...] = jnp.full(pick_ref.shape, jnp.where(steps == 0, here, steps + 1), jnp.int32)
     block = jnp.int32(0)
     for at in range(n_y * n_h):
-        block = jnp.where(reader_ref[0, at] == place_ref[0], at, block)
+        block = jnp.where(reader_ref[0, at] == own, at, block)
     for by, out_ref in enumerate(out_refs, 1):
-        to = lax.rem(place_ref[1] + by, n_y) * n_h + place_ref[2]
+        to = lax.rem(at_y + by, n_y) * n_h + at_h
 
         @pl.when(block == to)
         def _():
@@ -196,10 +201,7 @@
 
 
 def visibility_kernel(
-    n_y,
-    n_h,
-    place_ref,
-    reader_ref,
+    pick_ref,
     near_ref,
     far_ref,
     rows_ref,
@@ -207,7 +209,8 @@
     came_1_ref,
     came_2_ref,
     came_3_ref,
-    table_ref,
+    east_ref,
+    north_ref,
     resid_ref,
     grid_ref,
     cells_ref,
@@ -215,16 +218,13 @@
 ):
     rows, channels = (resid_ref.shape[0], resid_ref.shape[1] // 2)
     cells_ref[...] = near_ref[...] + far_ref[...]
-    source = reader_ref[0, place_ref[0]]
-    steps = lax.rem(place_ref[1] + n_y - lax.div(source, n_h), n_y)
-    here = jnp.where(lax.rem(source, n_h) == place_ref[2], 0, 1)
-    pick = jnp.where(steps == 0, here, steps + 1)
-    for at, ref in enumerate((rows_ref, other_ref, came_1_ref, came_2_ref, came_3_ref)):
-
-        @pl.when(pick == at)
-        def _():
-            resid_ref[...] = ref[...].astype(F32)
-
+    found = (rows_ref, other_ref, came_1_ref, came_2_ref, came_3_ref)
+    for at in range(0, 2 * channels, 128):
+        chans = pl.ds(at, 128)
+        visible = found[0][:, chans].astype(F32)
+        for which, ref in enumerate(found[1:], 1):
+            visible = jnp.where(pick_ref[...] == which, ref[:, chans].astype(F32), visible)
+        resid_ref[:, chans] = visible
     width = 256
 
     def degrid(b):
@@ -245,10 +245,10 @@
         operand = jnp.concatenate([high, low], axis=1)
         for at in range(0, channels, width):
             chans = pl.ds(at, width)
-            north = table_ref[1, b, :, chans]
+            north = north_ref[b, :, chans]
             inner = jnp.dot(operand, jnp.concatenate([north, north], axis=0), preferred_element_type=F32)
             inner_re, inner_im = (inner[:32], inner[32:])
-            east = table_ref[0, b, :, chans].astype(F32)
+            east = east_ref[b, :, chans].astype(F32)
             cos, sin = (east[:32], east[32:])
             vis_re = jnp.sum(cos * inner_re - sin * inner_im, axis=0, keepdims=True)
             vis_im = jnp.sum(cos * inner_im + sin * inner_re, axis=0, keepdims=True)
@@ -262,12 +262,12 @@
         for at in range(0, channels, width):
             chans, late = (pl.ds(at, width), pl.ds(channels + at, width))
             resid_re, resid_im = (resid_ref[pl.ds(b, 1), chans], resid_ref[pl.ds(b, 1), late])
-            east = table_ref[0, b, :, chans].astype(F32)
+            east = east_ref[b, :, chans].astype(F32)
             cos, sin = (east[:32], east[32:])
             weighted = jnp.concatenate([cos * resid_re + sin * resid_im, cos * resid_im - sin * resid_re], axis=0)
             products = products + lax.dot_general(
                 weighted.astype(BF16),
-                table_ref[1, b, :, chans],
+                north_ref[b, :, chans],
                 (((1,), (1,)), ((), ())),
                 preferred_element_type=F32,
             )
@@ -283,10 +283,10 @@
     grid_ref[...] = out_ref[...].astype(BF16)
 
 
-def regrid_kernel(scale, n_y, n_h, cores, owned, place_ref, subgrid_ref, screen_ref, *refs):
-    grids, (near_ref, far_ref) = (refs[:-2], refs[-2:])
-    blocks = blocks_from(place_ref, n_y, n_h, -1)
-    half = near_ref.shape[0]
+def regrid_kernel(scale, n_y, n_h, cores, owned, other, subgrid_ref, screen_ref, *refs):
+    grids, sum_ref = (refs[:-1], refs[-1])
+    blocks = blocks_from(n_y, n_h, -1)
+    half = sum_ref.shape[0]
     pixels = screen_ref.shape[1] // 2
     tiles = pixels // 128
     count = screen_ref.shape[0]
@@ -294,26 +294,23 @@
     def grid_of(q):
         return jnp.concatenate([ref[16 * q : 16 * q + 16, :] for ref in grids], axis=0).astype(F32)
 
-    subs = lax.broadcasted_iota(jnp.int32, (2 * half, count), 0)
+    subs = lax.broadcasted_iota(jnp.int32, (half, count), 0) + other * half
     target = jnp.concatenate([subgrid_ref[pl.ds(block, 1), :] for block in blocks], axis=1)
-    target = slot_of(target, place_ref[3], cores, owned)
+    target = slot_of(target, lax.axis_index("c"), cores, owned)
     sums = jnp.where(target == subs, 1.0, 0.0).astype(BF16)
-    near, far = (sums[:half], sums[half:])
+    sums = jnp.concatenate([sums, sums], axis=1)
     for q in range(tiles):
         re, im = pl.ds(128 * q, 128), pl.ds(pixels + 128 * q, 128)
         grid_re, grid_im = (grid_of(q), grid_of(q + tiles))
         screen_re, screen_im = (rows_of_blocks(screen_ref, blocks, re), rows_of_blocks(screen_ref, blocks, im))
         out_re = (screen_re * grid_re + screen_im * grid_im) * scale
         out_im = (screen_re * grid_im - screen_im * grid_re) * scale
-        for cells, value in ((re, out_re), (im, out_im)):
-            high = value.astype(BF16)
-            low = (value - high.astype(F32)).astype(BF16)
-            near_ref[:, cells] = jnp.dot(near, high, preferred_element_type=F32) + jnp.dot(
-                near, low, preferred_element_type=F32
-            )
-            far_ref[:, cells] = jnp.dot(far, high, preferred_element_type=F32) + jnp.dot(
-                far, low, preferred_element_type=F32
-            )
+        value = jnp.concatenate([out_re, out_im], axis=1)
+        high = value.astype(BF16)
+        low = (value - high.astype(F32)).astype(BF16)
+        both = jnp.dot(sums, jnp.concatenate([high, low], axis=0), preferred_element_type=F32)
+        sum_ref[:, re] = both[:, :128]
+        sum_ref[:, im] = both[:, 128:]
 
 
 def shift(value, axis, by):
@@ -334,7 +331,6 @@
     channel_freq,
 ):
     n_y, n_h, n_x, n_z, n_c = (lax.axis_size(axis) for axis in FACET + TILE)
-    at_y, at_h, at_x, at_z, at_c = (lax.axis_index(axis) for axis in FACET + TILE)
     n_facet = n_y * n_h
     channels = channel_freq.shape[0]
     pixels = plane_phase.shape[1]
@@ -344,11 +340,6 @@
     subgrid_count = owned * n_x * n_z * n_c
     cell_rows = 2 * pixels // 128 * row_block
     grid_scale = 1.0 / math.sqrt(channels * n_facet * (row_block * n_x * n_z * n_c) / subgrid_count)
-    ids = jnp.arange(4, dtype=jnp.int32)
-    place = jnp.where(
-        ids == 0, at_y * n_h + at_h, jnp.where(ids == 1, at_y, jnp.where(ids == 2, at_h, at_c))
-    ).astype(jnp.int32)
-
     with jax.named_scope("model_gather"):
         copies = jnp.broadcast_to(model_grid, (n_x * n_z, owned, 2 * pixels))
         near = lax.all_to_all(copies, ("x", "z"), split_axis=0, concat_axis=0, tiled=True)
@@ -361,7 +352,7 @@
         out_specs=VMEM,
         scratch_shapes=[pltpu.VMEM(value.shape, value.dtype) for value in operands]
         + [pltpu.SemaphoreType.DMA((len(operands),))],
-        compiler_params=params(58),
+        compiler_params=params(44),
         cost_estimate=pl.CostEstimate(flops=10**9, bytes_accessed=4 << 20, transcendentals=1 << 16),
         name="screens",
     )(*operands)
@@ -371,27 +362,45 @@
     images = pl.pallas_call(
         functools.partial(image_kernel, n_y, n_h, n_c, owned),
         out_shape=[jax.ShapeDtypeStruct((n_h, cell_rows, 128), BF16)] * n_y,
-        in_specs=[SMEM] + [VMEM] * 4,
+        in_specs=[VMEM] * 4,
         out_specs=[VMEM] * n_y,
         compiler_params=params(8),
         cost_estimate=pl.CostEstimate(flops=10**8, bytes_accessed=2 << 20, transcendentals=0),
         name="images",
-    )(place, subgrid_index, near, far, screen)
-    rows, *images = lax.optimization_barrier((sectioned_rows[0], *images))
+    )(subgrid_index, near, far, screen)
+    rows, soon, *images = lax.optimization_barrier((sectioned_rows[0], baseline_coords, *images))
 
     with jax.named_scope("visible_route"):
         other = shift(rows, "h", 1)
-        sent = pl.pallas_call(
+        pick, *sent = pl.pallas_call(
             functools.partial(route_kernel, n_y, n_h),
-            out_shape=[jax.ShapeDtypeStruct(rows.shape, BF16)] * (n_y - 1),
-            in_specs=[SMEM, SMEM, VMEM, VMEM],
-            out_specs=[VMEM] * (n_y - 1),
+            out_shape=[jax.ShapeDtypeStruct((row_block, 128), jnp.int32)]
+            + [jax.ShapeDtypeStruct(rows.shape, BF16)] * (n_y - 1),
+            in_specs=[SMEM, VMEM, VMEM],
+            out_specs=[VMEM] * n_y,
             compiler_params=params(4),
             cost_estimate=pl.CostEstimate(flops=10**6, bytes_accessed=1 << 18, transcendentals=0),
             name="route",
-        )(place, reader, rows, other)
+        )(reader, rows, other)
+
+    def table(kind, coords):
+        return pl.pallas_call(
+            functools.partial(table_kernel, n_h, kind),
+            out_shape=jax.ShapeDtypeStruct((row_block, 64, channels), BF16),
+            in_specs=[VMEM] * 2,
+            out_specs=VMEM,
+            scratch_shapes=[
+                pltpu.VMEM((10, row_block, channels), F32),
+                pltpu.VMEM((8, row_block, channels), F32),
+            ],
+            compiler_params=params(16),
+            cost_estimate=pl.CostEstimate(flops=10**9, bytes_accessed=4 << 20, transcendentals=1 << 16),
+            name=("east", "north")[kind],
+        )(coords, channel_freq.reshape(1, channels))
 
     with jax.named_scope("image_sum"):
+        north = table(1, soon)
+        images[0], north = lax.optimization_barrier((images[0], north))
         pieces = [images[0]] + [shift(images[by], "y", by) for by in range(1, n_y)]
         own_sum, other_sum = pl.pallas_call(
             sum_kernel,
@@ -402,37 +411,25 @@
             cost_estimate=pl.CostEstimate(flops=10**6, bytes_accessed=1 << 20, transcendentals=0),
             name="image_sums",
         )(*pieces)
-        later, own_sum = lax.optimization_barrier((place, own_sum))
+        later, own_sum = lax.optimization_barrier((baseline_coords, own_sum))
         beside_sum = shift(other_sum, "h", 1)
 
-    tables = pl.pallas_call(
-        table_kernel,
-        out_shape=jax.ShapeDtypeStruct((2, row_block, 64, channels), BF16),
-        in_specs=[SMEM, VMEM, VMEM],
-        out_specs=VMEM,
-        scratch_shapes=[
-            pltpu.VMEM((10, 2 * row_block, channels), F32),
-            pltpu.VMEM((8, 2 * row_block, channels), F32),
-        ],
-        compiler_params=params(16),
-        cost_estimate=pl.CostEstimate(flops=10**9, bytes_accessed=8 << 20, transcendentals=1 << 17),
-        name="tables",
-    )(later, baseline_coords, channel_freq.reshape(1, channels))
+    east = table(0, later)
     came = [shift(value, "y", by) for by, value in enumerate(sent, 1)]
 
     residual, gridded = pl.pallas_call(
-        functools.partial(visibility_kernel, n_y, n_h),
+        visibility_kernel,
         out_shape=[
             jax.ShapeDtypeStruct((row_block, 2 * channels), F32),
             jax.ShapeDtypeStruct((cell_rows, 128), BF16),
         ],
-        in_specs=[SMEM] * 2 + [VMEM] * 8,
+        in_specs=[VMEM] * 10,
         out_specs=[VMEM] * 2,
         scratch_shapes=[pltpu.VMEM((cell_rows, 128), F32), pltpu.VMEM((cell_rows, 128), F32)],
         compiler_params=params(16),
         cost_estimate=pl.CostEstimate(flops=10**9, bytes_accessed=8 << 20, transcendentals=0),
         name="visibilities",
-    )(place, reader, own_sum, beside_sum, rows, other, *came, tables)
+    )(pick, own_sum, beside_sum, rows, other, *came, east, north)
 
     with jax.named_scope("grid_gather"):
         beside = shift(gridded, "h", 1)
@@ -441,15 +438,21 @@
             grids += [shift(gridded, "y", by), shift(beside, "y", by)]
 
     half = subgrid_count // n_c
-    near_sum, far_sum = pl.pallas_call(
-        functools.partial(regrid_kernel, grid_scale, n_y, n_h, n_c, owned),
-        out_shape=[jax.ShapeDtypeStruct((half, 2 * pixels), F32)] * 2,
-        in_specs=[SMEM] + [VMEM] * (2 + n_facet),
-        out_specs=[VMEM] * 2,
-        compiler_params=params(8),
-        cost_estimate=pl.CostEstimate(flops=10**8, bytes_accessed=3 << 20, transcendentals=0),
-        name="regrid",
-    )(place, subgrid_index, screen, *grids)
+
+    def regrid(other, subgrids):
+        return pl.pallas_call(
+            functools.partial(regrid_kernel, grid_scale, n_y, n_h, n_c, owned, other),
+            out_shape=jax.ShapeDtypeStruct((half, 2 * pixels), F32),
+            in_specs=[VMEM] * (2 + n_facet),
+            out_specs=VMEM,
+            compiler_params=params(8),
+            cost_estimate=pl.CostEstimate(flops=10**8, bytes_accessed=3 << 20, transcendentals=0),
+            name=("regrid_near", "regrid_far")[other],
+        )(subgrids, screen, *grids)
+
+    far_sum = regrid(1, subgrid_index)
+    subgrids, far_sum = lax.optimization_barrier((subgrid_index, far_sum))
+    near_sum = regrid(0, subgrids)
 
     with jax.named_scope("dirty_scatter"):
         chip_sum = (near_sum + shift(far_sum, "c", 1)).astype(BF16).reshape(n_x * n_z, owned, 2 * pixels)

time: 90.3 us -> 86.8 us (0.961)
  Pallas kernels: 15.5 us -> 11 us
  waiting for transfers between devices: 16.3 us -> 13.7 us
  local copies, waits for them, and re-layouts: 2.92 us -> 5.52 us
  starting transfers between devices: 40.9 us -> 42 us
    unnamed x14 -> x18, local copies, waits for them, and re-layouts: 1.25 us -> 3.89 us
    pallas_call x1, Pallas kernels: 4.73 us -> 2.35 us  [local(): pl.pallas_call(screen_kernel, out_shape=jax.ShapeDtypeStruct((count, 2 *...]
    pallas_call x3 -> x5, Pallas kernels: 9.03 us -> 7.38 us  [the longest x1 3.48 us: local(): pl.pallas_call(visibility_kernel, out_shape=[jax.ShapeDtypeStruct((row_bl...]
    all_to_all x1, waiting for transfers between devices: 4.95 us -> 3.45 us  [local(): lax.all_to_all(copies, ('x', 'z'), split_axis=0, concat_axis=0, tiled=True)]
    ppermute x17, waiting for transfers between devices: 11.4 us -> 10.3 us  [shift(): lax.ppermute(value, axis, [(i, (i + by) % size) for i in range(size)])]
    ppermute x17, starting transfers between devices: 31.9 us -> 32.8 us  [shift(): lax.ppermute(value, axis, [(i, (i + by) % size) for i in range(size)])]
  transfers between devices with their start and end apart: 18 -> 18, of which waited for: 8 -> 9; matrix products, arithmetic and copies ran while one was open for 0% -> 0% of each run, Pallas kernels for 10% -> 7%
where the time goes in v5:
time: 86.8 us; the launch traced here: 86.3 us
  starting transfers between devices  42 us (48%)
  waiting for transfers between devices  13.7 us (16%)
  blocking collectives  12.6 us (15%)
  Pallas kernels  11 us (13%)
  local copies, waits for them, and re-layouts  5.52 us (6%)
    ppermute x17, starting transfers between devices, shift(): lax.ppermute(value, axis, [(i, (i + by) % size) for i in range(size)])  32.8 us
    all_to_all x1, blocking collectives, local(): lax.all_to_all(chip_sum, ('x', 'z'), split_axis=0, concat_axis=0, tiled=T...  12.6 us
    ppermute x17, waiting for transfers between devices, shift(): lax.ppermute(value, axis, [(i, (i + by) % size) for i in range(size)])  10.3 us
    all_to_all x1, starting transfers between devices, local(): lax.all_to_all(copies, ('x', 'z'), split_axis=0, concat_axis=0, tiled=True)  9.15 us
    unnamed x18, local copies, waits for them, and re-layouts  3.89 us
    pallas_call x1, Pallas kernels, local(): pl.pallas_call(visibility_kernel, out_shape=[jax.ShapeDtypeStruct((row_bl...  3.48 us
    all_to_all x1, waiting for transfers between devices, local(): lax.all_to_all(copies, ('x', 'z'), split_axis=0, concat_axis=0, tiled=True)  3.45 us
    pallas_call x2, Pallas kernels, table(): pl.pallas_call(functools.partial(table_kernel, n_h, kind), out_shape=jax....  2.94 us
  transfers between devices with their start and end apart: 18, of which 9 were waited for; matrix products, arithmetic and copies ran while one was open for 0% of the time, Pallas kernels for 7%

profile of v5, /device:TPU:1, one launch (start us, length us, event | category | flops | bytes accessed | tf_op | source)
XLA Modules:
  0.0 86.3 jit_solution(11002990266295242943)
XLA Ops:
  0.6 1.5 %broadcast_in_dim.14 = bf16[16,4,2048]{2,1,0:T(4,128)(2,1)} broadcast(bf16[4,2048]{1,0:T(4,128)(2,1)} %bitcast.13), dimensions={1,2} | broadcast | bytes 278528 | tf_op jit(solution)/shard_map/model_gather/broadcast_in_dim | solution.py:344
  2.2 9.1 %all-to-all-start = ((bf16[16,4,2048]{2,1,0:T(4,128)(2,1)}), bf16[16,4,2048]{2,1,0:T(4,128)(2,1)S(1)}, u32[]{:S(2)}, u32[]{:S(2)}) async-start(bf16[16,4,2048]{2,1,0:T(4,128)(2,1)} %broadcast_in_dim.14), calls=%async_computation | async-start | bytes 524288 | tf_op jit(solution)/shard_map/model_gather/all_to_all | solution.py:345
  11.3 0.0 copy-start.3
  11.3 1.6 %copy-done.3 = bf16[1,512,2048]{2,1,0:T(8,128)(2,1)S(1)} copy-done((bf16[1,512,2048]{2,1,0:T(8,128)(2,1)S(1)}, bf16[1,512,2048]{2,1,0:T(8,128)(2,1)}, u32[]{:S(2)}) %copy-start.3) | copy-done | bytes 2097176
  12.9 0.9 %copy-done.4 = f32[32,1024]{1,0:T(8,128)S(1)} copy-done((f32[32,1024]{1,0:T(8,128)S(1)}, f32[32,1024]{1,0:T(8,128)}, u32[]{:S(2)}) %copy-start.4) | copy-done | bytes 131096
  13.8 0.7 copy-done.5
  14.5 0.7 copy-done.7
  15.2 2.3 %screens.1.screen_ref = f32[128,2048]{1,0:T(8,128)S(1)} custom-call(s32[8,2,16]{2,1,0:T(2,128)S(1)} %copy-done.5, s32[8,16]{1,0:T(8,128)S(1)} %copy-done.7, f32[32,1024]{1,0:T(8,128)S(1)} %copy-done.4, bf16[512,2048]{1,0:T(8,128)(2,1)S(1)} %bitcast.9), custom_call_target="tpu_custom_call" | custom-call | flops 1000000000 | bytes 4194304 | tf_op jit(solution)/shard_map/screens/pallas_call | solution.py:348
  17.6 3.4 %all-to-all-done.near_ref = bf16[16,4,2048]{2,1,0:T(4,128)(2,1)S(1)} async-done(((bf16[16,4,2048]{2,1,0:T(4,128)(2,1)}), bf16[16,4,2048]{2,1,0:T(4,128)(2,1)S(1)}, u32[]{:S(2)}, u32[]{:S(2)}) %all-to-all-start) | async-done | bytes 262176 | tf_op jit(solution)/shard_map/model_gather/all_to_all | solution.py:345
  21.0 2.1 %collective-permute-start = (bf16[16,4,2048]{2,1,0:T(4,128)(2,1)S(1)}, bf16[16,4,2048]{2,1,0:T(4,128)(2,1)S(1)}, u32[]{:S(2)}, u32[]{:S(2)}) collective-permute-start(bf16[16,4,2048]{2,1,0:T(4,128)(2,1)S(1)} %all-to-all-done.near_ref), channel_id=1, source_target_pairs={{0,1},{1,0},{2,3},{3,2},{4,5},{5,4},{6,7},{7,6},{8,9},{9,8},{10,11... | collective-permute-start | bytes 786440 | tf_op jit(solution)/shard_map/ppermute | solution.py:318
  23.1 1.2 %collective-permute-done.far_ref = bf16[16,4,2048]{2,1,0:T(4,128)(2,1)S(1)} collective-permute-done((bf16[16,4,2048]{2,1,0:T(4,128)(2,1)S(1)}, bf16[16,4,2048]{2,1,0:T(4,128)(2,1)S(1)}, u32[]{:S(2)}, u32[]{:S(2)}) %collective-permute-start) | collective-permute-done | bytes 262176 | tf_op jit(solution)/shard_map/ppermute | solution.py:318
  24.3 0.6 images.1
  24.9 1.4 %collective-permute-start.2 = (bf16[2,256,128]{2,1,0:T(8,128)(2,1)S(1)}, bf16[2,256,128]{2,1,0:T(8,128)(2,1)S(1)}, u32[]{:S(2)}, u32[]{:S(2)}) collective-permute-start(bf16[2,256,128]{2,1,0:T(8,128)(2,1)S(1)} %get-tuple-element.39), channel_id=1, source_target_pairs={{0,64},{64,128},{128,192},{192,0},{1,65},{65,129},{129,193},{193,1... | collective-permute-start | bytes 393224 | tf_op jit(solution)/shard_map/image_sum/ppermute | solution.py:318
  26.3 2.6 %collective-permute-start.3 = (bf16[2,256,128]{2,1,0:T(8,128)(2,1)S(1)}, bf16[2,256,128]{2,1,0:T(8,128)(2,1)S(1)}, u32[]{:S(2)}, u32[]{:S(2)}) collective-permute-start(bf16[2,256,128]{2,1,0:T(8,128)(2,1)S(1)} %get-tuple-element.40), channel_id=1, source_target_pairs={{0,128},{64,192},{128,0},{192,64},{1,129},{65,193},{129,1},{193,65... | collective-permute-start | bytes 393224 | tf_op jit(solution)/shard_map/image_sum/ppermute | solution.py:318
  28.9 1.1 %collective-permute-start.4 = (bf16[2,256,128]{2,1,0:T(8,128)(2,1)S(1)}, bf16[2,256,128]{2,1,0:T(8,128)(2,1)S(1)}, u32[]{:S(2)}, u32[]{:S(2)}) collective-permute-start(bf16[2,256,128]{2,1,0:T(8,128)(2,1)S(1)} %get-tuple-element.41), channel_id=1, source_target_pairs={{0,192},{64,0},{128,64},{192,128},{1,193},{65,1},{129,65},{193,129... | collective-permute-start | bytes 393224 | tf_op jit(solution)/shard_map/image_sum/ppermute | solution.py:318
  30.0 4.2 %collective-permute-start.1 = (bf16[16,2048]{1,0:T(8,128)(2,1)S(1)}, bf16[16,2048]{1,0:T(8,128)(2,1)S(1)}, u32[]{:S(2)}, u32[]{:S(2)}) collective-permute-start(bf16[16,2048]{1,0:T(8,128)(2,1)S(1)} %bitcast.6), channel_id=1, source_target_pairs={{0,32},{32,0},{1,33},{33,1},{2,34},{34,2},{3,35},{35,3},{4,36},{36... | collective-permute-start | bytes 196616 | tf_op jit(solution)/shard_map/visible_route/ppermute | solution.py:318
  34.2 1.3 %north.1.north_ref = bf16[16,64,1024]{2,1,0:T(8,128)(2,1)S(1)} custom-call(f32[8,2,16]{2,1,0:T(2,128)S(1)} %copy-done.6, f32[1,1024]{1,0:T(1,128)S(1)} %bitcast.10), custom_call_target="tpu_custom_call" | custom-call | flops 1000000000 | bytes 4194304 | tf_op jit(solution)/shard_map/image_sum/north/pallas_call | solution.py:387
  35.5 0.0 collective-permute-done.3.refs_2_
  35.5 0.0 collective-permute-done.4.refs_3_
  35.6 0.1 image_sums.1
  35.6 3.7 %collective-permute-start.5 = (f32[256,128]{1,0:T(8,128)S(1)}, f32[256,128]{1,0:T(8,128)S(1)}, u32[]{:S(2)}, u32[]{:S(2)}) collective-permute-start(f32[256,128]{1,0:T(8,128)S(1)} %get-tuple-element.44), channel_id=1, source_target_pairs={{0,32},{32,0},{1,33},{33,1},{2,34},{34,2},{3,35},{35,3},{4,36},{36... | collective-permute-start | bytes 393224 | tf_op jit(solution)/shard_map/image_sum/ppermute | solution.py:318
  39.3 0.6 route.1
  39.9 1.0 %collective-permute-start.6 = (bf16[16,2048]{1,0:T(8,128)(2,1)S(1)}, bf16[16,2048]{1,0:T(8,128)(2,1)S(1)}, u32[]{:S(2)}, u32[]{:S(2)}) collective-permute-start(bf16[16,2048]{1,0:T(8,128)(2,1)S(1)} %get-tuple-element.45), channel_id=1, source_target_pairs={{0,64},{64,128},{128,192},{192,0},{1,65},{65,129},{129,193},{193,1... | collective-permute-start | bytes 196616 | tf_op jit(solution)/shard_map/ppermute | solution.py:318
  41.0 2.2 %collective-permute-start.7 = (bf16[16,2048]{1,0:T(8,128)(2,1)S(1)}, bf16[16,2048]{1,0:T(8,128)(2,1)S(1)}, u32[]{:S(2)}, u32[]{:S(2)}) collective-permute-start(bf16[16,2048]{1,0:T(8,128)(2,1)S(1)} %get-tuple-element.46), channel_id=1, source_target_pairs={{0,128},{64,192},{128,0},{192,64},{1,129},{65,193},{129,1},{193,65... | collective-permute-start | bytes 196616 | tf_op jit(solution)/shard_map/ppermute | solution.py:318
  43.2 0.9 %collective-permute-start.8 = (bf16[16,2048]{1,0:T(8,128)(2,1)S(1)}, bf16[16,2048]{1,0:T(8,128)(2,1)S(1)}, u32[]{:S(2)}, u32[]{:S(2)}) collective-permute-start(bf16[16,2048]{1,0:T(8,128)(2,1)S(1)} %get-tuple-element.47), channel_id=1, source_target_pairs={{0,192},{64,0},{128,64},{192,128},{1,193},{65,1},{129,65},{193,129... | collective-permute-start | bytes 196616 | tf_op jit(solution)/shard_map/ppermute | solution.py:318
  44.1 1.6 %east.1.east_ref = bf16[16,64,1024]{2,1,0:T(8,128)(2,1)S(1)} custom-call(f32[8,2,16]{2,1,0:T(2,128)S(1)} %copy-done.6, f32[1,1024]{1,0:T(1,128)S(1)} %bitcast.11), custom_call_target="tpu_custom_call" | custom-call | flops 1000000000 | bytes 4194304 | tf_op jit(solution)/shard_map/east/pallas_call | solution.py:387
  45.7 0.1 collective-permute-done.7.came_2_ref
  45.9 0.7 collective-permute-done.8.came_3_ref
  46.6 3.5 %visibilities.1 = (f32[16,2048]{1,0:T(8,128)}, bf16[256,128]{1,0:T(8,128)(2,1)S(1)}) custom-call(s32[16,128]{1,0:T(8,128)S(1)} %get-tuple-element.35.pick_ref, f32[256,128]{1,0:T(8,128)S(1)} %get-tuple-element.43.near_ref, f32[256,128]{1,0:T(8,128)S(1)} %collective-permute-done.5.far_ref, bf16[16,2048]{1,0:T(8,128)(2,1)S(1)} %bitcast.8, ...), custom_call_target="tpu_custom_call" | custom-call | flops 1000000000 | bytes 8388608 | tf_op jit(solution)/shard_map/visibilities/pallas_call | solution.py:420
  50.1 3.9 %collective-permute-start.9 = (bf16[256,128]{1,0:T(8,128)(2,1)S(1)}, bf16[256,128]{1,0:T(8,128)(2,1)S(1)}, u32[]{:S(2)}, u32[]{:S(2)}) collective-permute-start(bf16[256,128]{1,0:T(8,128)(2,1)S(1)} %get-tuple-element.51.refs_0_), channel_id=1, source_target_pairs={{0,32},{32,0},{1,33},{33,1},{2,34},{34,2},{3,35},{35,3},{4,36},{36... | collective-permute-start | bytes 196616 | tf_op jit(solution)/shard_map/grid_gather/ppermute | solution.py:318
  54.0 0.4 collective-permute-start.14
  54.3 0.0 collective-permute-start.12
  54.3 1.1 %collective-permute-start.10 = (bf16[256,128]{1,0:T(8,128)(2,1)S(1)}, bf16[256,128]{1,0:T(8,128)(2,1)S(1)}, u32[]{:S(2)}, u32[]{:S(2)}) collective-permute-start(bf16[256,128]{1,0:T(8,128)(2,1)S(1)} %get-tuple-element.51.refs_0_), channel_id=1, source_target_pairs={{0,64},{64,128},{128,192},{192,0},{1,65},{65,129},{129,193},{193,1... | collective-permute-start | bytes 196616 | tf_op jit(solution)/shard_map/grid_gather/ppermute | solution.py:318
  55.4 1.7 %collective-permute-done.9.refs_1_ = bf16[256,128]{1,0:T(8,128)(2,1)S(1)} collective-permute-done((bf16[256,128]{1,0:T(8,128)(2,1)S(1)}, bf16[256,128]{1,0:T(8,128)(2,1)S(1)}, u32[]{:S(2)}, u32[]{:S(2)}) %collective-permute-start.9) | collective-permute-done | bytes 65568 | tf_op jit(solution)/shard_map/grid_gather/ppermute | solution.py:318
  57.1 2.2 %collective-permute-start.15 = (bf16[256,128]{1,0:T(8,128)(2,1)S(1)}, bf16[256,128]{1,0:T(8,128)(2,1)S(1)}, u32[]{:S(2)}, u32[]{:S(2)}) collective-permute-start(bf16[256,128]{1,0:T(8,128)(2,1)S(1)} %collective-permute-done.9.refs_1_), channel_id=1, source_target_pairs={{0,192},{64,0},{128,64},{192,128},{1,193},{65,1},{129,65},{193,129... | collective-permute-start | bytes 196616 | tf_op jit(solution)/shard_map/grid_gather/ppermute | solution.py:318
  59.4 0.3 collective-permute-start.13
  59.6 0.3 collective-permute-start.11
  60.0 1.6 %collective-permute-done.15.refs_7_ = bf16[256,128]{1,0:T(8,128)(2,1)S(1)} collective-permute-done((bf16[256,128]{1,0:T(8,128)(2,1)S(1)}, bf16[256,128]{1,0:T(8,128)(2,1)S(1)}, u32[]{:S(2)}, u32[]{:S(2)}) %collective-permute-start.15) | collective-permute-done | bytes 65568 | tf_op jit(solution)/shard_map/grid_gather/ppermute | solution.py:318
  61.6 3.0 %collective-permute-done.13.refs_5_ = bf16[256,128]{1,0:T(8,128)(2,1)S(1)} collective-permute-done((bf16[256,128]{1,0:T(8,128)(2,1)S(1)}, bf16[256,128]{1,0:T(8,128)(2,1)S(1)}, u32[]{:S(2)}, u32[]{:S(2)}) %collective-permute-start.13) | collective-permute-done | bytes 65568 | tf_op jit(solution)/shard_map/grid_gather/ppermute | solution.py:318
  64.6 0.9 %collective-permute-done.11.refs_3_ = bf16[256,128]{1,0:T(8,128)(2,1)S(1)} collective-permute-done((bf16[256,128]{1,0:T(8,128)(2,1)S(1)}, bf16[256,128]{1,0:T(8,128)(2,1)S(1)}, u32[]{:S(2)}, u32[]{:S(2)}) %collective-permute-start.11) | collective-permute-done | bytes 65568 | tf_op jit(solution)/shard_map/grid_gather/ppermute | solution.py:318
  65.4 0.5 regrid_far.1
  65.9 5.4 %collective-permute-start.16 = (f32[64,2048]{1,0:T(8,128)S(1)}, f32[64,2048]{1,0:T(8,128)S(1)}, u32[]{:S(2)}, u32[]{:S(2)}) collective-permute-start(f32[64,2048]{1,0:T(8,128)S(1)} %regrid_far.1), channel_id=1, source_target_pairs={{0,1},{1,0},{2,3},{3,2},{4,5},{5,4},{6,7},{7,6},{8,9},{9,8},{10,11... | collective-permute-start | bytes 1572872 | tf_op jit(solution)/shard_map/dirty_scatter/ppermute | solution.py:318
  71.3 0.5 regrid_near.1
  71.8 1.1 %collective-permute-done.16 = f32[64,2048]{1,0:T(8,128)S(1)} collective-permute-done((f32[64,2048]{1,0:T(8,128)S(1)}, f32[64,2048]{1,0:T(8,128)S(1)}, u32[]{:S(2)}, u32[]{:S(2)}) %collective-permute-start.16) | collective-permute-done | bytes 524320 | tf_op jit(solution)/shard_map/dirty_scatter/ppermute | solution.py:318
  72.8 0.1 add_convert_fusion
  72.9 0.1 reshape.12
  73.0 12.6 %all_to_all.10 = bf16[16,4,2048]{2,1,0:T(4,128)(2,1)S(1)} all-to-all(bf16[16,4,2048]{2,1,0:T(4,128)(2,1)S(1)} %reshape.12), channel_id=1, replica_groups=mesh['y'=4,'h'=2,'x'=4,'z'=4,'c'=2] {'x','z'}, dimensions={0} | all-to-all | bytes 524288 | tf_op jit(solution)/shard_map/dirty_scatter/all_to_all | solution.py:459
  85.6 0.7 convert_reduce_fusion
  (20 shorter events, 0.0 us)
Async XLA Ops:
  2.2 22.2 %copy-start.1 = (s32[8,16]{1,0:T(8,128)S(1)}, s32[8,16]{1,0:T(8,128)}, u32[]{:S(2)}) copy-start(s32[8,16]{1,0:T(8,128)} %subgrid_ref.4) | copy-start | bytes 1540
  2.2 18.8 %all-to-all-start = ((bf16[16,4,2048]{2,1,0:T(4,128)(2,1)}), bf16[16,4,2048]{2,1,0:T(4,128)(2,1)S(1)}, u32[]{:S(2)}, u32[]{:S(2)}) async-start(bf16[16,4,2048]{2,1,0:T(4,128)(2,1)} %broadcast_in_dim.14), calls=%async_computation | async-start | bytes 524288 | tf_op jit(solution)/shard_map/model_gather/all_to_all | solution.py:345
  11.3 1.6 %copy-start.3 = (bf16[1,512,2048]{2,1,0:T(8,128)(2,1)S(1)}, bf16[1,512,2048]{2,1,0:T(8,128)(2,1)}, u32[]{:S(2)}) copy-start(bf16[1,512,2048]{2,1,0:T(8,128)(2,1)} %param.17) | copy-start | bytes 6291460
  12.9 0.9 %copy-start.4 = (f32[32,1024]{1,0:T(8,128)S(1)}, f32[32,1024]{1,0:T(8,128)}, u32[]{:S(2)}) copy-start(f32[32,1024]{1,0:T(8,128)} %phase_from.1) | copy-start | bytes 393220
  13.8 0.7 copy-start.5
  14.5 0.7 copy-start.7
  15.2 14.8 %copy-start = (bf16[1,16,2048]{2,1,0:T(8,128)(2,1)S(1)}, bf16[1,16,2048]{2,1,0:T(8,128)(2,1)}, u32[]{:S(2)}) copy-start(bf16[1,16,2048]{2,1,0:T(8,128)(2,1)} %param.10) | copy-start | bytes 196612
  15.2 19.0 %copy-start.6 = (f32[8,2,16]{2,1,0:T(2,128)S(1)}, f32[8,2,16]{2,1,0:T(2,128)}, u32[]{:S(2)}) copy-start(f32[8,2,16]{2,1,0:T(2,128)} %coords_ref.1) | copy-start | bytes 3076
  15.2 19.0 %copy-start.8 = (f32[1024]{0:T(1024)S(1)}, f32[1024]{0:T(1024)}, u32[]{:S(2)}) copy-start(f32[1024]{0:T(1024)} %param.19) | copy-start | bytes 12292
  21.0 3.3 %collective-permute-start = (bf16[16,4,2048]{2,1,0:T(4,128)(2,1)S(1)}, bf16[16,4,2048]{2,1,0:T(4,128)(2,1)S(1)}, u32[]{:S(2)}, u32[]{:S(2)}) collective-permute-start(bf16[16,4,2048]{2,1,0:T(4,128)(2,1)S(1)} %all-to-all-done.near_ref), channel_id=1, source_target_pairs={{0,1},{1,0},{2,3},{3,2},{4,5},{5,4},{6,7},{7,6},{8,9},{9,8},{10,11... | collective-permute-start | bytes 786440 | tf_op jit(solution)/shard_map/ppermute | solution.py:318
  24.9 10.6 %collective-permute-start.2 = (bf16[2,256,128]{2,1,0:T(8,128)(2,1)S(1)}, bf16[2,256,128]{2,1,0:T(8,128)(2,1)S(1)}, u32[]{:S(2)}, u32[]{:S(2)}) collective-permute-start(bf16[2,256,128]{2,1,0:T(8,128)(2,1)S(1)} %get-tuple-element.39), channel_id=1, source_target_pairs={{0,64},{64,128},{128,192},{192,0},{1,65},{65,129},{129,193},{193,1... | collective-permute-start | bytes 393224 | tf_op jit(solution)/shard_map/image_sum/ppermute | solution.py:318
  26.3 9.3 %collective-permute-start.3 = (bf16[2,256,128]{2,1,0:T(8,128)(2,1)S(1)}, bf16[2,256,128]{2,1,0:T(8,128)(2,1)S(1)}, u32[]{:S(2)}, u32[]{:S(2)}) collective-permute-start(bf16[2,256,128]{2,1,0:T(8,128)(2,1)S(1)} %get-tuple-element.40), channel_id=1, source_target_pairs={{0,128},{64,192},{128,0},{192,64},{1,129},{65,193},{129,1},{193,65... | collective-permute-start | bytes 393224 | tf_op jit(solution)/shard_map/image_sum/ppermute | solution.py:318
  28.9 6.7 %collective-permute-start.4 = (bf16[2,256,128]{2,1,0:T(8,128)(2,1)S(1)}, bf16[2,256,128]{2,1,0:T(8,128)(2,1)S(1)}, u32[]{:S(2)}, u32[]{:S(2)}) collective-permute-start(bf16[2,256,128]{2,1,0:T(8,128)(2,1)S(1)} %get-tuple-element.41), channel_id=1, source_target_pairs={{0,192},{64,0},{128,64},{192,128},{1,193},{65,1},{129,65},{193,129... | collective-permute-start | bytes 393224 | tf_op jit(solution)/shard_map/image_sum/ppermute | solution.py:318
  30.0 9.3 %collective-permute-start.1 = (bf16[16,2048]{1,0:T(8,128)(2,1)S(1)}, bf16[16,2048]{1,0:T(8,128)(2,1)S(1)}, u32[]{:S(2)}, u32[]{:S(2)}) collective-permute-start(bf16[16,2048]{1,0:T(8,128)(2,1)S(1)} %bitcast.6), channel_id=1, source_target_pairs={{0,32},{32,0},{1,33},{33,1},{2,34},{34,2},{3,35},{35,3},{4,36},{36... | collective-permute-start | bytes 196616 | tf_op jit(solution)/shard_map/visible_route/ppermute | solution.py:318
  34.2 5.1 %copy-start.2 = (s32[1,8]{1,0:T(1,128)S(1)}, s32[1,8]{1,0:T(1,128)}, u32[]{:S(2)}) copy-start(s32[1,8]{1,0:T(1,128)} %reader_ref.1) | copy-start | bytes 100
  35.6 11.0 %collective-permute-start.5 = (f32[256,128]{1,0:T(8,128)S(1)}, f32[256,128]{1,0:T(8,128)S(1)}, u32[]{:S(2)}, u32[]{:S(2)}) collective-permute-start(f32[256,128]{1,0:T(8,128)S(1)} %get-tuple-element.44), channel_id=1, source_target_pairs={{0,32},{32,0},{1,33},{33,1},{2,34},{34,2},{3,35},{35,3},{4,36},{36... | collective-permute-start | bytes 393224 | tf_op jit(solution)/shard_map/image_sum/ppermute | solution.py:318
  39.9 5.8 %collective-permute-start.6 = (bf16[16,2048]{1,0:T(8,128)(2,1)S(1)}, bf16[16,2048]{1,0:T(8,128)(2,1)S(1)}, u32[]{:S(2)}, u32[]{:S(2)}) collective-permute-start(bf16[16,2048]{1,0:T(8,128)(2,1)S(1)} %get-tuple-element.45), channel_id=1, source_target_pairs={{0,64},{64,128},{128,192},{192,0},{1,65},{65,129},{129,193},{193,1... | collective-permute-start | bytes 196616 | tf_op jit(solution)/shard_map/ppermute | solution.py:318
  41.0 4.9 %collective-permute-start.7 = (bf16[16,2048]{1,0:T(8,128)(2,1)S(1)}, bf16[16,2048]{1,0:T(8,128)(2,1)S(1)}, u32[]{:S(2)}, u32[]{:S(2)}) collective-permute-start(bf16[16,2048]{1,0:T(8,128)(2,1)S(1)} %get-tuple-element.46), channel_id=1, source_target_pairs={{0,128},{64,192},{128,0},{192,64},{1,129},{65,193},{129,1},{193,65... | collective-permute-start | bytes 196616 | tf_op jit(solution)/shard_map/ppermute | solution.py:318
  43.2 3.4 %collective-permute-start.8 = (bf16[16,2048]{1,0:T(8,128)(2,1)S(1)}, bf16[16,2048]{1,0:T(8,128)(2,1)S(1)}, u32[]{:S(2)}, u32[]{:S(2)}) collective-permute-start(bf16[16,2048]{1,0:T(8,128)(2,1)S(1)} %get-tuple-element.47), channel_id=1, source_target_pairs={{0,192},{64,0},{128,64},{192,128},{1,193},{65,1},{129,65},{193,129... | collective-permute-start | bytes 196616 | tf_op jit(solution)/shard_map/ppermute | solution.py:318
  50.1 7.0 %collective-permute-start.9 = (bf16[256,128]{1,0:T(8,128)(2,1)S(1)}, bf16[256,128]{1,0:T(8,128)(2,1)S(1)}, u32[]{:S(2)}, u32[]{:S(2)}) collective-permute-start(bf16[256,128]{1,0:T(8,128)(2,1)S(1)} %get-tuple-element.51.refs_0_), channel_id=1, source_target_pairs={{0,32},{32,0},{1,33},{33,1},{2,34},{34,2},{3,35},{35,3},{4,36},{36... | collective-permute-start | bytes 196616 | tf_op jit(solution)/shard_map/grid_gather/ppermute | solution.py:318
  54.0 5.7 %collective-permute-start.14 = (bf16[256,128]{1,0:T(8,128)(2,1)S(1)}, bf16[256,128]{1,0:T(8,128)(2,1)S(1)}, u32[]{:S(2)}, u32[]{:S(2)}) collective-permute-start(bf16[256,128]{1,0:T(8,128)(2,1)S(1)} %get-tuple-element.51.refs_0_), channel_id=1, source_target_pairs={{0,192},{64,0},{128,64},{192,128},{1,193},{65,1},{129,65},{193,129... | collective-permute-start | bytes 196616 | tf_op jit(solution)/shard_map/grid_gather/ppermute | solution.py:318
  54.3 5.6 %collective-permute-start.12 = (bf16[256,128]{1,0:T(8,128)(2,1)S(1)}, bf16[256,128]{1,0:T(8,128)(2,1)S(1)}, u32[]{:S(2)}, u32[]{:S(2)}) collective-permute-start(bf16[256,128]{1,0:T(8,128)(2,1)S(1)} %get-tuple-element.51.refs_0_), channel_id=1, source_target_pairs={{0,128},{64,192},{128,0},{192,64},{1,129},{65,193},{129,1},{193,65... | collective-permute-start | bytes 196616 | tf_op jit(solution)/shard_map/grid_gather/ppermute | solution.py:318
  54.3 5.6 %collective-permute-start.10 = (bf16[256,128]{1,0:T(8,128)(2,1)S(1)}, bf16[256,128]{1,0:T(8,128)(2,1)S(1)}, u32[]{:S(2)}, u32[]{:S(2)}) collective-permute-start(bf16[256,128]{1,0:T(8,128)(2,1)S(1)} %get-tuple-element.51.refs_0_), channel_id=1, source_target_pairs={{0,64},{64,128},{128,192},{192,0},{1,65},{65,129},{129,193},{193,1... | collective-permute-start | bytes 196616 | tf_op jit(solution)/shard_map/grid_gather/ppermute | solution.py:318
  57.1 4.5 %collective-permute-start.15 = (bf16[256,128]{1,0:T(8,128)(2,1)S(1)}, bf16[256,128]{1,0:T(8,128)(2,1)S(1)}, u32[]{:S(2)}, u32[]{:S(2)}) collective-permute-start(bf16[256,128]{1,0:T(8,128)(2,1)S(1)} %collective-permute-done.9.refs_1_), channel_id=1, source_target_pairs={{0,192},{64,0},{128,64},{192,128},{1,193},{65,1},{129,65},{193,129... | collective-permute-start | bytes 196616 | tf_op jit(solution)/shard_map/grid_gather/ppermute | solution.py:318
  59.4 5.2 %collective-permute-start.13 = (bf16[256,128]{1,0:T(8,128)(2,1)S(1)}, bf16[256,128]{1,0:T(8,128)(2,1)S(1)}, u32[]{:S(2)}, u32[]{:S(2)}) collective-permute-start(bf16[256,128]{1,0:T(8,128)(2,1)S(1)} %collective-permute-done.9.refs_1_), channel_id=1, source_target_pairs={{0,128},{64,192},{128,0},{192,64},{1,129},{65,193},{129,1},{193,65... | collective-permute-start | bytes 196616 | tf_op jit(solution)/shard_map/grid_gather/ppermute | solution.py:318
  59.6 5.8 %collective-permute-start.11 = (bf16[256,128]{1,0:T(8,128)(2,1)S(1)}, bf16[256,128]{1,0:T(8,128)(2,1)S(1)}, u32[]{:S(2)}, u32[]{:S(2)}) collective-permute-start(bf16[256,128]{1,0:T(8,128)(2,1)S(1)} %collective-permute-done.9.refs_1_), channel_id=1, source_target_pairs={{0,64},{64,128},{128,192},{192,0},{1,65},{65,129},{129,193},{193,1... | collective-permute-start | bytes 196616 | tf_op jit(solution)/shard_map/grid_gather/ppermute | solution.py:318
  65.9 6.9 %collective-permute-start.16 = (f32[64,2048]{1,0:T(8,128)S(1)}, f32[64,2048]{1,0:T(8,128)S(1)}, u32[]{:S(2)}, u32[]{:S(2)}) collective-permute-start(f32[64,2048]{1,0:T(8,128)S(1)} %regrid_far.1), channel_id=1, source_target_pairs={{0,1},{1,0},{2,3},{3,2},{4,5},{5,4},{6,7},{7,6},{8,9},{9,8},{10,11... | collective-permute-start | bytes 1572872 | tf_op jit(solution)/shard_map/dirty_scatter/ppermute | solution.py:318

commit v6 on v5

--- a/solution.py
+++ b/solution.py
@@ -200,31 +200,9 @@
             out_ref[...] = other_ref[...]
 
 
-def visibility_kernel(
-    pick_ref,
-    near_ref,
-    far_ref,
-    rows_ref,
-    other_ref,
-    came_1_ref,
-    came_2_ref,
-    came_3_ref,
-    east_ref,
-    north_ref,
-    resid_ref,
-    grid_ref,
-    cells_ref,
-    out_ref,
-):
-    rows, channels = (resid_ref.shape[0], resid_ref.shape[1] // 2)
+def degrid_kernel(near_ref, far_ref, east_ref, north_ref, predicted_ref, cells_ref):
+    rows, channels = (predicted_ref.shape[0], predicted_ref.shape[1] // 2)
     cells_ref[...] = near_ref[...] + far_ref[...]
-    found = (rows_ref, other_ref, came_1_ref, came_2_ref, came_3_ref)
-    for at in range(0, 2 * channels, 128):
-        chans = pl.ds(at, 128)
-        visible = found[0][:, chans].astype(F32)
-        for which, ref in enumerate(found[1:], 1):
-            visible = jnp.where(pick_ref[...] == which, ref[:, chans].astype(F32), visible)
-        resid_ref[:, chans] = visible
     width = 256
 
     def degrid(b):
@@ -254,8 +232,36 @@
             vis_im = jnp.sum(cos * inner_im + sin * inner_re, axis=0, keepdims=True)
             row = pl.ds(b, 1)
             late = pl.ds(channels + at, width)
-            resid_ref[row, chans] = resid_ref[row, chans] - vis_re
-            resid_ref[row, late] = resid_ref[row, late] - vis_im
+            predicted_ref[row, chans] = vis_re
+            predicted_ref[row, late] = vis_im
+
+    for b in range(rows):
+        degrid(b)
+
+
+def grid_kernel(
+    pick_ref,
+    rows_ref,
+    other_ref,
+    came_1_ref,
+    came_2_ref,
+    came_3_ref,
+    predicted_ref,
+    east_ref,
+    north_ref,
+    resid_ref,
+    grid_ref,
+    out_ref,
+):
+    rows, channels = (resid_ref.shape[0], resid_ref.shape[1] // 2)
+    found = (rows_ref, other_ref, came_1_ref, came_2_ref, came_3_ref)
+    for at in range(0, 2 * channels, 128):
+        chans = pl.ds(at, 128)
+        visible = found[0][:, chans].astype(F32)
+        for which, ref in enumerate(found[1:], 1):
+            visible = jnp.where(pick_ref[...] == which, ref[:, chans].astype(F32), visible)
+        resid_ref[:, chans] = visible - predicted_ref[:, chans]
+    width = 256
 
     def grid(b):
         products = jnp.zeros((64, 64), F32)
@@ -277,8 +283,6 @@
         )
 
     for b in range(rows):
-        degrid(b)
-    for b in range(rows):
         grid(b)
     grid_ref[...] = out_ref[...].astype(BF16)
 
@@ -316,6 +320,10 @@
 def shift(value, axis, by):
     size = lax.axis_size(axis)
     return lax.ppermute(value, axis, [(i, (i + by) % size) for i in range(size)])
+
+
+def far_first(size):
+    return sorted(range(1, size), key=lambda by: -min(by, size - by))
 
 
 def local(
@@ -401,7 +409,8 @@
     with jax.named_scope("image_sum"):
         north = table(1, soon)
         images[0], north = lax.optimization_barrier((images[0], north))
-        pieces = [images[0]] + [shift(images[by], "y", by) for by in range(1, n_y)]
+        pieces = dict((by, shift(images[by], "y", by)) for by in far_first(n_y))
+        pieces = [images[0]] + [pieces[by] for by in range(1, n_y)]
         own_sum, other_sum = pl.pallas_call(
             sum_kernel,
             out_shape=[jax.ShapeDtypeStruct((cell_rows, 128), F32)] * 2,
@@ -415,27 +424,40 @@
         beside_sum = shift(other_sum, "h", 1)
 
     east = table(0, later)
-    came = [shift(value, "y", by) for by, value in enumerate(sent, 1)]
+    came = dict((by, shift(sent[by - 1], "y", by)) for by in far_first(n_y))
+    came = [came[by] for by in range(1, n_y)]
+
+    predicted = pl.pallas_call(
+        degrid_kernel,
+        out_shape=jax.ShapeDtypeStruct((row_block, 2 * channels), F32),
+        in_specs=[VMEM] * 4,
+        out_specs=VMEM,
+        scratch_shapes=[pltpu.VMEM((cell_rows, 128), F32)],
+        compiler_params=params(16),
+        cost_estimate=pl.CostEstimate(flops=10**9, bytes_accessed=5 << 20, transcendentals=0),
+        name="degrid",
+    )(own_sum, beside_sum, east, north)
 
     residual, gridded = pl.pallas_call(
-        visibility_kernel,
+        grid_kernel,
         out_shape=[
             jax.ShapeDtypeStruct((row_block, 2 * channels), F32),
             jax.ShapeDtypeStruct((cell_rows, 128), BF16),
         ],
-        in_specs=[VMEM] * 10,
+        in_specs=[VMEM] * 9,
         out_specs=[VMEM] * 2,
-        scratch_shapes=[pltpu.VMEM((cell_rows, 128), F32), pltpu.VMEM((cell_rows, 128), F32)],
+        scratch_shapes=[pltpu.VMEM((cell_rows, 128), F32)],
         compiler_params=params(16),
-        cost_estimate=pl.CostEstimate(flops=10**9, bytes_accessed=8 << 20, transcendentals=0),
-        name="visibilities",
-    )(pick, own_sum, beside_sum, rows, other, *came, east, north)
+        cost_estimate=pl.CostEstimate(flops=10**9, bytes_accessed=5 << 20, transcendentals=0),
+        name="grid",
+    )(pick, rows, other, *came, predicted, east, north)
 
     with jax.named_scope("grid_gather"):
         beside = shift(gridded, "h", 1)
+        moved = dict((by, (shift(gridded, "y", by), shift(beside, "y", by))) for by in reversed(far_first(n_y)))
         grids = [gridded, beside]
         for by in range(1, n_y):
-            grids += [shift(gridded, "y", by), shift(beside, "y", by)]
+            grids += moved[by]
 
     half = subgrid_count // n_c
 

time: 86.8 us -> 84 us (0.968)
  waiting for transfers between devices: 13.7 us -> 7.69 us
  starting transfers between devices: 42 us -> 45.1 us
    ppermute x17, waiting for transfers between devices: 10.3 us -> 4.24 us  [shift(): lax.ppermute(value, axis, [(i, (i + by) % size) for i in range(size)])]
    ppermute x17, starting transfers between devices: 32.8 us -> 35.9 us  [shift(): lax.ppermute(value, axis, [(i, (i + by) % size) for i in range(size)])]
    pallas_call x1 -> x2, Pallas kernels: 3.48 us -> 3.57 us  [the longest x1 1.83 us: local(): pl.pallas_call(grid_kernel, out_shape=[jax.ShapeDtypeStruct((row_block, 2...]
  transfers between devices with their start and end apart: 18 -> 18, of which waited for: 9 -> 6; matrix products, arithmetic and copies ran while one was open for 0% -> 0% of each run, Pallas kernels for 7% -> 10%
where the time goes in v6:
time: 84 us; the launch traced here: 83.5 us
  starting transfers between devices  45.1 us (54%)
  blocking collectives  12.6 us (15%)
  Pallas kernels  11.1 us (13%)
  waiting for transfers between devices  7.69 us (9%)
  local copies, waits for them, and re-layouts  5.52 us (7%)
    ppermute x17, starting transfers between devices, shift(): lax.ppermute(value, axis, [(i, (i + by) % size) for i in range(size)])  35.9 us
    all_to_all x1, blocking collectives, local(): lax.all_to_all(chip_sum, ('x', 'z'), split_axis=0, concat_axis=0, tiled=T...  12.6 us
    all_to_all x1, starting transfers between devices, local(): lax.all_to_all(copies, ('x', 'z'), split_axis=0, concat_axis=0, tiled=True)  9.15 us
    ppermute x17, waiting for transfers between devices, shift(): lax.ppermute(value, axis, [(i, (i + by) % size) for i in range(size)])  4.24 us
    unnamed x18, local copies, waits for them, and re-layouts  3.89 us
    all_to_all x1, waiting for transfers between devices, local(): lax.all_to_all(copies, ('x', 'z'), split_axis=0, concat_axis=0, tiled=True)  3.45 us
    pallas_call x2, Pallas kernels, table(): pl.pallas_call(functools.partial(table_kernel, n_h, kind), out_shape=jax....  2.94 us
    pallas_call x1, Pallas kernels, local(): pl.pallas_call(screen_kernel, out_shape=jax.ShapeDtypeStruct((count, 2 *...  2.35 us
  transfers between devices with their start and end apart: 18, of which 6 were waited for; matrix products, arithmetic and copies ran while one was open for 0% of the time, Pallas kernels for 10%

profile of v6, /device:TPU:1, one launch (start us, length us, event | category | flops | bytes accessed | tf_op | source)
XLA Modules:
  0.0 83.5 jit_solution(15999202763729008340)
XLA Ops:
  0.6 1.5 %broadcast_in_dim.14 = bf16[16,4,2048]{2,1,0:T(4,128)(2,1)} broadcast(bf16[4,2048]{1,0:T(4,128)(2,1)} %bitcast.13), dimensions={1,2} | broadcast | bytes 278528 | tf_op jit(solution)/shard_map/model_gather/broadcast_in_dim | solution.py:352
  2.2 9.1 %all-to-all-start = ((bf16[16,4,2048]{2,1,0:T(4,128)(2,1)}), bf16[16,4,2048]{2,1,0:T(4,128)(2,1)S(1)}, u32[]{:S(2)}, u32[]{:S(2)}) async-start(bf16[16,4,2048]{2,1,0:T(4,128)(2,1)} %broadcast_in_dim.14), calls=%async_computation | async-start | bytes 524288 | tf_op jit(solution)/shard_map/model_gather/all_to_all | solution.py:353
  11.3 0.0 copy-start.3
  11.3 1.6 %copy-done.3 = bf16[1,512,2048]{2,1,0:T(8,128)(2,1)S(1)} copy-done((bf16[1,512,2048]{2,1,0:T(8,128)(2,1)S(1)}, bf16[1,512,2048]{2,1,0:T(8,128)(2,1)}, u32[]{:S(2)}) %copy-start.3) | copy-done | bytes 2097176
  12.9 0.9 %copy-done.4 = f32[32,1024]{1,0:T(8,128)S(1)} copy-done((f32[32,1024]{1,0:T(8,128)S(1)}, f32[32,1024]{1,0:T(8,128)}, u32[]{:S(2)}) %copy-start.4) | copy-done | bytes 131096
  13.8 0.7 copy-done.5
  14.5 0.7 copy-done.7
  15.2 2.3 %screens.1.screen_ref = f32[128,2048]{1,0:T(8,128)S(1)} custom-call(s32[8,2,16]{2,1,0:T(2,128)S(1)} %copy-done.5, s32[8,16]{1,0:T(8,128)S(1)} %copy-done.7, f32[32,1024]{1,0:T(8,128)S(1)} %copy-done.4, bf16[512,2048]{1,0:T(8,128)(2,1)S(1)} %bitcast.9), custom_call_target="tpu_custom_call" | custom-call | flops 1000000000 | bytes 4194304 | tf_op jit(solution)/shard_map/screens/pallas_call | solution.py:356
  17.6 3.4 %all-to-all-done.near_ref = bf16[16,4,2048]{2,1,0:T(4,128)(2,1)S(1)} async-done(((bf16[16,4,2048]{2,1,0:T(4,128)(2,1)}), bf16[16,4,2048]{2,1,0:T(4,128)(2,1)S(1)}, u32[]{:S(2)}, u32[]{:S(2)}) %all-to-all-start) | async-done | bytes 262176 | tf_op jit(solution)/shard_map/model_gather/all_to_all | solution.py:353
  21.0 2.1 %collective-permute-start = (bf16[16,4,2048]{2,1,0:T(4,128)(2,1)S(1)}, bf16[16,4,2048]{2,1,0:T(4,128)(2,1)S(1)}, u32[]{:S(2)}, u32[]{:S(2)}) collective-permute-start(bf16[16,4,2048]{2,1,0:T(4,128)(2,1)S(1)} %all-to-all-done.near_ref), channel_id=1, source_target_pairs={{0,1},{1,0},{2,3},{3,2},{4,5},{5,4},{6,7},{7,6},{8,9},{9,8},{10,11... | collective-permute-start | bytes 786440 | tf_op jit(solution)/shard_map/ppermute | solution.py:322
  23.1 1.2 %collective-permute-done.far_ref = bf16[16,4,2048]{2,1,0:T(4,128)(2,1)S(1)} collective-permute-done((bf16[16,4,2048]{2,1,0:T(4,128)(2,1)S(1)}, bf16[16,4,2048]{2,1,0:T(4,128)(2,1)S(1)}, u32[]{:S(2)}, u32[]{:S(2)}) %collective-permute-start) | collective-permute-done | bytes 262176 | tf_op jit(solution)/shard_map/ppermute | solution.py:322
  24.3 0.6 images.1
  24.9 1.4 %collective-permute-start.5 = (bf16[2,256,128]{2,1,0:T(8,128)(2,1)S(1)}, bf16[2,256,128]{2,1,0:T(8,128)(2,1)S(1)}, u32[]{:S(2)}, u32[]{:S(2)}) collective-permute-start(bf16[2,256,128]{2,1,0:T(8,128)(2,1)S(1)} %get-tuple-element.42), channel_id=1, source_target_pairs={{0,64},{64,128},{128,192},{192,0},{1,65},{65,129},{129,193},{193,1... | collective-permute-start | bytes 393224 | tf_op jit(solution)/shard_map/image_sum/ppermute | solution.py:322
  26.3 2.6 %collective-permute-start.6 = (bf16[2,256,128]{2,1,0:T(8,128)(2,1)S(1)}, bf16[2,256,128]{2,1,0:T(8,128)(2,1)S(1)}, u32[]{:S(2)}, u32[]{:S(2)}) collective-permute-start(bf16[2,256,128]{2,1,0:T(8,128)(2,1)S(1)} %get-tuple-element.43), channel_id=1, source_target_pairs={{0,128},{64,192},{128,0},{192,64},{1,129},{65,193},{129,1},{193,65... | collective-permute-start | bytes 393224 | tf_op jit(solution)/shard_map/image_sum/ppermute | solution.py:322
  28.9 1.1 %collective-permute-start.7 = (bf16[2,256,128]{2,1,0:T(8,128)(2,1)S(1)}, bf16[2,256,128]{2,1,0:T(8,128)(2,1)S(1)}, u32[]{:S(2)}, u32[]{:S(2)}) collective-permute-start(bf16[2,256,128]{2,1,0:T(8,128)(2,1)S(1)} %get-tuple-element.44), channel_id=1, source_target_pairs={{0,192},{64,0},{128,64},{192,128},{1,193},{65,1},{129,65},{193,129... | collective-permute-start | bytes 393224 | tf_op jit(solution)/shard_map/image_sum/ppermute | solution.py:322
  30.0 4.2 %collective-permute-start.1 = (bf16[16,2048]{1,0:T(8,128)(2,1)S(1)}, bf16[16,2048]{1,0:T(8,128)(2,1)S(1)}, u32[]{:S(2)}, u32[]{:S(2)}) collective-permute-start(bf16[16,2048]{1,0:T(8,128)(2,1)S(1)} %bitcast.6), channel_id=1, source_target_pairs={{0,32},{32,0},{1,33},{33,1},{2,34},{34,2},{3,35},{35,3},{4,36},{36... | collective-permute-start | bytes 196616 | tf_op jit(solution)/shard_map/visible_route/ppermute | solution.py:322
  34.2 1.3 %north.1.north_ref = bf16[16,64,1024]{2,1,0:T(8,128)(2,1)S(1)} custom-call(f32[8,2,16]{2,1,0:T(2,128)S(1)} %copy-done.6, f32[1,1024]{1,0:T(1,128)S(1)} %bitcast.10), custom_call_target="tpu_custom_call" | custom-call | flops 1000000000 | bytes 4194304 | tf_op jit(solution)/shard_map/image_sum/north/pallas_call | solution.py:395
  35.5 0.0 collective-permute-done.5.refs_1_
  35.6 0.1 image_sums.1
  35.6 3.7 %collective-permute-start.8 = (f32[256,128]{1,0:T(8,128)S(1)}, f32[256,128]{1,0:T(8,128)S(1)}, u32[]{:S(2)}, u32[]{:S(2)}) collective-permute-start(f32[256,128]{1,0:T(8,128)S(1)} %get-tuple-element.47), channel_id=1, source_target_pairs={{0,32},{32,0},{1,33},{33,1},{2,34},{34,2},{3,35},{35,3},{4,36},{36... | collective-permute-start | bytes 393224 | tf_op jit(solution)/shard_map/image_sum/ppermute | solution.py:322
  39.3 0.6 route.1
  39.9 1.0 %collective-permute-start.2 = (bf16[16,2048]{1,0:T(8,128)(2,1)S(1)}, bf16[16,2048]{1,0:T(8,128)(2,1)S(1)}, u32[]{:S(2)}, u32[]{:S(2)}) collective-permute-start(bf16[16,2048]{1,0:T(8,128)(2,1)S(1)} %get-tuple-element.36), channel_id=1, source_target_pairs={{0,64},{64,128},{128,192},{192,0},{1,65},{65,129},{129,193},{193,1... | collective-permute-start | bytes 196616 | tf_op jit(solution)/shard_map/ppermute | solution.py:322
  41.0 2.2 %collective-permute-start.3 = (bf16[16,2048]{1,0:T(8,128)(2,1)S(1)}, bf16[16,2048]{1,0:T(8,128)(2,1)S(1)}, u32[]{:S(2)}, u32[]{:S(2)}) collective-permute-start(bf16[16,2048]{1,0:T(8,128)(2,1)S(1)} %get-tuple-element.37), channel_id=1, source_target_pairs={{0,128},{64,192},{128,0},{192,64},{1,129},{65,193},{129,1},{193,65... | collective-permute-start | bytes 196616 | tf_op jit(solution)/shard_map/ppermute | solution.py:322
  43.2 0.9 %collective-permute-start.4 = (bf16[16,2048]{1,0:T(8,128)(2,1)S(1)}, bf16[16,2048]{1,0:T(8,128)(2,1)S(1)}, u32[]{:S(2)}, u32[]{:S(2)}) collective-permute-start(bf16[16,2048]{1,0:T(8,128)(2,1)S(1)} %get-tuple-element.38), channel_id=1, source_target_pairs={{0,192},{64,0},{128,64},{192,128},{1,193},{65,1},{129,65},{193,129... | collective-permute-start | bytes 196616 | tf_op jit(solution)/shard_map/ppermute | solution.py:322
  44.1 1.6 %east.1.east_ref = bf16[16,64,1024]{2,1,0:T(8,128)(2,1)S(1)} custom-call(f32[8,2,16]{2,1,0:T(2,128)S(1)} %copy-done.6, f32[1,1024]{1,0:T(1,128)S(1)} %bitcast.11), custom_call_target="tpu_custom_call" | custom-call | flops 1000000000 | bytes 4194304 | tf_op jit(solution)/shard_map/east/pallas_call | solution.py:395
  45.7 0.0 collective-permute-done.8.far_ref
  45.7 1.7 %degrid.1.predicted_ref = f32[16,2048]{1,0:T(8,128)S(1)} custom-call(f32[256,128]{1,0:T(8,128)S(1)} %get-tuple-element.46.near_ref, f32[256,128]{1,0:T(8,128)S(1)} %collective-permute-done.8.far_ref, bf16[16,64,1024]{2,1,0:T(8,128)(2,1)S(1)} %east.1.east_ref, bf16[16,64,1024]{2,1,0:T(8,128)(2,1)S(1)} %north.1.north_ref), custom_call_target="tpu_custom_call" | custom-call | flops 1000000000 | bytes 5242880 | tf_op jit(solution)/shard_map/degrid/pallas_call | solution.py:430
  47.5 0.0 collective-permute-done.3.came_2_ref
  47.5 1.8 %grid.1 = (f32[16,2048]{1,0:T(8,128)}, bf16[256,128]{1,0:T(8,128)(2,1)S(1)}) custom-call(s32[16,128]{1,0:T(8,128)S(1)} %get-tuple-element.35.pick_ref, bf16[16,2048]{1,0:T(8,128)(2,1)S(1)} %bitcast.8, bf16[16,2048]{1,0:T(8,128)(2,1)S(1)} %collective-permute-done.1.other_ref, bf16[16,2048]{1,0:T(8,128)(2,1)S(1)} %collective-permute-done.2.came_1_ref, ...), custom_call_target="tpu_custom_call" | custom-call | flops 1000000000 | bytes 5242880 | tf_op jit(solution)/shard_map/grid/pallas_call | solution.py:441
  49.4 4.7 %collective-permute-start.9 = (bf16[256,128]{1,0:T(8,128)(2,1)S(1)}, bf16[256,128]{1,0:T(8,128)(2,1)S(1)}, u32[]{:S(2)}, u32[]{:S(2)}) collective-permute-start(bf16[256,128]{1,0:T(8,128)(2,1)S(1)} %get-tuple-element.51.refs_0_), channel_id=1, source_target_pairs={{0,32},{32,0},{1,33},{33,1},{2,34},{34,2},{3,35},{35,3},{4,36},{36... | collective-permute-start | bytes 196616 | tf_op jit(solution)/shard_map/grid_gather/ppermute | solution.py:322
  54.1 0.0 collective-permute-start.10
  54.1 1.5 %collective-permute-start.12 = (bf16[256,128]{1,0:T(8,128)(2,1)S(1)}, bf16[256,128]{1,0:T(8,128)(2,1)S(1)}, u32[]{:S(2)}, u32[]{:S(2)}) collective-permute-start(bf16[256,128]{1,0:T(8,128)(2,1)S(1)} %get-tuple-element.51.refs_0_), channel_id=1, source_target_pairs={{0,128},{64,192},{128,0},{192,64},{1,129},{65,193},{129,1},{193,65... | collective-permute-start | bytes 196616 | tf_op jit(solution)/shard_map/grid_gather/ppermute | solution.py:322
  55.6 1.1 %collective-permute-start.14 = (bf16[256,128]{1,0:T(8,128)(2,1)S(1)}, bf16[256,128]{1,0:T(8,128)(2,1)S(1)}, u32[]{:S(2)}, u32[]{:S(2)}) collective-permute-start(bf16[256,128]{1,0:T(8,128)(2,1)S(1)} %get-tuple-element.51.refs_0_), channel_id=1, source_target_pairs={{0,192},{64,0},{128,64},{192,128},{1,193},{65,1},{129,65},{193,129... | collective-permute-start | bytes 196616 | tf_op jit(solution)/shard_map/grid_gather/ppermute | solution.py:322
  56.8 0.6 collective-permute-start.11
  57.4 2.1 %collective-permute-start.13 = (bf16[256,128]{1,0:T(8,128)(2,1)S(1)}, bf16[256,128]{1,0:T(8,128)(2,1)S(1)}, u32[]{:S(2)}, u32[]{:S(2)}) collective-permute-start(bf16[256,128]{1,0:T(8,128)(2,1)S(1)} %collective-permute-done.9.refs_1_), channel_id=1, source_target_pairs={{0,128},{64,192},{128,0},{192,64},{1,129},{65,193},{129,1},{193,65... | collective-permute-start | bytes 196616 | tf_op jit(solution)/shard_map/grid_gather/ppermute | solution.py:322
  59.5 0.0 collective-permute-done.10.refs_2_
  59.5 1.7 %collective-permute-start.15 = (bf16[256,128]{1,0:T(8,128)(2,1)S(1)}, bf16[256,128]{1,0:T(8,128)(2,1)S(1)}, u32[]{:S(2)}, u32[]{:S(2)}) collective-permute-start(bf16[256,128]{1,0:T(8,128)(2,1)S(1)} %collective-permute-done.9.refs_1_), channel_id=1, source_target_pairs={{0,192},{64,0},{128,64},{192,128},{1,193},{65,1},{129,65},{193,129... | collective-permute-start | bytes 196616 | tf_op jit(solution)/shard_map/grid_gather/ppermute | solution.py:322
  61.2 0.8 collective-permute-done.11.refs_3_
  62.0 0.5 collective-permute-done.13.refs_5_
  62.5 0.7 collective-permute-done.15.refs_7_
  63.2 0.5 regrid_far.1
  63.7 4.8 %collective-permute-start.16 = (f32[64,2048]{1,0:T(8,128)S(1)}, f32[64,2048]{1,0:T(8,128)S(1)}, u32[]{:S(2)}, u32[]{:S(2)}) collective-permute-start(f32[64,2048]{1,0:T(8,128)S(1)} %regrid_far.1), channel_id=1, source_target_pairs={{0,1},{1,0},{2,3},{3,2},{4,5},{5,4},{6,7},{7,6},{8,9},{9,8},{10,11... | collective-permute-start | bytes 1572872 | tf_op jit(solution)/shard_map/dirty_scatter/ppermute | solution.py:322
  68.5 0.5 regrid_near.1
  69.0 1.1 %collective-permute-done.16 = f32[64,2048]{1,0:T(8,128)S(1)} collective-permute-done((f32[64,2048]{1,0:T(8,128)S(1)}, f32[64,2048]{1,0:T(8,128)S(1)}, u32[]{:S(2)}, u32[]{:S(2)}) %collective-permute-start.16) | collective-permute-done | bytes 524320 | tf_op jit(solution)/shard_map/dirty_scatter/ppermute | solution.py:322
  70.0 0.1 add_convert_fusion
  70.1 0.1 reshape.12
  70.2 12.6 %all_to_all.10 = bf16[16,4,2048]{2,1,0:T(4,128)(2,1)S(1)} all-to-all(bf16[16,4,2048]{2,1,0:T(4,128)(2,1)S(1)} %reshape.12), channel_id=1, replica_groups=mesh['y'=4,'h'=2,'x'=4,'z'=4,'c'=2] {'x','z'}, dimensions={0} | all-to-all | bytes 524288 | tf_op jit(solution)/shard_map/dirty_scatter/all_to_all | solution.py:481
  82.8 0.7 convert_reduce_fusion
  (21 shorter events, 0.0 us)
Async XLA Ops:
  2.2 22.2 %copy-start.1 = (s32[8,16]{1,0:T(8,128)S(1)}, s32[8,16]{1,0:T(8,128)}, u32[]{:S(2)}) copy-start(s32[8,16]{1,0:T(8,128)} %subgrid_ref.4) | copy-start | bytes 1540
  2.2 18.8 %all-to-all-start = ((bf16[16,4,2048]{2,1,0:T(4,128)(2,1)}), bf16[16,4,2048]{2,1,0:T(4,128)(2,1)S(1)}, u32[]{:S(2)}, u32[]{:S(2)}) async-start(bf16[16,4,2048]{2,1,0:T(4,128)(2,1)} %broadcast_in_dim.14), calls=%async_computation | async-start | bytes 524288 | tf_op jit(solution)/shard_map/model_gather/all_to_all | solution.py:353
  11.3 1.6 %copy-start.3 = (bf16[1,512,2048]{2,1,0:T(8,128)(2,1)S(1)}, bf16[1,512,2048]{2,1,0:T(8,128)(2,1)}, u32[]{:S(2)}) copy-start(bf16[1,512,2048]{2,1,0:T(8,128)(2,1)} %param.17) | copy-start | bytes 6291460
  12.9 0.9 %copy-start.4 = (f32[32,1024]{1,0:T(8,128)S(1)}, f32[32,1024]{1,0:T(8,128)}, u32[]{:S(2)}) copy-start(f32[32,1024]{1,0:T(8,128)} %phase_from.1) | copy-start | bytes 393220
  13.8 0.7 copy-start.5
  14.5 0.7 copy-start.7
  15.2 14.8 %copy-start = (bf16[1,16,2048]{2,1,0:T(8,128)(2,1)S(1)}, bf16[1,16,2048]{2,1,0:T(8,128)(2,1)}, u32[]{:S(2)}) copy-start(bf16[1,16,2048]{2,1,0:T(8,128)(2,1)} %param.10) | copy-start | bytes 196612
  15.2 19.0 %copy-start.6 = (f32[8,2,16]{2,1,0:T(2,128)S(1)}, f32[8,2,16]{2,1,0:T(2,128)}, u32[]{:S(2)}) copy-start(f32[8,2,16]{2,1,0:T(2,128)} %coords_ref.1) | copy-start | bytes 3076
  15.2 19.0 %copy-start.8 = (f32[1024]{0:T(1024)S(1)}, f32[1024]{0:T(1024)}, u32[]{:S(2)}) copy-start(f32[1024]{0:T(1024)} %param.19) | copy-start | bytes 12292
  21.0 3.3 %collective-permute-start = (bf16[16,4,2048]{2,1,0:T(4,128)(2,1)S(1)}, bf16[16,4,2048]{2,1,0:T(4,128)(2,1)S(1)}, u32[]{:S(2)}, u32[]{:S(2)}) collective-permute-start(bf16[16,4,2048]{2,1,0:T(4,128)(2,1)S(1)} %all-to-all-done.near_ref), channel_id=1, source_target_pairs={{0,1},{1,0},{2,3},{3,2},{4,5},{5,4},{6,7},{7,6},{8,9},{9,8},{10,11... | collective-permute-start | bytes 786440 | tf_op jit(solution)/shard_map/ppermute | solution.py:322
  24.9 10.6 %collective-permute-start.5 = (bf16[2,256,128]{2,1,0:T(8,128)(2,1)S(1)}, bf16[2,256,128]{2,1,0:T(8,128)(2,1)S(1)}, u32[]{:S(2)}, u32[]{:S(2)}) collective-permute-start(bf16[2,256,128]{2,1,0:T(8,128)(2,1)S(1)} %get-tuple-element.42), channel_id=1, source_target_pairs={{0,64},{64,128},{128,192},{192,0},{1,65},{65,129},{129,193},{193,1... | collective-permute-start | bytes 393224 | tf_op jit(solution)/shard_map/image_sum/ppermute | solution.py:322
  26.3 9.3 %collective-permute-start.6 = (bf16[2,256,128]{2,1,0:T(8,128)(2,1)S(1)}, bf16[2,256,128]{2,1,0:T(8,128)(2,1)S(1)}, u32[]{:S(2)}, u32[]{:S(2)}) collective-permute-start(bf16[2,256,128]{2,1,0:T(8,128)(2,1)S(1)} %get-tuple-element.43), channel_id=1, source_target_pairs={{0,128},{64,192},{128,0},{192,64},{1,129},{65,193},{129,1},{193,65... | collective-permute-start | bytes 393224 | tf_op jit(solution)/shard_map/image_sum/ppermute | solution.py:322
  28.9 6.7 %collective-permute-start.7 = (bf16[2,256,128]{2,1,0:T(8,128)(2,1)S(1)}, bf16[2,256,128]{2,1,0:T(8,128)(2,1)S(1)}, u32[]{:S(2)}, u32[]{:S(2)}) collective-permute-start(bf16[2,256,128]{2,1,0:T(8,128)(2,1)S(1)} %get-tuple-element.44), channel_id=1, source_target_pairs={{0,192},{64,0},{128,64},{192,128},{1,193},{65,1},{129,65},{193,129... | collective-permute-start | bytes 393224 | tf_op jit(solution)/shard_map/image_sum/ppermute | solution.py:322
  30.0 9.3 %collective-permute-start.1 = (bf16[16,2048]{1,0:T(8,128)(2,1)S(1)}, bf16[16,2048]{1,0:T(8,128)(2,1)S(1)}, u32[]{:S(2)}, u32[]{:S(2)}) collective-permute-start(bf16[16,2048]{1,0:T(8,128)(2,1)S(1)} %bitcast.6), channel_id=1, source_target_pairs={{0,32},{32,0},{1,33},{33,1},{2,34},{34,2},{3,35},{35,3},{4,36},{36... | collective-permute-start | bytes 196616 | tf_op jit(solution)/shard_map/visible_route/ppermute | solution.py:322
  34.2 5.1 %copy-start.2 = (s32[1,8]{1,0:T(1,128)S(1)}, s32[1,8]{1,0:T(1,128)}, u32[]{:S(2)}) copy-start(s32[1,8]{1,0:T(1,128)} %reader_ref.1) | copy-start | bytes 100
  35.6 10.1 %collective-permute-start.8 = (f32[256,128]{1,0:T(8,128)S(1)}, f32[256,128]{1,0:T(8,128)S(1)}, u32[]{:S(2)}, u32[]{:S(2)}) collective-permute-start(f32[256,128]{1,0:T(8,128)S(1)} %get-tuple-element.47), channel_id=1, source_target_pairs={{0,32},{32,0},{1,33},{33,1},{2,34},{34,2},{3,35},{35,3},{4,36},{36... | collective-permute-start | bytes 393224 | tf_op jit(solution)/shard_map/image_sum/ppermute | solution.py:322
  39.9 7.6 %collective-permute-start.2 = (bf16[16,2048]{1,0:T(8,128)(2,1)S(1)}, bf16[16,2048]{1,0:T(8,128)(2,1)S(1)}, u32[]{:S(2)}, u32[]{:S(2)}) collective-permute-start(bf16[16,2048]{1,0:T(8,128)(2,1)S(1)} %get-tuple-element.36), channel_id=1, source_target_pairs={{0,64},{64,128},{128,192},{192,0},{1,65},{65,129},{129,193},{193,1... | collective-permute-start | bytes 196616 | tf_op jit(solution)/shard_map/ppermute | solution.py:322
  41.0 6.5 %collective-permute-start.3 = (bf16[16,2048]{1,0:T(8,128)(2,1)S(1)}, bf16[16,2048]{1,0:T(8,128)(2,1)S(1)}, u32[]{:S(2)}, u32[]{:S(2)}) collective-permute-start(bf16[16,2048]{1,0:T(8,128)(2,1)S(1)} %get-tuple-element.37), channel_id=1, source_target_pairs={{0,128},{64,192},{128,0},{192,64},{1,129},{65,193},{129,1},{193,65... | collective-permute-start | bytes 196616 | tf_op jit(solution)/shard_map/ppermute | solution.py:322
  43.2 4.3 %collective-permute-start.4 = (bf16[16,2048]{1,0:T(8,128)(2,1)S(1)}, bf16[16,2048]{1,0:T(8,128)(2,1)S(1)}, u32[]{:S(2)}, u32[]{:S(2)}) collective-permute-start(bf16[16,2048]{1,0:T(8,128)(2,1)S(1)} %get-tuple-element.38), channel_id=1, source_target_pairs={{0,192},{64,0},{128,64},{192,128},{1,193},{65,1},{129,65},{193,129... | collective-permute-start | bytes 196616 | tf_op jit(solution)/shard_map/ppermute | solution.py:322
  49.4 7.4 %collective-permute-start.9 = (bf16[256,128]{1,0:T(8,128)(2,1)S(1)}, bf16[256,128]{1,0:T(8,128)(2,1)S(1)}, u32[]{:S(2)}, u32[]{:S(2)}) collective-permute-start(bf16[256,128]{1,0:T(8,128)(2,1)S(1)} %get-tuple-element.51.refs_0_), channel_id=1, source_target_pairs={{0,32},{32,0},{1,33},{33,1},{2,34},{34,2},{3,35},{35,3},{4,36},{36... | collective-permute-start | bytes 196616 | tf_op jit(solution)/shard_map/grid_gather/ppermute | solution.py:322
  54.1 5.4 %collective-permute-start.10 = (bf16[256,128]{1,0:T(8,128)(2,1)S(1)}, bf16[256,128]{1,0:T(8,128)(2,1)S(1)}, u32[]{:S(2)}, u32[]{:S(2)}) collective-permute-start(bf16[256,128]{1,0:T(8,128)(2,1)S(1)} %get-tuple-element.51.refs_0_), channel_id=1, source_target_pairs={{0,64},{64,128},{128,192},{192,0},{1,65},{65,129},{129,193},{193,1... | collective-permute-start | bytes 196616 | tf_op jit(solution)/shard_map/grid_gather/ppermute | solution.py:322
  54.1 7.1 %collective-permute-start.12 = (bf16[256,128]{1,0:T(8,128)(2,1)S(1)}, bf16[256,128]{1,0:T(8,128)(2,1)S(1)}, u32[]{:S(2)}, u32[]{:S(2)}) collective-permute-start(bf16[256,128]{1,0:T(8,128)(2,1)S(1)} %get-tuple-element.51.refs_0_), channel_id=1, source_target_pairs={{0,128},{64,192},{128,0},{192,64},{1,129},{65,193},{129,1},{193,65... | collective-permute-start | bytes 196616 | tf_op jit(solution)/shard_map/grid_gather/ppermute | solution.py:322
  55.6 5.6 %collective-permute-start.14 = (bf16[256,128]{1,0:T(8,128)(2,1)S(1)}, bf16[256,128]{1,0:T(8,128)(2,1)S(1)}, u32[]{:S(2)}, u32[]{:S(2)}) collective-permute-start(bf16[256,128]{1,0:T(8,128)(2,1)S(1)} %get-tuple-element.51.refs_0_), channel_id=1, source_target_pairs={{0,192},{64,0},{128,64},{192,128},{1,193},{65,1},{129,65},{193,129... | collective-permute-start | bytes 196616 | tf_op jit(solution)/shard_map/grid_gather/ppermute | solution.py:322
  56.8 5.2 %collective-permute-start.11 = (bf16[256,128]{1,0:T(8,128)(2,1)S(1)}, bf16[256,128]{1,0:T(8,128)(2,1)S(1)}, u32[]{:S(2)}, u32[]{:S(2)}) collective-permute-start(bf16[256,128]{1,0:T(8,128)(2,1)S(1)} %collective-permute-done.9.refs_1_), channel_id=1, source_target_pairs={{0,64},{64,128},{128,192},{192,0},{1,65},{65,129},{129,193},{193,1... | collective-permute-start | bytes 196616 | tf_op jit(solution)/shard_map/grid_gather/ppermute | solution.py:322
  57.4 5.2 %collective-permute-start.13 = (bf16[256,128]{1,0:T(8,128)(2,1)S(1)}, bf16[256,128]{1,0:T(8,128)(2,1)S(1)}, u32[]{:S(2)}, u32[]{:S(2)}) collective-permute-start(bf16[256,128]{1,0:T(8,128)(2,1)S(1)} %collective-permute-done.9.refs_1_), channel_id=1, source_target_pairs={{0,128},{64,192},{128,0},{192,64},{1,129},{65,193},{129,1},{193,65... | collective-permute-start | bytes 196616 | tf_op jit(solution)/shard_map/grid_gather/ppermute | solution.py:322
  59.5 3.7 %collective-permute-start.15 = (bf16[256,128]{1,0:T(8,128)(2,1)S(1)}, bf16[256,128]{1,0:T(8,128)(2,1)S(1)}, u32[]{:S(2)}, u32[]{:S(2)}) collective-permute-start(bf16[256,128]{1,0:T(8,128)(2,1)S(1)} %collective-permute-done.9.refs_1_), channel_id=1, source_target_pairs={{0,192},{64,0},{128,64},{192,128},{1,193},{65,1},{129,65},{193,129... | collective-permute-start | bytes 196616 | tf_op jit(solution)/shard_map/grid_gather/ppermute | solution.py:322
  63.7 6.3 %collective-permute-start.16 = (f32[64,2048]{1,0:T(8,128)S(1)}, f32[64,2048]{1,0:T(8,128)S(1)}, u32[]{:S(2)}, u32[]{:S(2)}) collective-permute-start(f32[64,2048]{1,0:T(8,128)S(1)} %regrid_far.1), channel_id=1, source_target_pairs={{0,1},{1,0},{2,3},{3,2},{4,5},{5,4},{6,7},{7,6},{8,9},{9,8},{10,11... | collective-permute-start | bytes 1572872 | tf_op jit(solution)/shard_map/dirty_scatter/ppermute | solution.py:322

commit v7 on v6

--- a/solution.py
+++ b/solution.py
@@ -239,6 +239,16 @@
         degrid(b)
 
 
+def residual_kernel(pick_ref, *refs):
+    found, (predicted_ref, resid_ref) = (refs[:-2], refs[-2:])
+    for at in range(0, resid_ref.shape[1], 128):
+        chans = pl.ds(at, 128)
+        visible = found[0][:, chans].astype(F32)
+        for which, ref in enumerate(found[1:], 1):
+            visible = jnp.where(pick_ref[...] == which, ref[:, chans].astype(F32), visible)
+        resid_ref[:, chans] = visible - predicted_ref[:, chans]
+
+
 def grid_kernel(
     pick_ref,
     rows_ref,
@@ -249,18 +259,14 @@
     predicted_ref,
     east_ref,
     north_ref,
-    resid_ref,
     grid_ref,
     out_ref,
+    resid_ref,
 ):
     rows, channels = (resid_ref.shape[0], resid_ref.shape[1] // 2)
-    found = (rows_ref, other_ref, came_1_ref, came_2_ref, came_3_ref)
-    for at in range(0, 2 * channels, 128):
-        chans = pl.ds(at, 128)
-        visible = found[0][:, chans].astype(F32)
-        for which, ref in enumerate(found[1:], 1):
-            visible = jnp.where(pick_ref[...] == which, ref[:, chans].astype(F32), visible)
-        resid_ref[:, chans] = visible - predicted_ref[:, chans]
+    residual_kernel(
+        pick_ref, rows_ref, other_ref, came_1_ref, came_2_ref, came_3_ref, predicted_ref, resid_ref
+    )
     width = 256
 
     def grid(b):
@@ -438,19 +444,17 @@
         name="degrid",
     )(own_sum, beside_sum, east, north)
 
-    residual, gridded = pl.pallas_call(
+    operands = (pick, rows, other, *came, predicted)
+    gridded = pl.pallas_call(
         grid_kernel,
-        out_shape=[
-            jax.ShapeDtypeStruct((row_block, 2 * channels), F32),
-            jax.ShapeDtypeStruct((cell_rows, 128), BF16),
-        ],
+        out_shape=jax.ShapeDtypeStruct((cell_rows, 128), BF16),
         in_specs=[VMEM] * 9,
-        out_specs=[VMEM] * 2,
-        scratch_shapes=[pltpu.VMEM((cell_rows, 128), F32)],
+        out_specs=VMEM,
+        scratch_shapes=[pltpu.VMEM((cell_rows, 128), F32), pltpu.VMEM(predicted.shape, F32)],
         compiler_params=params(16),
         cost_estimate=pl.CostEstimate(flops=10**9, bytes_accessed=5 << 20, transcendentals=0),
         name="grid",
-    )(pick, rows, other, *came, predicted, east, north)
+    )(*operands, east, north)
 
     with jax.named_scope("grid_gather"):
         beside = shift(gridded, "h", 1)
@@ -458,6 +462,18 @@
         grids = [gridded, beside]
         for by in range(1, n_y):
             grids += moved[by]
+
+    first, *operands = operands
+    first, grids[1] = lax.optimization_barrier((first, grids[1]))
+    residual = pl.pallas_call(
+        residual_kernel,
+        out_shape=jax.ShapeDtypeStruct(predicted.shape, F32),
+        in_specs=[VMEM] * 7,
+        out_specs=VMEM,
+        compiler_params=params(4),
+        cost_estimate=pl.CostEstimate(flops=10**6, bytes_accessed=1 << 19, transcendentals=0),
+        name="residual",
+    )(first, *operands)
 
     half = subgrid_count // n_c
 
@@ -472,7 +488,8 @@
             name=("regrid_near", "regrid_far")[other],
         )(subgrids, screen, *grids)
 
-    far_sum = regrid(1, subgrid_index)
+    subgrids, residual = lax.optimization_barrier((subgrid_index, residual))
+    far_sum = regrid(1, subgrids)
     subgrids, far_sum = lax.optimization_barrier((subgrid_index, far_sum))
     near_sum = regrid(0, subgrids)
 

time: 84 us -> 83.6 us (level)
    pallas_call x1 -> x2, Pallas kernels: 1.83 us -> 1.99 us  [the longest x1 1.28 us: local(): pl.pallas_call(grid_kernel, out_shape=jax.ShapeDtypeStruct((cell_rows, 12...]
  transfers between devices with their start and end apart: 18 -> 18, of which waited for: 6 -> 5; matrix products, arithmetic and copies ran while one was open for 0% -> 0% of each run, Pallas kernels for 10% -> 11%
where the time goes in v7:
time: 83.6 us; the launch traced here: 83.1 us
  starting transfers between devices  45.2 us (54%)
  blocking collectives  12.6 us (15%)
  Pallas kernels  11.2 us (13%)
  waiting for transfers between devices  6.98 us (8%)
  local copies, waits for them, and re-layouts  5.53 us (7%)
    ppermute x17, starting transfers between devices, shift(): lax.ppermute(value, axis, [(i, (i + by) % size) for i in range(size)])  36 us
    all_to_all x1, blocking collectives, local(): lax.all_to_all(chip_sum, ('x', 'z'), split_axis=0, concat_axis=0, tiled=T...  12.6 us
    all_to_all x1, starting transfers between devices, local(): lax.all_to_all(copies, ('x', 'z'), split_axis=0, concat_axis=0, tiled=True)  9.15 us
    unnamed x18, local copies, waits for them, and re-layouts  3.89 us
    ppermute x17, waiting for transfers between devices, shift(): lax.ppermute(value, axis, [(i, (i + by) % size) for i in range(size)])  3.53 us
    all_to_all x1, waiting for transfers between devices, local(): lax.all_to_all(copies, ('x', 'z'), split_axis=0, concat_axis=0, tiled=True)  3.44 us
    pallas_call x2, Pallas kernels, table(): pl.pallas_call(functools.partial(table_kernel, n_h, kind), out_shape=jax....  2.94 us
    pallas_call x1, Pallas kernels, local(): pl.pallas_call(screen_kernel, out_shape=jax.ShapeDtypeStruct((count, 2 *...  2.35 us
  transfers between devices with their start and end apart: 18, of which 5 were waited for; matrix products, arithmetic and copies ran while one was open for 0% of the time, Pallas kernels for 11%

profile of v7, /device:TPU:1, one launch (start us, length us, event | category | flops | bytes accessed | tf_op | source)
XLA Modules:
  0.0 83.1 jit_solution(18051469054212128493)
XLA Ops:
  0.6 1.5 %broadcast_in_dim.14 = bf16[16,4,2048]{2,1,0:T(4,128)(2,1)} broadcast(bf16[4,2048]{1,0:T(4,128)(2,1)} %bitcast.15), dimensions={1,2} | broadcast | bytes 278528 | tf_op jit(solution)/shard_map/model_gather/broadcast_in_dim | solution.py:358
  2.2 9.1 %all-to-all-start = ((bf16[16,4,2048]{2,1,0:T(4,128)(2,1)}), bf16[16,4,2048]{2,1,0:T(4,128)(2,1)S(1)}, u32[]{:S(2)}, u32[]{:S(2)}) async-start(bf16[16,4,2048]{2,1,0:T(4,128)(2,1)} %broadcast_in_dim.14), calls=%async_computation | async-start | bytes 524288 | tf_op jit(solution)/shard_map/model_gather/all_to_all | solution.py:359
  11.3 0.0 copy-start.3
  11.3 1.6 %copy-done.3 = bf16[1,512,2048]{2,1,0:T(8,128)(2,1)S(1)} copy-done((bf16[1,512,2048]{2,1,0:T(8,128)(2,1)S(1)}, bf16[1,512,2048]{2,1,0:T(8,128)(2,1)}, u32[]{:S(2)}) %copy-start.3) | copy-done | bytes 2097176
  12.9 0.9 %copy-done.4 = f32[32,1024]{1,0:T(8,128)S(1)} copy-done((f32[32,1024]{1,0:T(8,128)S(1)}, f32[32,1024]{1,0:T(8,128)}, u32[]{:S(2)}) %copy-start.4) | copy-done | bytes 131096
  13.8 0.7 copy-done.5
  14.5 0.7 copy-done.7
  15.2 2.3 %screens.1.screen_ref = f32[128,2048]{1,0:T(8,128)S(1)} custom-call(s32[8,2,16]{2,1,0:T(2,128)S(1)} %copy-done.5, s32[8,16]{1,0:T(8,128)S(1)} %copy-done.7, f32[32,1024]{1,0:T(8,128)S(1)} %copy-done.4, bf16[512,2048]{1,0:T(8,128)(2,1)S(1)} %bitcast.10), custom_call_target="tpu_custom_call" | custom-call | flops 1000000000 | bytes 4194304 | tf_op jit(solution)/shard_map/screens/pallas_call | solution.py:362
  17.6 3.4 %all-to-all-done.near_ref = bf16[16,4,2048]{2,1,0:T(4,128)(2,1)S(1)} async-done(((bf16[16,4,2048]{2,1,0:T(4,128)(2,1)}), bf16[16,4,2048]{2,1,0:T(4,128)(2,1)S(1)}, u32[]{:S(2)}, u32[]{:S(2)}) %all-to-all-start) | async-done | bytes 262176 | tf_op jit(solution)/shard_map/model_gather/all_to_all | solution.py:359
  21.0 2.1 %collective-permute-start = (bf16[16,4,2048]{2,1,0:T(4,128)(2,1)S(1)}, bf16[16,4,2048]{2,1,0:T(4,128)(2,1)S(1)}, u32[]{:S(2)}, u32[]{:S(2)}) collective-permute-start(bf16[16,4,2048]{2,1,0:T(4,128)(2,1)S(1)} %all-to-all-done.near_ref), channel_id=1, source_target_pairs={{0,1},{1,0},{2,3},{3,2},{4,5},{5,4},{6,7},{7,6},{8,9},{9,8},{10,11... | collective-permute-start | bytes 786440 | tf_op jit(solution)/shard_map/ppermute | solution.py:328
  23.2 1.2 %collective-permute-done.far_ref = bf16[16,4,2048]{2,1,0:T(4,128)(2,1)S(1)} collective-permute-done((bf16[16,4,2048]{2,1,0:T(4,128)(2,1)S(1)}, bf16[16,4,2048]{2,1,0:T(4,128)(2,1)S(1)}, u32[]{:S(2)}, u32[]{:S(2)}) %collective-permute-start) | collective-permute-done | bytes 262176 | tf_op jit(solution)/shard_map/ppermute | solution.py:328
  24.3 0.6 images.1
  24.9 1.4 %collective-permute-start.5 = (bf16[2,256,128]{2,1,0:T(8,128)(2,1)S(1)}, bf16[2,256,128]{2,1,0:T(8,128)(2,1)S(1)}, u32[]{:S(2)}, u32[]{:S(2)}) collective-permute-start(bf16[2,256,128]{2,1,0:T(8,128)(2,1)S(1)} %get-tuple-element.44), channel_id=1, source_target_pairs={{0,64},{64,128},{128,192},{192,0},{1,65},{65,129},{129,193},{193,1... | collective-permute-start | bytes 393224 | tf_op jit(solution)/shard_map/image_sum/ppermute | solution.py:328
  26.3 2.6 %collective-permute-start.6 = (bf16[2,256,128]{2,1,0:T(8,128)(2,1)S(1)}, bf16[2,256,128]{2,1,0:T(8,128)(2,1)S(1)}, u32[]{:S(2)}, u32[]{:S(2)}) collective-permute-start(bf16[2,256,128]{2,1,0:T(8,128)(2,1)S(1)} %get-tuple-element.45), channel_id=1, source_target_pairs={{0,128},{64,192},{128,0},{192,64},{1,129},{65,193},{129,1},{193,65... | collective-permute-start | bytes 393224 | tf_op jit(solution)/shard_map/image_sum/ppermute | solution.py:328
  28.9 1.1 %collective-permute-start.7 = (bf16[2,256,128]{2,1,0:T(8,128)(2,1)S(1)}, bf16[2,256,128]{2,1,0:T(8,128)(2,1)S(1)}, u32[]{:S(2)}, u32[]{:S(2)}) collective-permute-start(bf16[2,256,128]{2,1,0:T(8,128)(2,1)S(1)} %get-tuple-element.46), channel_id=1, source_target_pairs={{0,192},{64,0},{128,64},{192,128},{1,193},{65,1},{129,65},{193,129... | collective-permute-start | bytes 393224 | tf_op jit(solution)/shard_map/image_sum/ppermute | solution.py:328
  30.0 4.2 %collective-permute-start.1 = (bf16[16,2048]{1,0:T(8,128)(2,1)S(1)}, bf16[16,2048]{1,0:T(8,128)(2,1)S(1)}, u32[]{:S(2)}, u32[]{:S(2)}) collective-permute-start(bf16[16,2048]{1,0:T(8,128)(2,1)S(1)} %bitcast.6), channel_id=1, source_target_pairs={{0,32},{32,0},{1,33},{33,1},{2,34},{34,2},{3,35},{35,3},{4,36},{36... | collective-permute-start | bytes 196616 | tf_op jit(solution)/shard_map/visible_route/ppermute | solution.py:328
  34.2 1.3 %north.1.north_ref = bf16[16,64,1024]{2,1,0:T(8,128)(2,1)S(1)} custom-call(f32[8,2,16]{2,1,0:T(2,128)S(1)} %copy-done.6, f32[1,1024]{1,0:T(1,128)S(1)} %bitcast.11), custom_call_target="tpu_custom_call" | custom-call | flops 1000000000 | bytes 4194304 | tf_op jit(solution)/shard_map/image_sum/north/pallas_call | solution.py:401
  35.6 0.0 collective-permute-done.6.refs_2_
  35.6 0.1 image_sums.1
  35.6 3.7 %collective-permute-start.8 = (f32[256,128]{1,0:T(8,128)S(1)}, f32[256,128]{1,0:T(8,128)S(1)}, u32[]{:S(2)}, u32[]{:S(2)}) collective-permute-start(f32[256,128]{1,0:T(8,128)S(1)} %get-tuple-element.49), channel_id=1, source_target_pairs={{0,32},{32,0},{1,33},{33,1},{2,34},{34,2},{3,35},{35,3},{4,36},{36... | collective-permute-start | bytes 393224 | tf_op jit(solution)/shard_map/image_sum/ppermute | solution.py:328
  39.3 0.6 route.1
  40.0 1.0 %collective-permute-start.2 = (bf16[16,2048]{1,0:T(8,128)(2,1)S(1)}, bf16[16,2048]{1,0:T(8,128)(2,1)S(1)}, u32[]{:S(2)}, u32[]{:S(2)}) collective-permute-start(bf16[16,2048]{1,0:T(8,128)(2,1)S(1)} %get-tuple-element.38), channel_id=1, source_target_pairs={{0,64},{64,128},{128,192},{192,0},{1,65},{65,129},{129,193},{193,1... | collective-permute-start | bytes 196616 | tf_op jit(solution)/shard_map/ppermute | solution.py:328
  41.0 2.2 %collective-permute-start.3 = (bf16[16,2048]{1,0:T(8,128)(2,1)S(1)}, bf16[16,2048]{1,0:T(8,128)(2,1)S(1)}, u32[]{:S(2)}, u32[]{:S(2)}) collective-permute-start(bf16[16,2048]{1,0:T(8,128)(2,1)S(1)} %get-tuple-element.39), channel_id=1, source_target_pairs={{0,128},{64,192},{128,0},{192,64},{1,129},{65,193},{129,1},{193,65... | collective-permute-start | bytes 196616 | tf_op jit(solution)/shard_map/ppermute | solution.py:328
  43.2 0.9 %collective-permute-start.4 = (bf16[16,2048]{1,0:T(8,128)(2,1)S(1)}, bf16[16,2048]{1,0:T(8,128)(2,1)S(1)}, u32[]{:S(2)}, u32[]{:S(2)}) collective-permute-start(bf16[16,2048]{1,0:T(8,128)(2,1)S(1)} %get-tuple-element.40), channel_id=1, source_target_pairs={{0,192},{64,0},{128,64},{192,128},{1,193},{65,1},{129,65},{193,129... | collective-permute-start | bytes 196616 | tf_op jit(solution)/shard_map/ppermute | solution.py:328
  44.1 1.6 %east.1.east_ref = bf16[16,64,1024]{2,1,0:T(8,128)(2,1)S(1)} custom-call(f32[8,2,16]{2,1,0:T(2,128)S(1)} %copy-done.6, f32[1,1024]{1,0:T(1,128)S(1)} %bitcast.12), custom_call_target="tpu_custom_call" | custom-call | flops 1000000000 | bytes 4194304 | tf_op jit(solution)/shard_map/east/pallas_call | solution.py:401
  45.7 0.0 collective-permute-done.8.far_ref
  45.8 1.7 %degrid.1.predicted_ref.refs_5_ = f32[16,2048]{1,0:T(8,128)S(1)} custom-call(f32[256,128]{1,0:T(8,128)S(1)} %get-tuple-element.48.near_ref, f32[256,128]{1,0:T(8,128)S(1)} %collective-permute-done.8.far_ref, bf16[16,64,1024]{2,1,0:T(8,128)(2,1)S(1)} %east.1.east_ref, bf16[16,64,1024]{2,1,0:T(8,128)(2,1)S(1)} %north.1.north_ref), custom_call_target="tpu_custom_call" | custom-call | flops 1000000000 | bytes 5242880 | tf_op jit(solution)/shard_map/degrid/pallas_call | solution.py:436
  47.5 0.0 collective-permute-done.3.came_2_ref.refs_3_
  47.5 0.0 collective-permute-done.4.came_3_ref.refs_4_
  47.5 1.3 %grid.1.refs_0_ = bf16[256,128]{1,0:T(8,128)(2,1)S(1)} custom-call(s32[16,128]{1,0:T(8,128)S(1)} %get-tuple-element.52.pick_ref, bf16[16,2048]{1,0:T(8,128)(2,1)S(1)} %bitcast.8, bf16[16,2048]{1,0:T(8,128)(2,1)S(1)} %collective-permute-done.1.other_ref.refs_1_, bf16[16,2048]{1,0:T(8,128)(2,1)S(1)} %collective-permute-done.2.came_1_ref.refs_2_, ...), custom_call_target="tpu_custom_call" | custom-call | flops 1000000000 | bytes 5242880 | tf_op jit(solution)/shard_map/grid/pallas_call | solution.py:448
  48.8 4.8 %collective-permute-start.9 = (bf16[256,128]{1,0:T(8,128)(2,1)S(1)}, bf16[256,128]{1,0:T(8,128)(2,1)S(1)}, u32[]{:S(2)}, u32[]{:S(2)}) collective-permute-start(bf16[256,128]{1,0:T(8,128)(2,1)S(1)} %grid.1.refs_0_), channel_id=1, source_target_pairs={{0,32},{32,0},{1,33},{33,1},{2,34},{34,2},{3,35},{35,3},{4,36},{36... | collective-permute-start | bytes 196616 | tf_op jit(solution)/shard_map/grid_gather/ppermute | solution.py:328
  53.6 1.5 %collective-permute-start.12 = (bf16[256,128]{1,0:T(8,128)(2,1)S(1)}, bf16[256,128]{1,0:T(8,128)(2,1)S(1)}, u32[]{:S(2)}, u32[]{:S(2)}) collective-permute-start(bf16[256,128]{1,0:T(8,128)(2,1)S(1)} %grid.1.refs_0_), channel_id=1, source_target_pairs={{0,128},{64,192},{128,0},{192,64},{1,129},{65,193},{129,1},{193,65... | collective-permute-start | bytes 196616 | tf_op jit(solution)/shard_map/grid_gather/ppermute | solution.py:328
  55.2 1.1 %collective-permute-start.14 = (bf16[256,128]{1,0:T(8,128)(2,1)S(1)}, bf16[256,128]{1,0:T(8,128)(2,1)S(1)}, u32[]{:S(2)}, u32[]{:S(2)}) collective-permute-start(bf16[256,128]{1,0:T(8,128)(2,1)S(1)} %grid.1.refs_0_), channel_id=1, source_target_pairs={{0,192},{64,0},{128,64},{192,128},{1,193},{65,1},{129,65},{193,129... | collective-permute-start | bytes 196616 | tf_op jit(solution)/shard_map/grid_gather/ppermute | solution.py:328
  56.3 0.6 collective-permute-start.11
  56.9 2.1 %collective-permute-start.13 = (bf16[256,128]{1,0:T(8,128)(2,1)S(1)}, bf16[256,128]{1,0:T(8,128)(2,1)S(1)}, u32[]{:S(2)}, u32[]{:S(2)}) collective-permute-start(bf16[256,128]{1,0:T(8,128)(2,1)S(1)} %collective-permute-done.9.refs_1_), channel_id=1, source_target_pairs={{0,128},{64,192},{128,0},{192,64},{1,129},{65,193},{129,1},{193,65... | collective-permute-start | bytes 196616 | tf_op jit(solution)/shard_map/grid_gather/ppermute | solution.py:328
  59.0 1.7 %collective-permute-start.15 = (bf16[256,128]{1,0:T(8,128)(2,1)S(1)}, bf16[256,128]{1,0:T(8,128)(2,1)S(1)}, u32[]{:S(2)}, u32[]{:S(2)}) collective-permute-start(bf16[256,128]{1,0:T(8,128)(2,1)S(1)} %collective-permute-done.9.refs_1_), channel_id=1, source_target_pairs={{0,192},{64,0},{128,64},{192,128},{1,193},{65,1},{129,65},{193,129... | collective-permute-start | bytes 196616 | tf_op jit(solution)/shard_map/grid_gather/ppermute | solution.py:328
  60.8 0.7 residual.1
  61.5 0.0 collective-permute-done.11.refs_3_
  61.5 0.6 collective-permute-done.13.refs_5_
  62.1 0.7 collective-permute-done.15.refs_7_
  62.8 0.5 regrid_far.1
  63.3 4.8 %collective-permute-start.16 = (f32[64,2048]{1,0:T(8,128)S(1)}, f32[64,2048]{1,0:T(8,128)S(1)}, u32[]{:S(2)}, u32[]{:S(2)}) collective-permute-start(f32[64,2048]{1,0:T(8,128)S(1)} %regrid_far.1), channel_id=1, source_target_pairs={{0,1},{1,0},{2,3},{3,2},{4,5},{5,4},{6,7},{7,6},{8,9},{9,8},{10,11... | collective-permute-start | bytes 1572872 | tf_op jit(solution)/shard_map/dirty_scatter/ppermute | solution.py:328
  68.0 0.5 regrid_near.1
  68.5 1.1 %collective-permute-done.16 = f32[64,2048]{1,0:T(8,128)S(1)} collective-permute-done((f32[64,2048]{1,0:T(8,128)S(1)}, f32[64,2048]{1,0:T(8,128)S(1)}, u32[]{:S(2)}, u32[]{:S(2)}) %collective-permute-start.16) | collective-permute-done | bytes 524320 | tf_op jit(solution)/shard_map/dirty_scatter/ppermute | solution.py:328
  69.6 0.1 add_convert_fusion
  69.6 0.1 reshape.12
  69.7 12.6 %all_to_all.10 = bf16[16,4,2048]{2,1,0:T(4,128)(2,1)S(1)} all-to-all(bf16[16,4,2048]{2,1,0:T(4,128)(2,1)S(1)} %reshape.12), channel_id=1, replica_groups=mesh['y'=4,'h'=2,'x'=4,'z'=4,'c'=2] {'x','z'}, dimensions={0} | all-to-all | bytes 524288 | tf_op jit(solution)/shard_map/dirty_scatter/all_to_all | solution.py:498
  82.4 0.7 convert_reduce_fusion
  (22 shorter events, 0.0 us)
Async XLA Ops:
  2.2 22.2 %copy-start.1 = (s32[8,16]{1,0:T(8,128)S(1)}, s32[8,16]{1,0:T(8,128)}, u32[]{:S(2)}) copy-start(s32[8,16]{1,0:T(8,128)} %subgrid_ref.3) | copy-start | bytes 1540
  2.2 18.8 %all-to-all-start = ((bf16[16,4,2048]{2,1,0:T(4,128)(2,1)}), bf16[16,4,2048]{2,1,0:T(4,128)(2,1)S(1)}, u32[]{:S(2)}, u32[]{:S(2)}) async-start(bf16[16,4,2048]{2,1,0:T(4,128)(2,1)} %broadcast_in_dim.14), calls=%async_computation | async-start | bytes 524288 | tf_op jit(solution)/shard_map/model_gather/all_to_all | solution.py:359
  11.3 1.6 %copy-start.3 = (bf16[1,512,2048]{2,1,0:T(8,128)(2,1)S(1)}, bf16[1,512,2048]{2,1,0:T(8,128)(2,1)}, u32[]{:S(2)}) copy-start(bf16[1,512,2048]{2,1,0:T(8,128)(2,1)} %param.17) | copy-start | bytes 6291460
  12.9 0.9 %copy-start.4 = (f32[32,1024]{1,0:T(8,128)S(1)}, f32[32,1024]{1,0:T(8,128)}, u32[]{:S(2)}) copy-start(f32[32,1024]{1,0:T(8,128)} %phase_from.1) | copy-start | bytes 393220
  13.8 0.7 copy-start.5
  14.5 0.7 copy-start.7
  15.2 14.8 %copy-start = (bf16[1,16,2048]{2,1,0:T(8,128)(2,1)S(1)}, bf16[1,16,2048]{2,1,0:T(8,128)(2,1)}, u32[]{:S(2)}) copy-start(bf16[1,16,2048]{2,1,0:T(8,128)(2,1)} %param.10) | copy-start | bytes 196612
  15.2 19.0 %copy-start.6 = (f32[8,2,16]{2,1,0:T(2,128)S(1)}, f32[8,2,16]{2,1,0:T(2,128)}, u32[]{:S(2)}) copy-start(f32[8,2,16]{2,1,0:T(2,128)} %coords_ref.1) | copy-start | bytes 3076
  15.2 19.0 %copy-start.8 = (f32[1024]{0:T(1024)S(1)}, f32[1024]{0:T(1024)}, u32[]{:S(2)}) copy-start(f32[1024]{0:T(1024)} %param.19) | copy-start | bytes 12292
  21.0 3.3 %collective-permute-start = (bf16[16,4,2048]{2,1,0:T(4,128)(2,1)S(1)}, bf16[16,4,2048]{2,1,0:T(4,128)(2,1)S(1)}, u32[]{:S(2)}, u32[]{:S(2)}) collective-permute-start(bf16[16,4,2048]{2,1,0:T(4,128)(2,1)S(1)} %all-to-all-done.near_ref), channel_id=1, source_target_pairs={{0,1},{1,0},{2,3},{3,2},{4,5},{5,4},{6,7},{7,6},{8,9},{9,8},{10,11... | collective-permute-start | bytes 786440 | tf_op jit(solution)/shard_map/ppermute | solution.py:328
  24.9 10.6 %collective-permute-start.5 = (bf16[2,256,128]{2,1,0:T(8,128)(2,1)S(1)}, bf16[2,256,128]{2,1,0:T(8,128)(2,1)S(1)}, u32[]{:S(2)}, u32[]{:S(2)}) collective-permute-start(bf16[2,256,128]{2,1,0:T(8,128)(2,1)S(1)} %get-tuple-element.44), channel_id=1, source_target_pairs={{0,64},{64,128},{128,192},{192,0},{1,65},{65,129},{129,193},{193,1... | collective-permute-start | bytes 393224 | tf_op jit(solution)/shard_map/image_sum/ppermute | solution.py:328
  26.3 9.3 %collective-permute-start.6 = (bf16[2,256,128]{2,1,0:T(8,128)(2,1)S(1)}, bf16[2,256,128]{2,1,0:T(8,128)(2,1)S(1)}, u32[]{:S(2)}, u32[]{:S(2)}) collective-permute-start(bf16[2,256,128]{2,1,0:T(8,128)(2,1)S(1)} %get-tuple-element.45), channel_id=1, source_target_pairs={{0,128},{64,192},{128,0},{192,64},{1,129},{65,193},{129,1},{193,65... | collective-permute-start | bytes 393224 | tf_op jit(solution)/shard_map/image_sum/ppermute | solution.py:328
  28.9 6.6 %collective-permute-start.7 = (bf16[2,256,128]{2,1,0:T(8,128)(2,1)S(1)}, bf16[2,256,128]{2,1,0:T(8,128)(2,1)S(1)}, u32[]{:S(2)}, u32[]{:S(2)}) collective-permute-start(bf16[2,256,128]{2,1,0:T(8,128)(2,1)S(1)} %get-tuple-element.46), channel_id=1, source_target_pairs={{0,192},{64,0},{128,64},{192,128},{1,193},{65,1},{129,65},{193,129... | collective-permute-start | bytes 393224 | tf_op jit(solution)/shard_map/image_sum/ppermute | solution.py:328
  30.0 9.4 %collective-permute-start.1 = (bf16[16,2048]{1,0:T(8,128)(2,1)S(1)}, bf16[16,2048]{1,0:T(8,128)(2,1)S(1)}, u32[]{:S(2)}, u32[]{:S(2)}) collective-permute-start(bf16[16,2048]{1,0:T(8,128)(2,1)S(1)} %bitcast.6), channel_id=1, source_target_pairs={{0,32},{32,0},{1,33},{33,1},{2,34},{34,2},{3,35},{35,3},{4,36},{36... | collective-permute-start | bytes 196616 | tf_op jit(solution)/shard_map/visible_route/ppermute | solution.py:328
  34.2 5.1 %copy-start.2 = (s32[1,8]{1,0:T(1,128)S(1)}, s32[1,8]{1,0:T(1,128)}, u32[]{:S(2)}) copy-start(s32[1,8]{1,0:T(1,128)} %reader_ref.1) | copy-start | bytes 100
  35.6 10.1 %collective-permute-start.8 = (f32[256,128]{1,0:T(8,128)S(1)}, f32[256,128]{1,0:T(8,128)S(1)}, u32[]{:S(2)}, u32[]{:S(2)}) collective-permute-start(f32[256,128]{1,0:T(8,128)S(1)} %get-tuple-element.49), channel_id=1, source_target_pairs={{0,32},{32,0},{1,33},{33,1},{2,34},{34,2},{3,35},{35,3},{4,36},{36... | collective-permute-start | bytes 393224 | tf_op jit(solution)/shard_map/image_sum/ppermute | solution.py:328
  40.0 7.5 %collective-permute-start.2 = (bf16[16,2048]{1,0:T(8,128)(2,1)S(1)}, bf16[16,2048]{1,0:T(8,128)(2,1)S(1)}, u32[]{:S(2)}, u32[]{:S(2)}) collective-permute-start(bf16[16,2048]{1,0:T(8,128)(2,1)S(1)} %get-tuple-element.38), channel_id=1, source_target_pairs={{0,64},{64,128},{128,192},{192,0},{1,65},{65,129},{129,193},{193,1... | collective-permute-start | bytes 196616 | tf_op jit(solution)/shard_map/ppermute | solution.py:328
  41.0 6.5 %collective-permute-start.3 = (bf16[16,2048]{1,0:T(8,128)(2,1)S(1)}, bf16[16,2048]{1,0:T(8,128)(2,1)S(1)}, u32[]{:S(2)}, u32[]{:S(2)}) collective-permute-start(bf16[16,2048]{1,0:T(8,128)(2,1)S(1)} %get-tuple-element.39), channel_id=1, source_target_pairs={{0,128},{64,192},{128,0},{192,64},{1,129},{65,193},{129,1},{193,65... | collective-permute-start | bytes 196616 | tf_op jit(solution)/shard_map/ppermute | solution.py:328
  43.2 4.3 %collective-permute-start.4 = (bf16[16,2048]{1,0:T(8,128)(2,1)S(1)}, bf16[16,2048]{1,0:T(8,128)(2,1)S(1)}, u32[]{:S(2)}, u32[]{:S(2)}) collective-permute-start(bf16[16,2048]{1,0:T(8,128)(2,1)S(1)} %get-tuple-element.40), channel_id=1, source_target_pairs={{0,192},{64,0},{128,64},{192,128},{1,193},{65,1},{129,65},{193,129... | collective-permute-start | bytes 196616 | tf_op jit(solution)/shard_map/ppermute | solution.py:328
  48.8 7.5 %collective-permute-start.9 = (bf16[256,128]{1,0:T(8,128)(2,1)S(1)}, bf16[256,128]{1,0:T(8,128)(2,1)S(1)}, u32[]{:S(2)}, u32[]{:S(2)}) collective-permute-start(bf16[256,128]{1,0:T(8,128)(2,1)S(1)} %grid.1.refs_0_), channel_id=1, source_target_pairs={{0,32},{32,0},{1,33},{33,1},{2,34},{34,2},{3,35},{35,3},{4,36},{36... | collective-permute-start | bytes 196616 | tf_op jit(solution)/shard_map/grid_gather/ppermute | solution.py:328
  53.6 5.4 %collective-permute-start.10 = (bf16[256,128]{1,0:T(8,128)(2,1)S(1)}, bf16[256,128]{1,0:T(8,128)(2,1)S(1)}, u32[]{:S(2)}, u32[]{:S(2)}) collective-permute-start(bf16[256,128]{1,0:T(8,128)(2,1)S(1)} %grid.1.refs_0_), channel_id=1, source_target_pairs={{0,64},{64,128},{128,192},{192,0},{1,65},{65,129},{129,193},{193,1... | collective-permute-start | bytes 196616 | tf_op jit(solution)/shard_map/grid_gather/ppermute | solution.py:328
  53.6 7.8 %collective-permute-start.12 = (bf16[256,128]{1,0:T(8,128)(2,1)S(1)}, bf16[256,128]{1,0:T(8,128)(2,1)S(1)}, u32[]{:S(2)}, u32[]{:S(2)}) collective-permute-start(bf16[256,128]{1,0:T(8,128)(2,1)S(1)} %grid.1.refs_0_), channel_id=1, source_target_pairs={{0,128},{64,192},{128,0},{192,64},{1,129},{65,193},{129,1},{193,65... | collective-permute-start | bytes 196616 | tf_op jit(solution)/shard_map/grid_gather/ppermute | solution.py:328
  55.2 6.3 %collective-permute-start.14 = (bf16[256,128]{1,0:T(8,128)(2,1)S(1)}, bf16[256,128]{1,0:T(8,128)(2,1)S(1)}, u32[]{:S(2)}, u32[]{:S(2)}) collective-permute-start(bf16[256,128]{1,0:T(8,128)(2,1)S(1)} %grid.1.refs_0_), channel_id=1, source_target_pairs={{0,192},{64,0},{128,64},{192,128},{1,193},{65,1},{129,65},{193,129... | collective-permute-start | bytes 196616 | tf_op jit(solution)/shard_map/grid_gather/ppermute | solution.py:328
  56.3 5.2 %collective-permute-start.11 = (bf16[256,128]{1,0:T(8,128)(2,1)S(1)}, bf16[256,128]{1,0:T(8,128)(2,1)S(1)}, u32[]{:S(2)}, u32[]{:S(2)}) collective-permute-start(bf16[256,128]{1,0:T(8,128)(2,1)S(1)} %collective-permute-done.9.refs_1_), channel_id=1, source_target_pairs={{0,64},{64,128},{128,192},{192,0},{1,65},{65,129},{129,193},{193,1... | collective-permute-start | bytes 196616 | tf_op jit(solution)/shard_map/grid_gather/ppermute | solution.py:328
  56.9 5.2 %collective-permute-start.13 = (bf16[256,128]{1,0:T(8,128)(2,1)S(1)}, bf16[256,128]{1,0:T(8,128)(2,1)S(1)}, u32[]{:S(2)}, u32[]{:S(2)}) collective-permute-start(bf16[256,128]{1,0:T(8,128)(2,1)S(1)} %collective-permute-done.9.refs_1_), channel_id=1, source_target_pairs={{0,128},{64,192},{128,0},{192,64},{1,129},{65,193},{129,1},{193,65... | collective-permute-start | bytes 196616 | tf_op jit(solution)/shard_map/grid_gather/ppermute | solution.py:328
  59.0 3.7 %collective-permute-start.15 = (bf16[256,128]{1,0:T(8,128)(2,1)S(1)}, bf16[256,128]{1,0:T(8,128)(2,1)S(1)}, u32[]{:S(2)}, u32[]{:S(2)}) collective-permute-start(bf16[256,128]{1,0:T(8,128)(2,1)S(1)} %collective-permute-done.9.refs_1_), channel_id=1, source_target_pairs={{0,192},{64,0},{128,64},{192,128},{1,193},{65,1},{129,65},{193,129... | collective-permute-start | bytes 196616 | tf_op jit(solution)/shard_map/grid_gather/ppermute | solution.py:328
  63.3 6.3 %collective-permute-start.16 = (f32[64,2048]{1,0:T(8,128)S(1)}, f32[64,2048]{1,0:T(8,128)S(1)}, u32[]{:S(2)}, u32[]{:S(2)}) collective-permute-start(f32[64,2048]{1,0:T(8,128)S(1)} %regrid_far.1), channel_id=1, source_target_pairs={{0,1},{1,0},{2,3},{3,2},{4,5},{5,4},{6,7},{7,6},{8,9},{9,8},{10,11... | collective-permute-start | bytes 1572872 | tf_op jit(solution)/shard_map/dirty_scatter/ppermute | solution.py:328

commit v8 on v7

--- a/solution.py
+++ b/solution.py
@@ -220,11 +220,10 @@
         image = jnp.concatenate([spread(cells[0:8], -cells[8:16]), spread(cells[8:16], cells[0:8])], axis=0)
         high = image.astype(BF16)
         low = (image - high.astype(F32)).astype(BF16)
-        operand = jnp.concatenate([high, low], axis=1)
         for at in range(0, channels, width):
             chans = pl.ds(at, width)
             north = north_ref[b, :, chans]
-            inner = jnp.dot(operand, jnp.concatenate([north, north], axis=0), preferred_element_type=F32)
+            inner = jnp.dot(high, north, preferred_element_type=F32) + jnp.dot(low, north, preferred_element_type=F32)
             inner_re, inner_im = (inner[:32], inner[32:])
             east = east_ref[b, :, chans].astype(F32)
             cos, sin = (east[:32], east[32:])
@@ -267,7 +266,7 @@
     residual_kernel(
         pick_ref, rows_ref, other_ref, came_1_ref, came_2_ref, came_3_ref, predicted_ref, resid_ref
     )
-    width = 256
+    width = 512
 
     def grid(b):
         products = jnp.zeros((64, 64), F32)
@@ -319,8 +318,8 @@
         high = value.astype(BF16)
         low = (value - high.astype(F32)).astype(BF16)
         both = jnp.dot(sums, jnp.concatenate([high, low], axis=0), preferred_element_type=F32)
-        sum_ref[:, re] = both[:, :128]
-        sum_ref[:, im] = both[:, 128:]
+        sum_ref[:, re] = both[:, :128].astype(sum_ref.dtype)
+        sum_ref[:, im] = both[:, 128:].astype(sum_ref.dtype)
 
 
 def shift(value, axis, by):
@@ -480,7 +479,7 @@
     def regrid(other, subgrids):
         return pl.pallas_call(
             functools.partial(regrid_kernel, grid_scale, n_y, n_h, n_c, owned, other),
-            out_shape=jax.ShapeDtypeStruct((half, 2 * pixels), F32),
+            out_shape=jax.ShapeDtypeStruct((half, 2 * pixels), (F32, BF16)[other]),
             in_specs=[VMEM] * (2 + n_facet),
             out_specs=VMEM,
             compiler_params=params(8),
@@ -494,7 +493,7 @@
     near_sum = regrid(0, subgrids)
 
     with jax.named_scope("dirty_scatter"):
-        chip_sum = (near_sum + shift(far_sum, "c", 1)).astype(BF16).reshape(n_x * n_z, owned, 2 * pixels)
+        chip_sum = (near_sum + shift(far_sum, "c", 1).astype(F32)).astype(BF16).reshape(n_x * n_z, owned, 2 * pixels)
         chips = lax.all_to_all(chip_sum, ("x", "z"), split_axis=0, concat_axis=0, tiled=True)
         dirty = jnp.sum(chips.astype(F32), axis=0)
     return (residual[None], dirty[None])

time: 83.6 us -> 83.2 us (level)
  no operation moved by 1% of the time
where the time goes in v8:
time: 83.2 us; the launch traced here: 82.7 us
  starting transfers between devices  45.3 us (54%)
  blocking collectives  12.6 us (15%)
  Pallas kernels  11.1 us (13%)
  waiting for transfers between devices  6.6 us (8%)
  local copies, waits for them, and re-layouts  5.53 us (7%)
    ppermute x17, starting transfers between devices, shift(): lax.ppermute(value, axis, [(i, (i + by) % size) for i in range(size)])  36.2 us
    all_to_all x1, blocking collectives, local(): lax.all_to_all(chip_sum, ('x', 'z'), split_axis=0, concat_axis=0, tiled=T...  12.6 us
    all_to_all x1, starting transfers between devices, local(): lax.all_to_all(copies, ('x', 'z'), split_axis=0, concat_axis=0, tiled=True)  9.15 us
    unnamed x18, local copies, waits for them, and re-layouts  3.89 us
    all_to_all x1, waiting for transfers between devices, local(): lax.all_to_all(copies, ('x', 'z'), split_axis=0, concat_axis=0, tiled=True)  3.44 us
    ppermute x17, waiting for transfers between devices, shift(): lax.ppermute(value, axis, [(i, (i + by) % size) for i in range(size)])  3.16 us
    pallas_call x2, Pallas kernels, table(): pl.pallas_call(functools.partial(table_kernel, n_h, kind), out_shape=jax....  2.94 us
    pallas_call x1, Pallas kernels, local(): pl.pallas_call(screen_kernel, out_shape=jax.ShapeDtypeStruct((count, 2 *...  2.35 us
  transfers between devices with their start and end apart: 18, of which 5 were waited for; matrix products, arithmetic and copies ran while one was open for 0% of the time, Pallas kernels for 11%

profile of v8, /device:TPU:1, one launch (start us, length us, event | category | flops | bytes accessed | tf_op | source)
XLA Modules:
  0.0 82.7 jit_solution(3259541852564791026)
XLA Ops:
  0.6 1.5 %broadcast_in_dim.14 = bf16[16,4,2048]{2,1,0:T(4,128)(2,1)} broadcast(bf16[4,2048]{1,0:T(4,128)(2,1)} %bitcast.15), dimensions={1,2} | broadcast | bytes 278528 | tf_op jit(solution)/shard_map/model_gather/broadcast_in_dim | solution.py:357
  2.2 9.1 %all-to-all-start = ((bf16[16,4,2048]{2,1,0:T(4,128)(2,1)}), bf16[16,4,2048]{2,1,0:T(4,128)(2,1)S(1)}, u32[]{:S(2)}, u32[]{:S(2)}) async-start(bf16[16,4,2048]{2,1,0:T(4,128)(2,1)} %broadcast_in_dim.14), calls=%async_computation | async-start | bytes 524288 | tf_op jit(solution)/shard_map/model_gather/all_to_all | solution.py:358
  11.3 0.0 copy-start.3
  11.3 1.6 %copy-done.3 = bf16[1,512,2048]{2,1,0:T(8,128)(2,1)S(1)} copy-done((bf16[1,512,2048]{2,1,0:T(8,128)(2,1)S(1)}, bf16[1,512,2048]{2,1,0:T(8,128)(2,1)}, u32[]{:S(2)}) %copy-start.3) | copy-done | bytes 2097176
  12.9 0.9 %copy-done.4 = f32[32,1024]{1,0:T(8,128)S(1)} copy-done((f32[32,1024]{1,0:T(8,128)S(1)}, f32[32,1024]{1,0:T(8,128)}, u32[]{:S(2)}) %copy-start.4) | copy-done | bytes 131096
  13.8 0.7 copy-done.5
  14.5 0.7 copy-done.7
  15.2 2.3 %screens.1.screen_ref = f32[128,2048]{1,0:T(8,128)S(1)} custom-call(s32[8,2,16]{2,1,0:T(2,128)S(1)} %copy-done.5, s32[8,16]{1,0:T(8,128)S(1)} %copy-done.7, f32[32,1024]{1,0:T(8,128)S(1)} %copy-done.4, bf16[512,2048]{1,0:T(8,128)(2,1)S(1)} %bitcast.10), custom_call_target="tpu_custom_call" | custom-call | flops 1000000000 | bytes 4194304 | tf_op jit(solution)/shard_map/screens/pallas_call | solution.py:361
  17.6 3.4 %all-to-all-done.near_ref = bf16[16,4,2048]{2,1,0:T(4,128)(2,1)S(1)} async-done(((bf16[16,4,2048]{2,1,0:T(4,128)(2,1)}), bf16[16,4,2048]{2,1,0:T(4,128)(2,1)S(1)}, u32[]{:S(2)}, u32[]{:S(2)}) %all-to-all-start) | async-done | bytes 262176 | tf_op jit(solution)/shard_map/model_gather/all_to_all | solution.py:358
  21.0 2.1 %collective-permute-start = (bf16[16,4,2048]{2,1,0:T(4,128)(2,1)S(1)}, bf16[16,4,2048]{2,1,0:T(4,128)(2,1)S(1)}, u32[]{:S(2)}, u32[]{:S(2)}) collective-permute-start(bf16[16,4,2048]{2,1,0:T(4,128)(2,1)S(1)} %all-to-all-done.near_ref), channel_id=1, source_target_pairs={{0,1},{1,0},{2,3},{3,2},{4,5},{5,4},{6,7},{7,6},{8,9},{9,8},{10,11... | collective-permute-start | bytes 786440 | tf_op jit(solution)/shard_map/ppermute | solution.py:327
  23.2 1.2 %collective-permute-done.far_ref = bf16[16,4,2048]{2,1,0:T(4,128)(2,1)S(1)} collective-permute-done((bf16[16,4,2048]{2,1,0:T(4,128)(2,1)S(1)}, bf16[16,4,2048]{2,1,0:T(4,128)(2,1)S(1)}, u32[]{:S(2)}, u32[]{:S(2)}) %collective-permute-start) | collective-permute-done | bytes 262176 | tf_op jit(solution)/shard_map/ppermute | solution.py:327
  24.3 0.6 images.1
  24.9 1.4 %collective-permute-start.5 = (bf16[2,256,128]{2,1,0:T(8,128)(2,1)S(1)}, bf16[2,256,128]{2,1,0:T(8,128)(2,1)S(1)}, u32[]{:S(2)}, u32[]{:S(2)}) collective-permute-start(bf16[2,256,128]{2,1,0:T(8,128)(2,1)S(1)} %get-tuple-element.44), channel_id=1, source_target_pairs={{0,64},{64,128},{128,192},{192,0},{1,65},{65,129},{129,193},{193,1... | collective-permute-start | bytes 393224 | tf_op jit(solution)/shard_map/image_sum/ppermute | solution.py:327
  26.3 2.6 %collective-permute-start.6 = (bf16[2,256,128]{2,1,0:T(8,128)(2,1)S(1)}, bf16[2,256,128]{2,1,0:T(8,128)(2,1)S(1)}, u32[]{:S(2)}, u32[]{:S(2)}) collective-permute-start(bf16[2,256,128]{2,1,0:T(8,128)(2,1)S(1)} %get-tuple-element.45), channel_id=1, source_target_pairs={{0,128},{64,192},{128,0},{192,64},{1,129},{65,193},{129,1},{193,65... | collective-permute-start | bytes 393224 | tf_op jit(solution)/shard_map/image_sum/ppermute | solution.py:327
  28.9 1.1 %collective-permute-start.7 = (bf16[2,256,128]{2,1,0:T(8,128)(2,1)S(1)}, bf16[2,256,128]{2,1,0:T(8,128)(2,1)S(1)}, u32[]{:S(2)}, u32[]{:S(2)}) collective-permute-start(bf16[2,256,128]{2,1,0:T(8,128)(2,1)S(1)} %get-tuple-element.46), channel_id=1, source_target_pairs={{0,192},{64,0},{128,64},{192,128},{1,193},{65,1},{129,65},{193,129... | collective-permute-start | bytes 393224 | tf_op jit(solution)/shard_map/image_sum/ppermute | solution.py:327
  30.0 4.2 %collective-permute-start.1 = (bf16[16,2048]{1,0:T(8,128)(2,1)S(1)}, bf16[16,2048]{1,0:T(8,128)(2,1)S(1)}, u32[]{:S(2)}, u32[]{:S(2)}) collective-permute-start(bf16[16,2048]{1,0:T(8,128)(2,1)S(1)} %bitcast.6), channel_id=1, source_target_pairs={{0,32},{32,0},{1,33},{33,1},{2,34},{34,2},{3,35},{35,3},{4,36},{36... | collective-permute-start | bytes 196616 | tf_op jit(solution)/shard_map/visible_route/ppermute | solution.py:327
  34.2 1.3 %north.1.north_ref = bf16[16,64,1024]{2,1,0:T(8,128)(2,1)S(1)} custom-call(f32[8,2,16]{2,1,0:T(2,128)S(1)} %copy-done.6, f32[1,1024]{1,0:T(1,128)S(1)} %bitcast.11), custom_call_target="tpu_custom_call" | custom-call | flops 1000000000 | bytes 4194304 | tf_op jit(solution)/shard_map/image_sum/north/pallas_call | solution.py:400
  35.6 0.0 collective-permute-done.7.refs_3_
  35.6 0.1 image_sums.1
  35.6 3.7 %collective-permute-start.8 = (f32[256,128]{1,0:T(8,128)S(1)}, f32[256,128]{1,0:T(8,128)S(1)}, u32[]{:S(2)}, u32[]{:S(2)}) collective-permute-start(f32[256,128]{1,0:T(8,128)S(1)} %get-tuple-element.49), channel_id=1, source_target_pairs={{0,32},{32,0},{1,33},{33,1},{2,34},{34,2},{3,35},{35,3},{4,36},{36... | collective-permute-start | bytes 393224 | tf_op jit(solution)/shard_map/image_sum/ppermute | solution.py:327
  39.3 0.0 collective-permute-done.1.other_ref.refs_1_
  39.3 0.6 route.1
  40.0 1.0 %collective-permute-start.2 = (bf16[16,2048]{1,0:T(8,128)(2,1)S(1)}, bf16[16,2048]{1,0:T(8,128)(2,1)S(1)}, u32[]{:S(2)}, u32[]{:S(2)}) collective-permute-start(bf16[16,2048]{1,0:T(8,128)(2,1)S(1)} %get-tuple-element.38), channel_id=1, source_target_pairs={{0,64},{64,128},{128,192},{192,0},{1,65},{65,129},{129,193},{193,1... | collective-permute-start | bytes 196616 | tf_op jit(solution)/shard_map/ppermute | solution.py:327
  41.0 2.2 %collective-permute-start.3 = (bf16[16,2048]{1,0:T(8,128)(2,1)S(1)}, bf16[16,2048]{1,0:T(8,128)(2,1)S(1)}, u32[]{:S(2)}, u32[]{:S(2)}) collective-permute-start(bf16[16,2048]{1,0:T(8,128)(2,1)S(1)} %get-tuple-element.39), channel_id=1, source_target_pairs={{0,128},{64,192},{128,0},{192,64},{1,129},{65,193},{129,1},{193,65... | collective-permute-start | bytes 196616 | tf_op jit(solution)/shard_map/ppermute | solution.py:327
  43.2 0.9 %collective-permute-start.4 = (bf16[16,2048]{1,0:T(8,128)(2,1)S(1)}, bf16[16,2048]{1,0:T(8,128)(2,1)S(1)}, u32[]{:S(2)}, u32[]{:S(2)}) collective-permute-start(bf16[16,2048]{1,0:T(8,128)(2,1)S(1)} %get-tuple-element.40), channel_id=1, source_target_pairs={{0,192},{64,0},{128,64},{192,128},{1,193},{65,1},{129,65},{193,129... | collective-permute-start | bytes 196616 | tf_op jit(solution)/shard_map/ppermute | solution.py:327
  44.1 1.6 %east.1.east_ref = bf16[16,64,1024]{2,1,0:T(8,128)(2,1)S(1)} custom-call(f32[8,2,16]{2,1,0:T(2,128)S(1)} %copy-done.6, f32[1,1024]{1,0:T(1,128)S(1)} %bitcast.12), custom_call_target="tpu_custom_call" | custom-call | flops 1000000000 | bytes 4194304 | tf_op jit(solution)/shard_map/east/pallas_call | solution.py:400
  45.8 1.6 %degrid.1.predicted_ref.refs_5_ = f32[16,2048]{1,0:T(8,128)S(1)} custom-call(f32[256,128]{1,0:T(8,128)S(1)} %get-tuple-element.48.near_ref, f32[256,128]{1,0:T(8,128)S(1)} %collective-permute-done.8.far_ref, bf16[16,64,1024]{2,1,0:T(8,128)(2,1)S(1)} %east.1.east_ref, bf16[16,64,1024]{2,1,0:T(8,128)(2,1)S(1)} %north.1.north_ref), custom_call_target="tpu_custom_call" | custom-call | flops 1000000000 | bytes 5242880 | tf_op jit(solution)/shard_map/degrid/pallas_call | solution.py:435
  47.4 0.0 collective-permute-done.3.came_2_ref.refs_3_
  47.4 0.0 collective-permute-done.4.came_3_ref.refs_4_
  47.4 1.2 %grid.1.refs_0_ = bf16[256,128]{1,0:T(8,128)(2,1)S(1)} custom-call(s32[16,128]{1,0:T(8,128)S(1)} %get-tuple-element.52.pick_ref, bf16[16,2048]{1,0:T(8,128)(2,1)S(1)} %bitcast.8, bf16[16,2048]{1,0:T(8,128)(2,1)S(1)} %collective-permute-done.1.other_ref.refs_1_, bf16[16,2048]{1,0:T(8,128)(2,1)S(1)} %collective-permute-done.2.came_1_ref.refs_2_, ...), custom_call_target="tpu_custom_call" | custom-call | flops 1000000000 | bytes 5242880 | tf_op jit(solution)/shard_map/grid/pallas_call | solution.py:447
  48.6 4.8 %collective-permute-start.9 = (bf16[256,128]{1,0:T(8,128)(2,1)S(1)}, bf16[256,128]{1,0:T(8,128)(2,1)S(1)}, u32[]{:S(2)}, u32[]{:S(2)}) collective-permute-start(bf16[256,128]{1,0:T(8,128)(2,1)S(1)} %grid.1.refs_0_), channel_id=1, source_target_pairs={{0,32},{32,0},{1,33},{33,1},{2,34},{34,2},{3,35},{35,3},{4,36},{36... | collective-permute-start | bytes 196616 | tf_op jit(solution)/shard_map/grid_gather/ppermute | solution.py:327
  53.5 1.5 %collective-permute-start.12 = (bf16[256,128]{1,0:T(8,128)(2,1)S(1)}, bf16[256,128]{1,0:T(8,128)(2,1)S(1)}, u32[]{:S(2)}, u32[]{:S(2)}) collective-permute-start(bf16[256,128]{1,0:T(8,128)(2,1)S(1)} %grid.1.refs_0_), channel_id=1, source_target_pairs={{0,128},{64,192},{128,0},{192,64},{1,129},{65,193},{129,1},{193,65... | collective-permute-start | bytes 196616 | tf_op jit(solution)/shard_map/grid_gather/ppermute | solution.py:327
  55.0 1.2 %collective-permute-start.14 = (bf16[256,128]{1,0:T(8,128)(2,1)S(1)}, bf16[256,128]{1,0:T(8,128)(2,1)S(1)}, u32[]{:S(2)}, u32[]{:S(2)}) collective-permute-start(bf16[256,128]{1,0:T(8,128)(2,1)S(1)} %grid.1.refs_0_), channel_id=1, source_target_pairs={{0,192},{64,0},{128,64},{192,128},{1,193},{65,1},{129,65},{193,129... | collective-permute-start | bytes 196616 | tf_op jit(solution)/shard_map/grid_gather/ppermute | solution.py:327
  56.2 0.6 collective-permute-start.11
  56.7 2.2 %collective-permute-start.13 = (bf16[256,128]{1,0:T(8,128)(2,1)S(1)}, bf16[256,128]{1,0:T(8,128)(2,1)S(1)}, u32[]{:S(2)}, u32[]{:S(2)}) collective-permute-start(bf16[256,128]{1,0:T(8,128)(2,1)S(1)} %collective-permute-done.9.refs_1_), channel_id=1, source_target_pairs={{0,128},{64,192},{128,0},{192,64},{1,129},{65,193},{129,1},{193,65... | collective-permute-start | bytes 196616 | tf_op jit(solution)/shard_map/grid_gather/ppermute | solution.py:327
  58.9 1.7 %collective-permute-start.15 = (bf16[256,128]{1,0:T(8,128)(2,1)S(1)}, bf16[256,128]{1,0:T(8,128)(2,1)S(1)}, u32[]{:S(2)}, u32[]{:S(2)}) collective-permute-start(bf16[256,128]{1,0:T(8,128)(2,1)S(1)} %collective-permute-done.9.refs_1_), channel_id=1, source_target_pairs={{0,192},{64,0},{128,64},{192,128},{1,193},{65,1},{129,65},{193,129... | collective-permute-start | bytes 196616 | tf_op jit(solution)/shard_map/grid_gather/ppermute | solution.py:327
  60.6 0.7 residual.1
  61.3 0.0 collective-permute-done.11.refs_3_
  61.3 0.6 collective-permute-done.13.refs_5_
  61.9 0.6 collective-permute-done.15.refs_7_
  62.6 0.5 regrid_far.1
  63.1 4.9 %collective-permute-start.16 = (bf16[64,2048]{1,0:T(8,128)(2,1)S(1)}, bf16[64,2048]{1,0:T(8,128)(2,1)S(1)}, u32[]{:S(2)}, u32[]{:S(2)}) collective-permute-start(bf16[64,2048]{1,0:T(8,128)(2,1)S(1)} %regrid_far.1), channel_id=1, source_target_pairs={{0,1},{1,0},{2,3},{3,2},{4,5},{5,4},{6,7},{7,6},{8,9},{9,8},{10,11... | collective-permute-start | bytes 786440 | tf_op jit(solution)/shard_map/dirty_scatter/ppermute | solution.py:327
  68.0 0.5 regrid_near.1
  68.5 0.7 collective-permute-done.16
  69.2 0.1 add_convert_fusion
  69.2 0.1 reshape.12
  69.3 12.6 %all_to_all.10 = bf16[16,4,2048]{2,1,0:T(4,128)(2,1)S(1)} all-to-all(bf16[16,4,2048]{2,1,0:T(4,128)(2,1)S(1)} %reshape.12), channel_id=1, replica_groups=mesh['y'=4,'h'=2,'x'=4,'z'=4,'c'=2] {'x','z'}, dimensions={0} | all-to-all | bytes 524288 | tf_op jit(solution)/shard_map/dirty_scatter/all_to_all | solution.py:497
  82.0 0.7 convert_reduce_fusion
  (22 shorter events, 0.0 us)
Async XLA Ops:
  2.2 22.2 %copy-start.1 = (s32[8,16]{1,0:T(8,128)S(1)}, s32[8,16]{1,0:T(8,128)}, u32[]{:S(2)}) copy-start(s32[8,16]{1,0:T(8,128)} %subgrid_ref.3) | copy-start | bytes 1540
  2.2 18.8 %all-to-all-start = ((bf16[16,4,2048]{2,1,0:T(4,128)(2,1)}), bf16[16,4,2048]{2,1,0:T(4,128)(2,1)S(1)}, u32[]{:S(2)}, u32[]{:S(2)}) async-start(bf16[16,4,2048]{2,1,0:T(4,128)(2,1)} %broadcast_in_dim.14), calls=%async_computation | async-start | bytes 524288 | tf_op jit(solution)/shard_map/model_gather/all_to_all | solution.py:358
  11.3 1.6 %copy-start.3 = (bf16[1,512,2048]{2,1,0:T(8,128)(2,1)S(1)}, bf16[1,512,2048]{2,1,0:T(8,128)(2,1)}, u32[]{:S(2)}) copy-start(bf16[1,512,2048]{2,1,0:T(8,128)(2,1)} %param.17) | copy-start | bytes 6291460
  12.9 0.9 %copy-start.4 = (f32[32,1024]{1,0:T(8,128)S(1)}, f32[32,1024]{1,0:T(8,128)}, u32[]{:S(2)}) copy-start(f32[32,1024]{1,0:T(8,128)} %phase_from.1) | copy-start | bytes 393220
  13.8 0.7 copy-start.5
  14.5 0.7 copy-start.7
  15.2 14.8 %copy-start = (bf16[1,16,2048]{2,1,0:T(8,128)(2,1)S(1)}, bf16[1,16,2048]{2,1,0:T(8,128)(2,1)}, u32[]{:S(2)}) copy-start(bf16[1,16,2048]{2,1,0:T(8,128)(2,1)} %param.10) | copy-start | bytes 196612
  15.2 19.0 %copy-start.6 = (f32[8,2,16]{2,1,0:T(2,128)S(1)}, f32[8,2,16]{2,1,0:T(2,128)}, u32[]{:S(2)}) copy-start(f32[8,2,16]{2,1,0:T(2,128)} %coords_ref.1) | copy-start | bytes 3076
  15.2 19.0 %copy-start.8 = (f32[1024]{0:T(1024)S(1)}, f32[1024]{0:T(1024)}, u32[]{:S(2)}) copy-start(f32[1024]{0:T(1024)} %param.19) | copy-start | bytes 12292
  21.0 3.3 %collective-permute-start = (bf16[16,4,2048]{2,1,0:T(4,128)(2,1)S(1)}, bf16[16,4,2048]{2,1,0:T(4,128)(2,1)S(1)}, u32[]{:S(2)}, u32[]{:S(2)}) collective-permute-start(bf16[16,4,2048]{2,1,0:T(4,128)(2,1)S(1)} %all-to-all-done.near_ref), channel_id=1, source_target_pairs={{0,1},{1,0},{2,3},{3,2},{4,5},{5,4},{6,7},{7,6},{8,9},{9,8},{10,11... | collective-permute-start | bytes 786440 | tf_op jit(solution)/shard_map/ppermute | solution.py:327
  24.9 10.6 %collective-permute-start.5 = (bf16[2,256,128]{2,1,0:T(8,128)(2,1)S(1)}, bf16[2,256,128]{2,1,0:T(8,128)(2,1)S(1)}, u32[]{:S(2)}, u32[]{:S(2)}) collective-permute-start(bf16[2,256,128]{2,1,0:T(8,128)(2,1)S(1)} %get-tuple-element.44), channel_id=1, source_target_pairs={{0,64},{64,128},{128,192},{192,0},{1,65},{65,129},{129,193},{193,1... | collective-permute-start | bytes 393224 | tf_op jit(solution)/shard_map/image_sum/ppermute | solution.py:327
  26.3 9.3 %collective-permute-start.6 = (bf16[2,256,128]{2,1,0:T(8,128)(2,1)S(1)}, bf16[2,256,128]{2,1,0:T(8,128)(2,1)S(1)}, u32[]{:S(2)}, u32[]{:S(2)}) collective-permute-start(bf16[2,256,128]{2,1,0:T(8,128)(2,1)S(1)} %get-tuple-element.45), channel_id=1, source_target_pairs={{0,128},{64,192},{128,0},{192,64},{1,129},{65,193},{129,1},{193,65... | collective-permute-start | bytes 393224 | tf_op jit(solution)/shard_map/image_sum/ppermute | solution.py:327
  28.9 6.6 %collective-permute-start.7 = (bf16[2,256,128]{2,1,0:T(8,128)(2,1)S(1)}, bf16[2,256,128]{2,1,0:T(8,128)(2,1)S(1)}, u32[]{:S(2)}, u32[]{:S(2)}) collective-permute-start(bf16[2,256,128]{2,1,0:T(8,128)(2,1)S(1)} %get-tuple-element.46), channel_id=1, source_target_pairs={{0,192},{64,0},{128,64},{192,128},{1,193},{65,1},{129,65},{193,129... | collective-permute-start | bytes 393224 | tf_op jit(solution)/shard_map/image_sum/ppermute | solution.py:327
  30.0 9.4 %collective-permute-start.1 = (bf16[16,2048]{1,0:T(8,128)(2,1)S(1)}, bf16[16,2048]{1,0:T(8,128)(2,1)S(1)}, u32[]{:S(2)}, u32[]{:S(2)}) collective-permute-start(bf16[16,2048]{1,0:T(8,128)(2,1)S(1)} %bitcast.6), channel_id=1, source_target_pairs={{0,32},{32,0},{1,33},{33,1},{2,34},{34,2},{3,35},{35,3},{4,36},{36... | collective-permute-start | bytes 196616 | tf_op jit(solution)/shard_map/visible_route/ppermute | solution.py:327
  34.2 5.1 %copy-start.2 = (s32[1,8]{1,0:T(1,128)S(1)}, s32[1,8]{1,0:T(1,128)}, u32[]{:S(2)}) copy-start(s32[1,8]{1,0:T(1,128)} %reader_ref.1) | copy-start | bytes 100
  35.6 10.1 %collective-permute-start.8 = (f32[256,128]{1,0:T(8,128)S(1)}, f32[256,128]{1,0:T(8,128)S(1)}, u32[]{:S(2)}, u32[]{:S(2)}) collective-permute-start(f32[256,128]{1,0:T(8,128)S(1)} %get-tuple-element.49), channel_id=1, source_target_pairs={{0,32},{32,0},{1,33},{33,1},{2,34},{34,2},{3,35},{35,3},{4,36},{36... | collective-permute-start | bytes 393224 | tf_op jit(solution)/shard_map/image_sum/ppermute | solution.py:327
  40.0 7.4 %collective-permute-start.2 = (bf16[16,2048]{1,0:T(8,128)(2,1)S(1)}, bf16[16,2048]{1,0:T(8,128)(2,1)S(1)}, u32[]{:S(2)}, u32[]{:S(2)}) collective-permute-start(bf16[16,2048]{1,0:T(8,128)(2,1)S(1)} %get-tuple-element.38), channel_id=1, source_target_pairs={{0,64},{64,128},{128,192},{192,0},{1,65},{65,129},{129,193},{193,1... | collective-permute-start | bytes 196616 | tf_op jit(solution)/shard_map/ppermute | solution.py:327
  41.0 6.4 %collective-permute-start.3 = (bf16[16,2048]{1,0:T(8,128)(2,1)S(1)}, bf16[16,2048]{1,0:T(8,128)(2,1)S(1)}, u32[]{:S(2)}, u32[]{:S(2)}) collective-permute-start(bf16[16,2048]{1,0:T(8,128)(2,1)S(1)} %get-tuple-element.39), channel_id=1, source_target_pairs={{0,128},{64,192},{128,0},{192,64},{1,129},{65,193},{129,1},{193,65... | collective-permute-start | bytes 196616 | tf_op jit(solution)/shard_map/ppermute | solution.py:327
  43.2 4.2 %collective-permute-start.4 = (bf16[16,2048]{1,0:T(8,128)(2,1)S(1)}, bf16[16,2048]{1,0:T(8,128)(2,1)S(1)}, u32[]{:S(2)}, u32[]{:S(2)}) collective-permute-start(bf16[16,2048]{1,0:T(8,128)(2,1)S(1)} %get-tuple-element.40), channel_id=1, source_target_pairs={{0,192},{64,0},{128,64},{192,128},{1,193},{65,1},{129,65},{193,129... | collective-permute-start | bytes 196616 | tf_op jit(solution)/shard_map/ppermute | solution.py:327
  48.6 7.5 %collective-permute-start.9 = (bf16[256,128]{1,0:T(8,128)(2,1)S(1)}, bf16[256,128]{1,0:T(8,128)(2,1)S(1)}, u32[]{:S(2)}, u32[]{:S(2)}) collective-permute-start(bf16[256,128]{1,0:T(8,128)(2,1)S(1)} %grid.1.refs_0_), channel_id=1, source_target_pairs={{0,32},{32,0},{1,33},{33,1},{2,34},{34,2},{3,35},{35,3},{4,36},{36... | collective-permute-start | bytes 196616 | tf_op jit(solution)/shard_map/grid_gather/ppermute | solution.py:327
  53.5 5.4 %collective-permute-start.10 = (bf16[256,128]{1,0:T(8,128)(2,1)S(1)}, bf16[256,128]{1,0:T(8,128)(2,1)S(1)}, u32[]{:S(2)}, u32[]{:S(2)}) collective-permute-start(bf16[256,128]{1,0:T(8,128)(2,1)S(1)} %grid.1.refs_0_), channel_id=1, source_target_pairs={{0,64},{64,128},{128,192},{192,0},{1,65},{65,129},{129,193},{193,1... | collective-permute-start | bytes 196616 | tf_op jit(solution)/shard_map/grid_gather/ppermute | solution.py:327
  53.5 7.8 %collective-permute-start.12 = (bf16[256,128]{1,0:T(8,128)(2,1)S(1)}, bf16[256,128]{1,0:T(8,128)(2,1)S(1)}, u32[]{:S(2)}, u32[]{:S(2)}) collective-permute-start(bf16[256,128]{1,0:T(8,128)(2,1)S(1)} %grid.1.refs_0_), channel_id=1, source_target_pairs={{0,128},{64,192},{128,0},{192,64},{1,129},{65,193},{129,1},{193,65... | collective-permute-start | bytes 196616 | tf_op jit(solution)/shard_map/grid_gather/ppermute | solution.py:327
  55.0 6.3 %collective-permute-start.14 = (bf16[256,128]{1,0:T(8,128)(2,1)S(1)}, bf16[256,128]{1,0:T(8,128)(2,1)S(1)}, u32[]{:S(2)}, u32[]{:S(2)}) collective-permute-start(bf16[256,128]{1,0:T(8,128)(2,1)S(1)} %grid.1.refs_0_), channel_id=1, source_target_pairs={{0,192},{64,0},{128,64},{192,128},{1,193},{65,1},{129,65},{193,129... | collective-permute-start | bytes 196616 | tf_op jit(solution)/shard_map/grid_gather/ppermute | solution.py:327
  56.2 5.2 %collective-permute-start.11 = (bf16[256,128]{1,0:T(8,128)(2,1)S(1)}, bf16[256,128]{1,0:T(8,128)(2,1)S(1)}, u32[]{:S(2)}, u32[]{:S(2)}) collective-permute-start(bf16[256,128]{1,0:T(8,128)(2,1)S(1)} %collective-permute-done.9.refs_1_), channel_id=1, source_target_pairs={{0,64},{64,128},{128,192},{192,0},{1,65},{65,129},{129,193},{193,1... | collective-permute-start | bytes 196616 | tf_op jit(solution)/shard_map/grid_gather/ppermute | solution.py:327
  56.7 5.2 %collective-permute-start.13 = (bf16[256,128]{1,0:T(8,128)(2,1)S(1)}, bf16[256,128]{1,0:T(8,128)(2,1)S(1)}, u32[]{:S(2)}, u32[]{:S(2)}) collective-permute-start(bf16[256,128]{1,0:T(8,128)(2,1)S(1)} %collective-permute-done.9.refs_1_), channel_id=1, source_target_pairs={{0,128},{64,192},{128,0},{192,64},{1,129},{65,193},{129,1},{193,65... | collective-permute-start | bytes 196616 | tf_op jit(solution)/shard_map/grid_gather/ppermute | solution.py:327
  58.9 3.7 %collective-permute-start.15 = (bf16[256,128]{1,0:T(8,128)(2,1)S(1)}, bf16[256,128]{1,0:T(8,128)(2,1)S(1)}, u32[]{:S(2)}, u32[]{:S(2)}) collective-permute-start(bf16[256,128]{1,0:T(8,128)(2,1)S(1)} %collective-permute-done.9.refs_1_), channel_id=1, source_target_pairs={{0,192},{64,0},{128,64},{192,128},{1,193},{65,1},{129,65},{193,129... | collective-permute-start | bytes 196616 | tf_op jit(solution)/shard_map/grid_gather/ppermute | solution.py:327
  63.1 6.1 %collective-permute-start.16 = (bf16[64,2048]{1,0:T(8,128)(2,1)S(1)}, bf16[64,2048]{1,0:T(8,128)(2,1)S(1)}, u32[]{:S(2)}, u32[]{:S(2)}) collective-permute-start(bf16[64,2048]{1,0:T(8,128)(2,1)S(1)} %regrid_far.1), channel_id=1, source_target_pairs={{0,1},{1,0},{2,3},{3,2},{4,5},{5,4},{6,7},{7,6},{8,9},{9,8},{10,11... | collective-permute-start | bytes 786440 | tf_op jit(solution)/shard_map/dirty_scatter/ppermute | solution.py:327

commit v9 on v8

--- a/solution.py
+++ b/solution.py
@@ -370,32 +370,6 @@
         name="screens",
     )(*operands)
 
-    near, screen = lax.optimization_barrier((near, screen))
-    far = shift(near, "c", 1)
-    images = pl.pallas_call(
-        functools.partial(image_kernel, n_y, n_h, n_c, owned),
-        out_shape=[jax.ShapeDtypeStruct((n_h, cell_rows, 128), BF16)] * n_y,
-        in_specs=[VMEM] * 4,
-        out_specs=[VMEM] * n_y,
-        compiler_params=params(8),
-        cost_estimate=pl.CostEstimate(flops=10**8, bytes_accessed=2 << 20, transcendentals=0),
-        name="images",
-    )(subgrid_index, near, far, screen)
-    rows, soon, *images = lax.optimization_barrier((sectioned_rows[0], baseline_coords, *images))
-
-    with jax.named_scope("visible_route"):
-        other = shift(rows, "h", 1)
-        pick, *sent = pl.pallas_call(
-            functools.partial(route_kernel, n_y, n_h),
-            out_shape=[jax.ShapeDtypeStruct((row_block, 128), jnp.int32)]
-            + [jax.ShapeDtypeStruct(rows.shape, BF16)] * (n_y - 1),
-            in_specs=[SMEM, VMEM, VMEM],
-            out_specs=[VMEM] * n_y,
-            compiler_params=params(4),
-            cost_estimate=pl.CostEstimate(flops=10**6, bytes_accessed=1 << 18, transcendentals=0),
-            name="route",
-        )(reader, rows, other)
-
     def table(kind, coords):
         return pl.pallas_call(
             functools.partial(table_kernel, n_h, kind),
@@ -411,11 +385,35 @@
             name=("east", "north")[kind],
         )(coords, channel_freq.reshape(1, channels))
 
+    north = table(1, baseline_coords)
+    near, screen, north = lax.optimization_barrier((near, screen, north))
+    far = shift(near, "c", 1)
+    images = pl.pallas_call(
+        functools.partial(image_kernel, n_y, n_h, n_c, owned),
+        out_shape=[jax.ShapeDtypeStruct((n_h, cell_rows, 128), BF16)] * n_y,
+        in_specs=[VMEM] * 4,
+        out_specs=[VMEM] * n_y,
+        compiler_params=params(8),
+        cost_estimate=pl.CostEstimate(flops=10**8, bytes_accessed=2 << 20, transcendentals=0),
+        name="images",
+    )(subgrid_index, near, far, screen)
+    rows, *images = lax.optimization_barrier((sectioned_rows[0], *images))
+
+    with jax.named_scope("visible_route"):
+        other = shift(rows, "h", 1)
+        pick, *sent = pl.pallas_call(
+            functools.partial(route_kernel, n_y, n_h),
+            out_shape=[jax.ShapeDtypeStruct((row_block, 128), jnp.int32)]
+            + [jax.ShapeDtypeStruct(rows.shape, BF16)] * (n_y - 1),
+            in_specs=[SMEM, VMEM, VMEM],
+            out_specs=[VMEM] * n_y,
+            compiler_params=params(4),
+            cost_estimate=pl.CostEstimate(flops=10**6, bytes_accessed=1 << 18, transcendentals=0),
+            name="route",
+        )(reader, rows, other)
+
     with jax.named_scope("image_sum"):
-        north = table(1, soon)
-        images[0], north = lax.optimization_barrier((images[0], north))
-        pieces = dict((by, shift(images[by], "y", by)) for by in far_first(n_y))
-        pieces = [images[0]] + [pieces[by] for by in range(1, n_y)]
+        pieces = [images[0]] + [shift(images[by], "y", by) for by in far_first(n_y)]
         own_sum, other_sum = pl.pallas_call(
             sum_kernel,
             out_shape=[jax.ShapeDtypeStruct((cell_rows, 128), F32)] * 2,

time: 83.2 us -> 82.6 us (level)
  local copies, waits for them, and re-layouts: 5.53 us -> 3.21 us
  waiting for transfers between devices: 6.6 us -> 8.29 us
    unnamed x18 -> x22, local copies, waits for them, and re-layouts: 3.89 us -> 1.58 us
    all_to_all x1, waiting for transfers between devices: 3.44 us -> 4.33 us  [local(): lax.all_to_all(copies, ('x', 'z'), split_axis=0, concat_axis=0, tiled=True)]
where the time goes in v9:
time: 82.6 us; the launch traced here: 82.1 us
  starting transfers between devices  44.9 us (54%)
  blocking collectives  13 us (16%)
  Pallas kernels  11.1 us (13%)
  waiting for transfers between devices  8.29 us (10%)
  local copies, waits for them, and re-layouts  3.21 us (4%)
  between operations  0.86 us (1%)
    ppermute x17, starting transfers between devices, shift(): lax.ppermute(value, axis, [(i, (i + by) % size) for i in range(size)])  35.8 us
    all_to_all x1, blocking collectives, local(): lax.all_to_all(chip_sum, ('x', 'z'), split_axis=0, concat_axis=0, tiled=T...  13 us
    all_to_all x1, starting transfers between devices, local(): lax.all_to_all(copies, ('x', 'z'), split_axis=0, concat_axis=0, tiled=True)  9.15 us
    all_to_all x1, waiting for transfers between devices, local(): lax.all_to_all(copies, ('x', 'z'), split_axis=0, concat_axis=0, tiled=True)  4.33 us
    ppermute x17, waiting for transfers between devices, shift(): lax.ppermute(value, axis, [(i, (i + by) % size) for i in range(size)])  3.96 us
    pallas_call x2, Pallas kernels, table(): pl.pallas_call(functools.partial(table_kernel, n_h, kind), out_shape=jax....  2.94 us
    pallas_call x1, Pallas kernels, local(): pl.pallas_call(screen_kernel, out_shape=jax.ShapeDtypeStruct((count, 2 *...  2.36 us
  transfers between devices with their start and end apart: 18, of which 5 were waited for; matrix products, arithmetic and copies ran while one was open for 0% of the time, Pallas kernels for 11%

profile of v9, /device:TPU:1, one launch (start us, length us, event | category | flops | bytes accessed | tf_op | source)
XLA Modules:
  0.0 82.1 jit_solution(17512316059434858368)
XLA Ops:
  0.6 1.5 %broadcast_in_dim.14 = bf16[16,4,2048]{2,1,0:T(4,128)(2,1)} broadcast(bf16[4,2048]{1,0:T(4,128)(2,1)} %bitcast.15), dimensions={1,2} | broadcast | bytes 278528 | tf_op jit(solution)/shard_map/model_gather/broadcast_in_dim | solution.py:357
  2.2 9.1 %all-to-all-start = ((bf16[16,4,2048]{2,1,0:T(4,128)(2,1)}), bf16[16,4,2048]{2,1,0:T(4,128)(2,1)S(1)}, u32[]{:S(2)}, u32[]{:S(2)}) async-start(bf16[16,4,2048]{2,1,0:T(4,128)(2,1)} %broadcast_in_dim.14), calls=%async_computation | async-start | bytes 524288 | tf_op jit(solution)/shard_map/model_gather/all_to_all | solution.py:358
  11.3 0.0 copy-start.3
  11.3 0.0 copy-start.4
  11.3 0.0 copy-start.6
  11.4 0.8 %copy-done.6 = f32[8,2,16]{2,1,0:T(2,128)S(1)} copy-done((f32[8,2,16]{2,1,0:T(2,128)S(1)}, f32[8,2,16]{2,1,0:T(2,128)}, u32[]{:S(2)}) %copy-start.6) | copy-done | bytes 1048
  12.2 0.7 copy-done.9
  12.9 1.3 %north.1.north_ref = bf16[16,64,1024]{2,1,0:T(8,128)(2,1)S(1)} custom-call(f32[8,2,16]{2,1,0:T(2,128)S(1)} %copy-done.6, f32[1,1024]{1,0:T(1,128)S(1)} %bitcast.11), custom_call_target="tpu_custom_call" | custom-call | flops 1000000000 | bytes 4194304 | tf_op jit(solution)/shard_map/north/pallas_call | solution.py:374
  14.2 0.0 copy-start.1
  14.3 0.0 copy-start
  14.3 0.0 copy-start.2
  14.3 0.0 copy-start.7
  14.3 0.0 copy-start.10
  14.3 2.4 %screens.1.screen_ref = f32[128,2048]{1,0:T(8,128)S(1)} custom-call(s32[8,2,16]{2,1,0:T(2,128)S(1)} %copy-done.5, s32[8,16]{1,0:T(8,128)S(1)} %copy-done.8, f32[32,1024]{1,0:T(8,128)S(1)} %copy-done.4, bf16[512,2048]{1,0:T(8,128)(2,1)S(1)} %bitcast.10), custom_call_target="tpu_custom_call" | custom-call | flops 1000000000 | bytes 4194304 | tf_op jit(solution)/shard_map/screens/pallas_call | solution.py:361
  16.7 4.3 %all-to-all-done.near_ref = bf16[16,4,2048]{2,1,0:T(4,128)(2,1)S(1)} async-done(((bf16[16,4,2048]{2,1,0:T(4,128)(2,1)}), bf16[16,4,2048]{2,1,0:T(4,128)(2,1)S(1)}, u32[]{:S(2)}, u32[]{:S(2)}) %all-to-all-start) | async-done | bytes 262176 | tf_op jit(solution)/shard_map/model_gather/all_to_all | solution.py:358
  21.0 2.1 %collective-permute-start = (bf16[16,4,2048]{2,1,0:T(4,128)(2,1)S(1)}, bf16[16,4,2048]{2,1,0:T(4,128)(2,1)S(1)}, u32[]{:S(2)}, u32[]{:S(2)}) collective-permute-start(bf16[16,4,2048]{2,1,0:T(4,128)(2,1)S(1)} %all-to-all-done.near_ref), channel_id=1, source_target_pairs={{0,1},{1,0},{2,3},{3,2},{4,5},{5,4},{6,7},{7,6},{8,9},{9,8},{10,11... | collective-permute-start | bytes 786440 | tf_op jit(solution)/shard_map/ppermute | solution.py:327
  23.2 1.2 %collective-permute-done.far_ref = bf16[16,4,2048]{2,1,0:T(4,128)(2,1)S(1)} collective-permute-done((bf16[16,4,2048]{2,1,0:T(4,128)(2,1)S(1)}, bf16[16,4,2048]{2,1,0:T(4,128)(2,1)S(1)}, u32[]{:S(2)}, u32[]{:S(2)}) %collective-permute-start) | collective-permute-done | bytes 262176 | tf_op jit(solution)/shard_map/ppermute | solution.py:327
  24.3 0.6 images.1
  24.9 3.0 %collective-permute-start.5 = (bf16[2,256,128]{2,1,0:T(8,128)(2,1)S(1)}, bf16[2,256,128]{2,1,0:T(8,128)(2,1)S(1)}, u32[]{:S(2)}, u32[]{:S(2)}) collective-permute-start(bf16[2,256,128]{2,1,0:T(8,128)(2,1)S(1)} %get-tuple-element.40), channel_id=1, source_target_pairs={{0,128},{64,192},{128,0},{192,64},{1,129},{65,193},{129,1},{193,65... | collective-permute-start | bytes 393224 | tf_op jit(solution)/shard_map/image_sum/ppermute | solution.py:327
  27.9 0.4 collective-permute-start.6
  28.3 2.3 %collective-permute-start.7 = (bf16[2,256,128]{2,1,0:T(8,128)(2,1)S(1)}, bf16[2,256,128]{2,1,0:T(8,128)(2,1)S(1)}, u32[]{:S(2)}, u32[]{:S(2)}) collective-permute-start(bf16[2,256,128]{2,1,0:T(8,128)(2,1)S(1)} %get-tuple-element.42), channel_id=1, source_target_pairs={{0,192},{64,0},{128,64},{192,128},{1,193},{65,1},{129,65},{193,129... | collective-permute-start | bytes 393224 | tf_op jit(solution)/shard_map/image_sum/ppermute | solution.py:327
  30.6 4.2 %collective-permute-start.1 = (bf16[16,2048]{1,0:T(8,128)(2,1)S(1)}, bf16[16,2048]{1,0:T(8,128)(2,1)S(1)}, u32[]{:S(2)}, u32[]{:S(2)}) collective-permute-start(bf16[16,2048]{1,0:T(8,128)(2,1)S(1)} %bitcast.6), channel_id=1, source_target_pairs={{0,32},{32,0},{1,33},{33,1},{2,34},{34,2},{3,35},{35,3},{4,36},{36... | collective-permute-start | bytes 196616 | tf_op jit(solution)/shard_map/visible_route/ppermute | solution.py:327
  34.8 0.1 image_sums.1
  34.9 4.0 %collective-permute-start.8 = (f32[256,128]{1,0:T(8,128)S(1)}, f32[256,128]{1,0:T(8,128)S(1)}, u32[]{:S(2)}, u32[]{:S(2)}) collective-permute-start(f32[256,128]{1,0:T(8,128)S(1)} %get-tuple-element.45), channel_id=1, source_target_pairs={{0,32},{32,0},{1,33},{33,1},{2,34},{34,2},{3,35},{35,3},{4,36},{36... | collective-permute-start | bytes 393224 | tf_op jit(solution)/shard_map/image_sum/ppermute | solution.py:327
  38.9 0.6 route.1
  39.5 1.6 %collective-permute-start.2 = (bf16[16,2048]{1,0:T(8,128)(2,1)S(1)}, bf16[16,2048]{1,0:T(8,128)(2,1)S(1)}, u32[]{:S(2)}, u32[]{:S(2)}) collective-permute-start(bf16[16,2048]{1,0:T(8,128)(2,1)S(1)} %get-tuple-element.36), channel_id=1, source_target_pairs={{0,64},{64,128},{128,192},{192,0},{1,65},{65,129},{129,193},{193,1... | collective-permute-start | bytes 196616 | tf_op jit(solution)/shard_map/ppermute | solution.py:327
  41.1 2.1 %collective-permute-start.3 = (bf16[16,2048]{1,0:T(8,128)(2,1)S(1)}, bf16[16,2048]{1,0:T(8,128)(2,1)S(1)}, u32[]{:S(2)}, u32[]{:S(2)}) collective-permute-start(bf16[16,2048]{1,0:T(8,128)(2,1)S(1)} %get-tuple-element.37), channel_id=1, source_target_pairs={{0,128},{64,192},{128,0},{192,64},{1,129},{65,193},{129,1},{193,65... | collective-permute-start | bytes 196616 | tf_op jit(solution)/shard_map/ppermute | solution.py:327
  43.2 0.4 collective-permute-start.4
  43.6 1.6 %east.1.east_ref = bf16[16,64,1024]{2,1,0:T(8,128)(2,1)S(1)} custom-call(f32[8,2,16]{2,1,0:T(2,128)S(1)} %copy-done.7, f32[1,1024]{1,0:T(1,128)S(1)} %bitcast.12), custom_call_target="tpu_custom_call" | custom-call | flops 1000000000 | bytes 4194304 | tf_op jit(solution)/shard_map/east/pallas_call | solution.py:374
  45.2 1.6 %degrid.1.predicted_ref.refs_5_ = f32[16,2048]{1,0:T(8,128)S(1)} custom-call(f32[256,128]{1,0:T(8,128)S(1)} %get-tuple-element.44.near_ref, f32[256,128]{1,0:T(8,128)S(1)} %collective-permute-done.8.far_ref, bf16[16,64,1024]{2,1,0:T(8,128)(2,1)S(1)} %east.1.east_ref, bf16[16,64,1024]{2,1,0:T(8,128)(2,1)S(1)} %north.1.north_ref), custom_call_target="tpu_custom_call" | custom-call | flops 1000000000 | bytes 5242880 | tf_op jit(solution)/shard_map/degrid/pallas_call | solution.py:433
  46.9 1.2 %grid.1.refs_0_ = bf16[256,128]{1,0:T(8,128)(2,1)S(1)} custom-call(s32[16,128]{1,0:T(8,128)S(1)} %get-tuple-element.48.pick_ref, bf16[16,2048]{1,0:T(8,128)(2,1)S(1)} %bitcast.8, bf16[16,2048]{1,0:T(8,128)(2,1)S(1)} %collective-permute-done.1.other_ref.refs_1_, bf16[16,2048]{1,0:T(8,128)(2,1)S(1)} %collective-permute-done.2.came_1_ref.refs_2_, ...), custom_call_target="tpu_custom_call" | custom-call | flops 1000000000 | bytes 5242880 | tf_op jit(solution)/shard_map/grid/pallas_call | solution.py:445
  48.1 4.9 %collective-permute-start.9 = (bf16[256,128]{1,0:T(8,128)(2,1)S(1)}, bf16[256,128]{1,0:T(8,128)(2,1)S(1)}, u32[]{:S(2)}, u32[]{:S(2)}) collective-permute-start(bf16[256,128]{1,0:T(8,128)(2,1)S(1)} %grid.1.refs_0_), channel_id=1, source_target_pairs={{0,32},{32,0},{1,33},{33,1},{2,34},{34,2},{3,35},{35,3},{4,36},{36... | collective-permute-start | bytes 196616 | tf_op jit(solution)/shard_map/grid_gather/ppermute | solution.py:327
  53.0 1.5 %collective-permute-start.10 = (bf16[256,128]{1,0:T(8,128)(2,1)S(1)}, bf16[256,128]{1,0:T(8,128)(2,1)S(1)}, u32[]{:S(2)}, u32[]{:S(2)}) collective-permute-start(bf16[256,128]{1,0:T(8,128)(2,1)S(1)} %grid.1.refs_0_), channel_id=1, source_target_pairs={{0,64},{64,128},{128,192},{192,0},{1,65},{65,129},{129,193},{193,1... | collective-permute-start | bytes 196616 | tf_op jit(solution)/shard_map/grid_gather/ppermute | solution.py:327
  54.5 2.4 %collective-permute-start.14 = (bf16[256,128]{1,0:T(8,128)(2,1)S(1)}, bf16[256,128]{1,0:T(8,128)(2,1)S(1)}, u32[]{:S(2)}, u32[]{:S(2)}) collective-permute-start(bf16[256,128]{1,0:T(8,128)(2,1)S(1)} %grid.1.refs_0_), channel_id=1, source_target_pairs={{0,192},{64,0},{128,64},{192,128},{1,193},{65,1},{129,65},{193,129... | collective-permute-start | bytes 196616 | tf_op jit(solution)/shard_map/grid_gather/ppermute | solution.py:327
  56.9 0.2 collective-permute-start.11
  57.1 1.9 %collective-permute-start.13 = (bf16[256,128]{1,0:T(8,128)(2,1)S(1)}, bf16[256,128]{1,0:T(8,128)(2,1)S(1)}, u32[]{:S(2)}, u32[]{:S(2)}) collective-permute-start(bf16[256,128]{1,0:T(8,128)(2,1)S(1)} %collective-permute-done.9.refs_1_), channel_id=1, source_target_pairs={{0,128},{64,192},{128,0},{192,64},{1,129},{65,193},{129,1},{193,65... | collective-permute-start | bytes 196616 | tf_op jit(solution)/shard_map/grid_gather/ppermute | solution.py:327
  58.9 1.2 %collective-permute-start.15 = (bf16[256,128]{1,0:T(8,128)(2,1)S(1)}, bf16[256,128]{1,0:T(8,128)(2,1)S(1)}, u32[]{:S(2)}, u32[]{:S(2)}) collective-permute-start(bf16[256,128]{1,0:T(8,128)(2,1)S(1)} %collective-permute-done.9.refs_1_), channel_id=1, source_target_pairs={{0,192},{64,0},{128,64},{192,128},{1,193},{65,1},{129,65},{193,129... | collective-permute-start | bytes 196616 | tf_op jit(solution)/shard_map/grid_gather/ppermute | solution.py:327
  60.1 0.7 residual.1
  60.8 1.5 %collective-permute-done.11.refs_3_ = bf16[256,128]{1,0:T(8,128)(2,1)S(1)} collective-permute-done((bf16[256,128]{1,0:T(8,128)(2,1)S(1)}, bf16[256,128]{1,0:T(8,128)(2,1)S(1)}, u32[]{:S(2)}, u32[]{:S(2)}) %collective-permute-start.11) | collective-permute-done | bytes 65568 | tf_op jit(solution)/shard_map/grid_gather/ppermute | solution.py:327
  62.3 0.6 collective-permute-done.15.refs_7_
  62.9 0.5 regrid_far.1
  63.4 3.7 %collective-permute-start.16 = (bf16[64,2048]{1,0:T(8,128)(2,1)S(1)}, bf16[64,2048]{1,0:T(8,128)(2,1)S(1)}, u32[]{:S(2)}, u32[]{:S(2)}) collective-permute-start(bf16[64,2048]{1,0:T(8,128)(2,1)S(1)} %regrid_far.1), channel_id=1, source_target_pairs={{0,1},{1,0},{2,3},{3,2},{4,5},{5,4},{6,7},{7,6},{8,9},{9,8},{10,11... | collective-permute-start | bytes 786440 | tf_op jit(solution)/shard_map/dirty_scatter/ppermute | solution.py:327
  67.1 0.5 regrid_near.1
  67.6 0.7 collective-permute-done.16
  68.2 0.1 add_convert_fusion
  68.3 0.1 reshape.12
  68.4 13.0 %all_to_all.10 = bf16[16,4,2048]{2,1,0:T(4,128)(2,1)S(1)} all-to-all(bf16[16,4,2048]{2,1,0:T(4,128)(2,1)S(1)} %reshape.12), channel_id=1, replica_groups=mesh['y'=4,'h'=2,'x'=4,'z'=4,'c'=2] {'x','z'}, dimensions={0} | all-to-all | bytes 524288 | tf_op jit(solution)/shard_map/dirty_scatter/all_to_all | solution.py:495
  81.4 0.7 convert_reduce_fusion
  (26 shorter events, 0.1 us)
Async XLA Ops:
  2.2 12.1 %copy-start.5 = (s32[8,2,16]{2,1,0:T(2,128)S(1)}, s32[8,2,16]{2,1,0:T(2,128)}, u32[]{:S(2)}) copy-start(s32[8,2,16]{2,1,0:T(2,128)} %stations_from.1) | copy-start | bytes 3076
  2.2 12.1 %copy-start.8 = (s32[8,16]{1,0:T(8,128)S(1)}, s32[8,16]{1,0:T(8,128)}, u32[]{:S(2)}) copy-start(s32[8,16]{1,0:T(8,128)} %plane_from.1) | copy-start | bytes 1540
  2.2 18.8 %all-to-all-start = ((bf16[16,4,2048]{2,1,0:T(4,128)(2,1)}), bf16[16,4,2048]{2,1,0:T(4,128)(2,1)S(1)}, u32[]{:S(2)}, u32[]{:S(2)}) async-start(bf16[16,4,2048]{2,1,0:T(4,128)(2,1)} %broadcast_in_dim.14), calls=%async_computation | async-start | bytes 524288 | tf_op jit(solution)/shard_map/model_gather/all_to_all | solution.py:358
  11.3 2.9 %copy-start.3 = (bf16[1,512,2048]{2,1,0:T(8,128)(2,1)S(1)}, bf16[1,512,2048]{2,1,0:T(8,128)(2,1)}, u32[]{:S(2)}) copy-start(bf16[1,512,2048]{2,1,0:T(8,128)(2,1)} %param.17) | copy-start | bytes 6291460
  11.3 2.9 %copy-start.4 = (f32[32,1024]{1,0:T(8,128)S(1)}, f32[32,1024]{1,0:T(8,128)}, u32[]{:S(2)}) copy-start(f32[32,1024]{1,0:T(8,128)} %phase_from.1) | copy-start | bytes 393220
  11.3 0.8 %copy-start.6 = (f32[8,2,16]{2,1,0:T(2,128)S(1)}, f32[8,2,16]{2,1,0:T(2,128)}, u32[]{:S(2)}) copy-start(f32[8,2,16]{2,1,0:T(2,128)} %coords_ref.2) | copy-start | bytes 3076
  12.2 0.7 copy-start.9
  14.2 10.1 %copy-start.1 = (s32[8,16]{1,0:T(8,128)S(1)}, s32[8,16]{1,0:T(8,128)}, u32[]{:S(2)}) copy-start(s32[8,16]{1,0:T(8,128)} %subgrid_ref.3) | copy-start | bytes 1540
  14.3 16.3 %copy-start = (bf16[1,16,2048]{2,1,0:T(8,128)(2,1)S(1)}, bf16[1,16,2048]{2,1,0:T(8,128)(2,1)}, u32[]{:S(2)}) copy-start(bf16[1,16,2048]{2,1,0:T(8,128)(2,1)} %param.10) | copy-start | bytes 196612
  14.3 24.6 %copy-start.2 = (s32[1,8]{1,0:T(1,128)S(1)}, s32[1,8]{1,0:T(1,128)}, u32[]{:S(2)}) copy-start(s32[1,8]{1,0:T(1,128)} %reader_ref.1) | copy-start | bytes 100
  14.3 29.3 %copy-start.7 = (f32[8,2,16]{2,1,0:T(2,128)S(1)}, f32[8,2,16]{2,1,0:T(2,128)}, u32[]{:S(2)}) copy-start(f32[8,2,16]{2,1,0:T(2,128)} %coords_ref.2) | copy-start | bytes 3076
  14.3 29.3 %copy-start.10 = (f32[1024]{0:T(1024)S(1)}, f32[1024]{0:T(1024)}, u32[]{:S(2)}) copy-start(f32[1024]{0:T(1024)} %param.19) | copy-start | bytes 12292
  21.0 3.3 %collective-permute-start = (bf16[16,4,2048]{2,1,0:T(4,128)(2,1)S(1)}, bf16[16,4,2048]{2,1,0:T(4,128)(2,1)S(1)}, u32[]{:S(2)}, u32[]{:S(2)}) collective-permute-start(bf16[16,4,2048]{2,1,0:T(4,128)(2,1)S(1)} %all-to-all-done.near_ref), channel_id=1, source_target_pairs={{0,1},{1,0},{2,3},{3,2},{4,5},{5,4},{6,7},{7,6},{8,9},{9,8},{10,11... | collective-permute-start | bytes 786440 | tf_op jit(solution)/shard_map/ppermute | solution.py:327
  24.9 9.9 %collective-permute-start.5 = (bf16[2,256,128]{2,1,0:T(8,128)(2,1)S(1)}, bf16[2,256,128]{2,1,0:T(8,128)(2,1)S(1)}, u32[]{:S(2)}, u32[]{:S(2)}) collective-permute-start(bf16[2,256,128]{2,1,0:T(8,128)(2,1)S(1)} %get-tuple-element.40), channel_id=1, source_target_pairs={{0,128},{64,192},{128,0},{192,64},{1,129},{65,193},{129,1},{193,65... | collective-permute-start | bytes 393224 | tf_op jit(solution)/shard_map/image_sum/ppermute | solution.py:327
  27.9 6.9 %collective-permute-start.6 = (bf16[2,256,128]{2,1,0:T(8,128)(2,1)S(1)}, bf16[2,256,128]{2,1,0:T(8,128)(2,1)S(1)}, u32[]{:S(2)}, u32[]{:S(2)}) collective-permute-start(bf16[2,256,128]{2,1,0:T(8,128)(2,1)S(1)} %get-tuple-element.41), channel_id=1, source_target_pairs={{0,64},{64,128},{128,192},{192,0},{1,65},{65,129},{129,193},{193,1... | collective-permute-start | bytes 393224 | tf_op jit(solution)/shard_map/image_sum/ppermute | solution.py:327
  28.3 6.5 %collective-permute-start.7 = (bf16[2,256,128]{2,1,0:T(8,128)(2,1)S(1)}, bf16[2,256,128]{2,1,0:T(8,128)(2,1)S(1)}, u32[]{:S(2)}, u32[]{:S(2)}) collective-permute-start(bf16[2,256,128]{2,1,0:T(8,128)(2,1)S(1)} %get-tuple-element.42), channel_id=1, source_target_pairs={{0,192},{64,0},{128,64},{192,128},{1,193},{65,1},{129,65},{193,129... | collective-permute-start | bytes 393224 | tf_op jit(solution)/shard_map/image_sum/ppermute | solution.py:327
  30.6 8.3 %collective-permute-start.1 = (bf16[16,2048]{1,0:T(8,128)(2,1)S(1)}, bf16[16,2048]{1,0:T(8,128)(2,1)S(1)}, u32[]{:S(2)}, u32[]{:S(2)}) collective-permute-start(bf16[16,2048]{1,0:T(8,128)(2,1)S(1)} %bitcast.6), channel_id=1, source_target_pairs={{0,32},{32,0},{1,33},{33,1},{2,34},{34,2},{3,35},{35,3},{4,36},{36... | collective-permute-start | bytes 196616 | tf_op jit(solution)/shard_map/visible_route/ppermute | solution.py:327
  34.9 10.3 %collective-permute-start.8 = (f32[256,128]{1,0:T(8,128)S(1)}, f32[256,128]{1,0:T(8,128)S(1)}, u32[]{:S(2)}, u32[]{:S(2)}) collective-permute-start(f32[256,128]{1,0:T(8,128)S(1)} %get-tuple-element.45), channel_id=1, source_target_pairs={{0,32},{32,0},{1,33},{33,1},{2,34},{34,2},{3,35},{35,3},{4,36},{36... | collective-permute-start | bytes 393224 | tf_op jit(solution)/shard_map/image_sum/ppermute | solution.py:327
  39.5 7.3 %collective-permute-start.2 = (bf16[16,2048]{1,0:T(8,128)(2,1)S(1)}, bf16[16,2048]{1,0:T(8,128)(2,1)S(1)}, u32[]{:S(2)}, u32[]{:S(2)}) collective-permute-start(bf16[16,2048]{1,0:T(8,128)(2,1)S(1)} %get-tuple-element.36), channel_id=1, source_target_pairs={{0,64},{64,128},{128,192},{192,0},{1,65},{65,129},{129,193},{193,1... | collective-permute-start | bytes 196616 | tf_op jit(solution)/shard_map/ppermute | solution.py:327
  41.1 5.8 %collective-permute-start.3 = (bf16[16,2048]{1,0:T(8,128)(2,1)S(1)}, bf16[16,2048]{1,0:T(8,128)(2,1)S(1)}, u32[]{:S(2)}, u32[]{:S(2)}) collective-permute-start(bf16[16,2048]{1,0:T(8,128)(2,1)S(1)} %get-tuple-element.37), channel_id=1, source_target_pairs={{0,128},{64,192},{128,0},{192,64},{1,129},{65,193},{129,1},{193,65... | collective-permute-start | bytes 196616 | tf_op jit(solution)/shard_map/ppermute | solution.py:327
  43.2 3.7 %collective-permute-start.4 = (bf16[16,2048]{1,0:T(8,128)(2,1)S(1)}, bf16[16,2048]{1,0:T(8,128)(2,1)S(1)}, u32[]{:S(2)}, u32[]{:S(2)}) collective-permute-start(bf16[16,2048]{1,0:T(8,128)(2,1)S(1)} %get-tuple-element.38), channel_id=1, source_target_pairs={{0,192},{64,0},{128,64},{192,128},{1,193},{65,1},{129,65},{193,129... | collective-permute-start | bytes 196616 | tf_op jit(solution)/shard_map/ppermute | solution.py:327
  48.1 8.8 %collective-permute-start.9 = (bf16[256,128]{1,0:T(8,128)(2,1)S(1)}, bf16[256,128]{1,0:T(8,128)(2,1)S(1)}, u32[]{:S(2)}, u32[]{:S(2)}) collective-permute-start(bf16[256,128]{1,0:T(8,128)(2,1)S(1)} %grid.1.refs_0_), channel_id=1, source_target_pairs={{0,32},{32,0},{1,33},{33,1},{2,34},{34,2},{3,35},{35,3},{4,36},{36... | collective-permute-start | bytes 196616 | tf_op jit(solution)/shard_map/grid_gather/ppermute | solution.py:327
  53.0 5.9 %collective-permute-start.10 = (bf16[256,128]{1,0:T(8,128)(2,1)S(1)}, bf16[256,128]{1,0:T(8,128)(2,1)S(1)}, u32[]{:S(2)}, u32[]{:S(2)}) collective-permute-start(bf16[256,128]{1,0:T(8,128)(2,1)S(1)} %grid.1.refs_0_), channel_id=1, source_target_pairs={{0,64},{64,128},{128,192},{192,0},{1,65},{65,129},{129,193},{193,1... | collective-permute-start | bytes 196616 | tf_op jit(solution)/shard_map/grid_gather/ppermute | solution.py:327
  54.5 6.3 %collective-permute-start.12 = (bf16[256,128]{1,0:T(8,128)(2,1)S(1)}, bf16[256,128]{1,0:T(8,128)(2,1)S(1)}, u32[]{:S(2)}, u32[]{:S(2)}) collective-permute-start(bf16[256,128]{1,0:T(8,128)(2,1)S(1)} %grid.1.refs_0_), channel_id=1, source_target_pairs={{0,128},{64,192},{128,0},{192,64},{1,129},{65,193},{129,1},{193,65... | collective-permute-start | bytes 196616 | tf_op jit(solution)/shard_map/grid_gather/ppermute | solution.py:327
  54.5 6.3 %collective-permute-start.14 = (bf16[256,128]{1,0:T(8,128)(2,1)S(1)}, bf16[256,128]{1,0:T(8,128)(2,1)S(1)}, u32[]{:S(2)}, u32[]{:S(2)}) collective-permute-start(bf16[256,128]{1,0:T(8,128)(2,1)S(1)} %grid.1.refs_0_), channel_id=1, source_target_pairs={{0,192},{64,0},{128,64},{192,128},{1,193},{65,1},{129,65},{193,129... | collective-permute-start | bytes 196616 | tf_op jit(solution)/shard_map/grid_gather/ppermute | solution.py:327
  56.9 5.5 %collective-permute-start.11 = (bf16[256,128]{1,0:T(8,128)(2,1)S(1)}, bf16[256,128]{1,0:T(8,128)(2,1)S(1)}, u32[]{:S(2)}, u32[]{:S(2)}) collective-permute-start(bf16[256,128]{1,0:T(8,128)(2,1)S(1)} %collective-permute-done.9.refs_1_), channel_id=1, source_target_pairs={{0,64},{64,128},{128,192},{192,0},{1,65},{65,129},{129,193},{193,1... | collective-permute-start | bytes 196616 | tf_op jit(solution)/shard_map/grid_gather/ppermute | solution.py:327
  57.1 5.3 %collective-permute-start.13 = (bf16[256,128]{1,0:T(8,128)(2,1)S(1)}, bf16[256,128]{1,0:T(8,128)(2,1)S(1)}, u32[]{:S(2)}, u32[]{:S(2)}) collective-permute-start(bf16[256,128]{1,0:T(8,128)(2,1)S(1)} %collective-permute-done.9.refs_1_), channel_id=1, source_target_pairs={{0,128},{64,192},{128,0},{192,64},{1,129},{65,193},{129,1},{193,65... | collective-permute-start | bytes 196616 | tf_op jit(solution)/shard_map/grid_gather/ppermute | solution.py:327
  58.9 4.0 %collective-permute-start.15 = (bf16[256,128]{1,0:T(8,128)(2,1)S(1)}, bf16[256,128]{1,0:T(8,128)(2,1)S(1)}, u32[]{:S(2)}, u32[]{:S(2)}) collective-permute-start(bf16[256,128]{1,0:T(8,128)(2,1)S(1)} %collective-permute-done.9.refs_1_), channel_id=1, source_target_pairs={{0,192},{64,0},{128,64},{192,128},{1,193},{65,1},{129,65},{193,129... | collective-permute-start | bytes 196616 | tf_op jit(solution)/shard_map/grid_gather/ppermute | solution.py:327
  63.4 4.8 %collective-permute-start.16 = (bf16[64,2048]{1,0:T(8,128)(2,1)S(1)}, bf16[64,2048]{1,0:T(8,128)(2,1)S(1)}, u32[]{:S(2)}, u32[]{:S(2)}) collective-permute-start(bf16[64,2048]{1,0:T(8,128)(2,1)S(1)} %regrid_far.1), channel_id=1, source_target_pairs={{0,1},{1,0},{2,3},{3,2},{4,5},{5,4},{6,7},{7,6},{8,9},{9,8},{10,11... | collective-permute-start | bytes 786440 | tf_op jit(solution)/shard_map/dirty_scatter/ppermute | solution.py:327

commit v10 on v9

--- a/solution.py
+++ b/solution.py
@@ -29,6 +29,11 @@
 
 def conj(a):
     return (a[0], -a[1])
+
+
+def repeat_kernel(rows_ref, copies_ref):
+    for at in range(copies_ref.shape[0]):
+        copies_ref[at] = rows_ref[0]
 
 
 def row_of_blocks(values):
@@ -96,6 +101,41 @@
 
     for b in range(rows):
         body(b)
+
+
+def target_of(subgrid, sizes, owned):
+    n_x, n_z, n_c = sizes
+    row, rest = (lax.rem(subgrid, owned), lax.div(subgrid, owned))
+    core, rest = (lax.rem(rest, n_c), lax.div(rest, n_c))
+    x = lax.rem(lax.div(rest, n_z) + n_x - lax.axis_index("x"), n_x)
+    z = lax.rem(lax.rem(rest, n_z) + n_z - lax.axis_index("z"), n_z)
+    core = lax.rem(core + n_c - lax.axis_index("c"), n_c)
+    return ((core * n_x + x) * n_z + z) * owned + row
+
+
+def chip_kernel(near_ref, far_ref, own_ref, *send_refs):
+    rows = own_ref.shape[0]
+    own_ref[...] = near_ref[:rows] + far_ref[:rows].astype(F32)
+    for at, ref in enumerate(send_refs, 1):
+        part = pl.ds(at * rows, rows)
+        ref[...] = (near_ref[part] + far_ref[part].astype(F32)).astype(BF16)
+
+
+def column_kernel(own_ref, *refs):
+    came, outs = (refs[:3], refs[3:])
+    total = own_ref[...]
+    for ref in came:
+        total = total + ref[...].astype(F32)
+    rows = outs[0].shape[0]
+    for at, ref in enumerate(outs):
+        ref[...] = total[at * rows : at * rows + rows]
+
+
+def total_kernel(*refs):
+    total = refs[0][...]
+    for ref in refs[1:-1]:
+        total = total + ref[...]
+    refs[-1][...] = total
 
 
 def screen_kernel(stations_from, plane_from, phase_from, beam_from, screen_ref, *refs):
@@ -292,7 +332,7 @@
     grid_ref[...] = out_ref[...].astype(BF16)
 
 
-def regrid_kernel(scale, n_y, n_h, cores, owned, other, subgrid_ref, screen_ref, *refs):
+def regrid_kernel(scale, n_y, n_h, sizes, owned, other, subgrid_ref, screen_ref, *refs):
     grids, sum_ref = (refs[:-1], refs[-1])
     blocks = blocks_from(n_y, n_h, -1)
     half = sum_ref.shape[0]
@@ -305,7 +345,7 @@
 
     subs = lax.broadcasted_iota(jnp.int32, (half, count), 0) + other * half
     target = jnp.concatenate([subgrid_ref[pl.ds(block, 1), :] for block in blocks], axis=1)
-    target = slot_of(target, lax.axis_index("c"), cores, owned)
+    target = target_of(target, sizes, owned)
     sums = jnp.where(target == subs, 1.0, 0.0).astype(BF16)
     sums = jnp.concatenate([sums, sums], axis=1)
     for q in range(tiles):
@@ -354,7 +394,15 @@
     cell_rows = 2 * pixels // 128 * row_block
     grid_scale = 1.0 / math.sqrt(channels * n_facet * (row_block * n_x * n_z * n_c) / subgrid_count)
     with jax.named_scope("model_gather"):
-        copies = jnp.broadcast_to(model_grid, (n_x * n_z, owned, 2 * pixels))
+        copies = pl.pallas_call(
+            repeat_kernel,
+            out_shape=jax.ShapeDtypeStruct((n_x * n_z, owned, 2 * pixels), BF16),
+            in_specs=[VMEM],
+            out_specs=VMEM,
+            compiler_params=params(61),
+            cost_estimate=pl.CostEstimate(flops=0, bytes_accessed=1 << 18, transcendentals=0),
+            name="repeat",
+        )(model_grid)
         near = lax.all_to_all(copies, ("x", "z"), split_axis=0, concat_axis=0, tiled=True)
 
     operands = (stations, plane_index, plane_phase, beam_screens[0])
@@ -476,7 +524,7 @@
 
     def regrid(other, subgrids):
         return pl.pallas_call(
-            functools.partial(regrid_kernel, grid_scale, n_y, n_h, n_c, owned, other),
+            functools.partial(regrid_kernel, grid_scale, n_y, n_h, (n_x, n_z, n_c), owned, other),
             out_shape=jax.ShapeDtypeStruct((half, 2 * pixels), (F32, BF16)[other]),
             in_specs=[VMEM] * (2 + n_facet),
             out_specs=VMEM,
@@ -491,9 +539,33 @@
     near_sum = regrid(0, subgrids)
 
     with jax.named_scope("dirty_scatter"):
-        chip_sum = (near_sum + shift(far_sum, "c", 1).astype(F32)).astype(BF16).reshape(n_x * n_z, owned, 2 * pixels)
-        chips = lax.all_to_all(chip_sum, ("x", "z"), split_axis=0, concat_axis=0, tiled=True)
-        dirty = jnp.sum(chips.astype(F32), axis=0)
+        far_sum = shift(far_sum, "c", 1)
+
+        def call(kernel, name, shapes, *operands):
+            return pl.pallas_call(
+                kernel,
+                out_shape=shapes,
+                in_specs=[VMEM] * len(operands),
+                out_specs=[VMEM] * len(shapes),
+                compiler_params=params(4),
+                cost_estimate=pl.CostEstimate(flops=10**6, bytes_accessed=1 << 20, transcendentals=0),
+                name=name,
+            )(*operands)
+
+        column = (n_z * owned, 2 * pixels)
+        own, *sent = call(
+            chip_kernel,
+            "chip_sums",
+            [jax.ShapeDtypeStruct(column, F32)] + [jax.ShapeDtypeStruct(column, BF16)] * (n_x - 1),
+            near_sum,
+            far_sum,
+        )
+        sent = [shift(sent[by - 1], "x", by) for by in far_first(n_x)]
+        own, *sent = call(
+            column_kernel, "column_sums", [jax.ShapeDtypeStruct((owned, 2 * pixels), F32)] * n_z, own, *sent
+        )
+        sent = [shift(value, "z", by) for by, value in enumerate(sent, 1)]
+        (dirty,) = call(total_kernel, "total", [jax.ShapeDtypeStruct(own.shape, F32)], own, *sent)
     return (residual[None], dirty[None])
 
 

time: 82.6 us -> 81.8 us (level)
  blocking collectives: 13 us -> 0 us
  starting transfers between devices: 44.9 us -> 51.6 us
  waiting for transfers between devices: 8.29 us -> 13.3 us
  Pallas kernels: 11.1 us -> 13.2 us
  local copies, waits for them, and re-layouts: 3.21 us -> 1.58 us
    all_to_all x1 -> x0, blocking collectives: 13 us -> none  [local(): lax.all_to_all(chip_sum, ('x', 'z'), split_axis=0, concat_axis=0, tiled=T...]
    ppermute x17 -> x23, starting transfers between devices: 35.8 us -> 42.5 us  [shift(): lax.ppermute(value, axis, [(i, (i + by) % size) for i in range(size)])]
    ppermute x17 -> x23, waiting for transfers between devices: 3.96 us -> 8.97 us  [shift(): lax.ppermute(value, axis, [(i, (i + by) % size) for i in range(size)])]
    pallas_call x2 -> x6, Pallas kernels: 0.97 us -> 3.1 us  [the longest x1 1.45 us: local(): pl.pallas_call(repeat_kernel, out_shape=jax.ShapeDtypeStruct((n_x * n_z,...]
    broadcast_in_dim x1 -> x0, local copies, waits for them, and re-layouts: 1.53 us -> none  [local(): copies = jnp.broadcast_to(model_grid, (n_x * n_z, owned, 2 * pixels))]
  transfers between devices with their start and end apart: 18 -> 24, of which waited for: 5 -> 9; matrix products, arithmetic and copies ran while one was open for 0% -> 0% of each run, Pallas kernels for 11% -> 11%
where the time goes in v10:
time: 81.8 us; the launch traced here: 80.6 us
  starting transfers between devices  51.6 us (63%)
  waiting for transfers between devices  13.3 us (16%)
  Pallas kernels  13.2 us (16%)
  local copies, waits for them, and re-layouts  1.58 us (2%)
  between operations  0.87 us (1%)
    ppermute x23, starting transfers between devices, shift(): lax.ppermute(value, axis, [(i, (i + by) % size) for i in range(size)])  42.5 us
    all_to_all x1, starting transfers between devices, local(): lax.all_to_all(copies, ('x', 'z'), split_axis=0, concat_axis=0, tiled=True)  9.15 us
    ppermute x23, waiting for transfers between devices, shift(): lax.ppermute(value, axis, [(i, (i + by) % size) for i in range(size)])  8.97 us
    all_to_all x1, waiting for transfers between devices, local(): lax.all_to_all(copies, ('x', 'z'), split_axis=0, concat_axis=0, tiled=True)  4.34 us
    pallas_call x2, Pallas kernels, table(): pl.pallas_call(functools.partial(table_kernel, n_h, kind), out_shape=jax....  2.94 us
    pallas_call x1, Pallas kernels, local(): pl.pallas_call(screen_kernel, out_shape=jax.ShapeDtypeStruct((count, 2 *...  2.35 us
    pallas_call x1, Pallas kernels, local(): pl.pallas_call(degrid_kernel, out_shape=jax.ShapeDtypeStruct((row_block,...  1.66 us
  transfers between devices with their start and end apart: 24, of which 9 were waited for; matrix products, arithmetic and copies ran while one was open for 0% of the time, Pallas kernels for 11%

profile of v10, /device:TPU:1, one launch (start us, length us, event | category | flops | bytes accessed | tf_op | source)
XLA Modules:
  0.0 80.6 jit_solution(4936118638020351090)
XLA Ops:
  0.6 1.4 %repeat.1 = bf16[16,4,2048]{2,1,0:T(4,128)(2,1)} custom-call(bf16[1,4,2048]{2,1,0:T(4,128)(2,1)} %rows_ref.1), custom_call_target="tpu_custom_call" | custom-call | bytes 262144 | tf_op jit(solution)/shard_map/model_gather/repeat/pallas_call | solution.py:397
  2.1 9.1 %all-to-all-start = ((bf16[16,4,2048]{2,1,0:T(4,128)(2,1)}), bf16[16,4,2048]{2,1,0:T(4,128)(2,1)S(1)}, u32[]{:S(2)}, u32[]{:S(2)}) async-start(bf16[16,4,2048]{2,1,0:T(4,128)(2,1)} %repeat.1), calls=%async_computation | async-start | bytes 524288 | tf_op jit(solution)/shard_map/model_gather/all_to_all | solution.py:406
  11.3 0.0 copy-start.6
  11.3 0.8 %copy-done.6 = f32[8,2,16]{2,1,0:T(2,128)S(1)} copy-done((f32[8,2,16]{2,1,0:T(2,128)S(1)}, f32[8,2,16]{2,1,0:T(2,128)}, u32[]{:S(2)}) %copy-start.6) | copy-done | bytes 1048
  12.1 0.7 copy-done.9
  12.8 1.3 %north.1.north_ref = bf16[16,64,1024]{2,1,0:T(8,128)(2,1)S(1)} custom-call(f32[8,2,16]{2,1,0:T(2,128)S(1)} %copy-done.6, f32[1,1024]{1,0:T(1,128)S(1)} %bitcast.10), custom_call_target="tpu_custom_call" | custom-call | flops 1000000000 | bytes 4194304 | tf_op jit(solution)/shard_map/north/pallas_call | solution.py:422
  14.2 2.4 %screens.1.screen_ref = f32[128,2048]{1,0:T(8,128)S(1)} custom-call(s32[8,2,16]{2,1,0:T(2,128)S(1)} %copy-done.5, s32[8,16]{1,0:T(8,128)S(1)} %copy-done.8, f32[32,1024]{1,0:T(8,128)S(1)} %copy-done.4, bf16[512,2048]{1,0:T(8,128)(2,1)S(1)} %bitcast.9), custom_call_target="tpu_custom_call" | custom-call | flops 1000000000 | bytes 4194304 | tf_op jit(solution)/shard_map/screens/pallas_call | solution.py:409
  16.6 4.3 %all-to-all-done.near_ref = bf16[16,4,2048]{2,1,0:T(4,128)(2,1)S(1)} async-done(((bf16[16,4,2048]{2,1,0:T(4,128)(2,1)}), bf16[16,4,2048]{2,1,0:T(4,128)(2,1)S(1)}, u32[]{:S(2)}, u32[]{:S(2)}) %all-to-all-start) | async-done | bytes 262176 | tf_op jit(solution)/shard_map/model_gather/all_to_all | solution.py:406
  20.9 2.1 %collective-permute-start = (bf16[16,4,2048]{2,1,0:T(4,128)(2,1)S(1)}, bf16[16,4,2048]{2,1,0:T(4,128)(2,1)S(1)}, u32[]{:S(2)}, u32[]{:S(2)}) collective-permute-start(bf16[16,4,2048]{2,1,0:T(4,128)(2,1)S(1)} %all-to-all-done.near_ref), channel_id=1, source_target_pairs={{0,1},{1,0},{2,3},{3,2},{4,5},{5,4},{6,7},{7,6},{8,9},{9,8},{10,11... | collective-permute-start | bytes 786440 | tf_op jit(solution)/shard_map/ppermute | solution.py:367
  23.1 1.2 %collective-permute-done.far_ref = bf16[16,4,2048]{2,1,0:T(4,128)(2,1)S(1)} collective-permute-done((bf16[16,4,2048]{2,1,0:T(4,128)(2,1)S(1)}, bf16[16,4,2048]{2,1,0:T(4,128)(2,1)S(1)}, u32[]{:S(2)}, u32[]{:S(2)}) %collective-permute-start) | collective-permute-done | bytes 262176 | tf_op jit(solution)/shard_map/ppermute | solution.py:367
  24.2 0.6 images.1
  24.8 3.0 %collective-permute-start.5 = (bf16[2,256,128]{2,1,0:T(8,128)(2,1)S(1)}, bf16[2,256,128]{2,1,0:T(8,128)(2,1)S(1)}, u32[]{:S(2)}, u32[]{:S(2)}) collective-permute-start(bf16[2,256,128]{2,1,0:T(8,128)(2,1)S(1)} %get-tuple-element.48), channel_id=1, source_target_pairs={{0,128},{64,192},{128,0},{192,64},{1,129},{65,193},{129,1},{193,65... | collective-permute-start | bytes 393224 | tf_op jit(solution)/shard_map/image_sum/ppermute | solution.py:367
  27.8 0.4 collective-permute-start.6
  28.2 2.3 %collective-permute-start.7 = (bf16[2,256,128]{2,1,0:T(8,128)(2,1)S(1)}, bf16[2,256,128]{2,1,0:T(8,128)(2,1)S(1)}, u32[]{:S(2)}, u32[]{:S(2)}) collective-permute-start(bf16[2,256,128]{2,1,0:T(8,128)(2,1)S(1)} %get-tuple-element.50), channel_id=1, source_target_pairs={{0,192},{64,0},{128,64},{192,128},{1,193},{65,1},{129,65},{193,129... | collective-permute-start | bytes 393224 | tf_op jit(solution)/shard_map/image_sum/ppermute | solution.py:367
  30.5 4.2 %collective-permute-start.1 = (bf16[16,2048]{1,0:T(8,128)(2,1)S(1)}, bf16[16,2048]{1,0:T(8,128)(2,1)S(1)}, u32[]{:S(2)}, u32[]{:S(2)}) collective-permute-start(bf16[16,2048]{1,0:T(8,128)(2,1)S(1)} %bitcast.5), channel_id=1, source_target_pairs={{0,32},{32,0},{1,33},{33,1},{2,34},{34,2},{3,35},{35,3},{4,36},{36... | collective-permute-start | bytes 196616 | tf_op jit(solution)/shard_map/visible_route/ppermute | solution.py:367
  34.7 0.1 image_sums.1
  34.8 4.0 %collective-permute-start.8 = (f32[256,128]{1,0:T(8,128)S(1)}, f32[256,128]{1,0:T(8,128)S(1)}, u32[]{:S(2)}, u32[]{:S(2)}) collective-permute-start(f32[256,128]{1,0:T(8,128)S(1)} %get-tuple-element.53), channel_id=1, source_target_pairs={{0,32},{32,0},{1,33},{33,1},{2,34},{34,2},{3,35},{35,3},{4,36},{36... | collective-permute-start | bytes 393224 | tf_op jit(solution)/shard_map/image_sum/ppermute | solution.py:367
  38.8 0.6 route.1
  39.4 1.6 %collective-permute-start.2 = (bf16[16,2048]{1,0:T(8,128)(2,1)S(1)}, bf16[16,2048]{1,0:T(8,128)(2,1)S(1)}, u32[]{:S(2)}, u32[]{:S(2)}) collective-permute-start(bf16[16,2048]{1,0:T(8,128)(2,1)S(1)} %get-tuple-element.44), channel_id=1, source_target_pairs={{0,64},{64,128},{128,192},{192,0},{1,65},{65,129},{129,193},{193,1... | collective-permute-start | bytes 196616 | tf_op jit(solution)/shard_map/ppermute | solution.py:367
  41.0 2.1 %collective-permute-start.3 = (bf16[16,2048]{1,0:T(8,128)(2,1)S(1)}, bf16[16,2048]{1,0:T(8,128)(2,1)S(1)}, u32[]{:S(2)}, u32[]{:S(2)}) collective-permute-start(bf16[16,2048]{1,0:T(8,128)(2,1)S(1)} %get-tuple-element.45), channel_id=1, source_target_pairs={{0,128},{64,192},{128,0},{192,64},{1,129},{65,193},{129,1},{193,65... | collective-permute-start | bytes 196616 | tf_op jit(solution)/shard_map/ppermute | solution.py:367
  43.1 0.4 collective-permute-start.4
  43.5 1.6 %east.1.east_ref = bf16[16,64,1024]{2,1,0:T(8,128)(2,1)S(1)} custom-call(f32[8,2,16]{2,1,0:T(2,128)S(1)} %copy-done.7, f32[1,1024]{1,0:T(1,128)S(1)} %bitcast.11), custom_call_target="tpu_custom_call" | custom-call | flops 1000000000 | bytes 4194304 | tf_op jit(solution)/shard_map/east/pallas_call | solution.py:422
  45.1 1.7 %degrid.1.predicted_ref.refs_5_ = f32[16,2048]{1,0:T(8,128)S(1)} custom-call(f32[256,128]{1,0:T(8,128)S(1)} %get-tuple-element.52.near_ref, f32[256,128]{1,0:T(8,128)S(1)} %collective-permute-done.8.far_ref, bf16[16,64,1024]{2,1,0:T(8,128)(2,1)S(1)} %east.1.east_ref, bf16[16,64,1024]{2,1,0:T(8,128)(2,1)S(1)} %north.1.north_ref), custom_call_target="tpu_custom_call" | custom-call | flops 1000000000 | bytes 5242880 | tf_op jit(solution)/shard_map/degrid/pallas_call | solution.py:481
  46.8 1.2 %grid.1.refs_0_ = bf16[256,128]{1,0:T(8,128)(2,1)S(1)} custom-call(s32[16,128]{1,0:T(8,128)S(1)} %get-tuple-element.56.pick_ref, bf16[16,2048]{1,0:T(8,128)(2,1)S(1)} %bitcast.7, bf16[16,2048]{1,0:T(8,128)(2,1)S(1)} %collective-permute-done.1.other_ref.refs_1_, bf16[16,2048]{1,0:T(8,128)(2,1)S(1)} %collective-permute-done.2.came_1_ref.refs_2_, ...), custom_call_target="tpu_custom_call" | custom-call | flops 1000000000 | bytes 5242880 | tf_op jit(solution)/shard_map/grid/pallas_call | solution.py:493
  48.1 4.9 %collective-permute-start.9 = (bf16[256,128]{1,0:T(8,128)(2,1)S(1)}, bf16[256,128]{1,0:T(8,128)(2,1)S(1)}, u32[]{:S(2)}, u32[]{:S(2)}) collective-permute-start(bf16[256,128]{1,0:T(8,128)(2,1)S(1)} %grid.1.refs_0_), channel_id=1, source_target_pairs={{0,32},{32,0},{1,33},{33,1},{2,34},{34,2},{3,35},{35,3},{4,36},{36... | collective-permute-start | bytes 196616 | tf_op jit(solution)/shard_map/grid_gather/ppermute | solution.py:367
  52.9 1.5 %collective-permute-start.10 = (bf16[256,128]{1,0:T(8,128)(2,1)S(1)}, bf16[256,128]{1,0:T(8,128)(2,1)S(1)}, u32[]{:S(2)}, u32[]{:S(2)}) collective-permute-start(bf16[256,128]{1,0:T(8,128)(2,1)S(1)} %grid.1.refs_0_), channel_id=1, source_target_pairs={{0,64},{64,128},{128,192},{192,0},{1,65},{65,129},{129,193},{193,1... | collective-permute-start | bytes 196616 | tf_op jit(solution)/shard_map/grid_gather/ppermute | solution.py:367
  54.4 2.4 %collective-permute-start.14 = (bf16[256,128]{1,0:T(8,128)(2,1)S(1)}, bf16[256,128]{1,0:T(8,128)(2,1)S(1)}, u32[]{:S(2)}, u32[]{:S(2)}) collective-permute-start(bf16[256,128]{1,0:T(8,128)(2,1)S(1)} %grid.1.refs_0_), channel_id=1, source_target_pairs={{0,192},{64,0},{128,64},{192,128},{1,193},{65,1},{129,65},{193,129... | collective-permute-start | bytes 196616 | tf_op jit(solution)/shard_map/grid_gather/ppermute | solution.py:367
  56.8 0.2 collective-permute-start.11
  57.0 1.8 %collective-permute-start.13 = (bf16[256,128]{1,0:T(8,128)(2,1)S(1)}, bf16[256,128]{1,0:T(8,128)(2,1)S(1)}, u32[]{:S(2)}, u32[]{:S(2)}) collective-permute-start(bf16[256,128]{1,0:T(8,128)(2,1)S(1)} %collective-permute-done.9.refs_1_), channel_id=1, source_target_pairs={{0,128},{64,192},{128,0},{192,64},{1,129},{65,193},{129,1},{193,65... | collective-permute-start | bytes 196616 | tf_op jit(solution)/shard_map/grid_gather/ppermute | solution.py:367
  58.9 1.2 %collective-permute-start.15 = (bf16[256,128]{1,0:T(8,128)(2,1)S(1)}, bf16[256,128]{1,0:T(8,128)(2,1)S(1)}, u32[]{:S(2)}, u32[]{:S(2)}) collective-permute-start(bf16[256,128]{1,0:T(8,128)(2,1)S(1)} %collective-permute-done.9.refs_1_), channel_id=1, source_target_pairs={{0,192},{64,0},{128,64},{192,128},{1,193},{65,1},{129,65},{193,129... | collective-permute-start | bytes 196616 | tf_op jit(solution)/shard_map/grid_gather/ppermute | solution.py:367
  60.1 0.7 residual.1
  60.8 1.5 %collective-permute-done.11.refs_3_ = bf16[256,128]{1,0:T(8,128)(2,1)S(1)} collective-permute-done((bf16[256,128]{1,0:T(8,128)(2,1)S(1)}, bf16[256,128]{1,0:T(8,128)(2,1)S(1)}, u32[]{:S(2)}, u32[]{:S(2)}) %collective-permute-start.11) | collective-permute-done | bytes 65568 | tf_op jit(solution)/shard_map/grid_gather/ppermute | solution.py:367
  62.3 0.6 collective-permute-done.15.refs_7_
  62.9 0.5 regrid_far.1
  63.4 3.7 %collective-permute-start.16 = (bf16[64,2048]{1,0:T(8,128)(2,1)S(1)}, bf16[64,2048]{1,0:T(8,128)(2,1)S(1)}, u32[]{:S(2)}, u32[]{:S(2)}) collective-permute-start(bf16[64,2048]{1,0:T(8,128)(2,1)S(1)} %regrid_far.1), channel_id=1, source_target_pairs={{0,1},{1,0},{2,3},{3,2},{4,5},{5,4},{6,7},{7,6},{8,9},{9,8},{10,11... | collective-permute-start | bytes 786440 | tf_op jit(solution)/shard_map/dirty_scatter/ppermute | solution.py:367
  67.1 0.5 regrid_near.1.near_ref
  67.5 0.7 collective-permute-done.16.far_ref
  68.3 0.7 collective-permute-start.17
  68.9 0.6 collective-permute-start.18
  69.5 2.1 %collective-permute-start.19 = (bf16[16,2048]{1,0:T(8,128)(2,1)S(1)}, bf16[16,2048]{1,0:T(8,128)(2,1)S(1)}, u32[]{:S(2)}, u32[]{:S(2)}) collective-permute-start(bf16[16,2048]{1,0:T(8,128)(2,1)S(1)} %get-tuple-element.65), channel_id=1, source_target_pairs={{0,24},{8,0},{16,8},{24,16},{1,25},{9,1},{17,9},{25,17},{2,26},{10... | collective-permute-start | bytes 196616 | tf_op jit(solution)/shard_map/dirty_scatter/ppermute | solution.py:367
  71.6 1.4 %collective-permute-done.17.refs_0_ = bf16[16,2048]{1,0:T(8,128)(2,1)S(1)} collective-permute-done((bf16[16,2048]{1,0:T(8,128)(2,1)S(1)}, bf16[16,2048]{1,0:T(8,128)(2,1)S(1)}, u32[]{:S(2)}, u32[]{:S(2)}) %collective-permute-start.17) | collective-permute-done | bytes 65568 | tf_op jit(solution)/shard_map/dirty_scatter/ppermute | solution.py:367
  73.0 1.9 %collective-permute-done.18.refs_1_ = bf16[16,2048]{1,0:T(8,128)(2,1)S(1)} collective-permute-done((bf16[16,2048]{1,0:T(8,128)(2,1)S(1)}, bf16[16,2048]{1,0:T(8,128)(2,1)S(1)}, u32[]{:S(2)}, u32[]{:S(2)}) %collective-permute-start.18) | collective-permute-done | bytes 65568 | tf_op jit(solution)/shard_map/dirty_scatter/ppermute | solution.py:367
  75.0 0.1 collective-permute-start.20
  75.1 0.4 collective-permute-start.21
  75.5 2.9 %collective-permute-start.22 = (f32[4,2048]{1,0:T(4,128)S(1)}, f32[4,2048]{1,0:T(4,128)S(1)}, u32[]{:S(2)}, u32[]{:S(2)}) collective-permute-start(f32[4,2048]{1,0:T(4,128)S(1)} %get-tuple-element.69), channel_id=1, source_target_pairs={{0,6},{2,0},{4,2},{6,4},{1,7},{3,1},{5,3},{7,5},{8,14},{10,8},{12,... | collective-permute-start | bytes 98312 | tf_op jit(solution)/shard_map/dirty_scatter/ppermute | solution.py:367
  78.3 1.3 %collective-permute-done.20.refs_1_ = f32[4,2048]{1,0:T(4,128)S(1)} collective-permute-done((f32[4,2048]{1,0:T(4,128)S(1)}, f32[4,2048]{1,0:T(4,128)S(1)}, u32[]{:S(2)}, u32[]{:S(2)}) %collective-permute-start.20) | collective-permute-done | bytes 32800 | tf_op jit(solution)/shard_map/dirty_scatter/ppermute | solution.py:367
  79.7 0.3 collective-permute-done.22.refs_3_
  80.0 0.6 total.1
  (37 shorter events, 0.2 us)
Async XLA Ops:
  2.1 12.1 %copy-start.5 = (s32[8,2,16]{2,1,0:T(2,128)S(1)}, s32[8,2,16]{2,1,0:T(2,128)}, u32[]{:S(2)}) copy-start(s32[8,2,16]{2,1,0:T(2,128)} %stations_from.1) | copy-start | bytes 3076
  2.1 12.1 %copy-start.8 = (s32[8,16]{1,0:T(8,128)S(1)}, s32[8,16]{1,0:T(8,128)}, u32[]{:S(2)}) copy-start(s32[8,16]{1,0:T(8,128)} %plane_from.1) | copy-start | bytes 1540
  2.1 18.8 %all-to-all-start = ((bf16[16,4,2048]{2,1,0:T(4,128)(2,1)}), bf16[16,4,2048]{2,1,0:T(4,128)(2,1)S(1)}, u32[]{:S(2)}, u32[]{:S(2)}) async-start(bf16[16,4,2048]{2,1,0:T(4,128)(2,1)} %repeat.1), calls=%async_computation | async-start | bytes 524288 | tf_op jit(solution)/shard_map/model_gather/all_to_all | solution.py:406
  11.2 2.9 %copy-start.3 = (bf16[1,512,2048]{2,1,0:T(8,128)(2,1)S(1)}, bf16[1,512,2048]{2,1,0:T(8,128)(2,1)}, u32[]{:S(2)}) copy-start(bf16[1,512,2048]{2,1,0:T(8,128)(2,1)} %param.17) | copy-start | bytes 6291460
  11.2 2.9 %copy-start.4 = (f32[32,1024]{1,0:T(8,128)S(1)}, f32[32,1024]{1,0:T(8,128)}, u32[]{:S(2)}) copy-start(f32[32,1024]{1,0:T(8,128)} %phase_from.1) | copy-start | bytes 393220
  11.3 0.8 %copy-start.6 = (f32[8,2,16]{2,1,0:T(2,128)S(1)}, f32[8,2,16]{2,1,0:T(2,128)}, u32[]{:S(2)}) copy-start(f32[8,2,16]{2,1,0:T(2,128)} %coords_ref.2) | copy-start | bytes 3076
  12.1 0.7 copy-start.9
  14.1 10.1 %copy-start.1 = (s32[8,16]{1,0:T(8,128)S(1)}, s32[8,16]{1,0:T(8,128)}, u32[]{:S(2)}) copy-start(s32[8,16]{1,0:T(8,128)} %subgrid_ref.3) | copy-start | bytes 1540
  14.2 16.3 %copy-start = (bf16[1,16,2048]{2,1,0:T(8,128)(2,1)S(1)}, bf16[1,16,2048]{2,1,0:T(8,128)(2,1)}, u32[]{:S(2)}) copy-start(bf16[1,16,2048]{2,1,0:T(8,128)(2,1)} %param.10) | copy-start | bytes 196612
  14.2 24.6 %copy-start.2 = (s32[1,8]{1,0:T(1,128)S(1)}, s32[1,8]{1,0:T(1,128)}, u32[]{:S(2)}) copy-start(s32[1,8]{1,0:T(1,128)} %reader_ref.1) | copy-start | bytes 100
  14.2 29.3 %copy-start.7 = (f32[8,2,16]{2,1,0:T(2,128)S(1)}, f32[8,2,16]{2,1,0:T(2,128)}, u32[]{:S(2)}) copy-start(f32[8,2,16]{2,1,0:T(2,128)} %coords_ref.2) | copy-start | bytes 3076
  14.2 29.3 %copy-start.10 = (f32[1024]{0:T(1024)S(1)}, f32[1024]{0:T(1024)}, u32[]{:S(2)}) copy-start(f32[1024]{0:T(1024)} %param.19) | copy-start | bytes 12292
  20.9 3.3 %collective-permute-start = (bf16[16,4,2048]{2,1,0:T(4,128)(2,1)S(1)}, bf16[16,4,2048]{2,1,0:T(4,128)(2,1)S(1)}, u32[]{:S(2)}, u32[]{:S(2)}) collective-permute-start(bf16[16,4,2048]{2,1,0:T(4,128)(2,1)S(1)} %all-to-all-done.near_ref), channel_id=1, source_target_pairs={{0,1},{1,0},{2,3},{3,2},{4,5},{5,4},{6,7},{7,6},{8,9},{9,8},{10,11... | collective-permute-start | bytes 786440 | tf_op jit(solution)/shard_map/ppermute | solution.py:367
  24.8 9.9 %collective-permute-start.5 = (bf16[2,256,128]{2,1,0:T(8,128)(2,1)S(1)}, bf16[2,256,128]{2,1,0:T(8,128)(2,1)S(1)}, u32[]{:S(2)}, u32[]{:S(2)}) collective-permute-start(bf16[2,256,128]{2,1,0:T(8,128)(2,1)S(1)} %get-tuple-element.48), channel_id=1, source_target_pairs={{0,128},{64,192},{128,0},{192,64},{1,129},{65,193},{129,1},{193,65... | collective-permute-start | bytes 393224 | tf_op jit(solution)/shard_map/image_sum/ppermute | solution.py:367
  27.8 6.9 %collective-permute-start.6 = (bf16[2,256,128]{2,1,0:T(8,128)(2,1)S(1)}, bf16[2,256,128]{2,1,0:T(8,128)(2,1)S(1)}, u32[]{:S(2)}, u32[]{:S(2)}) collective-permute-start(bf16[2,256,128]{2,1,0:T(8,128)(2,1)S(1)} %get-tuple-element.49), channel_id=1, source_target_pairs={{0,64},{64,128},{128,192},{192,0},{1,65},{65,129},{129,193},{193,1... | collective-permute-start | bytes 393224 | tf_op jit(solution)/shard_map/image_sum/ppermute | solution.py:367
  28.2 6.5 %collective-permute-start.7 = (bf16[2,256,128]{2,1,0:T(8,128)(2,1)S(1)}, bf16[2,256,128]{2,1,0:T(8,128)(2,1)S(1)}, u32[]{:S(2)}, u32[]{:S(2)}) collective-permute-start(bf16[2,256,128]{2,1,0:T(8,128)(2,1)S(1)} %get-tuple-element.50), channel_id=1, source_target_pairs={{0,192},{64,0},{128,64},{192,128},{1,193},{65,1},{129,65},{193,129... | collective-permute-start | bytes 393224 | tf_op jit(solution)/shard_map/image_sum/ppermute | solution.py:367
  30.5 8.3 %collective-permute-start.1 = (bf16[16,2048]{1,0:T(8,128)(2,1)S(1)}, bf16[16,2048]{1,0:T(8,128)(2,1)S(1)}, u32[]{:S(2)}, u32[]{:S(2)}) collective-permute-start(bf16[16,2048]{1,0:T(8,128)(2,1)S(1)} %bitcast.5), channel_id=1, source_target_pairs={{0,32},{32,0},{1,33},{33,1},{2,34},{34,2},{3,35},{35,3},{4,36},{36... | collective-permute-start | bytes 196616 | tf_op jit(solution)/shard_map/visible_route/ppermute | solution.py:367
  34.8 10.3 %collective-permute-start.8 = (f32[256,128]{1,0:T(8,128)S(1)}, f32[256,128]{1,0:T(8,128)S(1)}, u32[]{:S(2)}, u32[]{:S(2)}) collective-permute-start(f32[256,128]{1,0:T(8,128)S(1)} %get-tuple-element.53), channel_id=1, source_target_pairs={{0,32},{32,0},{1,33},{33,1},{2,34},{34,2},{3,35},{35,3},{4,36},{36... | collective-permute-start | bytes 393224 | tf_op jit(solution)/shard_map/image_sum/ppermute | solution.py:367
  39.4 7.4 %collective-permute-start.2 = (bf16[16,2048]{1,0:T(8,128)(2,1)S(1)}, bf16[16,2048]{1,0:T(8,128)(2,1)S(1)}, u32[]{:S(2)}, u32[]{:S(2)}) collective-permute-start(bf16[16,2048]{1,0:T(8,128)(2,1)S(1)} %get-tuple-element.44), channel_id=1, source_target_pairs={{0,64},{64,128},{128,192},{192,0},{1,65},{65,129},{129,193},{193,1... | collective-permute-start | bytes 196616 | tf_op jit(solution)/shard_map/ppermute | solution.py:367
  41.0 5.8 %collective-permute-start.3 = (bf16[16,2048]{1,0:T(8,128)(2,1)S(1)}, bf16[16,2048]{1,0:T(8,128)(2,1)S(1)}, u32[]{:S(2)}, u32[]{:S(2)}) collective-permute-start(bf16[16,2048]{1,0:T(8,128)(2,1)S(1)} %get-tuple-element.45), channel_id=1, source_target_pairs={{0,128},{64,192},{128,0},{192,64},{1,129},{65,193},{129,1},{193,65... | collective-permute-start | bytes 196616 | tf_op jit(solution)/shard_map/ppermute | solution.py:367
  43.1 3.8 %collective-permute-start.4 = (bf16[16,2048]{1,0:T(8,128)(2,1)S(1)}, bf16[16,2048]{1,0:T(8,128)(2,1)S(1)}, u32[]{:S(2)}, u32[]{:S(2)}) collective-permute-start(bf16[16,2048]{1,0:T(8,128)(2,1)S(1)} %get-tuple-element.46), channel_id=1, source_target_pairs={{0,192},{64,0},{128,64},{192,128},{1,193},{65,1},{129,65},{193,129... | collective-permute-start | bytes 196616 | tf_op jit(solution)/shard_map/ppermute | solution.py:367
  48.1 8.8 %collective-permute-start.9 = (bf16[256,128]{1,0:T(8,128)(2,1)S(1)}, bf16[256,128]{1,0:T(8,128)(2,1)S(1)}, u32[]{:S(2)}, u32[]{:S(2)}) collective-permute-start(bf16[256,128]{1,0:T(8,128)(2,1)S(1)} %grid.1.refs_0_), channel_id=1, source_target_pairs={{0,32},{32,0},{1,33},{33,1},{2,34},{34,2},{3,35},{35,3},{4,36},{36... | collective-permute-start | bytes 196616 | tf_op jit(solution)/shard_map/grid_gather/ppermute | solution.py:367
  52.9 5.9 %collective-permute-start.10 = (bf16[256,128]{1,0:T(8,128)(2,1)S(1)}, bf16[256,128]{1,0:T(8,128)(2,1)S(1)}, u32[]{:S(2)}, u32[]{:S(2)}) collective-permute-start(bf16[256,128]{1,0:T(8,128)(2,1)S(1)} %grid.1.refs_0_), channel_id=1, source_target_pairs={{0,64},{64,128},{128,192},{192,0},{1,65},{65,129},{129,193},{193,1... | collective-permute-start | bytes 196616 | tf_op jit(solution)/shard_map/grid_gather/ppermute | solution.py:367
  54.4 6.3 %collective-permute-start.12 = (bf16[256,128]{1,0:T(8,128)(2,1)S(1)}, bf16[256,128]{1,0:T(8,128)(2,1)S(1)}, u32[]{:S(2)}, u32[]{:S(2)}) collective-permute-start(bf16[256,128]{1,0:T(8,128)(2,1)S(1)} %grid.1.refs_0_), channel_id=1, source_target_pairs={{0,128},{64,192},{128,0},{192,64},{1,129},{65,193},{129,1},{193,65... | collective-permute-start | bytes 196616 | tf_op jit(solution)/shard_map/grid_gather/ppermute | solution.py:367
  54.4 6.3 %collective-permute-start.14 = (bf16[256,128]{1,0:T(8,128)(2,1)S(1)}, bf16[256,128]{1,0:T(8,128)(2,1)S(1)}, u32[]{:S(2)}, u32[]{:S(2)}) collective-permute-start(bf16[256,128]{1,0:T(8,128)(2,1)S(1)} %grid.1.refs_0_), channel_id=1, source_target_pairs={{0,192},{64,0},{128,64},{192,128},{1,193},{65,1},{129,65},{193,129... | collective-permute-start | bytes 196616 | tf_op jit(solution)/shard_map/grid_gather/ppermute | solution.py:367
  56.8 5.5 %collective-permute-start.11 = (bf16[256,128]{1,0:T(8,128)(2,1)S(1)}, bf16[256,128]{1,0:T(8,128)(2,1)S(1)}, u32[]{:S(2)}, u32[]{:S(2)}) collective-permute-start(bf16[256,128]{1,0:T(8,128)(2,1)S(1)} %collective-permute-done.9.refs_1_), channel_id=1, source_target_pairs={{0,64},{64,128},{128,192},{192,0},{1,65},{65,129},{129,193},{193,1... | collective-permute-start | bytes 196616 | tf_op jit(solution)/shard_map/grid_gather/ppermute | solution.py:367
  57.0 5.3 %collective-permute-start.13 = (bf16[256,128]{1,0:T(8,128)(2,1)S(1)}, bf16[256,128]{1,0:T(8,128)(2,1)S(1)}, u32[]{:S(2)}, u32[]{:S(2)}) collective-permute-start(bf16[256,128]{1,0:T(8,128)(2,1)S(1)} %collective-permute-done.9.refs_1_), channel_id=1, source_target_pairs={{0,128},{64,192},{128,0},{192,64},{1,129},{65,193},{129,1},{193,65... | collective-permute-start | bytes 196616 | tf_op jit(solution)/shard_map/grid_gather/ppermute | solution.py:367
  58.9 4.0 %collective-permute-start.15 = (bf16[256,128]{1,0:T(8,128)(2,1)S(1)}, bf16[256,128]{1,0:T(8,128)(2,1)S(1)}, u32[]{:S(2)}, u32[]{:S(2)}) collective-permute-start(bf16[256,128]{1,0:T(8,128)(2,1)S(1)} %collective-permute-done.9.refs_1_), channel_id=1, source_target_pairs={{0,192},{64,0},{128,64},{192,128},{1,193},{65,1},{129,65},{193,129... | collective-permute-start | bytes 196616 | tf_op jit(solution)/shard_map/grid_gather/ppermute | solution.py:367
  63.4 4.9 %collective-permute-start.16 = (bf16[64,2048]{1,0:T(8,128)(2,1)S(1)}, bf16[64,2048]{1,0:T(8,128)(2,1)S(1)}, u32[]{:S(2)}, u32[]{:S(2)}) collective-permute-start(bf16[64,2048]{1,0:T(8,128)(2,1)S(1)} %regrid_far.1), channel_id=1, source_target_pairs={{0,1},{1,0},{2,3},{3,2},{4,5},{5,4},{6,7},{7,6},{8,9},{9,8},{10,11... | collective-permute-start | bytes 786440 | tf_op jit(solution)/shard_map/dirty_scatter/ppermute | solution.py:367
  68.3 4.8 %collective-permute-start.17 = (bf16[16,2048]{1,0:T(8,128)(2,1)S(1)}, bf16[16,2048]{1,0:T(8,128)(2,1)S(1)}, u32[]{:S(2)}, u32[]{:S(2)}) collective-permute-start(bf16[16,2048]{1,0:T(8,128)(2,1)S(1)} %get-tuple-element.63), channel_id=1, source_target_pairs={{0,16},{8,24},{16,0},{24,8},{1,17},{9,25},{17,1},{25,9},{2,18},{10... | collective-permute-start | bytes 196616 | tf_op jit(solution)/shard_map/dirty_scatter/ppermute | solution.py:367
  68.9 6.0 %collective-permute-start.18 = (bf16[16,2048]{1,0:T(8,128)(2,1)S(1)}, bf16[16,2048]{1,0:T(8,128)(2,1)S(1)}, u32[]{:S(2)}, u32[]{:S(2)}) collective-permute-start(bf16[16,2048]{1,0:T(8,128)(2,1)S(1)} %get-tuple-element.64), channel_id=1, source_target_pairs={{0,8},{8,16},{16,24},{24,0},{1,9},{9,17},{17,25},{25,1},{2,10},{10... | collective-permute-start | bytes 196616 | tf_op jit(solution)/shard_map/dirty_scatter/ppermute | solution.py:367
  69.5 5.5 %collective-permute-start.19 = (bf16[16,2048]{1,0:T(8,128)(2,1)S(1)}, bf16[16,2048]{1,0:T(8,128)(2,1)S(1)}, u32[]{:S(2)}, u32[]{:S(2)}) collective-permute-start(bf16[16,2048]{1,0:T(8,128)(2,1)S(1)} %get-tuple-element.65), channel_id=1, source_target_pairs={{0,24},{8,0},{16,8},{24,16},{1,25},{9,1},{17,9},{25,17},{2,26},{10... | collective-permute-start | bytes 196616 | tf_op jit(solution)/shard_map/dirty_scatter/ppermute | solution.py:367
  75.0 4.6 %collective-permute-start.20 = (f32[4,2048]{1,0:T(4,128)S(1)}, f32[4,2048]{1,0:T(4,128)S(1)}, u32[]{:S(2)}, u32[]{:S(2)}) collective-permute-start(f32[4,2048]{1,0:T(4,128)S(1)} %get-tuple-element.67), channel_id=1, source_target_pairs={{0,2},{2,4},{4,6},{6,0},{1,3},{3,5},{5,7},{7,1},{8,10},{10,12},{12... | collective-permute-start | bytes 98312 | tf_op jit(solution)/shard_map/dirty_scatter/ppermute | solution.py:367
  75.1 4.6 %collective-permute-start.21 = (f32[4,2048]{1,0:T(4,128)S(1)}, f32[4,2048]{1,0:T(4,128)S(1)}, u32[]{:S(2)}, u32[]{:S(2)}) collective-permute-start(f32[4,2048]{1,0:T(4,128)S(1)} %get-tuple-element.68), channel_id=1, source_target_pairs={{0,4},{2,6},{4,0},{6,2},{1,5},{3,7},{5,1},{7,3},{8,12},{10,14},{12... | collective-permute-start | bytes 98312 | tf_op jit(solution)/shard_map/dirty_scatter/ppermute | solution.py:367
  75.5 4.5 %collective-permute-start.22 = (f32[4,2048]{1,0:T(4,128)S(1)}, f32[4,2048]{1,0:T(4,128)S(1)}, u32[]{:S(2)}, u32[]{:S(2)}) collective-permute-start(f32[4,2048]{1,0:T(4,128)S(1)} %get-tuple-element.69), channel_id=1, source_target_pairs={{0,6},{2,0},{4,2},{6,4},{1,7},{3,1},{5,3},{7,5},{8,14},{10,8},{12,... | collective-permute-start | bytes 98312 | tf_op jit(solution)/shard_map/dirty_scatter/ppermute | solution.py:367

commit v11 on v10

--- a/solution.py
+++ b/solution.py
@@ -108,7 +108,7 @@
     row, rest = (lax.rem(subgrid, owned), lax.div(subgrid, owned))
     core, rest = (lax.rem(rest, n_c), lax.div(rest, n_c))
     x = lax.rem(lax.div(rest, n_z) + n_x - lax.axis_index("x"), n_x)
-    z = lax.rem(lax.rem(rest, n_z) + n_z - lax.axis_index("z"), n_z)
+    z = lax.bitwise_xor(lax.rem(rest, n_z), jnp.full_like(rest, lax.axis_index("z")))
     core = lax.rem(core + n_c - lax.axis_index("c"), n_c)
     return ((core * n_x + x) * n_z + z) * owned + row
 
@@ -360,6 +360,10 @@
         both = jnp.dot(sums, jnp.concatenate([high, low], axis=0), preferred_element_type=F32)
         sum_ref[:, re] = both[:, :128].astype(sum_ref.dtype)
         sum_ref[:, im] = both[:, 128:].astype(sum_ref.dtype)
+
+
+def pair(value, axis, by):
+    return lax.ppermute(value, axis, [(i, i ^ by) for i in range(lax.axis_size(axis))])
 
 
 def shift(value, axis, by):
@@ -564,7 +568,7 @@
         own, *sent = call(
             column_kernel, "column_sums", [jax.ShapeDtypeStruct((owned, 2 * pixels), F32)] * n_z, own, *sent
         )
-        sent = [shift(value, "z", by) for by, value in enumerate(sent, 1)]
+        sent = [pair(sent[by - 1], "z", by) for by in reversed(range(1, n_z))]
         (dirty,) = call(total_kernel, "total", [jax.ShapeDtypeStruct(own.shape, F32)], own, *sent)
     return (residual[None], dirty[None])
 

time: 81.8 us -> 82.4 us (level)
    ppermute x0 -> x3, starting transfers between devices: none -> 3.63 us  [pair(): lax.ppermute(value, axis, [(i, i ^ by) for i in range(lax.axis_size(axis))])]
    ppermute x23 -> x20, starting transfers between devices: 42.5 us -> 39.1 us  [shift(): lax.ppermute(value, axis, [(i, (i + by) % size) for i in range(size)])]
    ppermute x0 -> x3, waiting for transfers between devices: none -> 1.68 us  [pair(): lax.ppermute(value, axis, [(i, i ^ by) for i in range(lax.axis_size(axis))])]
    ppermute x23 -> x20, waiting for transfers between devices: 8.97 us -> 7.33 us  [shift(): lax.ppermute(value, axis, [(i, (i + by) % size) for i in range(size)])]
where the time goes in v11:
time: 82.4 us; the launch traced here: 80.9 us
  starting transfers between devices  51.9 us (63%)
  Pallas kernels  13.3 us (16%)
  waiting for transfers between devices  13.3 us (16%)
  local copies, waits for them, and re-layouts  1.58 us (2%)
  between operations  0.87 us (1%)
    ppermute x20, starting transfers between devices, shift(): lax.ppermute(value, axis, [(i, (i + by) % size) for i in range(size)])  39.1 us
    all_to_all x1, starting transfers between devices, local(): lax.all_to_all(copies, ('x', 'z'), split_axis=0, concat_axis=0, tiled=True)  9.15 us
    ppermute x20, waiting for transfers between devices, shift(): lax.ppermute(value, axis, [(i, (i + by) % size) for i in range(size)])  7.33 us
    all_to_all x1, waiting for transfers between devices, local(): lax.all_to_all(copies, ('x', 'z'), split_axis=0, concat_axis=0, tiled=True)  4.34 us
    ppermute x3, starting transfers between devices, pair(): lax.ppermute(value, axis, [(i, i ^ by) for i in range(lax.axis_size(axis))])  3.63 us
    pallas_call x2, Pallas kernels, table(): pl.pallas_call(functools.partial(table_kernel, n_h, kind), out_shape=jax....  2.94 us
    pallas_call x1, Pallas kernels, local(): pl.pallas_call(screen_kernel, out_shape=jax.ShapeDtypeStruct((count, 2 *...  2.35 us
    ppermute x3, waiting for transfers between devices, pair(): lax.ppermute(value, axis, [(i, i ^ by) for i in range(lax.axis_size(axis))])  1.68 us
  transfers between devices with their start and end apart: 24, of which 9 were waited for; matrix products, arithmetic and copies ran while one was open for 0% of the time, Pallas kernels for 11%

profile of v11, /device:TPU:1, one launch (start us, length us, event | category | flops | bytes accessed | tf_op | source)
XLA Modules:
  0.0 80.9 jit_solution(11512058656272751702)
XLA Ops:
  0.6 1.4 %repeat.1 = bf16[16,4,2048]{2,1,0:T(4,128)(2,1)} custom-call(bf16[1,4,2048]{2,1,0:T(4,128)(2,1)} %rows_ref.1), custom_call_target="tpu_custom_call" | custom-call | bytes 262144 | tf_op jit(solution)/shard_map/model_gather/repeat/pallas_call | solution.py:401
  2.1 9.1 %all-to-all-start = ((bf16[16,4,2048]{2,1,0:T(4,128)(2,1)}), bf16[16,4,2048]{2,1,0:T(4,128)(2,1)S(1)}, u32[]{:S(2)}, u32[]{:S(2)}) async-start(bf16[16,4,2048]{2,1,0:T(4,128)(2,1)} %repeat.1), calls=%async_computation | async-start | bytes 524288 | tf_op jit(solution)/shard_map/model_gather/all_to_all | solution.py:410
  11.2 0.0 copy-start.3
  11.3 0.8 %copy-done.6 = f32[8,2,16]{2,1,0:T(2,128)S(1)} copy-done((f32[8,2,16]{2,1,0:T(2,128)S(1)}, f32[8,2,16]{2,1,0:T(2,128)}, u32[]{:S(2)}) %copy-start.6) | copy-done | bytes 1048
  12.1 0.7 copy-done.9
  12.8 1.3 %north.1.north_ref = bf16[16,64,1024]{2,1,0:T(8,128)(2,1)S(1)} custom-call(f32[8,2,16]{2,1,0:T(2,128)S(1)} %copy-done.6, f32[1,1024]{1,0:T(1,128)S(1)} %bitcast.10), custom_call_target="tpu_custom_call" | custom-call | flops 1000000000 | bytes 4194304 | tf_op jit(solution)/shard_map/north/pallas_call | solution.py:426
  14.2 2.4 %screens.1.screen_ref = f32[128,2048]{1,0:T(8,128)S(1)} custom-call(s32[8,2,16]{2,1,0:T(2,128)S(1)} %copy-done.5, s32[8,16]{1,0:T(8,128)S(1)} %copy-done.8, f32[32,1024]{1,0:T(8,128)S(1)} %copy-done.4, bf16[512,2048]{1,0:T(8,128)(2,1)S(1)} %bitcast.9), custom_call_target="tpu_custom_call" | custom-call | flops 1000000000 | bytes 4194304 | tf_op jit(solution)/shard_map/screens/pallas_call | solution.py:413
  16.6 4.3 %all-to-all-done.near_ref = bf16[16,4,2048]{2,1,0:T(4,128)(2,1)S(1)} async-done(((bf16[16,4,2048]{2,1,0:T(4,128)(2,1)}), bf16[16,4,2048]{2,1,0:T(4,128)(2,1)S(1)}, u32[]{:S(2)}, u32[]{:S(2)}) %all-to-all-start) | async-done | bytes 262176 | tf_op jit(solution)/shard_map/model_gather/all_to_all | solution.py:410
  20.9 2.1 %collective-permute-start = (bf16[16,4,2048]{2,1,0:T(4,128)(2,1)S(1)}, bf16[16,4,2048]{2,1,0:T(4,128)(2,1)S(1)}, u32[]{:S(2)}, u32[]{:S(2)}) collective-permute-start(bf16[16,4,2048]{2,1,0:T(4,128)(2,1)S(1)} %all-to-all-done.near_ref), channel_id=1, source_target_pairs={{0,1},{1,0},{2,3},{3,2},{4,5},{5,4},{6,7},{7,6},{8,9},{9,8},{10,11... | collective-permute-start | bytes 786440 | tf_op jit(solution)/shard_map/ppermute | solution.py:371
  23.1 1.2 %collective-permute-done.far_ref = bf16[16,4,2048]{2,1,0:T(4,128)(2,1)S(1)} collective-permute-done((bf16[16,4,2048]{2,1,0:T(4,128)(2,1)S(1)}, bf16[16,4,2048]{2,1,0:T(4,128)(2,1)S(1)}, u32[]{:S(2)}, u32[]{:S(2)}) %collective-permute-start) | collective-permute-done | bytes 262176 | tf_op jit(solution)/shard_map/ppermute | solution.py:371
  24.2 0.6 images.1
  24.8 3.0 %collective-permute-start.5 = (bf16[2,256,128]{2,1,0:T(8,128)(2,1)S(1)}, bf16[2,256,128]{2,1,0:T(8,128)(2,1)S(1)}, u32[]{:S(2)}, u32[]{:S(2)}) collective-permute-start(bf16[2,256,128]{2,1,0:T(8,128)(2,1)S(1)} %get-tuple-element.48), channel_id=1, source_target_pairs={{0,128},{64,192},{128,0},{192,64},{1,129},{65,193},{129,1},{193,65... | collective-permute-start | bytes 393224 | tf_op jit(solution)/shard_map/image_sum/ppermute | solution.py:371
  27.8 0.4 collective-permute-start.6
  28.2 2.3 %collective-permute-start.7 = (bf16[2,256,128]{2,1,0:T(8,128)(2,1)S(1)}, bf16[2,256,128]{2,1,0:T(8,128)(2,1)S(1)}, u32[]{:S(2)}, u32[]{:S(2)}) collective-permute-start(bf16[2,256,128]{2,1,0:T(8,128)(2,1)S(1)} %get-tuple-element.50), channel_id=1, source_target_pairs={{0,192},{64,0},{128,64},{192,128},{1,193},{65,1},{129,65},{193,129... | collective-permute-start | bytes 393224 | tf_op jit(solution)/shard_map/image_sum/ppermute | solution.py:371
  30.5 4.2 %collective-permute-start.1 = (bf16[16,2048]{1,0:T(8,128)(2,1)S(1)}, bf16[16,2048]{1,0:T(8,128)(2,1)S(1)}, u32[]{:S(2)}, u32[]{:S(2)}) collective-permute-start(bf16[16,2048]{1,0:T(8,128)(2,1)S(1)} %bitcast.5), channel_id=1, source_target_pairs={{0,32},{32,0},{1,33},{33,1},{2,34},{34,2},{3,35},{35,3},{4,36},{36... | collective-permute-start | bytes 196616 | tf_op jit(solution)/shard_map/visible_route/ppermute | solution.py:371
  34.7 0.1 image_sums.1
  34.8 4.0 %collective-permute-start.8 = (f32[256,128]{1,0:T(8,128)S(1)}, f32[256,128]{1,0:T(8,128)S(1)}, u32[]{:S(2)}, u32[]{:S(2)}) collective-permute-start(f32[256,128]{1,0:T(8,128)S(1)} %get-tuple-element.53), channel_id=1, source_target_pairs={{0,32},{32,0},{1,33},{33,1},{2,34},{34,2},{3,35},{35,3},{4,36},{36... | collective-permute-start | bytes 393224 | tf_op jit(solution)/shard_map/image_sum/ppermute | solution.py:371
  38.8 0.6 route.1
  39.4 1.6 %collective-permute-start.2 = (bf16[16,2048]{1,0:T(8,128)(2,1)S(1)}, bf16[16,2048]{1,0:T(8,128)(2,1)S(1)}, u32[]{:S(2)}, u32[]{:S(2)}) collective-permute-start(bf16[16,2048]{1,0:T(8,128)(2,1)S(1)} %get-tuple-element.44), channel_id=1, source_target_pairs={{0,64},{64,128},{128,192},{192,0},{1,65},{65,129},{129,193},{193,1... | collective-permute-start | bytes 196616 | tf_op jit(solution)/shard_map/ppermute | solution.py:371
  41.0 2.1 %collective-permute-start.3 = (bf16[16,2048]{1,0:T(8,128)(2,1)S(1)}, bf16[16,2048]{1,0:T(8,128)(2,1)S(1)}, u32[]{:S(2)}, u32[]{:S(2)}) collective-permute-start(bf16[16,2048]{1,0:T(8,128)(2,1)S(1)} %get-tuple-element.45), channel_id=1, source_target_pairs={{0,128},{64,192},{128,0},{192,64},{1,129},{65,193},{129,1},{193,65... | collective-permute-start | bytes 196616 | tf_op jit(solution)/shard_map/ppermute | solution.py:371
  43.1 0.4 collective-permute-start.4
  43.5 1.6 %east.1.east_ref = bf16[16,64,1024]{2,1,0:T(8,128)(2,1)S(1)} custom-call(f32[8,2,16]{2,1,0:T(2,128)S(1)} %copy-done.7, f32[1,1024]{1,0:T(1,128)S(1)} %bitcast.11), custom_call_target="tpu_custom_call" | custom-call | flops 1000000000 | bytes 4194304 | tf_op jit(solution)/shard_map/east/pallas_call | solution.py:426
  45.1 1.7 %degrid.1.predicted_ref.refs_5_ = f32[16,2048]{1,0:T(8,128)S(1)} custom-call(f32[256,128]{1,0:T(8,128)S(1)} %get-tuple-element.52.near_ref, f32[256,128]{1,0:T(8,128)S(1)} %collective-permute-done.8.far_ref, bf16[16,64,1024]{2,1,0:T(8,128)(2,1)S(1)} %east.1.east_ref, bf16[16,64,1024]{2,1,0:T(8,128)(2,1)S(1)} %north.1.north_ref), custom_call_target="tpu_custom_call" | custom-call | flops 1000000000 | bytes 5242880 | tf_op jit(solution)/shard_map/degrid/pallas_call | solution.py:485
  46.8 1.2 %grid.1.refs_0_ = bf16[256,128]{1,0:T(8,128)(2,1)S(1)} custom-call(s32[16,128]{1,0:T(8,128)S(1)} %get-tuple-element.56.pick_ref, bf16[16,2048]{1,0:T(8,128)(2,1)S(1)} %bitcast.7, bf16[16,2048]{1,0:T(8,128)(2,1)S(1)} %collective-permute-done.1.other_ref.refs_1_, bf16[16,2048]{1,0:T(8,128)(2,1)S(1)} %collective-permute-done.2.came_1_ref.refs_2_, ...), custom_call_target="tpu_custom_call" | custom-call | flops 1000000000 | bytes 5242880 | tf_op jit(solution)/shard_map/grid/pallas_call | solution.py:497
  48.1 4.9 %collective-permute-start.9 = (bf16[256,128]{1,0:T(8,128)(2,1)S(1)}, bf16[256,128]{1,0:T(8,128)(2,1)S(1)}, u32[]{:S(2)}, u32[]{:S(2)}) collective-permute-start(bf16[256,128]{1,0:T(8,128)(2,1)S(1)} %grid.1.refs_0_), channel_id=1, source_target_pairs={{0,32},{32,0},{1,33},{33,1},{2,34},{34,2},{3,35},{35,3},{4,36},{36... | collective-permute-start | bytes 196616 | tf_op jit(solution)/shard_map/grid_gather/ppermute | solution.py:371
  52.9 1.5 %collective-permute-start.10 = (bf16[256,128]{1,0:T(8,128)(2,1)S(1)}, bf16[256,128]{1,0:T(8,128)(2,1)S(1)}, u32[]{:S(2)}, u32[]{:S(2)}) collective-permute-start(bf16[256,128]{1,0:T(8,128)(2,1)S(1)} %grid.1.refs_0_), channel_id=1, source_target_pairs={{0,64},{64,128},{128,192},{192,0},{1,65},{65,129},{129,193},{193,1... | collective-permute-start | bytes 196616 | tf_op jit(solution)/shard_map/grid_gather/ppermute | solution.py:371
  54.4 2.4 %collective-permute-start.14 = (bf16[256,128]{1,0:T(8,128)(2,1)S(1)}, bf16[256,128]{1,0:T(8,128)(2,1)S(1)}, u32[]{:S(2)}, u32[]{:S(2)}) collective-permute-start(bf16[256,128]{1,0:T(8,128)(2,1)S(1)} %grid.1.refs_0_), channel_id=1, source_target_pairs={{0,192},{64,0},{128,64},{192,128},{1,193},{65,1},{129,65},{193,129... | collective-permute-start | bytes 196616 | tf_op jit(solution)/shard_map/grid_gather/ppermute | solution.py:371
  56.8 0.2 collective-permute-start.11
  57.0 1.8 %collective-permute-start.13 = (bf16[256,128]{1,0:T(8,128)(2,1)S(1)}, bf16[256,128]{1,0:T(8,128)(2,1)S(1)}, u32[]{:S(2)}, u32[]{:S(2)}) collective-permute-start(bf16[256,128]{1,0:T(8,128)(2,1)S(1)} %collective-permute-done.9.refs_1_), channel_id=1, source_target_pairs={{0,128},{64,192},{128,0},{192,64},{1,129},{65,193},{129,1},{193,65... | collective-permute-start | bytes 196616 | tf_op jit(solution)/shard_map/grid_gather/ppermute | solution.py:371
  58.9 1.2 %collective-permute-start.15 = (bf16[256,128]{1,0:T(8,128)(2,1)S(1)}, bf16[256,128]{1,0:T(8,128)(2,1)S(1)}, u32[]{:S(2)}, u32[]{:S(2)}) collective-permute-start(bf16[256,128]{1,0:T(8,128)(2,1)S(1)} %collective-permute-done.9.refs_1_), channel_id=1, source_target_pairs={{0,192},{64,0},{128,64},{192,128},{1,193},{65,1},{129,65},{193,129... | collective-permute-start | bytes 196616 | tf_op jit(solution)/shard_map/grid_gather/ppermute | solution.py:371
  60.1 0.7 residual.1
  60.8 1.5 %collective-permute-done.11.refs_3_ = bf16[256,128]{1,0:T(8,128)(2,1)S(1)} collective-permute-done((bf16[256,128]{1,0:T(8,128)(2,1)S(1)}, bf16[256,128]{1,0:T(8,128)(2,1)S(1)}, u32[]{:S(2)}, u32[]{:S(2)}) %collective-permute-start.11) | collective-permute-done | bytes 65568 | tf_op jit(solution)/shard_map/grid_gather/ppermute | solution.py:371
  62.3 0.6 collective-permute-done.15.refs_7_
  62.9 0.5 regrid_far.1
  63.4 3.7 %collective-permute-start.16 = (bf16[64,2048]{1,0:T(8,128)(2,1)S(1)}, bf16[64,2048]{1,0:T(8,128)(2,1)S(1)}, u32[]{:S(2)}, u32[]{:S(2)}) collective-permute-start(bf16[64,2048]{1,0:T(8,128)(2,1)S(1)} %regrid_far.1), channel_id=1, source_target_pairs={{0,1},{1,0},{2,3},{3,2},{4,5},{5,4},{6,7},{7,6},{8,9},{9,8},{10,11... | collective-permute-start | bytes 786440 | tf_op jit(solution)/shard_map/dirty_scatter/ppermute | solution.py:371
  67.1 0.5 regrid_near.1.near_ref
  67.5 0.7 collective-permute-done.16.far_ref
  68.3 0.7 collective-permute-start.17
  68.9 0.6 collective-permute-start.18
  69.5 2.1 %collective-permute-start.19 = (bf16[16,2048]{1,0:T(8,128)(2,1)S(1)}, bf16[16,2048]{1,0:T(8,128)(2,1)S(1)}, u32[]{:S(2)}, u32[]{:S(2)}) collective-permute-start(bf16[16,2048]{1,0:T(8,128)(2,1)S(1)} %get-tuple-element.65), channel_id=1, source_target_pairs={{0,24},{8,0},{16,8},{24,16},{1,25},{9,1},{17,9},{25,17},{2,26},{10... | collective-permute-start | bytes 196616 | tf_op jit(solution)/shard_map/dirty_scatter/ppermute | solution.py:371
  71.6 1.4 %collective-permute-done.17.refs_0_ = bf16[16,2048]{1,0:T(8,128)(2,1)S(1)} collective-permute-done((bf16[16,2048]{1,0:T(8,128)(2,1)S(1)}, bf16[16,2048]{1,0:T(8,128)(2,1)S(1)}, u32[]{:S(2)}, u32[]{:S(2)}) %collective-permute-start.17) | collective-permute-done | bytes 65568 | tf_op jit(solution)/shard_map/dirty_scatter/ppermute | solution.py:371
  73.0 1.9 %collective-permute-done.18.refs_1_ = bf16[16,2048]{1,0:T(8,128)(2,1)S(1)} collective-permute-done((bf16[16,2048]{1,0:T(8,128)(2,1)S(1)}, bf16[16,2048]{1,0:T(8,128)(2,1)S(1)}, u32[]{:S(2)}, u32[]{:S(2)}) %collective-permute-start.18) | collective-permute-done | bytes 65568 | tf_op jit(solution)/shard_map/dirty_scatter/ppermute | solution.py:371
  75.0 0.1 collective-permute-start.20
  75.1 1.1 %collective-permute-start.21 = (f32[4,2048]{1,0:T(4,128)S(1)}, f32[4,2048]{1,0:T(4,128)S(1)}, u32[]{:S(2)}, u32[]{:S(2)}) collective-permute-start(f32[4,2048]{1,0:T(4,128)S(1)} %get-tuple-element.68), channel_id=1, source_target_pairs={{0,4},{2,6},{4,0},{6,2},{1,5},{3,7},{5,1},{7,3},{8,12},{10,14},{12... | collective-permute-start | bytes 98312 | tf_op jit(solution)/shard_map/dirty_scatter/ppermute | solution.py:366
  76.2 2.5 %collective-permute-start.22 = (f32[4,2048]{1,0:T(4,128)S(1)}, f32[4,2048]{1,0:T(4,128)S(1)}, u32[]{:S(2)}, u32[]{:S(2)}) collective-permute-start(f32[4,2048]{1,0:T(4,128)S(1)} %get-tuple-element.69), channel_id=1, source_target_pairs={{0,2},{2,0},{4,6},{6,4},{1,3},{3,1},{5,7},{7,5},{8,10},{10,8},{12,... | collective-permute-start | bytes 98312 | tf_op jit(solution)/shard_map/dirty_scatter/ppermute | solution.py:366
  78.6 1.0 %collective-permute-done.20.refs_1_ = f32[4,2048]{1,0:T(4,128)S(1)} collective-permute-done((f32[4,2048]{1,0:T(4,128)S(1)}, f32[4,2048]{1,0:T(4,128)S(1)}, u32[]{:S(2)}, u32[]{:S(2)}) %collective-permute-start.20) | collective-permute-done | bytes 32800 | tf_op jit(solution)/shard_map/dirty_scatter/ppermute | solution.py:366
  79.7 0.6 collective-permute-done.22.refs_3_
  80.3 0.6 total.1
  (37 shorter events, 0.2 us)
Async XLA Ops:
  2.1 12.1 %copy-start.5 = (s32[8,2,16]{2,1,0:T(2,128)S(1)}, s32[8,2,16]{2,1,0:T(2,128)}, u32[]{:S(2)}) copy-start(s32[8,2,16]{2,1,0:T(2,128)} %stations_from.1) | copy-start | bytes 3076
  2.1 12.1 %copy-start.8 = (s32[8,16]{1,0:T(8,128)S(1)}, s32[8,16]{1,0:T(8,128)}, u32[]{:S(2)}) copy-start(s32[8,16]{1,0:T(8,128)} %plane_from.1) | copy-start | bytes 1540
  2.1 18.8 %all-to-all-start = ((bf16[16,4,2048]{2,1,0:T(4,128)(2,1)}), bf16[16,4,2048]{2,1,0:T(4,128)(2,1)S(1)}, u32[]{:S(2)}, u32[]{:S(2)}) async-start(bf16[16,4,2048]{2,1,0:T(4,128)(2,1)} %repeat.1), calls=%async_computation | async-start | bytes 524288 | tf_op jit(solution)/shard_map/model_gather/all_to_all | solution.py:410
  11.2 2.9 %copy-start.3 = (bf16[1,512,2048]{2,1,0:T(8,128)(2,1)S(1)}, bf16[1,512,2048]{2,1,0:T(8,128)(2,1)}, u32[]{:S(2)}) copy-start(bf16[1,512,2048]{2,1,0:T(8,128)(2,1)} %param.17) | copy-start | bytes 6291460
  11.2 2.9 %copy-start.4 = (f32[32,1024]{1,0:T(8,128)S(1)}, f32[32,1024]{1,0:T(8,128)}, u32[]{:S(2)}) copy-start(f32[32,1024]{1,0:T(8,128)} %phase_from.1) | copy-start | bytes 393220
  11.3 0.8 %copy-start.6 = (f32[8,2,16]{2,1,0:T(2,128)S(1)}, f32[8,2,16]{2,1,0:T(2,128)}, u32[]{:S(2)}) copy-start(f32[8,2,16]{2,1,0:T(2,128)} %coords_ref.2) | copy-start | bytes 3076
  12.1 0.7 copy-start.9
  14.1 10.1 %copy-start.1 = (s32[8,16]{1,0:T(8,128)S(1)}, s32[8,16]{1,0:T(8,128)}, u32[]{:S(2)}) copy-start(s32[8,16]{1,0:T(8,128)} %subgrid_ref.3) | copy-start | bytes 1540
  14.2 16.3 %copy-start = (bf16[1,16,2048]{2,1,0:T(8,128)(2,1)S(1)}, bf16[1,16,2048]{2,1,0:T(8,128)(2,1)}, u32[]{:S(2)}) copy-start(bf16[1,16,2048]{2,1,0:T(8,128)(2,1)} %param.10) | copy-start | bytes 196612
  14.2 24.6 %copy-start.2 = (s32[1,8]{1,0:T(1,128)S(1)}, s32[1,8]{1,0:T(1,128)}, u32[]{:S(2)}) copy-start(s32[1,8]{1,0:T(1,128)} %reader_ref.1) | copy-start | bytes 100
  14.2 29.3 %copy-start.7 = (f32[8,2,16]{2,1,0:T(2,128)S(1)}, f32[8,2,16]{2,1,0:T(2,128)}, u32[]{:S(2)}) copy-start(f32[8,2,16]{2,1,0:T(2,128)} %coords_ref.2) | copy-start | bytes 3076
  14.2 29.3 %copy-start.10 = (f32[1024]{0:T(1024)S(1)}, f32[1024]{0:T(1024)}, u32[]{:S(2)}) copy-start(f32[1024]{0:T(1024)} %param.19) | copy-start | bytes 12292
  20.9 3.3 %collective-permute-start = (bf16[16,4,2048]{2,1,0:T(4,128)(2,1)S(1)}, bf16[16,4,2048]{2,1,0:T(4,128)(2,1)S(1)}, u32[]{:S(2)}, u32[]{:S(2)}) collective-permute-start(bf16[16,4,2048]{2,1,0:T(4,128)(2,1)S(1)} %all-to-all-done.near_ref), channel_id=1, source_target_pairs={{0,1},{1,0},{2,3},{3,2},{4,5},{5,4},{6,7},{7,6},{8,9},{9,8},{10,11... | collective-permute-start | bytes 786440 | tf_op jit(solution)/shard_map/ppermute | solution.py:371
  24.8 9.9 %collective-permute-start.5 = (bf16[2,256,128]{2,1,0:T(8,128)(2,1)S(1)}, bf16[2,256,128]{2,1,0:T(8,128)(2,1)S(1)}, u32[]{:S(2)}, u32[]{:S(2)}) collective-permute-start(bf16[2,256,128]{2,1,0:T(8,128)(2,1)S(1)} %get-tuple-element.48), channel_id=1, source_target_pairs={{0,128},{64,192},{128,0},{192,64},{1,129},{65,193},{129,1},{193,65... | collective-permute-start | bytes 393224 | tf_op jit(solution)/shard_map/image_sum/ppermute | solution.py:371
  27.8 6.9 %collective-permute-start.6 = (bf16[2,256,128]{2,1,0:T(8,128)(2,1)S(1)}, bf16[2,256,128]{2,1,0:T(8,128)(2,1)S(1)}, u32[]{:S(2)}, u32[]{:S(2)}) collective-permute-start(bf16[2,256,128]{2,1,0:T(8,128)(2,1)S(1)} %get-tuple-element.49), channel_id=1, source_target_pairs={{0,64},{64,128},{128,192},{192,0},{1,65},{65,129},{129,193},{193,1... | collective-permute-start | bytes 393224 | tf_op jit(solution)/shard_map/image_sum/ppermute | solution.py:371
  28.2 6.5 %collective-permute-start.7 = (bf16[2,256,128]{2,1,0:T(8,128)(2,1)S(1)}, bf16[2,256,128]{2,1,0:T(8,128)(2,1)S(1)}, u32[]{:S(2)}, u32[]{:S(2)}) collective-permute-start(bf16[2,256,128]{2,1,0:T(8,128)(2,1)S(1)} %get-tuple-element.50), channel_id=1, source_target_pairs={{0,192},{64,0},{128,64},{192,128},{1,193},{65,1},{129,65},{193,129... | collective-permute-start | bytes 393224 | tf_op jit(solution)/shard_map/image_sum/ppermute | solution.py:371
  30.5 8.3 %collective-permute-start.1 = (bf16[16,2048]{1,0:T(8,128)(2,1)S(1)}, bf16[16,2048]{1,0:T(8,128)(2,1)S(1)}, u32[]{:S(2)}, u32[]{:S(2)}) collective-permute-start(bf16[16,2048]{1,0:T(8,128)(2,1)S(1)} %bitcast.5), channel_id=1, source_target_pairs={{0,32},{32,0},{1,33},{33,1},{2,34},{34,2},{3,35},{35,3},{4,36},{36... | collective-permute-start | bytes 196616 | tf_op jit(solution)/shard_map/visible_route/ppermute | solution.py:371
  34.8 10.3 %collective-permute-start.8 = (f32[256,128]{1,0:T(8,128)S(1)}, f32[256,128]{1,0:T(8,128)S(1)}, u32[]{:S(2)}, u32[]{:S(2)}) collective-permute-start(f32[256,128]{1,0:T(8,128)S(1)} %get-tuple-element.53), channel_id=1, source_target_pairs={{0,32},{32,0},{1,33},{33,1},{2,34},{34,2},{3,35},{35,3},{4,36},{36... | collective-permute-start | bytes 393224 | tf_op jit(solution)/shard_map/image_sum/ppermute | solution.py:371
  39.4 7.4 %collective-permute-start.2 = (bf16[16,2048]{1,0:T(8,128)(2,1)S(1)}, bf16[16,2048]{1,0:T(8,128)(2,1)S(1)}, u32[]{:S(2)}, u32[]{:S(2)}) collective-permute-start(bf16[16,2048]{1,0:T(8,128)(2,1)S(1)} %get-tuple-element.44), channel_id=1, source_target_pairs={{0,64},{64,128},{128,192},{192,0},{1,65},{65,129},{129,193},{193,1... | collective-permute-start | bytes 196616 | tf_op jit(solution)/shard_map/ppermute | solution.py:371
  41.0 5.8 %collective-permute-start.3 = (bf16[16,2048]{1,0:T(8,128)(2,1)S(1)}, bf16[16,2048]{1,0:T(8,128)(2,1)S(1)}, u32[]{:S(2)}, u32[]{:S(2)}) collective-permute-start(bf16[16,2048]{1,0:T(8,128)(2,1)S(1)} %get-tuple-element.45), channel_id=1, source_target_pairs={{0,128},{64,192},{128,0},{192,64},{1,129},{65,193},{129,1},{193,65... | collective-permute-start | bytes 196616 | tf_op jit(solution)/shard_map/ppermute | solution.py:371
  43.1 3.8 %collective-permute-start.4 = (bf16[16,2048]{1,0:T(8,128)(2,1)S(1)}, bf16[16,2048]{1,0:T(8,128)(2,1)S(1)}, u32[]{:S(2)}, u32[]{:S(2)}) collective-permute-start(bf16[16,2048]{1,0:T(8,128)(2,1)S(1)} %get-tuple-element.46), channel_id=1, source_target_pairs={{0,192},{64,0},{128,64},{192,128},{1,193},{65,1},{129,65},{193,129... | collective-permute-start | bytes 196616 | tf_op jit(solution)/shard_map/ppermute | solution.py:371
  48.1 8.8 %collective-permute-start.9 = (bf16[256,128]{1,0:T(8,128)(2,1)S(1)}, bf16[256,128]{1,0:T(8,128)(2,1)S(1)}, u32[]{:S(2)}, u32[]{:S(2)}) collective-permute-start(bf16[256,128]{1,0:T(8,128)(2,1)S(1)} %grid.1.refs_0_), channel_id=1, source_target_pairs={{0,32},{32,0},{1,33},{33,1},{2,34},{34,2},{3,35},{35,3},{4,36},{36... | collective-permute-start | bytes 196616 | tf_op jit(solution)/shard_map/grid_gather/ppermute | solution.py:371
  52.9 5.9 %collective-permute-start.10 = (bf16[256,128]{1,0:T(8,128)(2,1)S(1)}, bf16[256,128]{1,0:T(8,128)(2,1)S(1)}, u32[]{:S(2)}, u32[]{:S(2)}) collective-permute-start(bf16[256,128]{1,0:T(8,128)(2,1)S(1)} %grid.1.refs_0_), channel_id=1, source_target_pairs={{0,64},{64,128},{128,192},{192,0},{1,65},{65,129},{129,193},{193,1... | collective-permute-start | bytes 196616 | tf_op jit(solution)/shard_map/grid_gather/ppermute | solution.py:371
  54.4 6.3 %collective-permute-start.12 = (bf16[256,128]{1,0:T(8,128)(2,1)S(1)}, bf16[256,128]{1,0:T(8,128)(2,1)S(1)}, u32[]{:S(2)}, u32[]{:S(2)}) collective-permute-start(bf16[256,128]{1,0:T(8,128)(2,1)S(1)} %grid.1.refs_0_), channel_id=1, source_target_pairs={{0,128},{64,192},{128,0},{192,64},{1,129},{65,193},{129,1},{193,65... | collective-permute-start | bytes 196616 | tf_op jit(solution)/shard_map/grid_gather/ppermute | solution.py:371
  54.4 6.3 %collective-permute-start.14 = (bf16[256,128]{1,0:T(8,128)(2,1)S(1)}, bf16[256,128]{1,0:T(8,128)(2,1)S(1)}, u32[]{:S(2)}, u32[]{:S(2)}) collective-permute-start(bf16[256,128]{1,0:T(8,128)(2,1)S(1)} %grid.1.refs_0_), channel_id=1, source_target_pairs={{0,192},{64,0},{128,64},{192,128},{1,193},{65,1},{129,65},{193,129... | collective-permute-start | bytes 196616 | tf_op jit(solution)/shard_map/grid_gather/ppermute | solution.py:371
  56.8 5.5 %collective-permute-start.11 = (bf16[256,128]{1,0:T(8,128)(2,1)S(1)}, bf16[256,128]{1,0:T(8,128)(2,1)S(1)}, u32[]{:S(2)}, u32[]{:S(2)}) collective-permute-start(bf16[256,128]{1,0:T(8,128)(2,1)S(1)} %collective-permute-done.9.refs_1_), channel_id=1, source_target_pairs={{0,64},{64,128},{128,192},{192,0},{1,65},{65,129},{129,193},{193,1... | collective-permute-start | bytes 196616 | tf_op jit(solution)/shard_map/grid_gather/ppermute | solution.py:371
  57.0 5.3 %collective-permute-start.13 = (bf16[256,128]{1,0:T(8,128)(2,1)S(1)}, bf16[256,128]{1,0:T(8,128)(2,1)S(1)}, u32[]{:S(2)}, u32[]{:S(2)}) collective-permute-start(bf16[256,128]{1,0:T(8,128)(2,1)S(1)} %collective-permute-done.9.refs_1_), channel_id=1, source_target_pairs={{0,128},{64,192},{128,0},{192,64},{1,129},{65,193},{129,1},{193,65... | collective-permute-start | bytes 196616 | tf_op jit(solution)/shard_map/grid_gather/ppermute | solution.py:371
  58.9 4.0 %collective-permute-start.15 = (bf16[256,128]{1,0:T(8,128)(2,1)S(1)}, bf16[256,128]{1,0:T(8,128)(2,1)S(1)}, u32[]{:S(2)}, u32[]{:S(2)}) collective-permute-start(bf16[256,128]{1,0:T(8,128)(2,1)S(1)} %collective-permute-done.9.refs_1_), channel_id=1, source_target_pairs={{0,192},{64,0},{128,64},{192,128},{1,193},{65,1},{129,65},{193,129... | collective-permute-start | bytes 196616 | tf_op jit(solution)/shard_map/grid_gather/ppermute | solution.py:371
  63.4 4.9 %collective-permute-start.16 = (bf16[64,2048]{1,0:T(8,128)(2,1)S(1)}, bf16[64,2048]{1,0:T(8,128)(2,1)S(1)}, u32[]{:S(2)}, u32[]{:S(2)}) collective-permute-start(bf16[64,2048]{1,0:T(8,128)(2,1)S(1)} %regrid_far.1), channel_id=1, source_target_pairs={{0,1},{1,0},{2,3},{3,2},{4,5},{5,4},{6,7},{7,6},{8,9},{9,8},{10,11... | collective-permute-start | bytes 786440 | tf_op jit(solution)/shard_map/dirty_scatter/ppermute | solution.py:371
  68.3 4.8 %collective-permute-start.17 = (bf16[16,2048]{1,0:T(8,128)(2,1)S(1)}, bf16[16,2048]{1,0:T(8,128)(2,1)S(1)}, u32[]{:S(2)}, u32[]{:S(2)}) collective-permute-start(bf16[16,2048]{1,0:T(8,128)(2,1)S(1)} %get-tuple-element.63), channel_id=1, source_target_pairs={{0,16},{8,24},{16,0},{24,8},{1,17},{9,25},{17,1},{25,9},{2,18},{10... | collective-permute-start | bytes 196616 | tf_op jit(solution)/shard_map/dirty_scatter/ppermute | solution.py:371
  68.9 6.0 %collective-permute-start.18 = (bf16[16,2048]{1,0:T(8,128)(2,1)S(1)}, bf16[16,2048]{1,0:T(8,128)(2,1)S(1)}, u32[]{:S(2)}, u32[]{:S(2)}) collective-permute-start(bf16[16,2048]{1,0:T(8,128)(2,1)S(1)} %get-tuple-element.64), channel_id=1, source_target_pairs={{0,8},{8,16},{16,24},{24,0},{1,9},{9,17},{17,25},{25,1},{2,10},{10... | collective-permute-start | bytes 196616 | tf_op jit(solution)/shard_map/dirty_scatter/ppermute | solution.py:371
  69.5 5.5 %collective-permute-start.19 = (bf16[16,2048]{1,0:T(8,128)(2,1)S(1)}, bf16[16,2048]{1,0:T(8,128)(2,1)S(1)}, u32[]{:S(2)}, u32[]{:S(2)}) collective-permute-start(bf16[16,2048]{1,0:T(8,128)(2,1)S(1)} %get-tuple-element.65), channel_id=1, source_target_pairs={{0,24},{8,0},{16,8},{24,16},{1,25},{9,1},{17,9},{25,17},{2,26},{10... | collective-permute-start | bytes 196616 | tf_op jit(solution)/shard_map/dirty_scatter/ppermute | solution.py:371
  75.0 4.7 %collective-permute-start.20 = (f32[4,2048]{1,0:T(4,128)S(1)}, f32[4,2048]{1,0:T(4,128)S(1)}, u32[]{:S(2)}, u32[]{:S(2)}) collective-permute-start(f32[4,2048]{1,0:T(4,128)S(1)} %get-tuple-element.67), channel_id=1, source_target_pairs={{0,6},{2,4},{4,2},{6,0},{1,7},{3,5},{5,3},{7,1},{8,14},{10,12},{12... | collective-permute-start | bytes 98312 | tf_op jit(solution)/shard_map/dirty_scatter/ppermute | solution.py:366
  75.1 4.6 %collective-permute-start.21 = (f32[4,2048]{1,0:T(4,128)S(1)}, f32[4,2048]{1,0:T(4,128)S(1)}, u32[]{:S(2)}, u32[]{:S(2)}) collective-permute-start(f32[4,2048]{1,0:T(4,128)S(1)} %get-tuple-element.68), channel_id=1, source_target_pairs={{0,4},{2,6},{4,0},{6,2},{1,5},{3,7},{5,1},{7,3},{8,12},{10,14},{12... | collective-permute-start | bytes 98312 | tf_op jit(solution)/shard_map/dirty_scatter/ppermute | solution.py:366
  76.2 4.1 %collective-permute-start.22 = (f32[4,2048]{1,0:T(4,128)S(1)}, f32[4,2048]{1,0:T(4,128)S(1)}, u32[]{:S(2)}, u32[]{:S(2)}) collective-permute-start(f32[4,2048]{1,0:T(4,128)S(1)} %get-tuple-element.69), channel_id=1, source_target_pairs={{0,2},{2,0},{4,6},{6,4},{1,3},{3,1},{5,7},{7,5},{8,10},{10,8},{12,... | collective-permute-start | bytes 98312 | tf_op jit(solution)/shard_map/dirty_scatter/ppermute | solution.py:366

commit v12 on v11

--- a/solution.py
+++ b/solution.py
@@ -107,7 +107,7 @@
     n_x, n_z, n_c = sizes
     row, rest = (lax.rem(subgrid, owned), lax.div(subgrid, owned))
     core, rest = (lax.rem(rest, n_c), lax.div(rest, n_c))
-    x = lax.rem(lax.div(rest, n_z) + n_x - lax.axis_index("x"), n_x)
+    x = lax.bitwise_xor(lax.div(rest, n_z), jnp.full_like(rest, lax.axis_index("x")))
     z = lax.bitwise_xor(lax.rem(rest, n_z), jnp.full_like(rest, lax.axis_index("z")))
     core = lax.rem(core + n_c - lax.axis_index("c"), n_c)
     return ((core * n_x + x) * n_z + z) * owned + row
@@ -171,7 +171,7 @@
 def blocks_from(n_y, n_h, sign):
     at_y, at_h = (lax.axis_index("y"), lax.axis_index("h"))
     return [
-        lax.rem(at_y + (n_y + sign * by) % n_y, n_y) * n_h + lax.rem(at_h + flip, n_h)
+        lax.bitwise_xor(at_y, jnp.int32(by)) * n_h + lax.rem(at_h + flip, n_h)
         for by in range(n_y)
         for flip in range(n_h)
     ]
@@ -222,14 +222,14 @@
     at_y, at_h = (lax.axis_index("y"), lax.axis_index("h"))
     own = at_y * n_h + at_h
     source = reader_ref[0, own]
-    steps = lax.rem(at_y + n_y - lax.div(source, n_h), n_y)
+    steps = lax.bitwise_xor(at_y, lax.div(source, n_h))
     here = jnp.where(lax.rem(source, n_h) == at_h, 0, 1)
     pick_ref[...] = jnp.full(pick_ref.shape, jnp.where(steps == 0, here, steps + 1), jnp.int32)
     block = jnp.int32(0)
     for at in range(n_y * n_h):
         block = jnp.where(reader_ref[0, at] == own, at, block)
     for by, out_ref in enumerate(out_refs, 1):
-        to = lax.rem(at_y + by, n_y) * n_h + at_h
+        to = lax.bitwise_xor(at_y, jnp.int32(by)) * n_h + at_h
 
         @pl.when(block == to)
         def _():
@@ -465,7 +465,7 @@
         )(reader, rows, other)
 
     with jax.named_scope("image_sum"):
-        pieces = [images[0]] + [shift(images[by], "y", by) for by in far_first(n_y)]
+        pieces = [images[0]] + [pair(images[by], "y", by) for by in far_first(n_y)]
         own_sum, other_sum = pl.pallas_call(
             sum_kernel,
             out_shape=[jax.ShapeDtypeStruct((cell_rows, 128), F32)] * 2,
@@ -479,7 +479,7 @@
         beside_sum = shift(other_sum, "h", 1)
 
     east = table(0, later)
-    came = dict((by, shift(sent[by - 1], "y", by)) for by in far_first(n_y))
+    came = dict((by, pair(sent[by - 1], "y", by)) for by in far_first(n_y))
     came = [came[by] for by in range(1, n_y)]
 
     predicted = pl.pallas_call(
@@ -507,7 +507,7 @@
 
     with jax.named_scope("grid_gather"):
         beside = shift(gridded, "h", 1)
-        moved = dict((by, (shift(gridded, "y", by), shift(beside, "y", by))) for by in reversed(far_first(n_y)))
+        moved = dict((by, (pair(gridded, "y", by), pair(beside, "y", by))) for by in reversed(far_first(n_y)))
         grids = [gridded, beside]
         for by in range(1, n_y):
             grids += moved[by]
@@ -564,7 +564,7 @@
             near_sum,
             far_sum,
         )
-        sent = [shift(sent[by - 1], "x", by) for by in far_first(n_x)]
+        sent = [pair(sent[by - 1], "x", by) for by in far_first(n_x)]
         own, *sent = call(
             column_kernel, "column_sums", [jax.ShapeDtypeStruct((owned, 2 * pixels), F32)] * n_z, own, *sent
         )

time: 82.4 us -> 84.5 us (1.025)
  waiting for transfers between devices: 13.3 us -> 16.7 us
  starting transfers between devices: 51.9 us -> 50.6 us
    ppermute x20 -> x5, starting transfers between devices: 39.1 us -> 16.6 us  [shift(): lax.ppermute(value, axis, [(i, (i + by) % size) for i in range(size)])]
    ppermute x3 -> x18, starting transfers between devices: 3.63 us -> 24.8 us  [pair(): lax.ppermute(value, axis, [(i, i ^ by) for i in range(lax.axis_size(axis))])]
    ppermute x3 -> x18, waiting for transfers between devices: 1.68 us -> 10.5 us  [pair(): lax.ppermute(value, axis, [(i, i ^ by) for i in range(lax.axis_size(axis))])]
    ppermute x20 -> x5, waiting for transfers between devices: 7.33 us -> 1.86 us  [shift(): lax.ppermute(value, axis, [(i, (i + by) % size) for i in range(size)])]
  transfers between devices with their start and end apart: 24 -> 24, of which waited for: 9 -> 11; matrix products, arithmetic and copies ran while one was open for 0% -> 0% of each run, Pallas kernels for 11% -> 11%
where the time goes in v12:
time: 84.5 us; the launch traced here: 83 us
  starting transfers between devices  50.6 us (60%)
  waiting for transfers between devices  16.7 us (20%)
  Pallas kernels  13.2 us (16%)
  local copies, waits for them, and re-layouts  1.58 us (2%)
  between operations  0.87 us (1%)
    ppermute x18, starting transfers between devices, pair(): lax.ppermute(value, axis, [(i, i ^ by) for i in range(lax.axis_size(axis))])  24.8 us
    ppermute x5, starting transfers between devices, shift(): lax.ppermute(value, axis, [(i, (i + by) % size) for i in range(size)])  16.6 us
    ppermute x18, waiting for transfers between devices, pair(): lax.ppermute(value, axis, [(i, i ^ by) for i in range(lax.axis_size(axis))])  10.5 us
    all_to_all x1, starting transfers between devices, local(): lax.all_to_all(copies, ('x', 'z'), split_axis=0, concat_axis=0, tiled=True)  9.15 us
    all_to_all x1, waiting for transfers between devices, local(): lax.all_to_all(copies, ('x', 'z'), split_axis=0, concat_axis=0, tiled=True)  4.34 us
    pallas_call x2, Pallas kernels, table(): pl.pallas_call(functools.partial(table_kernel, n_h, kind), out_shape=jax....  2.95 us
    pallas_call x1, Pallas kernels, local(): pl.pallas_call(screen_kernel, out_shape=jax.ShapeDtypeStruct((count, 2 *...  2.35 us
    ppermute x5, waiting for transfers between devices, shift(): lax.ppermute(value, axis, [(i, (i + by) % size) for i in range(size)])  1.86 us
  transfers between devices with their start and end apart: 24, of which 11 were waited for; matrix products, arithmetic and copies ran while one was open for 0% of the time, Pallas kernels for 11%

profile of v12, /device:TPU:1, one launch (start us, length us, event | category | flops | bytes accessed | tf_op | source)
XLA Modules:
  0.0 83.0 jit_solution(12080021265389911130)
XLA Ops:
  0.6 1.4 %repeat.1 = bf16[16,4,2048]{2,1,0:T(4,128)(2,1)} custom-call(bf16[1,4,2048]{2,1,0:T(4,128)(2,1)} %rows_ref.1), custom_call_target="tpu_custom_call" | custom-call | bytes 262144 | tf_op jit(solution)/shard_map/model_gather/repeat/pallas_call | solution.py:401
  2.1 9.1 %all-to-all-start = ((bf16[16,4,2048]{2,1,0:T(4,128)(2,1)}), bf16[16,4,2048]{2,1,0:T(4,128)(2,1)S(1)}, u32[]{:S(2)}, u32[]{:S(2)}) async-start(bf16[16,4,2048]{2,1,0:T(4,128)(2,1)} %repeat.1), calls=%async_computation | async-start | bytes 524288 | tf_op jit(solution)/shard_map/model_gather/all_to_all | solution.py:410
  11.2 0.0 copy-start.3
  11.3 0.8 %copy-done.6 = f32[8,2,16]{2,1,0:T(2,128)S(1)} copy-done((f32[8,2,16]{2,1,0:T(2,128)S(1)}, f32[8,2,16]{2,1,0:T(2,128)}, u32[]{:S(2)}) %copy-start.6) | copy-done | bytes 1048
  12.1 0.7 copy-done.9
  12.8 1.3 %north.1.north_ref = bf16[16,64,1024]{2,1,0:T(8,128)(2,1)S(1)} custom-call(f32[8,2,16]{2,1,0:T(2,128)S(1)} %copy-done.6, f32[1,1024]{1,0:T(1,128)S(1)} %bitcast.10), custom_call_target="tpu_custom_call" | custom-call | flops 1000000000 | bytes 4194304 | tf_op jit(solution)/shard_map/north/pallas_call | solution.py:426
  14.1 0.0 copy-start.1
  14.2 2.4 %screens.1.screen_ref = f32[128,2048]{1,0:T(8,128)S(1)} custom-call(s32[8,2,16]{2,1,0:T(2,128)S(1)} %copy-done.5, s32[8,16]{1,0:T(8,128)S(1)} %copy-done.8, f32[32,1024]{1,0:T(8,128)S(1)} %copy-done.4, bf16[512,2048]{1,0:T(8,128)(2,1)S(1)} %bitcast.9), custom_call_target="tpu_custom_call" | custom-call | flops 1000000000 | bytes 4194304 | tf_op jit(solution)/shard_map/screens/pallas_call | solution.py:413
  16.6 4.3 %all-to-all-done.near_ref = bf16[16,4,2048]{2,1,0:T(4,128)(2,1)S(1)} async-done(((bf16[16,4,2048]{2,1,0:T(4,128)(2,1)}), bf16[16,4,2048]{2,1,0:T(4,128)(2,1)S(1)}, u32[]{:S(2)}, u32[]{:S(2)}) %all-to-all-start) | async-done | bytes 262176 | tf_op jit(solution)/shard_map/model_gather/all_to_all | solution.py:410
  20.9 2.1 %collective-permute-start = (bf16[16,4,2048]{2,1,0:T(4,128)(2,1)S(1)}, bf16[16,4,2048]{2,1,0:T(4,128)(2,1)S(1)}, u32[]{:S(2)}, u32[]{:S(2)}) collective-permute-start(bf16[16,4,2048]{2,1,0:T(4,128)(2,1)S(1)} %all-to-all-done.near_ref), channel_id=1, source_target_pairs={{0,1},{1,0},{2,3},{3,2},{4,5},{5,4},{6,7},{7,6},{8,9},{9,8},{10,11... | collective-permute-start | bytes 786440 | tf_op jit(solution)/shard_map/ppermute | solution.py:371
  23.1 1.2 %collective-permute-done.far_ref = bf16[16,4,2048]{2,1,0:T(4,128)(2,1)S(1)} collective-permute-done((bf16[16,4,2048]{2,1,0:T(4,128)(2,1)S(1)}, bf16[16,4,2048]{2,1,0:T(4,128)(2,1)S(1)}, u32[]{:S(2)}, u32[]{:S(2)}) %collective-permute-start) | collective-permute-done | bytes 262176 | tf_op jit(solution)/shard_map/ppermute | solution.py:371
  24.2 0.6 images.1
  24.8 3.0 %collective-permute-start.5 = (bf16[2,256,128]{2,1,0:T(8,128)(2,1)S(1)}, bf16[2,256,128]{2,1,0:T(8,128)(2,1)S(1)}, u32[]{:S(2)}, u32[]{:S(2)}) collective-permute-start(bf16[2,256,128]{2,1,0:T(8,128)(2,1)S(1)} %get-tuple-element.48), channel_id=1, source_target_pairs={{0,128},{64,192},{128,0},{192,64},{1,129},{65,193},{129,1},{193,65... | collective-permute-start | bytes 393224 | tf_op jit(solution)/shard_map/image_sum/ppermute | solution.py:366
  27.8 0.4 collective-permute-start.6
  28.2 0.4 collective-permute-start.7
  28.6 4.2 %collective-permute-start.1 = (bf16[16,2048]{1,0:T(8,128)(2,1)S(1)}, bf16[16,2048]{1,0:T(8,128)(2,1)S(1)}, u32[]{:S(2)}, u32[]{:S(2)}) collective-permute-start(bf16[16,2048]{1,0:T(8,128)(2,1)S(1)} %bitcast.5), channel_id=1, source_target_pairs={{0,32},{32,0},{1,33},{33,1},{2,34},{34,2},{3,35},{35,3},{4,36},{36... | collective-permute-start | bytes 196616 | tf_op jit(solution)/shard_map/visible_route/ppermute | solution.py:371
  32.8 1.5 %collective-permute-done.6.refs_2_ = bf16[2,256,128]{2,1,0:T(8,128)(2,1)S(1)} collective-permute-done((bf16[2,256,128]{2,1,0:T(8,128)(2,1)S(1)}, bf16[2,256,128]{2,1,0:T(8,128)(2,1)S(1)}, u32[]{:S(2)}, u32[]{:S(2)}) %collective-permute-start.6) | collective-permute-done | bytes 131104 | tf_op jit(solution)/shard_map/image_sum/ppermute | solution.py:366
  34.3 0.1 image_sums.1
  34.4 4.3 %collective-permute-start.8 = (f32[256,128]{1,0:T(8,128)S(1)}, f32[256,128]{1,0:T(8,128)S(1)}, u32[]{:S(2)}, u32[]{:S(2)}) collective-permute-start(f32[256,128]{1,0:T(8,128)S(1)} %get-tuple-element.53), channel_id=1, source_target_pairs={{0,32},{32,0},{1,33},{33,1},{2,34},{34,2},{3,35},{35,3},{4,36},{36... | collective-permute-start | bytes 393224 | tf_op jit(solution)/shard_map/image_sum/ppermute | solution.py:371
  38.7 0.6 route.1
  39.3 1.3 %collective-permute-start.2 = (bf16[16,2048]{1,0:T(8,128)(2,1)S(1)}, bf16[16,2048]{1,0:T(8,128)(2,1)S(1)}, u32[]{:S(2)}, u32[]{:S(2)}) collective-permute-start(bf16[16,2048]{1,0:T(8,128)(2,1)S(1)} %get-tuple-element.44), channel_id=1, source_target_pairs={{0,64},{64,0},{128,192},{192,128},{1,65},{65,1},{129,193},{193,129... | collective-permute-start | bytes 196616 | tf_op jit(solution)/shard_map/ppermute | solution.py:366
  40.6 3.1 %collective-permute-start.3 = (bf16[16,2048]{1,0:T(8,128)(2,1)S(1)}, bf16[16,2048]{1,0:T(8,128)(2,1)S(1)}, u32[]{:S(2)}, u32[]{:S(2)}) collective-permute-start(bf16[16,2048]{1,0:T(8,128)(2,1)S(1)} %get-tuple-element.45), channel_id=1, source_target_pairs={{0,128},{64,192},{128,0},{192,64},{1,129},{65,193},{129,1},{193,65... | collective-permute-start | bytes 196616 | tf_op jit(solution)/shard_map/ppermute | solution.py:366
  43.6 1.6 %east.1.east_ref = bf16[16,64,1024]{2,1,0:T(8,128)(2,1)S(1)} custom-call(f32[8,2,16]{2,1,0:T(2,128)S(1)} %copy-done.7, f32[1,1024]{1,0:T(1,128)S(1)} %bitcast.11), custom_call_target="tpu_custom_call" | custom-call | flops 1000000000 | bytes 4194304 | tf_op jit(solution)/shard_map/east/pallas_call | solution.py:426
  45.3 1.7 %degrid.1.predicted_ref.refs_5_ = f32[16,2048]{1,0:T(8,128)S(1)} custom-call(f32[256,128]{1,0:T(8,128)S(1)} %get-tuple-element.52.near_ref, f32[256,128]{1,0:T(8,128)S(1)} %collective-permute-done.8.far_ref, bf16[16,64,1024]{2,1,0:T(8,128)(2,1)S(1)} %east.1.east_ref, bf16[16,64,1024]{2,1,0:T(8,128)(2,1)S(1)} %north.1.north_ref), custom_call_target="tpu_custom_call" | custom-call | flops 1000000000 | bytes 5242880 | tf_op jit(solution)/shard_map/degrid/pallas_call | solution.py:485
  47.0 1.1 %collective-permute-done.4.came_3_ref.refs_4_ = bf16[16,2048]{1,0:T(8,128)(2,1)S(1)} collective-permute-done((bf16[16,2048]{1,0:T(8,128)(2,1)S(1)}, bf16[16,2048]{1,0:T(8,128)(2,1)S(1)}, u32[]{:S(2)}, u32[]{:S(2)}) %collective-permute-start.4) | collective-permute-done | bytes 65568 | tf_op jit(solution)/shard_map/ppermute | solution.py:366
  48.1 1.2 %grid.1.refs_0_ = bf16[256,128]{1,0:T(8,128)(2,1)S(1)} custom-call(s32[16,128]{1,0:T(8,128)S(1)} %get-tuple-element.56.pick_ref, bf16[16,2048]{1,0:T(8,128)(2,1)S(1)} %bitcast.7, bf16[16,2048]{1,0:T(8,128)(2,1)S(1)} %collective-permute-done.1.other_ref.refs_1_, bf16[16,2048]{1,0:T(8,128)(2,1)S(1)} %collective-permute-done.2.came_1_ref.refs_2_, ...), custom_call_target="tpu_custom_call" | custom-call | flops 1000000000 | bytes 5242880 | tf_op jit(solution)/shard_map/grid/pallas_call | solution.py:497
  49.3 1.9 %collective-permute-start.9 = (bf16[256,128]{1,0:T(8,128)(2,1)S(1)}, bf16[256,128]{1,0:T(8,128)(2,1)S(1)}, u32[]{:S(2)}, u32[]{:S(2)}) collective-permute-start(bf16[256,128]{1,0:T(8,128)(2,1)S(1)} %grid.1.refs_0_), channel_id=1, source_target_pairs={{0,32},{32,0},{1,33},{33,1},{2,34},{34,2},{3,35},{35,3},{4,36},{36... | collective-permute-start | bytes 196616 | tf_op jit(solution)/shard_map/grid_gather/ppermute | solution.py:371
  51.2 1.2 %collective-permute-start.10 = (bf16[256,128]{1,0:T(8,128)(2,1)S(1)}, bf16[256,128]{1,0:T(8,128)(2,1)S(1)}, u32[]{:S(2)}, u32[]{:S(2)}) collective-permute-start(bf16[256,128]{1,0:T(8,128)(2,1)S(1)} %grid.1.refs_0_), channel_id=1, source_target_pairs={{0,64},{64,0},{128,192},{192,128},{1,65},{65,1},{129,193},{193,129... | collective-permute-start | bytes 196616 | tf_op jit(solution)/shard_map/grid_gather/ppermute | solution.py:366
  52.4 4.7 %collective-permute-start.12 = (bf16[256,128]{1,0:T(8,128)(2,1)S(1)}, bf16[256,128]{1,0:T(8,128)(2,1)S(1)}, u32[]{:S(2)}, u32[]{:S(2)}) collective-permute-start(bf16[256,128]{1,0:T(8,128)(2,1)S(1)} %grid.1.refs_0_), channel_id=1, source_target_pairs={{0,128},{64,192},{128,0},{192,64},{1,129},{65,193},{129,1},{193,65... | collective-permute-start | bytes 196616 | tf_op jit(solution)/shard_map/grid_gather/ppermute | solution.py:366
  57.1 3.8 %collective-permute-start.13 = (bf16[256,128]{1,0:T(8,128)(2,1)S(1)}, bf16[256,128]{1,0:T(8,128)(2,1)S(1)}, u32[]{:S(2)}, u32[]{:S(2)}) collective-permute-start(bf16[256,128]{1,0:T(8,128)(2,1)S(1)} %collective-permute-done.9.refs_1_), channel_id=1, source_target_pairs={{0,128},{64,192},{128,0},{192,64},{1,129},{65,193},{129,1},{193,65... | collective-permute-start | bytes 196616 | tf_op jit(solution)/shard_map/grid_gather/ppermute | solution.py:366
  61.0 0.7 residual.1
  61.7 1.7 %collective-permute-done.13.refs_5_ = bf16[256,128]{1,0:T(8,128)(2,1)S(1)} collective-permute-done((bf16[256,128]{1,0:T(8,128)(2,1)S(1)}, bf16[256,128]{1,0:T(8,128)(2,1)S(1)}, u32[]{:S(2)}, u32[]{:S(2)}) %collective-permute-start.13) | collective-permute-done | bytes 65568 | tf_op jit(solution)/shard_map/grid_gather/ppermute | solution.py:366
  63.4 1.9 %collective-permute-done.15.refs_7_ = bf16[256,128]{1,0:T(8,128)(2,1)S(1)} collective-permute-done((bf16[256,128]{1,0:T(8,128)(2,1)S(1)}, bf16[256,128]{1,0:T(8,128)(2,1)S(1)}, u32[]{:S(2)}, u32[]{:S(2)}) %collective-permute-start.15) | collective-permute-done | bytes 65568 | tf_op jit(solution)/shard_map/grid_gather/ppermute | solution.py:366
  65.3 0.5 regrid_far.1
  65.8 4.0 %collective-permute-start.16 = (bf16[64,2048]{1,0:T(8,128)(2,1)S(1)}, bf16[64,2048]{1,0:T(8,128)(2,1)S(1)}, u32[]{:S(2)}, u32[]{:S(2)}) collective-permute-start(bf16[64,2048]{1,0:T(8,128)(2,1)S(1)} %regrid_far.1), channel_id=1, source_target_pairs={{0,1},{1,0},{2,3},{3,2},{4,5},{5,4},{6,7},{7,6},{8,9},{9,8},{10,11... | collective-permute-start | bytes 786440 | tf_op jit(solution)/shard_map/dirty_scatter/ppermute | solution.py:371
  69.8 0.5 regrid_near.1.near_ref
  70.3 0.7 collective-permute-done.16.far_ref
  71.0 0.6 collective-permute-start.17
  71.6 0.4 collective-permute-start.18
  72.0 2.4 %collective-permute-start.19 = (bf16[16,2048]{1,0:T(8,128)(2,1)S(1)}, bf16[16,2048]{1,0:T(8,128)(2,1)S(1)}, u32[]{:S(2)}, u32[]{:S(2)}) collective-permute-start(bf16[16,2048]{1,0:T(8,128)(2,1)S(1)} %get-tuple-element.65), channel_id=1, source_target_pairs={{0,24},{8,16},{16,8},{24,0},{1,25},{9,17},{17,9},{25,1},{2,26},{10... | collective-permute-start | bytes 196616 | tf_op jit(solution)/shard_map/dirty_scatter/ppermute | solution.py:366
  74.3 1.4 %collective-permute-done.17.refs_0_ = bf16[16,2048]{1,0:T(8,128)(2,1)S(1)} collective-permute-done((bf16[16,2048]{1,0:T(8,128)(2,1)S(1)}, bf16[16,2048]{1,0:T(8,128)(2,1)S(1)}, u32[]{:S(2)}, u32[]{:S(2)}) %collective-permute-start.17) | collective-permute-done | bytes 65568 | tf_op jit(solution)/shard_map/dirty_scatter/ppermute | solution.py:366
  75.7 1.6 %collective-permute-done.19.refs_2_ = bf16[16,2048]{1,0:T(8,128)(2,1)S(1)} collective-permute-done((bf16[16,2048]{1,0:T(8,128)(2,1)S(1)}, bf16[16,2048]{1,0:T(8,128)(2,1)S(1)}, u32[]{:S(2)}, u32[]{:S(2)}) %collective-permute-start.19) | collective-permute-done | bytes 65568 | tf_op jit(solution)/shard_map/dirty_scatter/ppermute | solution.py:366
  77.3 0.1 collective-permute-start.20
  77.4 1.2 %collective-permute-start.21 = (f32[4,2048]{1,0:T(4,128)S(1)}, f32[4,2048]{1,0:T(4,128)S(1)}, u32[]{:S(2)}, u32[]{:S(2)}) collective-permute-start(f32[4,2048]{1,0:T(4,128)S(1)} %get-tuple-element.68), channel_id=1, source_target_pairs={{0,4},{2,6},{4,0},{6,2},{1,5},{3,7},{5,1},{7,3},{8,12},{10,14},{12... | collective-permute-start | bytes 98312 | tf_op jit(solution)/shard_map/dirty_scatter/ppermute | solution.py:366
  78.7 2.3 %collective-permute-start.22 = (f32[4,2048]{1,0:T(4,128)S(1)}, f32[4,2048]{1,0:T(4,128)S(1)}, u32[]{:S(2)}, u32[]{:S(2)}) collective-permute-start(f32[4,2048]{1,0:T(4,128)S(1)} %get-tuple-element.69), channel_id=1, source_target_pairs={{0,2},{2,0},{4,6},{6,4},{1,3},{3,1},{5,7},{7,5},{8,10},{10,8},{12,... | collective-permute-start | bytes 98312 | tf_op jit(solution)/shard_map/dirty_scatter/ppermute | solution.py:366
  81.0 1.0 %collective-permute-done.20.refs_1_ = f32[4,2048]{1,0:T(4,128)S(1)} collective-permute-done((f32[4,2048]{1,0:T(4,128)S(1)}, f32[4,2048]{1,0:T(4,128)S(1)}, u32[]{:S(2)}, u32[]{:S(2)}) %collective-permute-start.20) | collective-permute-done | bytes 32800 | tf_op jit(solution)/shard_map/dirty_scatter/ppermute | solution.py:366
  82.0 0.3 collective-permute-done.22.refs_3_
  82.3 0.6 total.1
  (37 shorter events, 0.2 us)
Async XLA Ops:
  2.1 12.1 %copy-start.5 = (s32[8,2,16]{2,1,0:T(2,128)S(1)}, s32[8,2,16]{2,1,0:T(2,128)}, u32[]{:S(2)}) copy-start(s32[8,2,16]{2,1,0:T(2,128)} %stations_from.1) | copy-start | bytes 3076
  2.1 12.1 %copy-start.8 = (s32[8,16]{1,0:T(8,128)S(1)}, s32[8,16]{1,0:T(8,128)}, u32[]{:S(2)}) copy-start(s32[8,16]{1,0:T(8,128)} %plane_from.1) | copy-start | bytes 1540
  2.1 18.8 %all-to-all-start = ((bf16[16,4,2048]{2,1,0:T(4,128)(2,1)}), bf16[16,4,2048]{2,1,0:T(4,128)(2,1)S(1)}, u32[]{:S(2)}, u32[]{:S(2)}) async-start(bf16[16,4,2048]{2,1,0:T(4,128)(2,1)} %repeat.1), calls=%async_computation | async-start | bytes 524288 | tf_op jit(solution)/shard_map/model_gather/all_to_all | solution.py:410
  11.2 2.9 %copy-start.3 = (bf16[1,512,2048]{2,1,0:T(8,128)(2,1)S(1)}, bf16[1,512,2048]{2,1,0:T(8,128)(2,1)}, u32[]{:S(2)}) copy-start(bf16[1,512,2048]{2,1,0:T(8,128)(2,1)} %param.17) | copy-start | bytes 6291460
  11.2 2.9 %copy-start.4 = (f32[32,1024]{1,0:T(8,128)S(1)}, f32[32,1024]{1,0:T(8,128)}, u32[]{:S(2)}) copy-start(f32[32,1024]{1,0:T(8,128)} %phase_from.1) | copy-start | bytes 393220
  11.3 0.8 %copy-start.6 = (f32[8,2,16]{2,1,0:T(2,128)S(1)}, f32[8,2,16]{2,1,0:T(2,128)}, u32[]{:S(2)}) copy-start(f32[8,2,16]{2,1,0:T(2,128)} %coords_ref.2) | copy-start | bytes 3076
  12.1 0.7 copy-start.9
  14.1 10.1 %copy-start.1 = (s32[8,16]{1,0:T(8,128)S(1)}, s32[8,16]{1,0:T(8,128)}, u32[]{:S(2)}) copy-start(s32[8,16]{1,0:T(8,128)} %subgrid_ref.3) | copy-start | bytes 1540
  14.2 14.4 %copy-start = (bf16[1,16,2048]{2,1,0:T(8,128)(2,1)S(1)}, bf16[1,16,2048]{2,1,0:T(8,128)(2,1)}, u32[]{:S(2)}) copy-start(bf16[1,16,2048]{2,1,0:T(8,128)(2,1)} %param.10) | copy-start | bytes 196612
  14.2 24.5 %copy-start.2 = (s32[1,8]{1,0:T(1,128)S(1)}, s32[1,8]{1,0:T(1,128)}, u32[]{:S(2)}) copy-start(s32[1,8]{1,0:T(1,128)} %reader_ref.1) | copy-start | bytes 100
  14.2 29.4 %copy-start.7 = (f32[8,2,16]{2,1,0:T(2,128)S(1)}, f32[8,2,16]{2,1,0:T(2,128)}, u32[]{:S(2)}) copy-start(f32[8,2,16]{2,1,0:T(2,128)} %coords_ref.2) | copy-start | bytes 3076
  14.2 29.4 %copy-start.10 = (f32[1024]{0:T(1024)S(1)}, f32[1024]{0:T(1024)}, u32[]{:S(2)}) copy-start(f32[1024]{0:T(1024)} %param.19) | copy-start | bytes 12292
  20.9 3.3 %collective-permute-start = (bf16[16,4,2048]{2,1,0:T(4,128)(2,1)S(1)}, bf16[16,4,2048]{2,1,0:T(4,128)(2,1)S(1)}, u32[]{:S(2)}, u32[]{:S(2)}) collective-permute-start(bf16[16,4,2048]{2,1,0:T(4,128)(2,1)S(1)} %all-to-all-done.near_ref), channel_id=1, source_target_pairs={{0,1},{1,0},{2,3},{3,2},{4,5},{5,4},{6,7},{7,6},{8,9},{9,8},{10,11... | collective-permute-start | bytes 786440 | tf_op jit(solution)/shard_map/ppermute | solution.py:371
  24.8 8.0 %collective-permute-start.5 = (bf16[2,256,128]{2,1,0:T(8,128)(2,1)S(1)}, bf16[2,256,128]{2,1,0:T(8,128)(2,1)S(1)}, u32[]{:S(2)}, u32[]{:S(2)}) collective-permute-start(bf16[2,256,128]{2,1,0:T(8,128)(2,1)S(1)} %get-tuple-element.48), channel_id=1, source_target_pairs={{0,128},{64,192},{128,0},{192,64},{1,129},{65,193},{129,1},{193,65... | collective-permute-start | bytes 393224 | tf_op jit(solution)/shard_map/image_sum/ppermute | solution.py:366
  27.8 6.5 %collective-permute-start.6 = (bf16[2,256,128]{2,1,0:T(8,128)(2,1)S(1)}, bf16[2,256,128]{2,1,0:T(8,128)(2,1)S(1)}, u32[]{:S(2)}, u32[]{:S(2)}) collective-permute-start(bf16[2,256,128]{2,1,0:T(8,128)(2,1)S(1)} %get-tuple-element.49), channel_id=1, source_target_pairs={{0,64},{64,0},{128,192},{192,128},{1,65},{65,1},{129,193},{193,129... | collective-permute-start | bytes 393224 | tf_op jit(solution)/shard_map/image_sum/ppermute | solution.py:366
  28.2 6.1 %collective-permute-start.7 = (bf16[2,256,128]{2,1,0:T(8,128)(2,1)S(1)}, bf16[2,256,128]{2,1,0:T(8,128)(2,1)S(1)}, u32[]{:S(2)}, u32[]{:S(2)}) collective-permute-start(bf16[2,256,128]{2,1,0:T(8,128)(2,1)S(1)} %get-tuple-element.50), channel_id=1, source_target_pairs={{0,192},{64,128},{128,64},{192,0},{1,193},{65,129},{129,65},{193,1... | collective-permute-start | bytes 393224 | tf_op jit(solution)/shard_map/image_sum/ppermute | solution.py:366
  28.6 10.0 %collective-permute-start.1 = (bf16[16,2048]{1,0:T(8,128)(2,1)S(1)}, bf16[16,2048]{1,0:T(8,128)(2,1)S(1)}, u32[]{:S(2)}, u32[]{:S(2)}) collective-permute-start(bf16[16,2048]{1,0:T(8,128)(2,1)S(1)} %bitcast.5), channel_id=1, source_target_pairs={{0,32},{32,0},{1,33},{33,1},{2,34},{34,2},{3,35},{35,3},{4,36},{36... | collective-permute-start | bytes 196616 | tf_op jit(solution)/shard_map/visible_route/ppermute | solution.py:371
  34.4 10.9 %collective-permute-start.8 = (f32[256,128]{1,0:T(8,128)S(1)}, f32[256,128]{1,0:T(8,128)S(1)}, u32[]{:S(2)}, u32[]{:S(2)}) collective-permute-start(f32[256,128]{1,0:T(8,128)S(1)} %get-tuple-element.53), channel_id=1, source_target_pairs={{0,32},{32,0},{1,33},{33,1},{2,34},{34,2},{3,35},{35,3},{4,36},{36... | collective-permute-start | bytes 393224 | tf_op jit(solution)/shard_map/image_sum/ppermute | solution.py:371
  39.3 7.7 %collective-permute-start.2 = (bf16[16,2048]{1,0:T(8,128)(2,1)S(1)}, bf16[16,2048]{1,0:T(8,128)(2,1)S(1)}, u32[]{:S(2)}, u32[]{:S(2)}) collective-permute-start(bf16[16,2048]{1,0:T(8,128)(2,1)S(1)} %get-tuple-element.44), channel_id=1, source_target_pairs={{0,64},{64,0},{128,192},{192,128},{1,65},{65,1},{129,193},{193,129... | collective-permute-start | bytes 196616 | tf_op jit(solution)/shard_map/ppermute | solution.py:366
  40.6 6.4 %collective-permute-start.3 = (bf16[16,2048]{1,0:T(8,128)(2,1)S(1)}, bf16[16,2048]{1,0:T(8,128)(2,1)S(1)}, u32[]{:S(2)}, u32[]{:S(2)}) collective-permute-start(bf16[16,2048]{1,0:T(8,128)(2,1)S(1)} %get-tuple-element.45), channel_id=1, source_target_pairs={{0,128},{64,192},{128,0},{192,64},{1,129},{65,193},{129,1},{193,65... | collective-permute-start | bytes 196616 | tf_op jit(solution)/shard_map/ppermute | solution.py:366
  43.6 4.5 %collective-permute-start.4 = (bf16[16,2048]{1,0:T(8,128)(2,1)S(1)}, bf16[16,2048]{1,0:T(8,128)(2,1)S(1)}, u32[]{:S(2)}, u32[]{:S(2)}) collective-permute-start(bf16[16,2048]{1,0:T(8,128)(2,1)S(1)} %get-tuple-element.46), channel_id=1, source_target_pairs={{0,192},{64,128},{128,64},{192,0},{1,193},{65,129},{129,65},{193,1... | collective-permute-start | bytes 196616 | tf_op jit(solution)/shard_map/ppermute | solution.py:366
  49.3 7.8 %collective-permute-start.9 = (bf16[256,128]{1,0:T(8,128)(2,1)S(1)}, bf16[256,128]{1,0:T(8,128)(2,1)S(1)}, u32[]{:S(2)}, u32[]{:S(2)}) collective-permute-start(bf16[256,128]{1,0:T(8,128)(2,1)S(1)} %grid.1.refs_0_), channel_id=1, source_target_pairs={{0,32},{32,0},{1,33},{33,1},{2,34},{34,2},{3,35},{35,3},{4,36},{36... | collective-permute-start | bytes 196616 | tf_op jit(solution)/shard_map/grid_gather/ppermute | solution.py:371
  51.2 9.7 %collective-permute-start.10 = (bf16[256,128]{1,0:T(8,128)(2,1)S(1)}, bf16[256,128]{1,0:T(8,128)(2,1)S(1)}, u32[]{:S(2)}, u32[]{:S(2)}) collective-permute-start(bf16[256,128]{1,0:T(8,128)(2,1)S(1)} %grid.1.refs_0_), channel_id=1, source_target_pairs={{0,64},{64,0},{128,192},{192,128},{1,65},{65,1},{129,193},{193,129... | collective-permute-start | bytes 196616 | tf_op jit(solution)/shard_map/grid_gather/ppermute | solution.py:366
  52.4 9.2 %collective-permute-start.12 = (bf16[256,128]{1,0:T(8,128)(2,1)S(1)}, bf16[256,128]{1,0:T(8,128)(2,1)S(1)}, u32[]{:S(2)}, u32[]{:S(2)}) collective-permute-start(bf16[256,128]{1,0:T(8,128)(2,1)S(1)} %grid.1.refs_0_), channel_id=1, source_target_pairs={{0,128},{64,192},{128,0},{192,64},{1,129},{65,193},{129,1},{193,65... | collective-permute-start | bytes 196616 | tf_op jit(solution)/shard_map/grid_gather/ppermute | solution.py:366
  57.1 4.6 %collective-permute-start.14 = (bf16[256,128]{1,0:T(8,128)(2,1)S(1)}, bf16[256,128]{1,0:T(8,128)(2,1)S(1)}, u32[]{:S(2)}, u32[]{:S(2)}) collective-permute-start(bf16[256,128]{1,0:T(8,128)(2,1)S(1)} %grid.1.refs_0_), channel_id=1, source_target_pairs={{0,192},{64,128},{128,64},{192,0},{1,193},{65,129},{129,65},{193,1... | collective-permute-start | bytes 196616 | tf_op jit(solution)/shard_map/grid_gather/ppermute | solution.py:366
  57.1 4.6 %collective-permute-start.11 = (bf16[256,128]{1,0:T(8,128)(2,1)S(1)}, bf16[256,128]{1,0:T(8,128)(2,1)S(1)}, u32[]{:S(2)}, u32[]{:S(2)}) collective-permute-start(bf16[256,128]{1,0:T(8,128)(2,1)S(1)} %collective-permute-done.9.refs_1_), channel_id=1, source_target_pairs={{0,64},{64,0},{128,192},{192,128},{1,65},{65,1},{129,193},{193,129... | collective-permute-start | bytes 196616 | tf_op jit(solution)/shard_map/grid_gather/ppermute | solution.py:366
  57.1 6.3 %collective-permute-start.13 = (bf16[256,128]{1,0:T(8,128)(2,1)S(1)}, bf16[256,128]{1,0:T(8,128)(2,1)S(1)}, u32[]{:S(2)}, u32[]{:S(2)}) collective-permute-start(bf16[256,128]{1,0:T(8,128)(2,1)S(1)} %collective-permute-done.9.refs_1_), channel_id=1, source_target_pairs={{0,128},{64,192},{128,0},{192,64},{1,129},{65,193},{129,1},{193,65... | collective-permute-start | bytes 196616 | tf_op jit(solution)/shard_map/grid_gather/ppermute | solution.py:366
  61.0 4.3 %collective-permute-start.15 = (bf16[256,128]{1,0:T(8,128)(2,1)S(1)}, bf16[256,128]{1,0:T(8,128)(2,1)S(1)}, u32[]{:S(2)}, u32[]{:S(2)}) collective-permute-start(bf16[256,128]{1,0:T(8,128)(2,1)S(1)} %collective-permute-done.9.refs_1_), channel_id=1, source_target_pairs={{0,192},{64,128},{128,64},{192,0},{1,193},{65,129},{129,65},{193,1... | collective-permute-start | bytes 196616 | tf_op jit(solution)/shard_map/grid_gather/ppermute | solution.py:366
  65.8 5.2 %collective-permute-start.16 = (bf16[64,2048]{1,0:T(8,128)(2,1)S(1)}, bf16[64,2048]{1,0:T(8,128)(2,1)S(1)}, u32[]{:S(2)}, u32[]{:S(2)}) collective-permute-start(bf16[64,2048]{1,0:T(8,128)(2,1)S(1)} %regrid_far.1), channel_id=1, source_target_pairs={{0,1},{1,0},{2,3},{3,2},{4,5},{5,4},{6,7},{7,6},{8,9},{9,8},{10,11... | collective-permute-start | bytes 786440 | tf_op jit(solution)/shard_map/dirty_scatter/ppermute | solution.py:371
  71.0 4.7 %collective-permute-start.17 = (bf16[16,2048]{1,0:T(8,128)(2,1)S(1)}, bf16[16,2048]{1,0:T(8,128)(2,1)S(1)}, u32[]{:S(2)}, u32[]{:S(2)}) collective-permute-start(bf16[16,2048]{1,0:T(8,128)(2,1)S(1)} %get-tuple-element.63), channel_id=1, source_target_pairs={{0,16},{8,24},{16,0},{24,8},{1,17},{9,25},{17,1},{25,9},{2,18},{10... | collective-permute-start | bytes 196616 | tf_op jit(solution)/shard_map/dirty_scatter/ppermute | solution.py:366
  71.6 4.1 %collective-permute-start.18 = (bf16[16,2048]{1,0:T(8,128)(2,1)S(1)}, bf16[16,2048]{1,0:T(8,128)(2,1)S(1)}, u32[]{:S(2)}, u32[]{:S(2)}) collective-permute-start(bf16[16,2048]{1,0:T(8,128)(2,1)S(1)} %get-tuple-element.64), channel_id=1, source_target_pairs={{0,8},{8,0},{16,24},{24,16},{1,9},{9,1},{17,25},{25,17},{2,10},{10... | collective-permute-start | bytes 196616 | tf_op jit(solution)/shard_map/dirty_scatter/ppermute | solution.py:366
  72.0 5.3 %collective-permute-start.19 = (bf16[16,2048]{1,0:T(8,128)(2,1)S(1)}, bf16[16,2048]{1,0:T(8,128)(2,1)S(1)}, u32[]{:S(2)}, u32[]{:S(2)}) collective-permute-start(bf16[16,2048]{1,0:T(8,128)(2,1)S(1)} %get-tuple-element.65), channel_id=1, source_target_pairs={{0,24},{8,16},{16,8},{24,0},{1,25},{9,17},{17,9},{25,1},{2,26},{10... | collective-permute-start | bytes 196616 | tf_op jit(solution)/shard_map/dirty_scatter/ppermute | solution.py:366
  77.3 4.7 %collective-permute-start.20 = (f32[4,2048]{1,0:T(4,128)S(1)}, f32[4,2048]{1,0:T(4,128)S(1)}, u32[]{:S(2)}, u32[]{:S(2)}) collective-permute-start(f32[4,2048]{1,0:T(4,128)S(1)} %get-tuple-element.67), channel_id=1, source_target_pairs={{0,6},{2,4},{4,2},{6,0},{1,7},{3,5},{5,3},{7,1},{8,14},{10,12},{12... | collective-permute-start | bytes 98312 | tf_op jit(solution)/shard_map/dirty_scatter/ppermute | solution.py:366
  77.4 4.6 %collective-permute-start.21 = (f32[4,2048]{1,0:T(4,128)S(1)}, f32[4,2048]{1,0:T(4,128)S(1)}, u32[]{:S(2)}, u32[]{:S(2)}) collective-permute-start(f32[4,2048]{1,0:T(4,128)S(1)} %get-tuple-element.68), channel_id=1, source_target_pairs={{0,4},{2,6},{4,0},{6,2},{1,5},{3,7},{5,1},{7,3},{8,12},{10,14},{12... | collective-permute-start | bytes 98312 | tf_op jit(solution)/shard_map/dirty_scatter/ppermute | solution.py:366
  78.7 3.7 %collective-permute-start.22 = (f32[4,2048]{1,0:T(4,128)S(1)}, f32[4,2048]{1,0:T(4,128)S(1)}, u32[]{:S(2)}, u32[]{:S(2)}) collective-permute-start(f32[4,2048]{1,0:T(4,128)S(1)} %get-tuple-element.69), channel_id=1, source_target_pairs={{0,2},{2,0},{4,6},{6,4},{1,3},{3,1},{5,7},{7,5},{8,10},{10,8},{12,... | collective-permute-start | bytes 98312 | tf_op jit(solution)/shard_map/dirty_scatter/ppermute | solution.py:366
